TPU v7x, 128 devices: a whole 4x4x4 slice. The times are simulated.
128 devices in a mesh: dp: 2 (over core), ctx: 16 (over z, x), tp: 4 (over y).
Axes of the slice: x: 4, y: 4, z: 4, core: 2. Of those that a mesh axis runs over, the one named last changes fastest.
Arguments:
- tokens: bfloat16 [8192, 4096], P(('ctx', 'tp'), 'dp'), may hold values from -6 to 6
- cotangent: bfloat16 [8192, 4096], P(('ctx', 'tp'), 'dp'), may hold values from -0.29882812 to 0.29882812
- probs: bfloat16 [8192, 8], P(('ctx', 'tp')), may hold values from 0.019897461 to 0.59765625
- expert_ids: int32 [8192, 8], P(('ctx', 'tp')), may hold values from 0 to 63, all different within a row; in each aligned block of 128 rows (0 to 127, 128 to 255, ...) at most 18 rows name the same one
- gate_weight: bfloat16 [64, 4096, 768], P(('ctx', 'tp'), 'dp'), may hold values from -0.09375 to 0.09375
- up_weight: bfloat16 [64, 4096, 768], P(('ctx', 'tp'), 'dp'), may hold values from -0.09375 to 0.09375
- down_weight: bfloat16 [64, 768, 4096], P(('ctx', 'tp'), None, 'dp'), may hold values from -0.21875 to 0.21875
Outputs:
- grad_tokens: bfloat16 [8192, 4096], P(('ctx', 'tp'), 'dp')
- grad_probs: bfloat16 [8192, 8], P(('ctx', 'tp'))
- grad_gate: bfloat16 [64, 4096, 768], P(('ctx', 'tp'), 'dp')
- grad_up: bfloat16 [64, 4096, 768], P(('ctx', 'tp'), 'dp')
- grad_down: bfloat16 [64, 768, 4096], P(('ctx', 'tp'), None, 'dp')
Inputs may be any that keep to these rules, and one draw needn't show every extreme that they name: `expert_ids`: each row names 8 different experts; among the tokens of one index of ctx+tp no expert is named by more than 18 rows, and in every draw some expert is named exactly 18 times in some block.
All inputs are finite; a program needn't handle non-finite values.
Results may differ from a plain program's by a relative error of at most 0.023.
Values may be sent and summed in bfloat16 or wider, within the bound.
No kernel may reach another device: no remote copies, remote signals or barrier semaphores. Data moves between devices by JAX's collectives and lax.ppermute only.
A program may use at most 192 MiB of HBM per device.

v0:
```python
import jax
import jax.numpy as jnp
from jax import lax
from jax.sharding import PartitionSpec as P


def finish(gate_pre, up_pre, back_grad, weight):
    sigmoid_gate = jax.nn.sigmoid(gate_pre)
    silu_gate = gate_pre * sigmoid_gate
    activation = silu_gate * up_pre
    prob_grad = jnp.sum(activation * back_grad, axis=-1).astype(jnp.bfloat16)
    act_grad = weight[:, None] * back_grad
    gate_grad = (act_grad * up_pre * sigmoid_gate * (1.0 + gate_pre * (1.0 - sigmoid_gate))).astype(
        jnp.bfloat16
    )
    up_grad = (act_grad * silu_gate).astype(jnp.bfloat16)
    weighted = (weight[:, None] * activation).astype(jnp.bfloat16)
    return (weighted, gate_grad, up_grad, prob_grad)


def contract_rows(left, right):
    return lax.dot_general(
        left, right, (((0,), (0,)), ((), ())), preferred_element_type=jnp.float32
    )


def contract_cols(left, right):
    return lax.dot_general(
        left, right, (((1,), (1,)), ((), ())), preferred_element_type=jnp.float32
    )


def per_device(tokens, cotangent, probs, expert_ids, gate_weight, up_weight, down_weight):
    token_count, half_width = tokens.shape
    top_count = expert_ids.shape[1]
    ctx_count = lax.axis_size("ctx")
    tp_count = lax.axis_size("tp")
    experts = ctx_count * tp_count
    pair_count = token_count * top_count
    capacity = (pair_count + experts - 1) // experts + max(1, pair_count // (8 * experts))
    slot_total = experts * capacity
    flat_ids = expert_ids.reshape(pair_count)
    onehot = (flat_ids[:, None] == lax.iota(jnp.int32, experts)[None, :]).astype(jnp.int32)
    slot_rank = jnp.sum((jnp.cumsum(onehot, axis=0) - onehot) * onehot, axis=1)
    slot_index = flat_ids * capacity + slot_rank
    slot_owner = (
        jnp.full((slot_total,), pair_count, jnp.int32)
        .at[slot_index]
        .set(lax.iota(jnp.int32, pair_count))
    )
    live_slot = slot_owner < pair_count
    safe_pair = jnp.minimum(slot_owner, pair_count - 1)
    token_row = safe_pair // top_count
    zero_bf = jnp.zeros((), jnp.bfloat16)
    send_tokens = jnp.where(live_slot[:, None], tokens[token_row], zero_bf)
    send_cot = jnp.where(live_slot[:, None], cotangent[token_row], zero_bf)
    send_probs = jnp.where(live_slot, probs.reshape(pair_count)[safe_pair], zero_bf)
    got_tokens, got_cot, got_probs = (
        lax.all_to_all(
            send_tokens.reshape(experts, capacity, half_width),
            ("ctx", "tp"),
            split_axis=0,
            concat_axis=0,
            tiled=True,
        ),
        lax.all_to_all(
            send_cot.reshape(experts, capacity, half_width),
            ("ctx", "tp"),
            split_axis=0,
            concat_axis=0,
            tiled=True,
        ),
        lax.all_to_all(
            send_probs.reshape(experts, capacity),
            ("ctx", "tp"),
            split_axis=0,
            concat_axis=0,
            tiled=True,
        ),
    )
    got_tokens = got_tokens.reshape(slot_total, half_width)
    got_cot = got_cot.reshape(slot_total, half_width)
    prob_vals = got_probs.reshape(slot_total).astype(jnp.float32)
    gate_mat = gate_weight[0]
    up_mat = up_weight[0]
    down_mat = down_weight[0]
    part_gate = jnp.dot(got_tokens, gate_mat, preferred_element_type=jnp.float32)
    part_up = jnp.dot(got_tokens, up_mat, preferred_element_type=jnp.float32)
    part_back = contract_cols(got_cot, down_mat)
    gate_pre, up_pre, back_grad = (
        lax.psum(part_gate.astype(jnp.bfloat16), "dp").astype(jnp.float32),
        lax.psum(part_up.astype(jnp.bfloat16), "dp").astype(jnp.float32),
        lax.psum(part_back.astype(jnp.bfloat16), "dp").astype(jnp.float32),
    )
    weighted, gate_grad, up_grad, prob_grad = finish(gate_pre, up_pre, back_grad, prob_vals)
    grad_down = contract_rows(weighted, got_cot).astype(jnp.bfloat16)
    grad_gate = contract_rows(got_tokens, gate_grad).astype(jnp.bfloat16)
    grad_up = contract_rows(got_tokens, up_grad).astype(jnp.bfloat16)
    pair_grad = (contract_cols(gate_grad, gate_mat) + contract_cols(up_grad, up_mat)).astype(
        jnp.bfloat16
    )
    back_rows, back_probs = (
        lax.all_to_all(
            pair_grad.reshape(experts, capacity, half_width),
            ("ctx", "tp"),
            split_axis=0,
            concat_axis=0,
            tiled=True,
        ),
        lax.all_to_all(
            prob_grad.reshape(experts, capacity),
            ("ctx", "tp"),
            split_axis=0,
            concat_axis=0,
            tiled=True,
        ),
    )
    back_rows = back_rows.reshape(slot_total, half_width)
    picked_rows = back_rows[slot_index].reshape(token_count, top_count, half_width)
    grad_tokens = jnp.sum(picked_rows.astype(jnp.float32), axis=1).astype(jnp.bfloat16)
    grad_probs = back_probs.reshape(slot_total)[slot_index].reshape(token_count, top_count)
    return (grad_tokens, grad_probs, grad_gate[None], grad_up[None], grad_down[None])


def solution(mesh):
    return jax.shard_map(
        per_device,
        mesh=mesh,
        in_specs=(
            P(("ctx", "tp"), "dp"),
            P(("ctx", "tp"), "dp"),
            P(("ctx", "tp"), None),
            P(("ctx", "tp"), None),
            P(("ctx", "tp"), "dp", None),
            P(("ctx", "tp"), "dp", None),
            P(("ctx", "tp"), None, "dp"),
        ),
        out_specs=(
            P(("ctx", "tp"), "dp"),
            P(("ctx", "tp"), None),
            P(("ctx", "tp"), "dp", None),
            P(("ctx", "tp"), "dp", None),
            P(("ctx", "tp"), None, "dp"),
        ),
        check_vma=False,
    )
```

profile of v0, /device:TPU:34, one launch (start us, length us, event | category | flops | bytes accessed | tf_op | source)
XLA Modules:
  0.0 506.1 jit_solution(4612757379960756038)
XLA Ops:
  7.2 0.8 broadcast_multiply_fusion
  8.0 0.9 copy.20
  9.1 0.8 copy.24
  9.9 0.1 reshape.124
  10.0 0.1 copy.19
  10.2 0.7 fusion.23
  10.9 31.1 %reduce-window.6 = s32[64,8,128]{2,1,0:T(8,128)S(1)} reduce-window(s32[64,8,128]{2,1,0:T(8,128)} %fusion.23, s32[]{:T(128)} %constant.15.clone.1), window={size=1x1x128 pad=0_0x0_0x127_0}, to_apply=%region_0.0 | reduce-window | flops 8323072 | bytes 524292 | tf_op jit(solution)/shard_map/reduce-window
  42.0 0.8 slice.18
  42.9 1.1 copy.22
  44.1 0.1 broadcast_add_fusion
  44.3 4.3 scatter_custom_fusion
  48.7 7.3 %gather_fusion = bf16[1152]{0:T(1024)(128)(2,1)S(1)} fusion(bf16[1024]{0:T(1024)(128)(2,1)S(1)} %reshape.124, s32[2048]{0:T(1024)S(1)} %get-tuple-element.25), kind=kCustom, calls=%fused_computation | custom fusion | bytes 9216 | tf_op jit(solution)/shard_map/gather | solution.py:57
  56.0 0.1 broadcast_in_dim.48
  56.1 11.8 %gather_fusion.2 = bf16[1152,2048]{1,0:T(8,128)(2,1)} fusion(bf16[128,2048]{1,0:T(8,128)(2,1)} %param.7, s32[2048]{0:T(1024)S(1)} %get-tuple-element.24), kind=kCustom, calls=%fused_computation.2 | custom fusion | bytes 9441792 | tf_op jit(solution)/shard_map/gather | solution.py:55
  67.9 7.6 %gather.23 = bf16[64,18,2048]{2,1,0:T(8,128)(2,1)} reshape(bf16[1152,2048]{1,0:T(8,128)(2,1)} %gather_fusion.2) | data formatting | bytes 9437184 | tf_op jit(solution)/shard_map/gather | solution.py:55
  75.5 11.8 %gather_fusion.1 = bf16[1152,2048]{1,0:T(8,128)(2,1)} fusion(bf16[128,2048]{1,0:T(8,128)(2,1)} %param.8, s32[2048]{0:T(1024)S(1)} %get-tuple-element.24), kind=kCustom, calls=%fused_computation.1 | custom fusion | bytes 9441792 | tf_op jit(solution)/shard_map/gather | solution.py:56
  87.2 7.6 %gather.21 = bf16[64,18,2048]{2,1,0:T(8,128)(2,1)} reshape(bf16[1152,2048]{1,0:T(8,128)(2,1)} %gather_fusion.1) | data formatting | bytes 9437184 | tf_op jit(solution)/shard_map/gather | solution.py:56
  94.8 8.2 %broadcast_select_fusion.1 = (bf16[64,18,2048]{2,1,0:T(8,128)(2,1)}, bf16[64,18,2048]{2,1,0:T(8,128)(2,1)S(1)}) fusion(bf16[64,18,2048]{2,1,0:T(8,128)(2,1)} %gather.21, pred[64,18]{1,0:T(8,128)(4,1)S(1)} %broadcast_in_dim.48, bf16[64,18,2048]{2,1,0:T(8,128)(2,1)} %gather.23), kind=kLoop, calls=%fused_computation.8 | loop fusion | flops 4718592 | bytes 18875520 | tf_op jit(solution)/shard_map/jit(_where)/select_n | solution.py:56
  103.1 85.6 %all_to_all.31 = bf16[64,18,2048]{2,1,0:T(8,128)(2,1)} all-to-all(bf16[64,18,2048]{2,1,0:T(8,128)(2,1)S(1)} %get-tuple-element.21), channel_id=1, replica_groups=mesh['dp'=2,'ctx'=16,'tp'=4] {'ctx','tp'}, dimensions={0} | all-to-all | bytes 9437184 | tf_op jit(solution)/shard_map/all_to_all | solution.py:59
  188.7 6.9 %all-to-all-start.1 = ((bf16[64,18,2048]{2,1,0:T(8,128)(2,1)}), bf16[64,18,2048]{2,1,0:T(8,128)(2,1)}, u32[]{:S(2)}, u32[]{:S(2)}) async-start(bf16[64,18,2048]{2,1,0:T(8,128)(2,1)} %get-tuple-element.20), calls=%async_computation.1 | async-start | bytes 12582912 | tf_op jit(solution)/shard_map/all_to_all | solution.py:66
  195.6 0.2 all-reduce.3.cloned.1.call-start
  195.9 7.7 %reshape.126 = bf16[1152,2048]{1,0:T(8,128)(2,1)} reshape(bf16[64,18,2048]{2,1,0:T(8,128)(2,1)} %all_to_all.31) | data formatting | bytes 9437184 | tf_op jit(solution)/shard_map/reshape | solution.py:81
  203.6 7.5 %convolution_convert_fusion.3 = bf16[1152,768]{1,0:T(8,128)(2,1)} fusion(bf16[1152,2048]{1,0:T(8,128)(2,1)} %reshape.126, bf16[1,2048,768]{2,1,0:T(8,128)(2,1)S(1)} %copy-done), kind=kOutput, calls=%fused_computation.31 | convolution fusion | flops 3624763392 | bytes 9633792 | tf_op jit(solution)/shard_map/dot_general | solution.py:87
  211.1 4.9 convolution_convert_fusion.4
  216.1 63.0 %all-to-all-done.1 = bf16[64,18,2048]{2,1,0:T(8,128)(2,1)} async-done(((bf16[64,18,2048]{2,1,0:T(8,128)(2,1)}), bf16[64,18,2048]{2,1,0:T(8,128)(2,1)}, u32[]{:S(2)}, u32[]{:S(2)}) %all-to-all-start.1) | async-done | bytes 4718624 | tf_op jit(solution)/shard_map/all_to_all | solution.py:66
  279.1 7.8 %reshape.125 = bf16[1152,2048]{1,0:T(8,128)(2,1)} reshape(bf16[64,18,2048]{2,1,0:T(8,128)(2,1)} %all-to-all-done.1) | data formatting | bytes 9437184 | tf_op jit(solution)/shard_map/reshape | solution.py:82
  286.8 8.4 %convolution_convert_fusion.5 = bf16[1152,768]{1,0:T(8,128)(2,1)} fusion(bf16[1152,2048]{1,0:T(8,128)(2,1)} %reshape.125, bf16[1,768,2048]{2,1,0:T(8,128)(2,1)} %param.13), kind=kOutput, calls=%fused_computation.33 | convolution fusion | flops 3624763392 | bytes 9633792 | tf_op jit(solution)/shard_map/dot_general | solution.py:28
  295.3 0.2 all_to_all.25
  295.4 16.9 %all_to_all.32 = bf16[64,1,18]{2,1,0:T(2,128)(2,1)S(1)} all-to-all(bf16[64,1,18]{2,1,0:T(2,128)(2,1)S(1)} %all_to_all.25), channel_id=1, replica_groups=mesh['dp'=2,'ctx'=16,'tp'=4] {'ctx','tp'}, dimensions={0} | all-to-all | bytes 4608 | tf_op jit(solution)/shard_map/all_to_all | solution.py:73
  312.4 0.1 reshape.132
  312.6 19.3 %all-reduce.3.cloned.1.call-done = (bf16[1152,768]{1,0:T(8,128)(2,1)}, bf16[1152,768]{1,0:T(8,128)(2,1)}, bf16[1152,768]{1,0:T(8,128)(2,1)}) async-done(((bf16[1152,768]{1,0:T(8,128)(2,1)}, bf16[1152,768]{1,0:T(8,128)(2,1)}, bf16[1152,768]{1,0:T(8,128)(2,1)}), (bf16[1152,768]{1,0:T(8,128)(2,1)}, bf16[1152,768]{1,0:T(8,128)(2,1)}, bf16[1152,768]{1,0:T(8,128)(2,1)})) %all-reduce.3.cloned.1.call-update) | async-done | bytes 5308432 | tf_op jit(solution)/shard_map/psum | solution.py:92
  331.9 3.9 fusion.2
  335.8 0.8 convert_element_type.92
  336.6 10.7 %all-to-all-start.4 = ((bf16[64,1,18]{2,1,0:T(2,128)(2,1)}), bf16[64,1,18]{2,1,0:T(2,128)(2,1)S(1)}, u32[]{:S(2)}, u32[]{:S(2)}) async-start(bf16[64,1,18]{2,1,0:T(2,128)(2,1)} %convert_element_type.92), calls=%async_computation.4 | async-start | bytes 65536 | tf_op jit(solution)/shard_map/all_to_all | solution.py:110
  347.3 11.4 %fusion.10 = f32[1152,2048]{1,0:T(8,128)} fusion(bf16[1,2048,768]{2,1,0:T(8,128)(2,1)S(1)} %copy-done, bf16[1152,768]{1,0:T(8,128)(2,1)} %get-tuple-element.15, bf16[1152,768]{1,0:T(8,128)(2,1)} %get-tuple-element.16, bf16[1152,768]{1,0:T(8,128)(2,1)} %get-tuple-element.17, f32[1152]{0:T(1024)S(1)} %reshape.132), kind=kOutput, calls=%fused_computation.34 | convolution fusion | flops 3636264960 | bytes 17895936 | tf_op jit(solution)/shard_map/dot_general | solution.py:28
  358.7 8.7 %add_convert_fusion = bf16[1152,2048]{1,0:T(8,128)(2,1)} fusion(f32[1152,2048]{1,0:T(8,128)} %fusion.10, bf16[1,2048,768]{2,1,0:T(8,128)(2,1)S(1)} %copy-done.9, bf16[1152,768]{1,0:T(8,128)(2,1)S(1)} %copy-done.4, f32[1152]{0:T(1024)S(1)} %reshape.132, bf16[1152,768]{1,0:T(8,128)(2,1)S(1)} %copy-done.6), kind=kOutput, calls=%fused_computation.6 | convolution fusion | flops 3636559872 | bytes 20845056 | tf_op jit(solution)/shard_map/dot_general | solution.py:28
  367.4 7.5 %reshape.127 = bf16[64,18,2048]{2,1,0:T(8,128)(2,1)} reshape(bf16[1152,2048]{1,0:T(8,128)(2,1)} %add_convert_fusion) | data formatting | bytes 9437184 | tf_op jit(solution)/shard_map/reshape | solution.py:104
  374.9 11.1 %all-to-all-start.3 = ((bf16[64,18,2048]{2,1,0:T(8,128)(2,1)}), bf16[64,18,2048]{2,1,0:T(8,128)(2,1)}, u32[]{:S(2)}, u32[]{:S(2)}) async-start(bf16[64,18,2048]{2,1,0:T(8,128)(2,1)} %reshape.127), calls=%async_computation.3 | async-start | bytes 12582912 | tf_op jit(solution)/shard_map/all_to_all | solution.py:103
  386.0 9.5 %fusion.18 = bf16[1,768,2048]{2,1,0:T(8,128)(2,1)} fusion(bf16[1152,2048]{1,0:T(8,128)(2,1)} %reshape.125, bf16[1152,768]{1,0:T(8,128)(2,1)S(1)} %copy-done.3, f32[1152]{0:T(1024)S(1)} %reshape.132, bf16[1152,768]{1,0:T(8,128)(2,1)} %get-tuple-element.17), kind=kOutput, calls=%fused_computation.42 | convolution fusion | flops 3633414144 | bytes 11407872 | tf_op jit(solution)/shard_map/dot_general | solution.py:22
  395.6 9.1 %fusion.17 = bf16[1,2048,768]{2,1,0:T(8,128)(2,1)} fusion(bf16[1152,2048]{1,0:T(8,128)(2,1)} %reshape.126, bf16[1152,768]{1,0:T(8,128)(2,1)S(1)} %copy-done.5, f32[1152]{0:T(1024)S(1)} %reshape.132, bf16[1152,768]{1,0:T(8,128)(2,1)S(1)} %copy-done.7), kind=kOutput, calls=%fused_computation.41 | convolution fusion | flops 3633414144 | bytes 11407872 | tf_op jit(solution)/shard_map/dot_general | solution.py:22
  404.7 7.8 %fusion.16 = bf16[1,2048,768]{2,1,0:T(8,128)(2,1)} fusion(bf16[1152,2048]{1,0:T(8,128)(2,1)S(1)} %bitcast.49, bf16[1152,768]{1,0:T(8,128)(2,1)S(1)} %copy-done.3, bf16[1152,768]{1,0:T(8,128)(2,1)S(1)} %copy-done.5, bf16[1152,768]{1,0:T(8,128)(2,1)S(1)} %copy-done.7, f32[1152]{0:T(1024)S(1)} %reshape.132), kind=kOutput, calls=%fused_computation.40 | convolution fusion | flops 3637837824 | bytes 13177344 | tf_op jit(solution)/shard_map/dot_general | solution.py:22
  412.6 0.1 reshape.130
  412.7 6.8 %gather_fusion.4 = bf16[1024]{0:T(1024)(128)(2,1)S(1)} fusion(bf16[1152]{0:T(1024)(128)(2,1)S(1)} %reshape.130, s32[1024]{0:T(1024)S(1)} %broadcast_clamp_fusion), kind=kCustom, calls=%fused_computation.4 | custom fusion | bytes 8192 | tf_op jit(solution)/shard_map/gather | solution.py:121
  419.6 0.7 copy.27
  420.3 52.7 %all-to-all-done.3 = bf16[64,18,2048]{2,1,0:T(8,128)(2,1)} async-done(((bf16[64,18,2048]{2,1,0:T(8,128)(2,1)}), bf16[64,18,2048]{2,1,0:T(8,128)(2,1)}, u32[]{:S(2)}, u32[]{:S(2)}) %all-to-all-start.3) | async-done | bytes 4718624 | tf_op jit(solution)/shard_map/all_to_all | solution.py:103
  472.9 7.7 %reshape.128 = bf16[1152,2048]{1,0:T(8,128)(2,1)} reshape(bf16[64,18,2048]{2,1,0:T(8,128)(2,1)} %all-to-all-done.3) | data formatting | bytes 9437184 | tf_op jit(solution)/shard_map/reshape | solution.py:118
  480.7 12.2 %gather_fusion.3 = bf16[1024,2048]{1,0:T(8,128)(2,1)} fusion(bf16[1152,2048]{1,0:T(8,128)(2,1)} %reshape.128, s32[1024]{0:T(1024)S(1)} %broadcast_clamp_fusion), kind=kCustom, calls=%fused_computation.3 | custom fusion | bytes 8392704 | tf_op jit(solution)/shard_map/gather | solution.py:119
  492.9 5.9 %bitcast_reduce_fusion = bf16[128,2048]{1,0:T(8,128)(2,1)} fusion(bf16[1024,2048]{1,0:T(8,128)(2,1)} %gather_fusion.3), kind=kLoop, calls=%fused_computation.17 | loop fusion | flops 1835008 | bytes 4718592 | tf_op jit(solution)/shard_map/reduce_sum | solution.py:120
  (43 shorter events, 0.9 us)
Async XLA Ops:
  7.2 196.4 %copy-start = (bf16[1,2048,768]{2,1,0:T(8,128)(2,1)S(1)}, bf16[1,2048,768]{2,1,0:T(8,128)(2,1)}, u32[]{:S(2)}) copy-start(bf16[1,2048,768]{2,1,0:T(8,128)(2,1)} %param.11) | copy-start | bytes 9437188
  188.7 90.4 %all-to-all-start.1 = ((bf16[64,18,2048]{2,1,0:T(8,128)(2,1)}), bf16[64,18,2048]{2,1,0:T(8,128)(2,1)}, u32[]{:S(2)}, u32[]{:S(2)}) async-start(bf16[64,18,2048]{2,1,0:T(8,128)(2,1)} %get-tuple-element.20), calls=%async_computation.1 | async-start | bytes 12582912 | tf_op jit(solution)/shard_map/all_to_all | solution.py:66
  195.6 136.3 %all-reduce.3.cloned.1.call-start = ((), (), s32[]{:S(2)}) async-start(), calls=%async_computation.5 | async-start | bytes 10616832 | tf_op jit(solution)/shard_map/psum | solution.py:92
  203.6 7.5 %copy-start.2 = (bf16[1152,2048]{1,0:T(8,128)(2,1)S(1)}, bf16[1152,2048]{1,0:T(8,128)(2,1)}, u32[]{:S(2)}) copy-start(bf16[1152,2048]{1,0:T(8,128)(2,1)} %reshape.126) | copy-start | bytes 14155780
  203.6 7.5 %copy-start.8 = (bf16[1,2048,768]{2,1,0:T(8,128)(2,1)S(1)}, bf16[1,2048,768]{2,1,0:T(8,128)(2,1)}, u32[]{:S(2)}) copy-start(bf16[1,2048,768]{2,1,0:T(8,128)(2,1)} %param.12) | copy-start | bytes 9437188
  336.6 38.3 %all-to-all-start.4 = ((bf16[64,1,18]{2,1,0:T(2,128)(2,1)}), bf16[64,1,18]{2,1,0:T(2,128)(2,1)S(1)}, u32[]{:S(2)}, u32[]{:S(2)}) async-start(bf16[64,1,18]{2,1,0:T(2,128)(2,1)} %convert_element_type.92), calls=%async_computation.4 | async-start | bytes 65536 | tf_op jit(solution)/shard_map/all_to_all | solution.py:110
  347.2 11.4 %copy-start.4 = (bf16[1152,768]{1,0:T(8,128)(2,1)S(1)}, bf16[1152,768]{1,0:T(8,128)(2,1)}, u32[]{:S(2)}) copy-start(bf16[1152,768]{1,0:T(8,128)(2,1)} %get-tuple-element.16) | copy-start | bytes 5308420
  347.2 11.4 %copy-start.6 = (bf16[1152,768]{1,0:T(8,128)(2,1)S(1)}, bf16[1152,768]{1,0:T(8,128)(2,1)}, u32[]{:S(2)}) copy-start(bf16[1152,768]{1,0:T(8,128)(2,1)} %get-tuple-element.17) | copy-start | bytes 5308420
  347.3 11.4 %copy-start.9 = (bf16[1,2048,768]{2,1,0:T(8,128)(2,1)S(1)}, bf16[1,2048,768]{2,1,0:T(8,128)(2,1)}, u32[]{:S(2)}) copy-start(bf16[1,2048,768]{2,1,0:T(8,128)(2,1)} %param.12) | copy-start | bytes 9437188
  374.9 11.1 %copy-start.3 = (bf16[1152,768]{1,0:T(8,128)(2,1)S(1)}, bf16[1152,768]{1,0:T(8,128)(2,1)}, u32[]{:S(2)}) copy-start(bf16[1152,768]{1,0:T(8,128)(2,1)} %get-tuple-element.15) | copy-start | bytes 5308420
  374.9 98.0 %all-to-all-start.3 = ((bf16[64,18,2048]{2,1,0:T(8,128)(2,1)}), bf16[64,18,2048]{2,1,0:T(8,128)(2,1)}, u32[]{:S(2)}, u32[]{:S(2)}) async-start(bf16[64,18,2048]{2,1,0:T(8,128)(2,1)} %reshape.127), calls=%async_computation.3 | async-start | bytes 12582912 | tf_op jit(solution)/shard_map/all_to_all | solution.py:103
  386.0 9.6 %copy-start.5 = (bf16[1152,768]{1,0:T(8,128)(2,1)S(1)}, bf16[1152,768]{1,0:T(8,128)(2,1)}, u32[]{:S(2)}) copy-start(bf16[1152,768]{1,0:T(8,128)(2,1)} %get-tuple-element.16) | copy-start | bytes 5308420
  386.0 9.6 %copy-start.7 = (bf16[1152,768]{1,0:T(8,128)(2,1)S(1)}, bf16[1152,768]{1,0:T(8,128)(2,1)}, u32[]{:S(2)}) copy-start(bf16[1152,768]{1,0:T(8,128)(2,1)} %get-tuple-element.17) | copy-start | bytes 5308420
  386.0 18.6 %slice-start = ((s8[4718592]{0:T(1024)(128)(4,1)}), s8[4194304]{0:T(1024)(128)(4,1)S(1)}, s32[]{:S(2)}) async-start(s8[4718592]{0:T(1024)(128)(4,1)} %bitcast.48), calls=%async_computation.6 | async-start | bytes 8388608
  395.6 9.1 %slice-start.1 = ((s8[4718592]{0:T(1024)(128)(4,1)}), s8[524288]{0:T(1024)(128)(4,1)S(1)}, s32[]{:S(2)}) async-start(s8[4718592]{0:T(1024)(128)(4,1)} %bitcast.48), calls=%async_computation.7 | async-start | bytes 1048576
  480.7 18.1 %copy-start.1 = (bf16[1,2048,768]{2,1,0:T(8,128)(2,1)S(1)}, bf16[1,2048,768]{2,1,0:T(8,128)(2,1)}, u32[]{:S(2)}) copy-start(bf16[1,2048,768]{2,1,0:T(8,128)(2,1)} %param.11) | copy-start | bytes 9437188
Sparse Core Ops, SparseCore 0:
  295.4 36.4 all-reduce.2
where the time goes:
time: 516 us; the launch traced here: 506 us
  waiting for transfers between devices  135 us (26%)
  local copies, waits for them, and re-layouts  106 us (21%)
  blocking collectives  103 us (20%)
  matrix products  67.4 us (13%)
  other arithmetic  51.1 us (10%)
  starting transfers between devices  28.9 us (6%)
  between operations  14.8 us (3%)
    all_to_all x1, blocking collectives, per_device(): lax.all_to_all(send_tokens.reshape(experts, capacity, half_width), ('ctx'...  85.6 us
    all_to_all x1, waiting for transfers between devices, per_device(): lax.all_to_all(send_cot.reshape(experts, capacity, half_width), ('ctx', '...  63 us
    all_to_all x1, waiting for transfers between devices, per_device(): lax.all_to_all(pair_grad.reshape(experts, capacity, half_width), ('ctx',...  52.7 us
    another operation x3, other arithmetic  31.3 us
    dot_general x3, matrix products, contract_cols(): lax.dot_general(left, right, (((1,), (1,)), ((), ())), preferred_element_...  28.5 us
    dot_general x3, matrix products, contract_rows(): lax.dot_general(left, right, (((0,), (0,)), ((), ())), preferred_element_...  26.4 us
    gather x2, local copies, waits for them, and re-layouts, per_device(): send_cot = jnp.where(live_slot[:, None], cotangent[token_row], zero_bf)  19.4 us
    gather x2, local copies, waits for them, and re-layouts, per_device(): send_tokens = jnp.where(live_slot[:, None], tokens[token_row], zero_bf)  19.3 us
  transfers between devices with their start and end apart: 4, of which 3 were waited for; matrix products, arithmetic and copies ran while one was open for 16% of the time, Pallas kernels for 0%

commit v1 on v0

v1 whole, which is shorter than its diff:
```python
import functools

import jax
import jax.numpy as jnp
from jax import lax
from jax.experimental import pallas as pl
from jax.experimental.pallas import tpu as pltpu
from jax.sharding import PartitionSpec as P

BF = jnp.bfloat16
F32 = jnp.float32
LANE = 128
MAIN = 16
EXTRA = 2
PEERS = 16
CAP = MAIN + EXTRA
ROWS = PEERS * CAP
VMEM = 60 * 2**20


def iota(shape, dim):
    return lax.broadcasted_iota(jnp.int32, shape, dim)


def dot(a, b):
    return jnp.dot(a, b, preferred_element_type=F32)


def expert_ranks(ids, experts):
    top, tokens = ids.shape
    expert = iota((experts, tokens), 0)
    hit = jnp.zeros((experts, tokens), F32)
    for k in range(top):
        hit = hit + jnp.where(ids[k : k + 1] == expert, 1.0, 0.0)
    earlier = jnp.where(iota((tokens, tokens), 0) < iota((tokens, tokens), 1), 1.0, 0.0)
    rank = dot(hit.astype(BF), earlier.astype(BF))
    return jnp.where(hit > 0.0, rank, -1.0)


def expert_probs(ids, probs, experts):
    top, tokens = ids.shape
    expert = iota((experts, tokens), 0)
    out = jnp.zeros((experts, tokens), F32)
    for k in range(top):
        out = out + jnp.where(ids[k : k + 1] == expert, probs[k : k + 1], 0.0)
    return out


def by_slot(a):
    return jnp.broadcast_to(a[:, None, :], (PEERS, MAIN, a.shape[1])).reshape(PEERS * MAIN, a.shape[1])


def extra_order(pack):
    shape = (PEERS * MAIN, PEERS * MAIN)
    row, col = iota(shape, 0), iota(shape, 1)
    if pack:
        source = (row % 16) // 2 * 32 + row // 16 * 2 + row % 2
    else:
        source = (row % 32) // 2 * 16 + row // 32 * 2 + row % 2
    return jnp.where(col == source, 1.0, 0.0).astype(BF)


def store_main(out_ref, values):
    for c in range(values.shape[1] // LANE):
        out_ref[:, c * MAIN : (c + 1) * MAIN, :] = values[:, c * LANE : (c + 1) * LANE].reshape(PEERS, MAIN, LANE)


def store_extra(out_ref, values, start):
    for g in range(values.shape[1] // LANE):
        at = start + g * MAIN
        out_ref[:, at : at + MAIN, :] = values[:, g * LANE : (g + 1) * LANE].reshape(PEERS, MAIN, LANE)


def unpack(in_ref, out_ref):
    width = out_ref.shape[1]
    tiles = width // LANE
    for c in range(tiles):
        out_ref[: PEERS * MAIN, c * LANE : (c + 1) * LANE] = in_ref[:, c * MAIN : (c + 1) * MAIN, :].reshape(
            PEERS * MAIN, LANE
        )
    groups = tiles // 8
    start = tiles * MAIN
    extra = jnp.concatenate(
        [
            in_ref[:, start + g * MAIN : start + (g + 1) * MAIN, :].reshape(PEERS * MAIN, LANE)
            for g in range(groups)
        ],
        axis=1,
    )
    ordered = dot(extra_order(False), extra).astype(BF)
    for g in range(groups):
        for c in range(8):
            at = (g * 8 + c) * LANE
            out_ref[PEERS * MAIN :, at : at + LANE] = ordered[
                c * 2 * PEERS : (c + 1) * 2 * PEERS, g * LANE : (g + 1) * LANE
            ]


def pack_kernel(weighted, ids_ref, probs_ref, x_ref, out_ref, rank_ref, prob_ref, side_ref):
    step = pl.program_id(0)
    tokens, width = x_ref.shape
    groups = width // LANE // 8
    experts = rank_ref.shape[0]

    @pl.when(step == 0)
    def _():
        rank_ref[...] = expert_ranks(ids_ref[...], experts)
        if weighted:
            prob_ref[...] = expert_probs(ids_ref[...], probs_ref[...].astype(F32), experts)
        for c in range(8):
            for g in range(groups):
                at = (g * 8 + c) * LANE
                side_ref[c * tokens : (c + 1) * tokens, g * LANE : (g + 1) * LANE] = x_ref[:, at : at + LANE]

    peers = pl.ds(pl.multiple_of(step * PEERS, PEERS), PEERS)
    rank = by_slot(rank_ref[peers, :])
    value = by_slot(prob_ref[peers, :]) if weighted else jnp.ones(rank.shape, F32)
    row = iota(rank.shape, 0)
    main = jnp.where(rank == (row % MAIN).astype(F32), value, 0.0).astype(BF)
    store_main(out_ref, dot(main, x_ref[...]).astype(BF))
    extra = jnp.where(rank == (MAIN + row % EXTRA).astype(F32), value, 0.0)
    column = (row % MAIN) // EXTRA
    spread = jnp.concatenate([jnp.where(column == c, extra, 0.0).astype(BF) for c in range(8)], axis=1)
    store_extra(out_ref, dot(spread, side_ref[...]).astype(BF), width // LANE * MAIN)


def pack(weighted, ids, probs, x, experts):
    tokens, width = x.shape
    rows = width // LANE * CAP
    return pl.pallas_call(
        functools.partial(pack_kernel, weighted),
        grid=(experts // PEERS,),
        out_shape=jax.ShapeDtypeStruct((experts, rows, LANE), BF),
        in_specs=[
            pl.BlockSpec(ids.shape, lambda i: (0, 0)),
            pl.BlockSpec(probs.shape, lambda i: (0, 0)),
            pl.BlockSpec(x.shape, lambda i: (0, 0)),
        ],
        out_specs=pl.BlockSpec((PEERS, rows, LANE), lambda i: (i, 0, 0)),
        scratch_shapes=[
            pltpu.VMEM((experts, tokens), F32),
            pltpu.VMEM((experts, tokens), F32),
            pltpu.VMEM((8 * tokens, width // 8), BF),
        ],
        compiler_params=pltpu.CompilerParams(vmem_limit_bytes=VMEM),
        cost_estimate=pl.CostEstimate(
            flops=4 * experts * MAIN * tokens * width, bytes_accessed=2 * experts * rows * LANE, transcendentals=0
        ),
        name="pack_cotangent" if weighted else "pack_tokens",
    )(ids, probs, x)


def project_kernel(in_ref, *refs):
    count = (len(refs) - 1) // 2
    weights, rows_ref, outs = refs[:count], refs[count], refs[count + 1 :]
    unpack(in_ref, rows_ref)
    for weight, out in zip(weights, outs):
        out[...] = dot(rows_ref[...], weight[...]).astype(BF)


def project(name, got, weights):
    experts, rows, _ = got.shape
    width = rows // CAP * LANE
    hidden = weights[0].shape[1]
    total = experts * CAP
    return pl.pallas_call(
        project_kernel,
        grid=(experts // PEERS,),
        out_shape=[jax.ShapeDtypeStruct((total, width), BF)]
        + [jax.ShapeDtypeStruct((total, hidden), BF) for _ in weights],
        in_specs=[pl.BlockSpec((PEERS, rows, LANE), lambda i: (i, 0, 0))]
        + [pl.BlockSpec(w.shape, lambda i: (0, 0)) for w in weights],
        out_specs=[pl.BlockSpec((ROWS, width), lambda i: (i, 0))]
        + [pl.BlockSpec((ROWS, hidden), lambda i: (i, 0)) for _ in weights],
        compiler_params=pltpu.CompilerParams(vmem_limit_bytes=VMEM),
        cost_estimate=pl.CostEstimate(
            flops=2 * total * width * hidden * len(weights),
            bytes_accessed=2 * (2 * total * width + len(weights) * (width + total) * hidden),
            transcendentals=0,
        ),
        name=name,
    )(got, *weights)


def pair_kernel(gate, gate_far, up, up_far, back, back_far, gate_t, up_t, out_ref, act_ref, gg_ref, ug_ref):
    g = gate[...].astype(F32) + gate_far[...].astype(F32)
    u = up[...].astype(F32) + up_far[...].astype(F32)
    b = back[...].astype(F32) + back_far[...].astype(F32)
    sigmoid = jax.nn.sigmoid(g)
    silu = g * sigmoid
    act = silu * u
    act_ref[...] = act.astype(BF)
    gg_ref[...] = (b * u * sigmoid * (1.0 + g * (1.0 - sigmoid))).astype(BF)
    ug_ref[...] = (b * silu).astype(BF)
    prob_grad = jnp.sum(act * b, axis=1, keepdims=True).astype(BF).astype(F32)
    y = (dot(gg_ref[...], gate_t[...]) + dot(ug_ref[...], up_t[...])).astype(BF)
    width = y.shape[1]
    tiles = width // LANE
    groups = tiles // 8
    store_main(out_ref, y[: PEERS * MAIN])
    extra = jnp.concatenate(
        [
            jnp.concatenate(
                [y[PEERS * MAIN :, (g * 8 + c) * LANE : (g * 8 + c + 1) * LANE] for g in range(groups)], axis=1
            )
            for c in range(8)
        ],
        axis=0,
    )
    store_extra(out_ref, dot(extra_order(True), extra).astype(BF), tiles * MAIN)
    row, lane = iota((ROWS, LANE), 0), iota((ROWS, LANE), 1)
    slot = jnp.where(row < PEERS * MAIN, row % MAIN, MAIN + row % EXTRA)
    by_lane = jnp.where(lane == slot, prob_grad, 0.0).astype(BF)
    peer, of = iota((PEERS, ROWS), 0), iota((PEERS, ROWS), 1)
    owner = jnp.where(of < PEERS * MAIN, of // MAIN, (of - PEERS * MAIN) // EXTRA)
    slots = dot(jnp.where(peer == owner, 1.0, 0.0).astype(BF), by_lane)
    out_ref[:, tiles * CAP :, :] = by_slot(slots).astype(BF).reshape(PEERS, MAIN, LANE)


def pair(gate, gate_far, up, up_far, back, back_far, gate_t, up_t):
    total, hidden = gate.shape
    width = gate_t.shape[1]
    experts = total // CAP
    rows = width // LANE * CAP + MAIN
    block = pl.BlockSpec((ROWS, hidden), lambda i: (i, 0))
    whole = pl.BlockSpec(gate_t.shape, lambda i: (0, 0))
    return pl.pallas_call(
        pair_kernel,
        grid=(experts // PEERS,),
        out_shape=[jax.ShapeDtypeStruct((experts, rows, LANE), BF)]
        + [jax.ShapeDtypeStruct((total, hidden), BF)] * 3,
        in_specs=[block] * 6 + [whole] * 2,
        out_specs=[pl.BlockSpec((PEERS, rows, LANE), lambda i: (i, 0, 0))] + [block] * 3,
        compiler_params=pltpu.CompilerParams(vmem_limit_bytes=VMEM),
        cost_estimate=pl.CostEstimate(
            flops=4 * total * width * hidden,
            bytes_accessed=2 * (total * width + 9 * total * hidden + 2 * width * hidden),
            transcendentals=total * hidden,
        ),
        name="pair_grad",
    )(gate, gate_far, up, up_far, back, back_far, gate_t, up_t)


def combine_kernel(ids_ref, probs_ref, in_ref, slots_ref, out_ref, probs_out_ref, rank_ref, rows_ref, total_ref):
    step = pl.program_id(0)
    experts, tokens = rank_ref.shape

    @pl.when(step == 0)
    def _():
        rank_ref[...] = expert_ranks(ids_ref[...], experts)
        total_ref[...] = jnp.zeros_like(total_ref)

    unpack(in_ref, rows_ref)
    some = rank_ref[pl.ds(pl.multiple_of(step * PEERS, PEERS), PEERS), :]
    rank = by_slot(some)
    row = iota(rank.shape, 0)
    main = jnp.where(rank == (row % MAIN).astype(F32), 1.0, 0.0)
    rank = jnp.broadcast_to(some[:, None, :], (PEERS, 8, tokens)).reshape(PEERS * 8, tokens)
    row = iota(rank.shape, 0)
    extra = jnp.where(rank == (MAIN + row % 8).astype(F32), 1.0, 0.0)
    shape = (PEERS * EXTRA, PEERS * 8)
    keep = jnp.where(iota(shape, 1) == iota(shape, 0) // EXTRA * 8 + iota(shape, 0) % EXTRA, 1.0, 0.0)
    extra = dot(keep.astype(BF), extra.astype(BF))
    which = jnp.concatenate([main, extra], axis=0).astype(BF)
    total_ref[...] += lax.dot_general(which, rows_ref[...], (((0,), (0,)), ((), ())), preferred_element_type=F32)

    @pl.when(step == pl.num_programs(0) - 1)
    def _():
        out_ref[...] = total_ref[...].astype(BF)
        slots = slots_ref[:, 0, :].astype(F32)
        rank = rank_ref[...]
        found = jnp.zeros((experts, tokens), F32)
        for s in range(CAP):
            found = found + jnp.where(rank == float(s), slots[:, s : s + 1], 0.0)
        ids = ids_ref[...]
        expert = iota((experts, tokens), 0)
        grads = [
            jnp.sum(jnp.where(ids[k : k + 1] == expert, found, 0.0), axis=0, keepdims=True)
            for k in range(ids.shape[0])
        ]
        probs_out_ref[...] = (jnp.concatenate(grads, axis=0) / probs_ref[...].astype(F32)).astype(BF)


def combine(ids, probs, got):
    experts, rows, _ = got.shape
    tiles = (rows - MAIN) // CAP
    top, tokens = ids.shape
    width = tiles * LANE
    small = pl.BlockSpec(ids.shape, lambda i: (0, 0))
    return pl.pallas_call(
        combine_kernel,
        grid=(experts // PEERS,),
        out_shape=[jax.ShapeDtypeStruct((tokens, width), BF), jax.ShapeDtypeStruct((top, tokens), BF)],
        in_specs=[
            small,
            small,
            pl.BlockSpec((PEERS, rows, LANE), lambda i: (i, 0, 0)),
            pl.BlockSpec((experts, MAIN, LANE), lambda i: (0, tiles * CAP // MAIN, 0)),
        ],
        out_specs=[pl.BlockSpec((tokens, width), lambda i: (0, 0)), small],
        scratch_shapes=[
            pltpu.VMEM((experts, tokens), F32),
            pltpu.VMEM((ROWS, width), BF),
            pltpu.VMEM((tokens, width), F32),
        ],
        compiler_params=pltpu.CompilerParams(vmem_limit_bytes=VMEM),
        cost_estimate=pl.CostEstimate(
            flops=2 * experts * CAP * tokens * width, bytes_accessed=2 * experts * rows * LANE, transcendentals=0
        ),
        name="combine",
    )(ids, probs, got, got)


def exchange(x):
    return lax.all_to_all(x, ("ctx", "tp"), split_axis=0, concat_axis=0, tiled=True)


def other_core(x):
    return lax.ppermute(x, "dp", [(0, 1), (1, 0)])


def contract_rows(left, right):
    return lax.dot_general(left, right, (((0,), (0,)), ((), ())), preferred_element_type=F32).astype(BF)


def per_device(tokens, cotangent, probs, expert_ids, gate_weight, up_weight, down_weight):
    experts = lax.axis_size("ctx") * lax.axis_size("tp")
    gate_mat, up_mat, down_mat = gate_weight[0], up_weight[0], down_weight[0]
    ids, weights = expert_ids.T, probs.T
    got_tokens = exchange(pack(False, ids, weights, tokens, experts))
    got_cot = exchange(pack(True, ids, weights, cotangent, experts))
    rows, gate, up = project("gate_up", got_tokens, (gate_mat, up_mat))
    gate_far, up_far = other_core(gate), other_core(up)
    cot_rows, back = project("back", got_cot, (down_mat.T,))
    back_far = other_core(back)
    sent, act, gate_grad, up_grad = pair(gate, gate_far, up, up_far, back, back_far, gate_mat.T, up_mat.T)
    got_pairs = exchange(sent)
    grad_down = contract_rows(act, cot_rows)
    grad_gate = contract_rows(rows, gate_grad)
    grad_up = contract_rows(rows, up_grad)
    grad_tokens, grad_probs = combine(ids, weights, got_pairs)
    return (grad_tokens, grad_probs.T, grad_gate[None], grad_up[None], grad_down[None])


def solution(mesh):
    return jax.shard_map(
        per_device,
        mesh=mesh,
        in_specs=(
            P(("ctx", "tp"), "dp"),
            P(("ctx", "tp"), "dp"),
            P(("ctx", "tp"), None),
            P(("ctx", "tp"), None),
            P(("ctx", "tp"), "dp", None),
            P(("ctx", "tp"), "dp", None),
            P(("ctx", "tp"), None, "dp"),
        ),
        out_specs=(
            P(("ctx", "tp"), "dp"),
            P(("ctx", "tp"), None),
            P(("ctx", "tp"), "dp", None),
            P(("ctx", "tp"), "dp", None),
            P(("ctx", "tp"), None, "dp"),
        ),
        check_vma=False,
    )
```

time: 516 us -> 260 us (0.50)
  the two profiles are of different devices: /device:TPU:34 before, /device:TPU:0 now
where the time goes in v1:
time: 260 us; the launch traced here: 259 us
  waiting for transfers between devices  148 us (57%)
  Pallas kernels  52.6 us (20%)
  starting transfers between devices  27.7 us (11%)
  matrix products  19.6 us (8%)
  local copies, waits for them, and re-layouts  10.3 us (4%)
    all_to_all x3, waiting for transfers between devices, exchange(): lax.all_to_all(x, ('ctx', 'tp'), split_axis=0, concat_axis=0, tiled=True)  148 us
    all_to_all x3, starting transfers between devices, exchange(): lax.all_to_all(x, ('ctx', 'tp'), split_axis=0, concat_axis=0, tiled=True)  27.2 us
    pallas_call x2, Pallas kernels, project(): pl.pallas_call(project_kernel, grid=(experts // PEERS,), out_shape=[jax.S...  20.9 us
    dot_general x3, matrix products, contract_rows(): lax.dot_general(left, right, (((0,), (0,)), ((), ())), preferred_element_...  19.6 us
    pallas_call x1, Pallas kernels, pair(): pl.pallas_call(pair_kernel, grid=(experts // PEERS,), out_shape=[jax.Shap...  14.9 us
    unnamed x21, local copies, waits for them, and re-layouts  10.3 us
    pallas_call x2, Pallas kernels, pack(): pl.pallas_call(functools.partial(pack_kernel, weighted), grid=(experts //...  10.2 us
    pallas_call x1, Pallas kernels, combine(): pl.pallas_call(combine_kernel, grid=(experts // PEERS,), out_shape=[jax.S...  6.49 us
  transfers between devices with their start and end apart: 6, of which 3 were waited for; matrix products, arithmetic and copies ran while one was open for 12% of the time, Pallas kernels for 10%

profile of v1, /device:TPU:0, one launch (start us, length us, event | category | flops | bytes accessed | tf_op | source)
XLA Modules:
  0.0 258.5 jit_solution(15314030731490475971)
XLA Ops:
  0.6 5.0 %pack_tokens.1 = bf16[64,288,128]{2,1,0:T(8,128)(2,1)} custom-call(s32[8,128]{1,0:T(8,128)} %bitcast.31, bf16[8,128]{1,0:T(8,128)(2,1)} %bitcast.34, bf16[128,2048]{1,0:T(8,128)(2,1)} %x_ref.2), custom_call_target="tpu_custom_call" | custom-call | flops 1073741824 | bytes 4718592 | tf_op jit(solution)/shard_map/pack_tokens/pallas_call | solution.py:130
  5.6 11.7 %all-to-all-start = ((bf16[64,288,128]{2,1,0:T(8,128)(2,1)}), bf16[64,288,128]{2,1,0:T(8,128)(2,1)}, u32[]{:S(2)}, u32[]{:S(2)}) async-start(bf16[64,288,128]{2,1,0:T(8,128)(2,1)} %pack_tokens.1), calls=%async_computation | async-start | bytes 9437184 | tf_op jit(solution)/shard_map/all_to_all | solution.py:315
  17.4 5.2 %pack_cotangent.1 = bf16[64,288,128]{2,1,0:T(8,128)(2,1)} custom-call(s32[8,128]{1,0:T(8,128)} %bitcast.32, bf16[8,128]{1,0:T(8,128)(2,1)} %bitcast.35, bf16[128,2048]{1,0:T(8,128)(2,1)} %x_ref.3), custom_call_target="tpu_custom_call" | custom-call | flops 1073741824 | bytes 4718592 | tf_op jit(solution)/shard_map/pack_cotangent/pallas_call | solution.py:130
  22.6 0.0 copy-start
  22.6 55.8 %all-to-all-done.in_ref = bf16[64,288,128]{2,1,0:T(8,128)(2,1)} async-done(((bf16[64,288,128]{2,1,0:T(8,128)(2,1)}), bf16[64,288,128]{2,1,0:T(8,128)(2,1)}, u32[]{:S(2)}, u32[]{:S(2)}) %all-to-all-start) | async-done | bytes 4718624 | tf_op jit(solution)/shard_map/all_to_all | solution.py:315
  78.3 6.6 %all-to-all-start.1 = ((bf16[64,288,128]{2,1,0:T(8,128)(2,1)}), bf16[64,288,128]{2,1,0:T(8,128)(2,1)}, u32[]{:S(2)}, u32[]{:S(2)}) async-start(bf16[64,288,128]{2,1,0:T(8,128)(2,1)} %pack_cotangent.1), calls=%async_computation.1 | async-start | bytes 9437184 | tf_op jit(solution)/shard_map/all_to_all | solution.py:315
  85.0 0.0 copy-done
  85.0 2.8 %copy.16 = bf16[1,768,2048]{1,2,0:T(8,128)(2,1)} copy(bf16[1,768,2048]{2,1,0:T(8,128)(2,1)S(1)} %copy-done) | data formatting | bytes 6291456 | tf_op args[6]
  87.8 12.4 %gate_up.1 = (bf16[1152,2048]{1,0:T(8,128)(2,1)}, bf16[1152,768]{1,0:T(8,128)(2,1)}, bf16[1152,768]{1,0:T(8,128)(2,1)}) custom-call(bf16[64,288,128]{2,1,0:T(8,128)(2,1)} %all-to-all-done.in_ref, bf16[2048,768]{1,0:T(8,128)(2,1)} %bitcast.26, bf16[2048,768]{1,0:T(8,128)(2,1)} %bitcast.27), custom_call_target="tpu_custom_call" | custom-call | flops 7247757312 | bytes 19267584 | tf_op jit(solution)/shard_map/gate_up/pallas_call | solution.py:166
  100.2 0.0 collective-permute-start
  100.2 0.5 collective-permute-start.1
  100.7 42.1 %all-to-all-done.1.in_ref = bf16[64,288,128]{2,1,0:T(8,128)(2,1)} async-done(((bf16[64,288,128]{2,1,0:T(8,128)(2,1)}), bf16[64,288,128]{2,1,0:T(8,128)(2,1)}, u32[]{:S(2)}, u32[]{:S(2)}) %all-to-all-start.1) | async-done | bytes 4718624 | tf_op jit(solution)/shard_map/all_to_all | solution.py:315
  142.9 0.0 copy-start.1
  142.9 8.5 %back.1 = (bf16[1152,2048]{1,0:T(8,128)(2,1)}, bf16[1152,768]{1,0:T(8,128)(2,1)}) custom-call(bf16[64,288,128]{2,1,0:T(8,128)(2,1)} %all-to-all-done.1.in_ref, bf16[2048,768]{1,0:T(8,128)(2,1)} %bitcast.28), custom_call_target="tpu_custom_call" | custom-call | flops 3623878656 | bytes 14352384 | tf_op jit(solution)/shard_map/back/pallas_call | solution.py:166
  151.4 0.0 collective-permute-start.2
  151.4 0.0 copy-done.1
  151.4 2.9 %copy.12 = bf16[1,2048,768]{1,2,0:T(8,128)(2,1)} copy(bf16[1,2048,768]{2,1,0:T(8,128)(2,1)S(1)} %copy-done.1) | data formatting | bytes 6291456 | tf_op args[4]
  154.2 4.6 %copy.13 = bf16[1,2048,768]{1,2,0:T(8,128)(2,1)} copy(bf16[1,2048,768]{2,1,0:T(8,128)(2,1)} %param.12) | data formatting | bytes 6291456 | tf_op args[5]
  158.9 0.0 collective-permute-done.gate_far
  158.9 0.0 collective-permute-done.1.up_far
  158.9 0.0 collective-permute-done.2.back_far
  158.9 14.9 %pair_grad.1 = (bf16[64,304,128]{2,1,0:T(8,128)(2,1)}, bf16[1152,768]{1,0:T(8,128)(2,1)}, bf16[1152,768]{1,0:T(8,128)(2,1)}, bf16[1152,768]{1,0:T(8,128)(2,1)}) custom-call(bf16[1152,768]{1,0:T(8,128)(2,1)} %get-tuple-element.16.gate, bf16[1152,768]{1,0:T(8,128)(2,1)} %collective-permute-done.gate_far, bf16[1152,768]{1,0:T(8,128)(2,1)} %get-tuple-element.17.up, ...), custom_call_target="tpu_custom_call" | custom-call | flops 7247757312 | bytes 26935296 | tf_op jit(solution)/shard_map/pair_grad/pallas_call | solution.py:227
  173.8 0.0 copy-start.4
  173.8 0.0 slice-start.2
  173.8 8.8 %all-to-all-start.2 = ((bf16[64,304,128]{2,1,0:T(8,128)(2,1)}), bf16[64,304,128]{2,1,0:T(8,128)(2,1)}, u32[]{:S(2)}, u32[]{:S(2)}) async-start(bf16[64,304,128]{2,1,0:T(8,128)(2,1)} %get-tuple-element.19), calls=%async_computation.2 | async-start | bytes 9961472 | tf_op jit(solution)/shard_map/all_to_all | solution.py:315
  182.7 0.0 copy-done.4
  182.7 0.0 slice-start.3
  182.7 0.0 copy-start.3
  182.7 0.0 slice-start
  182.7 8.3 %fusion = bf16[1,2048,768]{2,1,0:T(8,128)(2,1)} fusion(bf16[1152,2048]{1,0:T(8,128)(2,1)} %get-tuple-element.22, bf16[1152,768]{1,0:T(8,128)(2,1)S(1)} %copy-done.4), kind=kOutput, calls=%fused_computation.3 | convolution fusion | flops 3625451520 | bytes 9633792 | tf_op jit(solution)/shard_map/dot_general | solution.py:323
  191.0 0.0 slice-done.2
  191.0 0.0 slice-done.3
  191.0 0.0 copy-done.3
  191.0 0.0 slice-start.1
  191.0 0.0 copy-start.2
  191.0 5.7 %fusion.1 = bf16[1,2048,768]{2,1,0:T(8,128)(2,1)} fusion(bf16[1152,2048]{1,0:T(8,128)(2,1)S(1)} %bitcast.41, bf16[1152,768]{1,0:T(8,128)(2,1)S(1)} %copy-done.3), kind=kOutput, calls=%fused_computation.4 | convolution fusion | flops 3625451520 | bytes 9633792 | tf_op jit(solution)/shard_map/dot_general | solution.py:323
  196.7 0.0 slice-done
  196.7 0.0 slice-done.1
  196.8 0.0 copy-done.2
  196.8 5.6 %fusion.2 = bf16[1,768,2048]{2,1,0:T(8,128)(2,1)} fusion(bf16[1152,768]{1,0:T(8,128)(2,1)S(1)} %copy-done.2, bf16[1152,2048]{1,0:T(8,128)(2,1)S(1)} %bitcast.39), kind=kOutput, calls=%fused_computation.5 | convolution fusion | flops 3625451520 | bytes 9633792 | tf_op jit(solution)/shard_map/dot_general | solution.py:323
  202.4 49.6 %all-to-all-done.2.in_ref.slots_ref = bf16[64,304,128]{2,1,0:T(8,128)(2,1)} async-done(((bf16[64,304,128]{2,1,0:T(8,128)(2,1)}), bf16[64,304,128]{2,1,0:T(8,128)(2,1)}, u32[]{:S(2)}, u32[]{:S(2)}) %all-to-all-start.2) | async-done | bytes 4980768 | tf_op jit(solution)/shard_map/all_to_all | solution.py:315
  252.0 6.5 %combine.1 = (bf16[128,2048]{1,0:T(8,128)(2,1)}, bf16[8,128]{1,0:T(8,128)(2,1)}) custom-call(s32[8,128]{1,0:T(8,128)} %bitcast.33, bf16[8,128]{1,0:T(8,128)(2,1)} %bitcast.36, bf16[64,304,128]{2,1,0:T(8,128)(2,1)} %all-to-all-done.2.in_ref.slots_ref, bf16[64,304,128]{2,1,0:T(8,128)(2,1)} %all-to-all-done.2.in_ref.slots_ref), custom_call_target="tpu_custom_call" | custom-call | flops 603979776 | bytes 4980736 | tf_op jit(solution)/shard_map/combine/pallas_call | solution.py:290
  (2 shorter events, 0.0 us)
Async XLA Ops:
  5.6 72.7 %all-to-all-start = ((bf16[64,288,128]{2,1,0:T(8,128)(2,1)}), bf16[64,288,128]{2,1,0:T(8,128)(2,1)}, u32[]{:S(2)}, u32[]{:S(2)}) async-start(bf16[64,288,128]{2,1,0:T(8,128)(2,1)} %pack_tokens.1), calls=%async_computation | async-start | bytes 9437184 | tf_op jit(solution)/shard_map/all_to_all | solution.py:315
  22.6 62.4 %copy-start = (bf16[1,768,2048]{2,1,0:T(8,128)(2,1)S(1)}, bf16[1,768,2048]{2,1,0:T(8,128)(2,1)}, u32[]{:S(2)}) copy-start(bf16[1,768,2048]{2,1,0:T(8,128)(2,1)} %param.13) | copy-start | bytes 9437188
  78.3 64.5 %all-to-all-start.1 = ((bf16[64,288,128]{2,1,0:T(8,128)(2,1)}), bf16[64,288,128]{2,1,0:T(8,128)(2,1)}, u32[]{:S(2)}, u32[]{:S(2)}) async-start(bf16[64,288,128]{2,1,0:T(8,128)(2,1)} %pack_cotangent.1), calls=%async_computation.1 | async-start | bytes 9437184 | tf_op jit(solution)/shard_map/all_to_all | solution.py:315
  100.2 58.6 %collective-permute-start = (bf16[1152,768]{1,0:T(8,128)(2,1)}, bf16[1152,768]{1,0:T(8,128)(2,1)}, u32[]{:S(2)}, u32[]{:S(2)}) collective-permute-start(bf16[1152,768]{1,0:T(8,128)(2,1)} %get-tuple-element.16.gate), channel_id=1, source_target_pairs={{0,64},{64,0},{1,65},{65,1},{2,66},{66,2},{3,67},{67,3},{4,68},{68... | collective-permute-start | bytes 5308424 | tf_op jit(solution)/shard_map/ppermute | solution.py:319
  100.2 58.6 %collective-permute-start.1 = (bf16[1152,768]{1,0:T(8,128)(2,1)}, bf16[1152,768]{1,0:T(8,128)(2,1)}, u32[]{:S(2)}, u32[]{:S(2)}) collective-permute-start(bf16[1152,768]{1,0:T(8,128)(2,1)} %get-tuple-element.17.up), channel_id=1, source_target_pairs={{0,64},{64,0},{1,65},{65,1},{2,66},{66,2},{3,67},{67,3},{4,68},{68... | collective-permute-start | bytes 5308424 | tf_op jit(solution)/shard_map/ppermute | solution.py:319
  142.9 8.5 %copy-start.1 = (bf16[1,2048,768]{2,1,0:T(8,128)(2,1)S(1)}, bf16[1,2048,768]{2,1,0:T(8,128)(2,1)}, u32[]{:S(2)}) copy-start(bf16[1,2048,768]{2,1,0:T(8,128)(2,1)} %param.11) | copy-start | bytes 9437188
  151.4 7.5 %collective-permute-start.2 = (bf16[1152,768]{1,0:T(8,128)(2,1)}, bf16[1152,768]{1,0:T(8,128)(2,1)}, u32[]{:S(2)}, u32[]{:S(2)}) collective-permute-start(bf16[1152,768]{1,0:T(8,128)(2,1)} %get-tuple-element.18.back), channel_id=1, source_target_pairs={{0,64},{64,0},{1,65},{65,1},{2,66},{66,2},{3,67},{67,3},{4,68},{68... | collective-permute-start | bytes 5308424 | tf_op jit(solution)/shard_map/ppermute | solution.py:319
  173.8 8.9 %copy-start.4 = (bf16[1152,768]{1,0:T(8,128)(2,1)S(1)}, bf16[1152,768]{1,0:T(8,128)(2,1)}, u32[]{:S(2)}) copy-start(bf16[1152,768]{1,0:T(8,128)(2,1)} %get-tuple-element.23) | copy-start | bytes 5308420
  173.8 17.1 %slice-start.2 = ((s8[4718592]{0:T(1024)(128)(4,1)}), s8[524288]{0:T(1024)(128)(4,1)S(1)}, s32[]{:S(2)}) async-start(s8[4718592]{0:T(1024)(128)(4,1)} %bitcast.40), calls=%async_computation.5 | async-start | bytes 1048576
  173.8 78.2 %all-to-all-start.2 = ((bf16[64,304,128]{2,1,0:T(8,128)(2,1)}), bf16[64,304,128]{2,1,0:T(8,128)(2,1)}, u32[]{:S(2)}, u32[]{:S(2)}) async-start(bf16[64,304,128]{2,1,0:T(8,128)(2,1)} %get-tuple-element.19), calls=%async_computation.2 | async-start | bytes 9961472 | tf_op jit(solution)/shard_map/all_to_all | solution.py:315
  182.7 8.3 %slice-start.3 = ((s8[4718592]{0:T(1024)(128)(4,1)}), s8[4194304]{0:T(1024)(128)(4,1)S(1)}, s32[]{:S(2)}) async-start(s8[4718592]{0:T(1024)(128)(4,1)} %bitcast.40), calls=%async_computation.6 | async-start | bytes 8388608
  182.7 8.3 %copy-start.3 = (bf16[1152,768]{1,0:T(8,128)(2,1)S(1)}, bf16[1152,768]{1,0:T(8,128)(2,1)}, u32[]{:S(2)}) copy-start(bf16[1152,768]{1,0:T(8,128)(2,1)} %get-tuple-element.24) | copy-start | bytes 5308420
  182.7 14.1 %slice-start = ((s8[4718592]{0:T(1024)(128)(4,1)}), s8[4194304]{0:T(1024)(128)(4,1)S(1)}, s32[]{:S(2)}) async-start(s8[4718592]{0:T(1024)(128)(4,1)} %bitcast.38), calls=%async_computation.3 | async-start | bytes 8388608
  191.0 5.8 %slice-start.1 = ((s8[4718592]{0:T(1024)(128)(4,1)}), s8[524288]{0:T(1024)(128)(4,1)S(1)}, s32[]{:S(2)}) async-start(s8[4718592]{0:T(1024)(128)(4,1)} %bitcast.38), calls=%async_computation.4 | async-start | bytes 1048576
  191.0 5.8 %copy-start.2 = (bf16[1152,768]{1,0:T(8,128)(2,1)S(1)}, bf16[1152,768]{1,0:T(8,128)(2,1)}, u32[]{:S(2)}) copy-start(bf16[1152,768]{1,0:T(8,128)(2,1)} %get-tuple-element.25) | copy-start | bytes 5308420

commit v2 on v1

--- a/solution.py
+++ b/solution.py
@@ -12,10 +12,11 @@
 LANE = 128
 MAIN = 16
 EXTRA = 2
+PACK_PEERS = 32
 PEERS = 16
+SUM_PEERS = 16
 CAP = MAIN + EXTRA
-ROWS = PEERS * CAP
-VMEM = 60 * 2**20
+VMEM = 32 * 2**20
 
 
 def iota(shape, dim):
@@ -46,54 +47,48 @@
     return out
 
 
-def by_slot(a):
-    return jnp.broadcast_to(a[:, None, :], (PEERS, MAIN, a.shape[1])).reshape(PEERS * MAIN, a.shape[1])
-
-
-def extra_order(pack):
-    shape = (PEERS * MAIN, PEERS * MAIN)
+def by_slot(a, slots=MAIN):
+    peers, tokens = a.shape
+    return jnp.broadcast_to(a[:, None, :], (peers, slots, tokens)).reshape(peers * slots, tokens)
+
+
+def extra_order(peers, pack):
+    shape = (peers * MAIN, peers * MAIN)
     row, col = iota(shape, 0), iota(shape, 1)
+    step = peers * EXTRA
     if pack:
-        source = (row % 16) // 2 * 32 + row // 16 * 2 + row % 2
+        source = (row % MAIN) // EXTRA * step + row // MAIN * EXTRA + row % EXTRA
     else:
-        source = (row % 32) // 2 * 16 + row // 32 * 2 + row % 2
+        source = (row % step) // EXTRA * MAIN + row // step * EXTRA + row % EXTRA
     return jnp.where(col == source, 1.0, 0.0).astype(BF)
 
 
 def store_main(out_ref, values):
     for c in range(values.shape[1] // LANE):
-        out_ref[:, c * MAIN : (c + 1) * MAIN, :] = values[:, c * LANE : (c + 1) * LANE].reshape(PEERS, MAIN, LANE)
+        out_ref[:, c * MAIN : (c + 1) * MAIN, :] = values[:, c * LANE : (c + 1) * LANE].reshape(-1, MAIN, LANE)
 
 
 def store_extra(out_ref, values, start):
     for g in range(values.shape[1] // LANE):
         at = start + g * MAIN
-        out_ref[:, at : at + MAIN, :] = values[:, g * LANE : (g + 1) * LANE].reshape(PEERS, MAIN, LANE)
+        out_ref[:, at : at + MAIN, :] = values[:, g * LANE : (g + 1) * LANE].reshape(-1, MAIN, LANE)
 
 
 def unpack(in_ref, out_ref):
-    width = out_ref.shape[1]
-    tiles = width // LANE
+    peers, width = in_ref.shape[0], out_ref.shape[1]
+    tiles, main, step = width // LANE, peers * MAIN, peers * EXTRA
     for c in range(tiles):
-        out_ref[: PEERS * MAIN, c * LANE : (c + 1) * LANE] = in_ref[:, c * MAIN : (c + 1) * MAIN, :].reshape(
-            PEERS * MAIN, LANE
-        )
+        out_ref[:main, c * LANE : (c + 1) * LANE] = in_ref[:, c * MAIN : (c + 1) * MAIN, :].reshape(main, LANE)
     groups = tiles // 8
     start = tiles * MAIN
     extra = jnp.concatenate(
-        [
-            in_ref[:, start + g * MAIN : start + (g + 1) * MAIN, :].reshape(PEERS * MAIN, LANE)
-            for g in range(groups)
-        ],
-        axis=1,
+        [in_ref[:, start + g * MAIN : start + (g + 1) * MAIN, :].reshape(main, LANE) for g in range(groups)], axis=1
     )
-    ordered = dot(extra_order(False), extra).astype(BF)
+    ordered = dot(extra_order(peers, False), extra).astype(BF)
     for g in range(groups):
         for c in range(8):
             at = (g * 8 + c) * LANE
-            out_ref[PEERS * MAIN :, at : at + LANE] = ordered[
-                c * 2 * PEERS : (c + 1) * 2 * PEERS, g * LANE : (g + 1) * LANE
-            ]
+            out_ref[main:, at : at + LANE] = ordered[c * step : (c + 1) * step, g * LANE : (g + 1) * LANE]
 
 
 def pack_kernel(weighted, ids_ref, probs_ref, x_ref, out_ref, rank_ref, prob_ref, side_ref):
@@ -112,7 +107,8 @@
                 at = (g * 8 + c) * LANE
                 side_ref[c * tokens : (c + 1) * tokens, g * LANE : (g + 1) * LANE] = x_ref[:, at : at + LANE]
 
-    peers = pl.ds(pl.multiple_of(step * PEERS, PEERS), PEERS)
+    count = out_ref.shape[0]
+    peers = pl.ds(pl.multiple_of(step * count, count), count)
     rank = by_slot(rank_ref[peers, :])
     value = by_slot(prob_ref[peers, :]) if weighted else jnp.ones(rank.shape, F32)
     row = iota(rank.shape, 0)
@@ -129,14 +125,14 @@
     rows = width // LANE * CAP
     return pl.pallas_call(
         functools.partial(pack_kernel, weighted),
-        grid=(experts // PEERS,),
+        grid=(experts // PACK_PEERS,),
         out_shape=jax.ShapeDtypeStruct((experts, rows, LANE), BF),
         in_specs=[
             pl.BlockSpec(ids.shape, lambda i: (0, 0)),
             pl.BlockSpec(probs.shape, lambda i: (0, 0)),
             pl.BlockSpec(x.shape, lambda i: (0, 0)),
         ],
-        out_specs=pl.BlockSpec((PEERS, rows, LANE), lambda i: (i, 0, 0)),
+        out_specs=pl.BlockSpec((PACK_PEERS, rows, LANE), lambda i: (i, 0, 0)),
         scratch_shapes=[
             pltpu.VMEM((experts, tokens), F32),
             pltpu.VMEM((experts, tokens), F32),
@@ -169,9 +165,9 @@
         out_shape=[jax.ShapeDtypeStruct((total, width), BF)]
         + [jax.ShapeDtypeStruct((total, hidden), BF) for _ in weights],
         in_specs=[pl.BlockSpec((PEERS, rows, LANE), lambda i: (i, 0, 0))]
-        + [pl.BlockSpec(w.shape, lambda i: (0, 0)) for w in weights],
-        out_specs=[pl.BlockSpec((ROWS, width), lambda i: (i, 0))]
-        + [pl.BlockSpec((ROWS, hidden), lambda i: (i, 0)) for _ in weights],
+        + [pl.BlockSpec(memory_space=pltpu.VMEM) for _ in weights],
+        out_specs=[pl.BlockSpec((PEERS * CAP, width), lambda i: (i, 0))]
+        + [pl.BlockSpec((PEERS * CAP, hidden), lambda i: (i, 0)) for _ in weights],
         compiler_params=pltpu.CompilerParams(vmem_limit_bytes=VMEM),
         cost_estimate=pl.CostEstimate(
             flops=2 * total * width * hidden * len(weights),
@@ -182,68 +178,89 @@
     )(got, *weights)
 
 
-def pair_kernel(gate, gate_far, up, up_far, back, back_far, gate_t, up_t, out_ref, act_ref, gg_ref, ug_ref):
+def prepare_kernel(gate, gate_far, up, up_far, act_ref, slope_ref, silu_ref):
     g = gate[...].astype(F32) + gate_far[...].astype(F32)
     u = up[...].astype(F32) + up_far[...].astype(F32)
-    b = back[...].astype(F32) + back_far[...].astype(F32)
     sigmoid = jax.nn.sigmoid(g)
     silu = g * sigmoid
-    act = silu * u
-    act_ref[...] = act.astype(BF)
-    gg_ref[...] = (b * u * sigmoid * (1.0 + g * (1.0 - sigmoid))).astype(BF)
-    ug_ref[...] = (b * silu).astype(BF)
-    prob_grad = jnp.sum(act * b, axis=1, keepdims=True).astype(BF).astype(F32)
+    act_ref[...] = (silu * u).astype(BF)
+    slope_ref[...] = (u * sigmoid * (1.0 + g * (1.0 - sigmoid))).astype(BF)
+    silu_ref[...] = silu.astype(BF)
+
+
+def prepare(gate, gate_far, up, up_far):
+    total, hidden = gate.shape
+    block = pl.BlockSpec((PEERS * CAP, hidden), lambda i: (i, 0))
+    return pl.pallas_call(
+        prepare_kernel,
+        grid=(total // (PEERS * CAP),),
+        out_shape=[jax.ShapeDtypeStruct((total, hidden), BF)] * 3,
+        in_specs=[block] * 4,
+        out_specs=[block] * 3,
+        compiler_params=pltpu.CompilerParams(vmem_limit_bytes=VMEM),
+        cost_estimate=pl.CostEstimate(
+            flops=12 * total * hidden, bytes_accessed=14 * total * hidden, transcendentals=total * hidden
+        ),
+        name="prepare",
+    )(gate, gate_far, up, up_far)
+
+
+def pair_kernel(act, slope, silu, back, back_far, gate_t, up_t, out_ref, gg_ref, ug_ref):
+    peers = out_ref.shape[0]
+    main, total = peers * MAIN, peers * CAP
+    b = back[...].astype(F32) + back_far[...].astype(F32)
+    gg_ref[...] = (b * slope[...].astype(F32)).astype(BF)
+    ug_ref[...] = (b * silu[...].astype(F32)).astype(BF)
+    prob_grad = jnp.sum(act[...].astype(F32) * b, axis=1, keepdims=True)
     y = (dot(gg_ref[...], gate_t[...]) + dot(ug_ref[...], up_t[...])).astype(BF)
-    width = y.shape[1]
-    tiles = width // LANE
+    tiles = y.shape[1] // LANE
     groups = tiles // 8
-    store_main(out_ref, y[: PEERS * MAIN])
+    store_main(out_ref, y[:main])
     extra = jnp.concatenate(
         [
-            jnp.concatenate(
-                [y[PEERS * MAIN :, (g * 8 + c) * LANE : (g * 8 + c + 1) * LANE] for g in range(groups)], axis=1
-            )
+            jnp.concatenate([y[main:, (g * 8 + c) * LANE : (g * 8 + c + 1) * LANE] for g in range(groups)], axis=1)
             for c in range(8)
         ],
         axis=0,
     )
-    store_extra(out_ref, dot(extra_order(True), extra).astype(BF), tiles * MAIN)
-    row, lane = iota((ROWS, LANE), 0), iota((ROWS, LANE), 1)
-    slot = jnp.where(row < PEERS * MAIN, row % MAIN, MAIN + row % EXTRA)
+    store_extra(out_ref, dot(extra_order(peers, True), extra).astype(BF), tiles * MAIN)
+    row, lane = iota((total, LANE), 0), iota((total, LANE), 1)
+    slot = jnp.where(row < main, row % MAIN, MAIN + row % EXTRA)
     by_lane = jnp.where(lane == slot, prob_grad, 0.0).astype(BF)
-    peer, of = iota((PEERS, ROWS), 0), iota((PEERS, ROWS), 1)
-    owner = jnp.where(of < PEERS * MAIN, of // MAIN, (of - PEERS * MAIN) // EXTRA)
+    peer, of = iota((peers, total), 0), iota((peers, total), 1)
+    owner = jnp.where(of < main, of // MAIN, (of - main) // EXTRA)
     slots = dot(jnp.where(peer == owner, 1.0, 0.0).astype(BF), by_lane)
-    out_ref[:, tiles * CAP :, :] = by_slot(slots).astype(BF).reshape(PEERS, MAIN, LANE)
-
-
-def pair(gate, gate_far, up, up_far, back, back_far, gate_t, up_t):
-    total, hidden = gate.shape
+    out_ref[:, tiles * CAP :, :] = by_slot(slots).astype(BF).reshape(peers, MAIN, LANE)
+
+
+def pair(act, slope, silu, back, back_far, gate_t, up_t):
+    total, hidden = act.shape
     width = gate_t.shape[1]
     experts = total // CAP
     rows = width // LANE * CAP + MAIN
-    block = pl.BlockSpec((ROWS, hidden), lambda i: (i, 0))
-    whole = pl.BlockSpec(gate_t.shape, lambda i: (0, 0))
+    block = pl.BlockSpec((PEERS * CAP, hidden), lambda i: (i, 0))
+    whole = pl.BlockSpec(memory_space=pltpu.VMEM)
     return pl.pallas_call(
         pair_kernel,
         grid=(experts // PEERS,),
         out_shape=[jax.ShapeDtypeStruct((experts, rows, LANE), BF)]
-        + [jax.ShapeDtypeStruct((total, hidden), BF)] * 3,
-        in_specs=[block] * 6 + [whole] * 2,
-        out_specs=[pl.BlockSpec((PEERS, rows, LANE), lambda i: (i, 0, 0))] + [block] * 3,
+        + [jax.ShapeDtypeStruct((total, hidden), BF)] * 2,
+        in_specs=[block] * 5 + [whole] * 2,
+        out_specs=[pl.BlockSpec((PEERS, rows, LANE), lambda i: (i, 0, 0))] + [block] * 2,
         compiler_params=pltpu.CompilerParams(vmem_limit_bytes=VMEM),
         cost_estimate=pl.CostEstimate(
             flops=4 * total * width * hidden,
-            bytes_accessed=2 * (total * width + 9 * total * hidden + 2 * width * hidden),
-            transcendentals=total * hidden,
+            bytes_accessed=2 * (total * width + 7 * total * hidden + 2 * width * hidden),
+            transcendentals=0,
         ),
         name="pair_grad",
-    )(gate, gate_far, up, up_far, back, back_far, gate_t, up_t)
+    )(act, slope, silu, back, back_far, gate_t, up_t)
 
 
 def combine_kernel(ids_ref, probs_ref, in_ref, slots_ref, out_ref, probs_out_ref, rank_ref, rows_ref, total_ref):
     step = pl.program_id(0)
     experts, tokens = rank_ref.shape
+    peers = in_ref.shape[0]
 
     @pl.when(step == 0)
     def _():
@@ -251,14 +268,12 @@
         total_ref[...] = jnp.zeros_like(total_ref)
 
     unpack(in_ref, rows_ref)
-    some = rank_ref[pl.ds(pl.multiple_of(step * PEERS, PEERS), PEERS), :]
+    some = rank_ref[pl.ds(pl.multiple_of(step * peers, peers), peers), :]
     rank = by_slot(some)
-    row = iota(rank.shape, 0)
-    main = jnp.where(rank == (row % MAIN).astype(F32), 1.0, 0.0)
-    rank = jnp.broadcast_to(some[:, None, :], (PEERS, 8, tokens)).reshape(PEERS * 8, tokens)
-    row = iota(rank.shape, 0)
-    extra = jnp.where(rank == (MAIN + row % 8).astype(F32), 1.0, 0.0)
-    shape = (PEERS * EXTRA, PEERS * 8)
+    main = jnp.where(rank == (iota(rank.shape, 0) % MAIN).astype(F32), 1.0, 0.0)
+    rank = by_slot(some, 8)
+    extra = jnp.where(rank == (MAIN + iota(rank.shape, 0) % 8).astype(F32), 1.0, 0.0)
+    shape = (peers * EXTRA, peers * 8)
     keep = jnp.where(iota(shape, 1) == iota(shape, 0) // EXTRA * 8 + iota(shape, 0) % EXTRA, 1.0, 0.0)
     extra = dot(keep.astype(BF), extra.astype(BF))
     which = jnp.concatenate([main, extra], axis=0).astype(BF)
@@ -289,18 +304,18 @@
     small = pl.BlockSpec(ids.shape, lambda i: (0, 0))
     return pl.pallas_call(
         combine_kernel,
-        grid=(experts // PEERS,),
+        grid=(experts // SUM_PEERS,),
         out_shape=[jax.ShapeDtypeStruct((tokens, width), BF), jax.ShapeDtypeStruct((top, tokens), BF)],
         in_specs=[
             small,
             small,
-            pl.BlockSpec((PEERS, rows, LANE), lambda i: (i, 0, 0)),
+            pl.BlockSpec((SUM_PEERS, rows, LANE), lambda i: (i, 0, 0)),
             pl.BlockSpec((experts, MAIN, LANE), lambda i: (0, tiles * CAP // MAIN, 0)),
         ],
         out_specs=[pl.BlockSpec((tokens, width), lambda i: (0, 0)), small],
         scratch_shapes=[
             pltpu.VMEM((experts, tokens), F32),
-            pltpu.VMEM((ROWS, width), BF),
+            pltpu.VMEM((SUM_PEERS * CAP, width), BF),
             pltpu.VMEM((tokens, width), F32),
         ],
         compiler_params=pltpu.CompilerParams(vmem_limit_bytes=VMEM),
@@ -330,10 +345,12 @@
     got_tokens = exchange(pack(False, ids, weights, tokens, experts))
     got_cot = exchange(pack(True, ids, weights, cotangent, experts))
     rows, gate, up = project("gate_up", got_tokens, (gate_mat, up_mat))
-    gate_far, up_far = other_core(gate), other_core(up)
-    cot_rows, back = project("back", got_cot, (down_mat.T,))
-    back_far = other_core(back)
-    sent, act, gate_grad, up_grad = pair(gate, gate_far, up, up_far, back, back_far, gate_mat.T, up_mat.T)
+    act, slope, silu = prepare(gate, other_core(gate), up, other_core(up))
+    got_cot, gate_t, up_t, down_t, act, slope, silu = lax.optimization_barrier(
+        (got_cot, gate_mat.T, up_mat.T, down_mat.T, act, slope, silu)
+    )
+    cot_rows, back = project("back", got_cot, (down_t,))
+    sent, gate_grad, up_grad = pair(act, slope, silu, back, other_core(back), gate_t, up_t)
     got_pairs = exchange(sent)
     grad_down = contract_rows(act, cot_rows)
     grad_gate = contract_rows(rows, gate_grad)

time: 260 us -> 255 us (0.981); the launches traced: 259 us -> 250 us
  waiting for transfers between devices: 148 us -> 124 us
  local copies, waits for them, and re-layouts: 10.3 us -> 31.7 us
  Pallas kernels: 52.6 us -> 43.5 us
  matrix products: 19.6 us -> 22.3 us
    all_to_all x3, waiting for transfers between devices: 148 us -> 121 us  [exchange(): lax.all_to_all(x, ('ctx', 'tp'), split_axis=0, concat_axis=0, tiled=True)]
    unnamed x21 -> x57, local copies, waits for them, and re-layouts: 10.3 us -> 31.7 us
    pallas_call x2, Pallas kernels: 10.2 us -> 4.32 us  [pack(): pl.pallas_call(functools.partial(pack_kernel, weighted), grid=(experts //...]
    pallas_call x1, Pallas kernels: 14.9 us -> 10.2 us  [pair(): pl.pallas_call(pair_kernel, grid=(experts // PEERS,), out_shape=[jax.Shap...]
    pallas_call x1 -> x2, Pallas kernels: 6.49 us -> 11.2 us  [the longest x1 6.44 us: combine(): pl.pallas_call(combine_kernel, grid=(experts // SUM_PEERS,), out_shape=[j...]
    ppermute x3, waiting for transfers between devices: 0.01 us -> 3.69 us  [other_core(): return lax.ppermute(x, 'dp', [(0, 1), (1, 0)])]
    pallas_call x2, Pallas kernels: 20.9 us -> 17.8 us  [project(): pl.pallas_call(project_kernel, grid=(experts // PEERS,), out_shape=[jax.S...]
    dot_general x3, matrix products: 19.6 us -> 22.3 us  [contract_rows(): lax.dot_general(left, right, (((0,), (0,)), ((), ())), preferred_element_...]
  transfers between devices with their start and end apart: 6 -> 6, of which waited for: 3 -> 4; matrix products, arithmetic and copies ran while one was open for 12% -> 13% of each run, Pallas kernels for 10% -> 7%
where the time goes in v2:
time: 255 us; the launch traced here: 250 us
  waiting for transfers between devices  124 us (49%)
  Pallas kernels  43.5 us (17%)
  local copies, waits for them, and re-layouts  31.7 us (12%)
  starting transfers between devices  27.1 us (11%)
  matrix products  22.3 us (9%)
    all_to_all x3, waiting for transfers between devices, exchange(): lax.all_to_all(x, ('ctx', 'tp'), split_axis=0, concat_axis=0, tiled=True)  121 us
    unnamed x57, local copies, waits for them, and re-layouts  31.7 us
    all_to_all x3, starting transfers between devices, exchange(): lax.all_to_all(x, ('ctx', 'tp'), split_axis=0, concat_axis=0, tiled=True)  26.6 us
    dot_general x3, matrix products, contract_rows(): lax.dot_general(left, right, (((0,), (0,)), ((), ())), preferred_element_...  22.3 us
    pallas_call x2, Pallas kernels, project(): pl.pallas_call(project_kernel, grid=(experts // PEERS,), out_shape=[jax.S...  17.8 us
    pallas_call x1, Pallas kernels, pair(): pl.pallas_call(pair_kernel, grid=(experts // PEERS,), out_shape=[jax.Shap...  10.2 us
    pallas_call x1, Pallas kernels, combine(): pl.pallas_call(combine_kernel, grid=(experts // SUM_PEERS,), out_shape=[j...  6.44 us
  transfers between devices with their start and end apart: 6, of which 4 were waited for; matrix products, arithmetic and copies ran while one was open for 13% of the time, Pallas kernels for 7%

profile of v2, /device:TPU:0, one launch (start us, length us, event | category | flops | bytes accessed | tf_op | source)
XLA Modules:
  0.0 250.0 jit_solution(15401528982216740550)
XLA Ops:
  0.6 0.0 copy-start.6
  0.6 1.0 copy-done.6
  1.7 0.7 copy-done.8
  2.4 0.7 copy-done.10
  3.0 2.1 pack_tokens.1
  5.2 2.2 copy-done.1
  7.4 11.9 %all-to-all-start.1 = ((bf16[64,288,128]{2,1,0:T(8,128)(2,1)}), bf16[64,288,128]{2,1,0:T(8,128)(2,1)}, u32[]{:S(2)}, u32[]{:S(2)}) async-start(bf16[64,288,128]{2,1,0:T(8,128)(2,1)} %copy-done.1), calls=%async_computation.1 | async-start | bytes 9437184 | tf_op jit(solution)/shard_map/all_to_all | solution.py:330
  19.3 2.2 pack_cotangent.1
  21.5 0.0 copy-start
  21.5 2.1 copy-done
  23.7 56.7 %all-to-all-done.1.in_ref = bf16[64,288,128]{2,1,0:T(8,128)(2,1)} async-done(((bf16[64,288,128]{2,1,0:T(8,128)(2,1)}), bf16[64,288,128]{2,1,0:T(8,128)(2,1)}, u32[]{:S(2)}, u32[]{:S(2)}) %all-to-all-start.1) | async-done | bytes 4718624 | tf_op jit(solution)/shard_map/all_to_all | solution.py:330
  80.3 6.7 %all-to-all-start = ((bf16[64,288,128]{2,1,0:T(8,128)(2,1)}), bf16[64,288,128]{2,1,0:T(8,128)(2,1)}, u32[]{:S(2)}, u32[]{:S(2)}) async-start(bf16[64,288,128]{2,1,0:T(8,128)(2,1)} %copy-done), calls=%async_computation | async-start | bytes 9437184 | tf_op jit(solution)/shard_map/all_to_all | solution.py:330
  87.1 0.0 copy-start.3
  87.1 1.9 copy-done.3
  89.0 10.7 %gate_up.1 = (bf16[1152,2048]{1,0:T(8,128)(2,1)S(1)}, bf16[1152,768]{1,0:T(8,128)(2,1)}, bf16[1152,768]{1,0:T(8,128)(2,1)}) custom-call(bf16[64,288,128]{2,1,0:T(8,128)(2,1)} %all-to-all-done.1.in_ref, bf16[2048,768]{1,0:T(8,128)(2,1)S(1)} %bitcast.26, bf16[2048,768]{1,0:T(8,128)(2,1)S(1)} %bitcast.27), custom_call_target="tpu_custom_call" | custom-call | flops 7247757312 | bytes 19267584 | tf_op jit(solution)/shard_map/gate_up/pallas_call | solution.py:162
  99.7 2.1 copy-done.20
  101.8 0.0 collective-permute-start
  101.8 0.5 collective-permute-start.1
  102.3 2.9 %copy.12 = bf16[1,2048,768]{1,2,0:T(8,128)(2,1)} copy(bf16[1,2048,768]{2,1,0:T(8,128)(2,1)S(1)} %copy-done.2) | data formatting | bytes 6291456 | tf_op args[4]
  105.2 3.2 %copy.13 = bf16[1,2048,768]{1,2,0:T(8,128)(2,1)S(1)} copy(bf16[1,2048,768]{2,1,0:T(8,128)(2,1)} %param.12) | data formatting | bytes 6291456 | tf_op args[5]
  108.3 4.6 %copy.14 = bf16[1,768,2048]{1,2,0:T(8,128)(2,1)} copy(bf16[1,768,2048]{2,1,0:T(8,128)(2,1)} %param.13) | data formatting | bytes 6291456 | tf_op args[6]
  113.0 0.0 collective-permute-done.gate_far
  113.0 0.0 collective-permute-done.1.up_far
  113.0 4.7 %prepare.1 = (bf16[1152,768]{1,0:T(8,128)(2,1)S(1)}, bf16[1152,768]{1,0:T(8,128)(2,1)S(1)}, bf16[1152,768]{1,0:T(8,128)(2,1)S(1)}) custom-call(bf16[1152,768]{1,0:T(8,128)(2,1)} %get-tuple-element.25.gate, bf16[1152,768]{1,0:T(8,128)(2,1)} %collective-permute-done.gate_far, bf16[1152,768]{1,0:T(8,128)(2,1)} %get-tuple-element.26.up, ...), custom_call_target="tpu_custom_call" | custom-call | flops 10616832 | bytes 12386304 | tf_op jit(solution)/shard_map/prepare/pallas_call | solution.py:194
  117.7 0.0 copy-start.12
  117.7 1.2 copy-done.12
  118.9 1.2 copy-done.15
  120.2 1.2 copy-done.17
  121.4 23.4 %all-to-all-done.in_ref = bf16[64,288,128]{2,1,0:T(8,128)(2,1)} async-done(((bf16[64,288,128]{2,1,0:T(8,128)(2,1)}), bf16[64,288,128]{2,1,0:T(8,128)(2,1)}, u32[]{:S(2)}, u32[]{:S(2)}) %all-to-all-start) | async-done | bytes 4718624 | tf_op jit(solution)/shard_map/all_to_all | solution.py:330
  144.8 1.9 copy-done.5
  146.7 7.1 %back.1 = (bf16[1152,2048]{1,0:T(8,128)(2,1)S(1)}, bf16[1152,768]{1,0:T(8,128)(2,1)S(1)}) custom-call(bf16[64,288,128]{2,1,0:T(8,128)(2,1)} %all-to-all-done.in_ref, bf16[2048,768]{1,0:T(8,128)(2,1)S(1)} %bitcast.30), custom_call_target="tpu_custom_call" | custom-call | flops 3623878656 | bytes 14352384 | tf_op jit(solution)/shard_map/back/pallas_call | solution.py:162
  153.9 2.2 copy-done.19
  156.1 0.0 collective-permute-start.2
  156.1 3.7 %collective-permute-done.2.back_far = bf16[1152,768]{1,0:T(8,128)(2,1)S(1)} collective-permute-done((bf16[1152,768]{1,0:T(8,128)(2,1)S(1)}, bf16[1152,768]{1,0:T(8,128)(2,1)S(1)}, u32[]{:S(2)}, u32[]{:S(2)}) %collective-permute-start.2) | collective-permute-done | bytes 1769504 | tf_op jit(solution)/shard_map/ppermute | solution.py:334
  159.8 0.0 copy-done.16
  159.8 0.0 copy-done.18
  159.8 10.2 %pair_grad.1 = (bf16[64,304,128]{2,1,0:T(8,128)(2,1)}, bf16[1152,768]{1,0:T(8,128)(2,1)S(1)}, bf16[1152,768]{1,0:T(8,128)(2,1)S(1)}) custom-call(bf16[1152,768]{1,0:T(8,128)(2,1)S(1)} %copy-done.13, bf16[1152,768]{1,0:T(8,128)(2,1)S(1)} %copy-done.16, bf16[1152,768]{1,0:T(8,128)(2,1)S(1)} %copy-done.18, bf16[1152,768]{1,0:T(8,128)(2,1)S(1)} %get-tuple-element.35.back, ...), custom_call_target="tpu_custom_call" | custom-call | flops 7247757312 | bytes 23396352 | tf_op jit(solution)/shard_map/pair_grad/pallas_call | solution.py:243
  170.0 1.2 copy-done.21
  171.2 1.2 copy-done.23
  172.4 8.0 %all-to-all-start.2 = ((bf16[64,304,128]{2,1,0:T(8,128)(2,1)}), bf16[64,304,128]{2,1,0:T(8,128)(2,1)}, u32[]{:S(2)}, u32[]{:S(2)}) async-start(bf16[64,304,128]{2,1,0:T(8,128)(2,1)} %get-tuple-element.38), calls=%async_computation.2 | async-start | bytes 9961472 | tf_op jit(solution)/shard_map/all_to_all | solution.py:330
  180.4 0.0 copy-start.24
  180.4 0.0 slice-start
  180.4 8.2 %fusion.2 = bf16[1,768,2048]{2,1,0:T(8,128)(2,1)} fusion(bf16[1152,768]{1,0:T(8,128)(2,1)S(1)} %copy-done.14, bf16[1152,2048]{1,0:T(8,128)(2,1)} %copy-done.19), kind=kOutput, calls=%fused_computation.5 | convolution fusion | flops 3625451520 | bytes 9633792 | tf_op jit(solution)/shard_map/dot_general | solution.py:338
  188.6 8.3 %fusion = bf16[1,2048,768]{2,1,0:T(8,128)(2,1)} fusion(bf16[1152,2048]{1,0:T(8,128)(2,1)} %copy-done.20, bf16[1152,768]{1,0:T(8,128)(2,1)S(1)} %copy-done.24), kind=kOutput, calls=%fused_computation.3 | convolution fusion | flops 3625451520 | bytes 9633792 | tf_op jit(solution)/shard_map/dot_general | solution.py:338
  196.9 0.0 slice-done
  196.9 5.9 %fusion.1 = bf16[1,2048,768]{2,1,0:T(8,128)(2,1)} fusion(bf16[1152,2048]{1,0:T(8,128)(2,1)S(1)} %bitcast.38, bf16[1152,768]{1,0:T(8,128)(2,1)S(1)} %copy-done.22), kind=kOutput, calls=%fused_computation.4 | convolution fusion | flops 3625451520 | bytes 9633792 | tf_op jit(solution)/shard_map/dot_general | solution.py:338
  202.8 40.7 %all-to-all-done.2.in_ref.slots_ref = bf16[64,304,128]{2,1,0:T(8,128)(2,1)} async-done(((bf16[64,304,128]{2,1,0:T(8,128)(2,1)}), bf16[64,304,128]{2,1,0:T(8,128)(2,1)}, u32[]{:S(2)}, u32[]{:S(2)}) %all-to-all-start.2) | async-done | bytes 4980768 | tf_op jit(solution)/shard_map/all_to_all | solution.py:330
  243.5 6.4 %combine.1 = (bf16[128,2048]{1,0:T(8,128)(2,1)}, bf16[8,128]{1,0:T(8,128)(2,1)}) custom-call(s32[8,128]{1,0:T(8,128)S(1)} %bitcast.33, bf16[8,128]{1,0:T(8,128)(2,1)S(1)} %bitcast.36, bf16[64,304,128]{2,1,0:T(8,128)(2,1)} %all-to-all-done.2.in_ref.slots_ref, bf16[64,304,128]{2,1,0:T(8,128)(2,1)} %all-to-all-done.2.in_ref.slots_ref), custom_call_target="tpu_custom_call" | custom-call | flops 603979776 | bytes 4980736 | tf_op jit(solution)/shard_map/combine/pallas_call | solution.py:305
  (32 shorter events, 0.1 us)
Async XLA Ops:
  0.6 1.0 copy-start.6
  1.7 0.7 copy-start.8
  2.4 0.7 copy-start.10
  5.2 2.2 copy-start.1
  7.4 11.9 %copy-start.7 = (bf16[128,2048]{1,0:T(8,128)(2,1)S(1)}, bf16[128,2048]{1,0:T(8,128)(2,1)}, u32[]{:S(2)}) copy-start(bf16[128,2048]{1,0:T(8,128)(2,1)} %x_ref.2) | copy-start | bytes 1572868
  7.4 11.9 %copy-start.9 = (s32[128,8]{0,1:T(8,128)S(1)}, s32[128,8]{0,1:T(8,128)}, u32[]{:S(2)}) copy-start(s32[128,8]{0,1:T(8,128)} %param.10) | copy-start | bytes 12292
  7.4 11.9 %copy-start.11 = (bf16[128,8]{0,1:T(8,128)(2,1)S(1)}, bf16[128,8]{0,1:T(8,128)(2,1)}, u32[]{:S(2)}) copy-start(bf16[128,8]{0,1:T(8,128)(2,1)} %param.9) | copy-start | bytes 6148
  7.4 72.9 %all-to-all-start.1 = ((bf16[64,288,128]{2,1,0:T(8,128)(2,1)}), bf16[64,288,128]{2,1,0:T(8,128)(2,1)}, u32[]{:S(2)}, u32[]{:S(2)}) async-start(bf16[64,288,128]{2,1,0:T(8,128)(2,1)} %copy-done.1), calls=%async_computation.1 | async-start | bytes 9437184 | tf_op jit(solution)/shard_map/all_to_all | solution.py:330
  21.5 2.2 copy-start
  23.7 63.4 %copy-start.2 = (bf16[1,2048,768]{2,1,0:T(8,128)(2,1)S(1)}, bf16[1,2048,768]{2,1,0:T(8,128)(2,1)}, u32[]{:S(2)}) copy-start(bf16[1,2048,768]{2,1,0:T(8,128)(2,1)} %param.11) | copy-start | bytes 9437188
  80.3 64.5 %all-to-all-start = ((bf16[64,288,128]{2,1,0:T(8,128)(2,1)}), bf16[64,288,128]{2,1,0:T(8,128)(2,1)}, u32[]{:S(2)}, u32[]{:S(2)}) async-start(bf16[64,288,128]{2,1,0:T(8,128)(2,1)} %copy-done), calls=%async_computation | async-start | bytes 9437184 | tf_op jit(solution)/shard_map/all_to_all | solution.py:330
  87.1 1.9 copy-start.3
  99.7 2.1 copy-start.20
  101.8 11.2 %collective-permute-start = (bf16[1152,768]{1,0:T(8,128)(2,1)}, bf16[1152,768]{1,0:T(8,128)(2,1)}, u32[]{:S(2)}, u32[]{:S(2)}) collective-permute-start(bf16[1152,768]{1,0:T(8,128)(2,1)} %get-tuple-element.25.gate), channel_id=1, source_target_pairs={{0,64},{64,0},{1,65},{65,1},{2,66},{66,2},{3,67},{67,3},{4,68},{68... | collective-permute-start | bytes 5308424 | tf_op jit(solution)/shard_map/ppermute | solution.py:334
  101.8 11.2 %collective-permute-start.1 = (bf16[1152,768]{1,0:T(8,128)(2,1)}, bf16[1152,768]{1,0:T(8,128)(2,1)}, u32[]{:S(2)}, u32[]{:S(2)}) collective-permute-start(bf16[1152,768]{1,0:T(8,128)(2,1)} %get-tuple-element.26.up), channel_id=1, source_target_pairs={{0,64},{64,0},{1,65},{65,1},{2,66},{66,2},{3,67},{67,3},{4,68},{68... | collective-permute-start | bytes 5308424 | tf_op jit(solution)/shard_map/ppermute | solution.py:334
  117.7 1.2 copy-start.12
  118.9 1.2 copy-start.15
  120.2 1.3 copy-start.17
  144.8 1.9 copy-start.5
  146.7 13.1 %copy-start.4 = (bf16[1,2048,768]{1,2,0:T(8,128)(2,1)S(1)}, bf16[1,2048,768]{1,2,0:T(8,128)(2,1)}, u32[]{:S(2)}) copy-start(bf16[1,2048,768]{1,2,0:T(8,128)(2,1)} %copy.12) | copy-start | bytes 9437188
  146.7 13.1 %copy-start.13 = (bf16[1152,768]{1,0:T(8,128)(2,1)S(1)}, bf16[1152,768]{1,0:T(8,128)(2,1)}, u32[]{:S(2)}) copy-start(bf16[1152,768]{1,0:T(8,128)(2,1)} %copy-done.12) | copy-start | bytes 5308420
  146.7 13.1 %copy-start.16 = (bf16[1152,768]{1,0:T(8,128)(2,1)S(1)}, bf16[1152,768]{1,0:T(8,128)(2,1)}, u32[]{:S(2)}) copy-start(bf16[1152,768]{1,0:T(8,128)(2,1)} %copy-done.15) | copy-start | bytes 5308420
  146.7 13.1 %copy-start.18 = (bf16[1152,768]{1,0:T(8,128)(2,1)S(1)}, bf16[1152,768]{1,0:T(8,128)(2,1)}, u32[]{:S(2)}) copy-start(bf16[1152,768]{1,0:T(8,128)(2,1)} %copy-done.17) | copy-start | bytes 5308420
  153.9 2.2 copy-start.19
  156.1 3.7 %collective-permute-start.2 = (bf16[1152,768]{1,0:T(8,128)(2,1)S(1)}, bf16[1152,768]{1,0:T(8,128)(2,1)S(1)}, u32[]{:S(2)}, u32[]{:S(2)}) collective-permute-start(bf16[1152,768]{1,0:T(8,128)(2,1)S(1)} %get-tuple-element.35.back), channel_id=1, source_target_pairs={{0,64},{64,0},{1,65},{65,1},{2,66},{66,2},{3,67},{67,3},{4,68},{68... | collective-permute-start | bytes 5308424 | tf_op jit(solution)/shard_map/ppermute | solution.py:334
  170.0 1.2 copy-start.21
  171.2 1.2 copy-start.23
  172.4 8.0 %copy-start.14 = (bf16[1152,768]{1,0:T(8,128)(2,1)S(1)}, bf16[1152,768]{1,0:T(8,128)(2,1)}, u32[]{:S(2)}) copy-start(bf16[1152,768]{1,0:T(8,128)(2,1)} %copy-done.12) | copy-start | bytes 5308420
  172.4 71.1 %all-to-all-start.2 = ((bf16[64,304,128]{2,1,0:T(8,128)(2,1)}), bf16[64,304,128]{2,1,0:T(8,128)(2,1)}, u32[]{:S(2)}, u32[]{:S(2)}) async-start(bf16[64,304,128]{2,1,0:T(8,128)(2,1)} %get-tuple-element.38), calls=%async_computation.2 | async-start | bytes 9961472 | tf_op jit(solution)/shard_map/all_to_all | solution.py:330
  180.4 8.2 %copy-start.24 = (bf16[1152,768]{1,0:T(8,128)(2,1)S(1)}, bf16[1152,768]{1,0:T(8,128)(2,1)}, u32[]{:S(2)}) copy-start(bf16[1152,768]{1,0:T(8,128)(2,1)} %copy-done.23) | copy-start | bytes 5308420
  180.4 16.5 %slice-start = ((s8[4718592]{0:T(1024)(128)(4,1)}), s8[4194304]{0:T(1024)(128)(4,1)S(1)}, s32[]{:S(2)}) async-start(s8[4718592]{0:T(1024)(128)(4,1)} %bitcast.37), calls=%async_computation.3 | async-start | bytes 8388608
  188.6 8.3 %slice-start.1 = ((s8[4718592]{0:T(1024)(128)(4,1)}), s8[524288]{0:T(1024)(128)(4,1)S(1)}, s32[]{:S(2)}) async-start(s8[4718592]{0:T(1024)(128)(4,1)} %bitcast.37), calls=%async_computation.4 | async-start | bytes 1048576
  188.6 8.3 %copy-start.22 = (bf16[1152,768]{1,0:T(8,128)(2,1)S(1)}, bf16[1152,768]{1,0:T(8,128)(2,1)}, u32[]{:S(2)}) copy-start(bf16[1152,768]{1,0:T(8,128)(2,1)} %copy-done.21) | copy-start | bytes 5308420

commit v3 on v2

v3 whole, which is shorter than its diff:
```python
import functools

import jax
import jax.numpy as jnp
from jax import lax
from jax.experimental import pallas as pl
from jax.experimental.pallas import tpu as pltpu
from jax.sharding import PartitionSpec as P

BF = jnp.bfloat16
F32 = jnp.float32
LANE = 128
HALF = 8
EXTRA = 2
CAP = 2 * HALF + EXTRA
FIRST = HALF + EXTRA
TILE = 16
GROUP = 16
PEERS = 32
SUM_PEERS = 16
VMEM = 60 * 2**20


def iota(shape, dim):
    return lax.broadcasted_iota(jnp.int32, shape, dim)


def dot(a, b):
    return jnp.dot(a, b, preferred_element_type=F32)


def expert_ranks(ids, experts):
    top, tokens = ids.shape
    expert = iota((experts, tokens), 0)
    hit = jnp.zeros((experts, tokens), F32)
    for k in range(top):
        hit = hit + jnp.where(ids[k : k + 1] == expert, 1.0, 0.0)
    earlier = jnp.where(iota((tokens, tokens), 0) < iota((tokens, tokens), 1), 1.0, 0.0)
    rank = dot(hit.astype(BF), earlier.astype(BF))
    return jnp.where(hit > 0.0, rank, -1.0)


def expert_probs(ids, probs, experts):
    top, tokens = ids.shape
    expert = iota((experts, tokens), 0)
    out = jnp.zeros((experts, tokens), F32)
    for k in range(top):
        out = out + jnp.where(ids[k : k + 1] == expert, probs[k : k + 1], 0.0)
    return out


def by_slot(a, slots):
    peers, tokens = a.shape
    return jnp.broadcast_to(a[:, None, :], (peers, slots, tokens)).reshape(peers * slots, tokens)


def extra_order(pack):
    shape = (GROUP * TILE, GROUP * TILE)
    row, col = iota(shape, 0), iota(shape, 1)
    step = GROUP * EXTRA
    if pack:
        source = (row % TILE) // EXTRA * step + row // TILE * EXTRA + row % EXTRA
    else:
        source = (row % step) // EXTRA * TILE + row // step * EXTRA + row % EXTRA
    return jnp.where(col == source, 1.0, 0.0).astype(BF)


def store_half(out_ref, start, values):
    for c in range(0, values.shape[1] // LANE, 2):
        pair = [values[:, k * LANE : (k + 1) * LANE].reshape(-1, HALF, LANE) for k in (c, c + 1)]
        at = start + c * HALF
        out_ref[:, at : at + TILE, :] = jnp.concatenate(pair, axis=1).astype(BF)


def store_extra(out_ref, start, values):
    for g in range(values.shape[1] // LANE):
        at = start + g * TILE
        out_ref[:, at : at + TILE, :] = values[:, g * LANE : (g + 1) * LANE].reshape(-1, TILE, LANE)


def order_extra(out_ref, start, values):
    groups = values.shape[1] // LANE // 8
    order = extra_order(True)
    step = GROUP * EXTRA
    parts = []
    for p in range(values.shape[0] // step):
        some = values[p * step : (p + 1) * step]
        columns = [
            jnp.concatenate([some[:, (g * 8 + c) * LANE : (g * 8 + c + 1) * LANE] for g in range(groups)], axis=1)
            for c in range(8)
        ]
        parts.append(dot(order, jnp.concatenate(columns, axis=0)).astype(BF))
    store_extra(out_ref, start, jnp.concatenate(parts, axis=0))


def unpack_half(in_ref, start, out_ref, first, count):
    rows = in_ref.shape[0] * HALF
    for c in range(0, count, 2):
        at = start + c * HALF
        pair = in_ref[:, at : at + TILE, :].astype(F32)
        for k in range(2):
            column = first + c + k
            out_ref[:rows, column * LANE : (column + 1) * LANE] = (
                pair[:, k * HALF : (k + 1) * HALF, :].reshape(rows, LANE).astype(BF)
            )


def unpack_extra(in_ref, start, out_ref, base):
    groups = out_ref.shape[1] // LANE // 8
    order = extra_order(False)
    step = GROUP * EXTRA
    for p in range(in_ref.shape[0] // GROUP):
        some = in_ref.at[p * GROUP : (p + 1) * GROUP]
        values = jnp.concatenate(
            [some[:, start + g * TILE : start + (g + 1) * TILE, :].reshape(-1, LANE) for g in range(groups)], axis=1
        )
        ordered = dot(order, values).astype(BF)
        for g in range(groups):
            for c in range(8):
                at = (g * 8 + c) * LANE
                out_ref[base + p * step : base + (p + 1) * step, at : at + LANE] = ordered[
                    c * step : (c + 1) * step, g * LANE : (g + 1) * LANE
                ]


def half_rows(rank, value, start):
    rank = by_slot(rank, HALF)
    hit = rank == (start + iota(rank.shape, 0) % HALF).astype(F32)
    return jnp.where(hit, 1.0 if value is None else by_slot(value, HALF), 0.0).astype(BF)


def extra_rows(rank, value):
    rank = by_slot(rank, TILE)
    row = iota(rank.shape, 0)
    hit = rank == (2 * HALF + row % EXTRA).astype(F32)
    extra = jnp.where(hit, 1.0 if value is None else by_slot(value, TILE), 0.0)
    column = (row % TILE) // EXTRA
    return jnp.concatenate([jnp.where(column == c, extra, 0.0).astype(BF) for c in range(8)], axis=1)


def stack_columns(x_ref, side_ref):
    tokens, width = x_ref.shape
    groups = width // LANE // 8
    for c in range(8):
        for g in range(groups):
            at = (g * 8 + c) * LANE
            side_ref[c * tokens : (c + 1) * tokens, g * LANE : (g + 1) * LANE] = x_ref[:, at : at + LANE]


def pack_first_kernel(ids_ref, probs_ref, x_ref, cot_ref, out_ref, rank_ref, prob_ref, side_ref, cot_side_ref):
    step = pl.program_id(0)
    experts = rank_ref.shape[0]
    half = x_ref.shape[1] // LANE * HALF
    part = x_ref.shape[1] // LANE * FIRST

    @pl.when(step == 0)
    def _():
        rank_ref[...] = expert_ranks(ids_ref[...], experts)
        prob_ref[...] = expert_probs(ids_ref[...], probs_ref[...].astype(F32), experts)
        stack_columns(x_ref, side_ref)
        stack_columns(cot_ref, cot_side_ref)

    peers = pl.ds(pl.multiple_of(step * PEERS, PEERS), PEERS)
    rank, prob = rank_ref[peers, :], prob_ref[peers, :]
    store_half(out_ref, 0, dot(half_rows(rank, None, 0), x_ref[...]))
    store_extra(out_ref, half, dot(extra_rows(rank, None), side_ref[...]).astype(BF))
    store_half(out_ref, part, dot(half_rows(rank, prob, 0), cot_ref[...]))
    store_extra(out_ref, part + half, dot(extra_rows(rank, prob), cot_side_ref[...]).astype(BF))
    store_half(out_ref, 2 * part, dot(half_rows(rank, None, HALF), x_ref[...]))


def pack_second_kernel(ids_ref, probs_ref, cot_ref, out_ref, rank_ref, prob_ref):
    step = pl.program_id(0)
    experts = rank_ref.shape[0]

    @pl.when(step == 0)
    def _():
        rank_ref[...] = expert_ranks(ids_ref[...], experts)
        prob_ref[...] = expert_probs(ids_ref[...], probs_ref[...].astype(F32), experts)

    peers = pl.ds(pl.multiple_of(step * PEERS, PEERS), PEERS)
    store_half(out_ref, 0, dot(half_rows(rank_ref[peers, :], prob_ref[peers, :], HALF), cot_ref[...]))


def pack(name, kernel, slots, sides, ids, probs, values, experts):
    tokens, width = values[0].shape
    rows = width // LANE * slots
    return pl.pallas_call(
        kernel,
        grid=(experts // PEERS,),
        out_shape=jax.ShapeDtypeStruct((experts, rows, LANE), BF),
        in_specs=[pl.BlockSpec(a.shape, lambda i: (0, 0)) for a in (ids, probs, *values)],
        out_specs=pl.BlockSpec((PEERS, rows, LANE), lambda i: (i, 0, 0)),
        scratch_shapes=[pltpu.VMEM((experts, tokens), F32)] * 2 + [pltpu.VMEM((8 * tokens, width // 8), BF)] * sides,
        compiler_params=pltpu.CompilerParams(vmem_limit_bytes=VMEM),
        cost_estimate=pl.CostEstimate(
            flops=4 * experts * slots * tokens * width, bytes_accessed=2 * experts * rows * LANE, transcendentals=0
        ),
        name=name,
    )(ids, probs, *values)


def project_kernel(count, extra, *refs):
    ins, refs = refs[: len(refs) - 2 * count - 1], refs[len(refs) - 2 * count - 1 :]
    weights, rows_ref, outs = refs[:count], refs[count], refs[count + 1 :]
    peers = ins[0].shape[0]
    tiles = rows_ref.shape[1] // LANE
    for n, in_ref in enumerate(ins):
        unpack_half(in_ref, 0, rows_ref, n * tiles // len(ins), tiles // len(ins))
    if extra:
        unpack_extra(ins[0], tiles * HALF, rows_ref, peers * HALF)
    for weight, out in zip(weights, outs):
        out[...] = dot(rows_ref[...], weight[...]).astype(BF)


def project(name, got, parts, slots, weights):
    experts = got.shape[0]
    width, hidden = weights[0].shape
    total, rows = experts * slots, PEERS * slots
    return pl.pallas_call(
        functools.partial(project_kernel, len(weights), slots == FIRST),
        grid=(experts // PEERS,),
        out_shape=[jax.ShapeDtypeStruct((total, width), BF)]
        + [jax.ShapeDtypeStruct((total, hidden), BF) for _ in weights],
        in_specs=[pl.BlockSpec((PEERS, size, LANE), lambda i, at=at: (i, at, 0)) for size, at in parts]
        + [pl.BlockSpec(w.shape, lambda i: (0, 0)) for w in weights],
        out_specs=[pl.BlockSpec((rows, width), lambda i: (i, 0))]
        + [pl.BlockSpec((rows, hidden), lambda i: (i, 0)) for _ in weights],
        compiler_params=pltpu.CompilerParams(vmem_limit_bytes=VMEM),
        cost_estimate=pl.CostEstimate(
            flops=2 * total * width * hidden * len(weights),
            bytes_accessed=2 * (2 * total * width + len(weights) * (width + total) * hidden),
            transcendentals=0,
        ),
        name=name,
    )(*[got] * len(parts), *weights)


def prepare_kernel(gate, gate_far, up, up_far, act_ref, slope_ref, silu_ref):
    g = gate[...].astype(F32) + gate_far[...].astype(F32)
    u = up[...].astype(F32) + up_far[...].astype(F32)
    sigmoid = jax.nn.sigmoid(g)
    silu = g * sigmoid
    act_ref[...] = (silu * u).astype(BF)
    slope_ref[...] = (u * sigmoid * (1.0 + g * (1.0 - sigmoid))).astype(BF)
    silu_ref[...] = silu.astype(BF)


def prepare(name, gate, gate_far, up, up_far):
    total, hidden = gate.shape
    block = pl.BlockSpec((total // 2, hidden), lambda i: (i, 0))
    return pl.pallas_call(
        prepare_kernel,
        grid=(2,),
        out_shape=[jax.ShapeDtypeStruct((total, hidden), BF)] * 3,
        in_specs=[block] * 4,
        out_specs=[block] * 3,
        compiler_params=pltpu.CompilerParams(vmem_limit_bytes=VMEM),
        cost_estimate=pl.CostEstimate(
            flops=12 * total * hidden, bytes_accessed=14 * total * hidden, transcendentals=total * hidden
        ),
        name=name,
    )(gate, gate_far, up, up_far)


def pair_core(act, slope, silu, back, back_far, gate_t, up_t, gg_ref, ug_ref):
    b = back[...].astype(F32) + back_far[...].astype(F32)
    gg_ref[...] = (b * slope[...].astype(F32)).astype(BF)
    ug_ref[...] = (b * silu[...].astype(F32)).astype(BF)
    prob_grad = jnp.sum(act[...].astype(F32) * b, axis=1, keepdims=True)
    return dot(gg_ref[...], gate_t[...]) + dot(ug_ref[...], up_t[...]), prob_grad


def slots_of(prob_grad, peers, extra):
    total = prob_grad.shape[0]
    main = peers * HALF
    row, lane = iota((total, LANE), 0), iota((total, LANE), 1)
    peer, of = iota((peers, total), 0), iota((peers, total), 1)
    slot, owner = row % HALF, of // HALF
    if extra:
        slot = jnp.where(row < main, slot, 2 * HALF + row % EXTRA)
        owner = jnp.where(of < main, owner, (of - main) // EXTRA)
    else:
        slot = slot + HALF
    by_lane = jnp.where(lane == slot, prob_grad, 0.0).astype(BF)
    return dot(jnp.where(peer == owner, 1.0, 0.0).astype(BF), by_lane)


def pair_first_kernel(act, slope, silu, back, back_far, gate_t, up_t, out_ref, gg_ref, ug_ref, slots_ref):
    y, prob_grad = pair_core(act, slope, silu, back, back_far, gate_t, up_t, gg_ref, ug_ref)
    half = y.shape[1] // LANE * HALF
    start = half + TILE
    main = PEERS * HALF
    store_half(out_ref, start, y[:main])
    order_extra(out_ref, start + half, y[main:].astype(BF))
    slots_ref[...] = slots_of(prob_grad, PEERS, True)


def pair_second_kernel(act, slope, silu, back, back_far, gate_t, up_t, slots, sent, out_ref, gg_ref, ug_ref):
    y, prob_grad = pair_core(act, slope, silu, back, back_far, gate_t, up_t, gg_ref, ug_ref)
    half = y.shape[1] // LANE * HALF
    store_half(out_ref, 0, y)
    grads = slots[...] + slots_of(prob_grad, PEERS, False)
    out_ref[:, half:, :] = by_slot(grads, TILE).astype(BF).reshape(PEERS, TILE, LANE)


def pair(name, act, slope, silu, back, back_far, gate_t, up_t, slots=None, sent=None):
    total, hidden = act.shape
    width = gate_t.shape[1]
    count = FIRST if sent is None else HALF
    experts = total // count
    rows = width // LANE * CAP + TILE
    block = pl.BlockSpec((PEERS * count, hidden), lambda i: (i, 0))
    whole = pl.BlockSpec(gate_t.shape, lambda i: (0, 0))
    small = pl.BlockSpec((PEERS, LANE), lambda i: (i, 0))
    written = rows if sent is None else width // LANE * HALF + TILE
    out_shape = [jax.ShapeDtypeStruct((experts, rows, LANE), BF)] + [jax.ShapeDtypeStruct((total, hidden), BF)] * 2
    out_specs = [pl.BlockSpec((PEERS, written, LANE), lambda i: (i, 0, 0))] + [block] * 2
    in_specs = [block] * 5 + [whole] * 2
    if sent is None:
        out_shape.append(jax.ShapeDtypeStruct((experts, LANE), F32))
        out_specs.append(small)
        more, aliases = (), {}
    else:
        in_specs += [small, pl.BlockSpec(memory_space=pl.ANY)]
        more, aliases = (slots, sent), {8: 0}
    return pl.pallas_call(
        pair_first_kernel if sent is None else pair_second_kernel,
        grid=(experts // PEERS,),
        out_shape=out_shape,
        in_specs=in_specs,
        out_specs=out_specs,
        input_output_aliases=aliases,
        compiler_params=pltpu.CompilerParams(vmem_limit_bytes=VMEM),
        cost_estimate=pl.CostEstimate(
            flops=4 * total * width * hidden,
            bytes_accessed=2 * (total * width + 7 * total * hidden + 2 * width * hidden),
            transcendentals=0,
        ),
        name=name,
    )(act, slope, silu, back, back_far, gate_t, up_t, *more)


def combine_kernel(ids_ref, probs_ref, in_ref, slots_ref, out_ref, probs_out_ref, rank_ref, rows_ref, total_ref):
    step = pl.program_id(0)
    experts, tokens = rank_ref.shape
    peers, tiles = in_ref.shape[0], out_ref.shape[1] // LANE
    half = tiles * HALF

    @pl.when(step == 0)
    def _():
        rank_ref[...] = expert_ranks(ids_ref[...], experts)
        total_ref[...] = jnp.zeros_like(total_ref)

    rows_first, rows_second = rows_ref.at[: peers * FIRST], rows_ref.at[peers * FIRST :]
    unpack_half(in_ref, 0, rows_second, 0, tiles)
    unpack_half(in_ref, half + TILE, rows_first, 0, tiles)
    unpack_extra(in_ref, 2 * half + TILE, rows_first, peers * HALF)
    rank = rank_ref[pl.ds(pl.multiple_of(step * peers, peers), peers), :]
    extra = by_slot(rank, 8)
    extra = jnp.where(extra == (2 * HALF + iota(extra.shape, 0) % 8).astype(F32), 1.0, 0.0).astype(BF)
    shape = (peers * EXTRA, peers * 8)
    keep = jnp.where(iota(shape, 1) == iota(shape, 0) // EXTRA * 8 + iota(shape, 0) % EXTRA, 1.0, 0.0).astype(BF)
    which = jnp.concatenate(
        [half_rows(rank, None, 0), dot(keep, extra).astype(BF), half_rows(rank, None, HALF)], axis=0
    )
    total_ref[...] += lax.dot_general(which, rows_ref[...], (((0,), (0,)), ((), ())), preferred_element_type=F32)

    @pl.when(step == pl.num_programs(0) - 1)
    def _():
        out_ref[...] = total_ref[...].astype(BF)
        slots = slots_ref[:, 0, :].astype(F32)
        rank = rank_ref[...]
        found = jnp.zeros((experts, tokens), F32)
        for s in range(CAP):
            found = found + jnp.where(rank == float(s), slots[:, s : s + 1], 0.0)
        ids = ids_ref[...]
        expert = iota((experts, tokens), 0)
        grads = [
            jnp.sum(jnp.where(ids[k : k + 1] == expert, found, 0.0), axis=0, keepdims=True)
            for k in range(ids.shape[0])
        ]
        probs_out_ref[...] = (jnp.concatenate(grads, axis=0) / probs_ref[...].astype(F32)).astype(BF)


def combine(ids, probs, got):
    experts, rows, _ = got.shape
    tiles = (rows - TILE) // CAP
    top, tokens = ids.shape
    width = tiles * LANE
    small = pl.BlockSpec(ids.shape, lambda i: (0, 0))
    return pl.pallas_call(
        combine_kernel,
        grid=(experts // SUM_PEERS,),
        out_shape=[jax.ShapeDtypeStruct((tokens, width), BF), jax.ShapeDtypeStruct((top, tokens), BF)],
        in_specs=[
            small,
            small,
            pl.BlockSpec((SUM_PEERS, rows, LANE), lambda i: (i, 0, 0)),
            pl.BlockSpec((experts, TILE, LANE), lambda i: (0, tiles * HALF // TILE, 0)),
        ],
        out_specs=[pl.BlockSpec((tokens, width), lambda i: (0, 0)), small],
        scratch_shapes=[
            pltpu.VMEM((experts, tokens), F32),
            pltpu.VMEM((SUM_PEERS * CAP, width), BF),
            pltpu.VMEM((tokens, width), F32),
        ],
        compiler_params=pltpu.CompilerParams(vmem_limit_bytes=VMEM),
        cost_estimate=pl.CostEstimate(
            flops=2 * experts * CAP * tokens * width, bytes_accessed=2 * experts * rows * LANE, transcendentals=0
        ),
        name="combine",
    )(ids, probs, got, got)


def exchange(x):
    return lax.all_to_all(x, ("ctx", "tp"), split_axis=0, concat_axis=0, tiled=True)


def other_core(x):
    return lax.ppermute(x, "dp", [(0, 1), (1, 0)])


def contract_rows(left, right):
    return lax.dot_general(left, right, (((0,), (0,)), ((), ())), preferred_element_type=F32).astype(BF)


def per_device(tokens, cotangent, probs, expert_ids, gate_weight, up_weight, down_weight):
    experts = lax.axis_size("ctx") * lax.axis_size("tp")
    gate_mat, up_mat, down_mat = gate_weight[0], up_weight[0], down_weight[0]
    ids, weights = expert_ids.T, probs.T
    tiles = tokens.shape[1] // LANE
    first, second = tiles * FIRST, tiles * HALF
    got = exchange(
        pack("pack_first", pack_first_kernel, 2 * FIRST + HALF, 2, ids, weights, (tokens, cotangent), experts)
    )
    got_b = exchange(pack("pack_second", pack_second_kernel, HALF, 0, ids, weights, (cotangent,), experts))
    got, gate_t, up_t, down_t = lax.optimization_barrier((got, gate_mat.T, up_mat.T, down_mat.T))
    rows_a, gate_a, up_a = project("gate_up_a", got, [(first, 0)], FIRST, (gate_mat, up_mat))
    cot_a, back_a = project("back_a", got, [(first, 1)], FIRST, (down_t,))
    at = 2 * first // (second // 2)
    rows_b, gate_b, up_b = project(
        "gate_up_b", got, [(second // 2, at), (second // 2, at + 1)], HALF, (gate_mat, up_mat)
    )
    act_a, slope_a, silu_a = prepare("prepare_a", gate_a, other_core(gate_a), up_a, other_core(up_a))
    act_b, slope_b, silu_b = prepare("prepare_b", gate_b, other_core(gate_b), up_b, other_core(up_b))
    sent, gate_grad_a, up_grad_a, slots = pair(
        "pair_a", act_a, slope_a, silu_a, back_a, other_core(back_a), gate_t, up_t
    )
    got_b, sent, slots, act_b, slope_b, silu_b = lax.optimization_barrier((got_b, sent, slots, act_b, slope_b, silu_b))
    cot_b, back_b = project("back_b", got_b, [(second, 0)], HALF, (down_t,))
    sent, gate_grad_b, up_grad_b = pair(
        "pair_b", act_b, slope_b, silu_b, back_b, other_core(back_b), gate_t, up_t, slots, sent
    )
    got_pairs = exchange(sent)
    rows, cot_rows = jnp.concatenate([rows_a, rows_b]), jnp.concatenate([cot_a, cot_b])
    grad_down = contract_rows(jnp.concatenate([act_a, act_b]), cot_rows)
    grad_gate = contract_rows(rows, jnp.concatenate([gate_grad_a, gate_grad_b]))
    grad_up = contract_rows(rows, jnp.concatenate([up_grad_a, up_grad_b]))
    grad_tokens, grad_probs = combine(ids, weights, got_pairs)
    return (grad_tokens, grad_probs.T, grad_gate[None], grad_up[None], grad_down[None])


def solution(mesh):
    return jax.shard_map(
        per_device,
        mesh=mesh,
        in_specs=(
            P(("ctx", "tp"), "dp"),
            P(("ctx", "tp"), "dp"),
            P(("ctx", "tp"), None),
            P(("ctx", "tp"), None),
            P(("ctx", "tp"), "dp", None),
            P(("ctx", "tp"), "dp", None),
            P(("ctx", "tp"), None, "dp"),
        ),
        out_specs=(
            P(("ctx", "tp"), "dp"),
            P(("ctx", "tp"), None),
            P(("ctx", "tp"), "dp", None),
            P(("ctx", "tp"), "dp", None),
            P(("ctx", "tp"), None, "dp"),
        ),
        check_vma=False,
    )
```

time: 255 us -> 296 us (1.16); the launches traced: 250 us -> 295 us
  waiting for transfers between devices: 124 us -> 154 us
  Pallas kernels: 43.5 us -> 69.4 us
  local copies, waits for them, and re-layouts: 31.7 us -> 19.4 us
  starting transfers between devices: 27.1 us -> 33.8 us
  matrix products: 22.3 us -> 17.3 us
    all_to_all x3, waiting for transfers between devices: 121 us -> 149 us  [exchange(): lax.all_to_all(x, ('ctx', 'tp'), split_axis=0, concat_axis=0, tiled=True)]
    pallas_call x6 -> x10, Pallas kernels: 37 us -> 62.8 us  [the longest x4 27.2 us: project(): pl.pallas_call(functools.partial(project_kernel, len(weights), slots == F...]
    unnamed x57 -> x36, local copies, waits for them, and re-layouts: 31.7 us -> 19.2 us
    all_to_all x3, starting transfers between devices: 26.6 us -> 32.1 us  [exchange(): lax.all_to_all(x, ('ctx', 'tp'), split_axis=0, concat_axis=0, tiled=True)]
    dot_general x3, matrix products: 22.3 us -> 17.3 us  [contract_rows(): lax.dot_general(left, right, (((0,), (0,)), ((), ())), preferred_element_...]
  transfers between devices with their start and end apart: 6 -> 9, of which waited for: 4 -> 5; matrix products, arithmetic and copies ran while one was open for 13% -> 10% of each run, Pallas kernels for 7% -> 14%
where the time goes in v3:
time: 296 us; the launch traced here: 295 us
  waiting for transfers between devices  154 us (52%)
  Pallas kernels  69.4 us (23%)
  starting transfers between devices  33.8 us (11%)
  local copies, waits for them, and re-layouts  19.4 us (7%)
  matrix products  17.3 us (6%)
    all_to_all x3, waiting for transfers between devices, exchange(): lax.all_to_all(x, ('ctx', 'tp'), split_axis=0, concat_axis=0, tiled=True)  149 us
    all_to_all x3, starting transfers between devices, exchange(): lax.all_to_all(x, ('ctx', 'tp'), split_axis=0, concat_axis=0, tiled=True)  32.1 us
    pallas_call x4, Pallas kernels, project(): pl.pallas_call(functools.partial(project_kernel, len(weights), slots == F...  27.2 us
    unnamed x36, local copies, waits for them, and re-layouts  19.2 us
    pallas_call x2, Pallas kernels, pair(): pl.pallas_call(pair_first_kernel if sent is None else pair_second_kernel,...  19 us
    dot_general x3, matrix products, contract_rows(): lax.dot_general(left, right, (((0,), (0,)), ((), ())), preferred_element_...  17.3 us
    pallas_call x2, Pallas kernels, pack(): pl.pallas_call(kernel, grid=(experts // PEERS,), out_shape=jax.ShapeDtype...  9.6 us
    pallas_call x2, Pallas kernels, prepare(): pl.pallas_call(prepare_kernel, grid=(2,), out_shape=[jax.ShapeDtypeStruct...  7 us
  transfers between devices with their start and end apart: 9, of which 5 were waited for; matrix products, arithmetic and copies ran while one was open for 10% of the time, Pallas kernels for 14%

profile of v3, /device:TPU:0, one launch (start us, length us, event | category | flops | bytes accessed | tf_op | source)
XLA Modules:
  0.0 294.7 jit_solution(1167379765790144239)
XLA Ops:
  0.6 6.4 %pack_first.1 = bf16[64,448,128]{2,1,0:T(8,128)(2,1)} custom-call(s32[8,128]{1,0:T(8,128)} %bitcast.34, bf16[8,128]{1,0:T(8,128)(2,1)} %bitcast.37, bf16[128,2048]{1,0:T(8,128)(2,1)} %x_ref.1, bf16[128,2048]{1,0:T(8,128)(2,1)} %cot_ref.3), custom_call_target="tpu_custom_call" | custom-call | flops 1879048192 | bytes 7340032 | tf_op jit(solution)/shard_map/pack_first/pallas_call | solution.py:188
  7.1 11.7 %all-to-all-start.1 = ((bf16[64,448,128]{2,1,0:T(8,128)(2,1)}), bf16[64,448,128]{2,1,0:T(8,128)(2,1)}, u32[]{:S(2)}, u32[]{:S(2)}) async-start(bf16[64,448,128]{2,1,0:T(8,128)(2,1)} %pack_first.1), calls=%async_computation.1 | async-start | bytes 14680064 | tf_op jit(solution)/shard_map/all_to_all | solution.py:417
  18.8 3.2 %pack_second.1 = bf16[64,128,128]{2,1,0:T(8,128)(2,1)} custom-call(s32[8,128]{1,0:T(8,128)} %bitcast.35, bf16[8,128]{1,0:T(8,128)(2,1)} %bitcast.38, bf16[128,2048]{1,0:T(8,128)(2,1)} %cot_ref.3), custom_call_target="tpu_custom_call" | custom-call | flops 536870912 | bytes 2097152 | tf_op jit(solution)/shard_map/pack_second/pallas_call | solution.py:188
  22.0 100.0 %all-to-all-done.1.refs_0_.refs_1_ = bf16[64,448,128]{2,1,0:T(8,128)(2,1)} async-done(((bf16[64,448,128]{2,1,0:T(8,128)(2,1)}), bf16[64,448,128]{2,1,0:T(8,128)(2,1)}, u32[]{:S(2)}, u32[]{:S(2)}) %all-to-all-start.1) | async-done | bytes 7340064 | tf_op jit(solution)/shard_map/all_to_all | solution.py:417
  122.0 9.5 %all-to-all-start = ((bf16[64,128,128]{2,1,0:T(8,128)(2,1)}), bf16[64,128,128]{2,1,0:T(8,128)(2,1)}, u32[]{:S(2)}, u32[]{:S(2)}) async-start(bf16[64,128,128]{2,1,0:T(8,128)(2,1)} %pack_second.1), calls=%async_computation | async-start | bytes 4194304 | tf_op jit(solution)/shard_map/all_to_all | solution.py:417
  131.5 0.0 copy-start
  131.5 4.8 %copy.15 = bf16[1,768,2048]{1,2,0:T(8,128)(2,1)} copy(bf16[1,768,2048]{2,1,0:T(8,128)(2,1)} %param.13) | data formatting | bytes 6291456 | tf_op args[6]
  136.3 2.9 copy.13
  139.2 4.6 %copy.14 = bf16[1,2048,768]{1,2,0:T(8,128)(2,1)} copy(bf16[1,2048,768]{2,1,0:T(8,128)(2,1)} %param.12) | data formatting | bytes 6291456 | tf_op args[5]
  143.8 5.7 %back_a.1 = (bf16[640,2048]{1,0:T(8,128)(2,1)}, bf16[640,768]{1,0:T(8,128)(2,1)}) custom-call(bf16[64,448,128]{2,1,0:T(8,128)(2,1)} %all-to-all-done.1.refs_0_.refs_1_, bf16[2048,768]{1,0:T(8,128)(2,1)} %bitcast.28), custom_call_target="tpu_custom_call" | custom-call | flops 2013265920 | bytes 9371648 | tf_op jit(solution)/shard_map/back_a/pallas_call | solution.py:220
  149.5 0.0 collective-permute-start.2
  149.5 8.7 %gate_up_a.1 = (bf16[640,2048]{1,0:T(8,128)(2,1)}, bf16[640,768]{1,0:T(8,128)(2,1)}, bf16[640,768]{1,0:T(8,128)(2,1)}) custom-call(bf16[64,448,128]{2,1,0:T(8,128)(2,1)} %all-to-all-done.1.refs_0_.refs_1_, bf16[2048,768]{1,0:T(8,128)(2,1)} %bitcast.24, bf16[2048,768]{1,0:T(8,128)(2,1)} %bitcast.26), custom_call_target="tpu_custom_call" | custom-call | flops 4026531840 | bytes 13500416 | tf_op jit(solution)/shard_map/gate_up_a/pallas_call | solution.py:220
  158.2 0.5 collective-permute-start
  158.7 0.0 collective-permute-start.1
  158.7 7.6 %gate_up_b.1 = (bf16[512,2048]{1,0:T(8,128)(2,1)}, bf16[512,768]{1,0:T(8,128)(2,1)}, bf16[512,768]{1,0:T(8,128)(2,1)}) custom-call(bf16[64,448,128]{2,1,0:T(8,128)(2,1)} %all-to-all-done.1.refs_0_.refs_1_, bf16[64,448,128]{2,1,0:T(8,128)(2,1)} %all-to-all-done.1.refs_0_.refs_1_, bf16[2048,768]{1,0:T(8,128)(2,1)} %bitcast.25, bf16[2048,768]{1,0:T(8,128)(2,1)} %bitcast.27), custom_call_target="tpu_custom_call" | custom-call | flops 3221225472 | bytes 12058624 | tf_op jit(solution)/shard_map/gate_up_b/pallas_call | solution.py:220
  166.2 0.5 collective-permute-start.3
  166.7 0.3 collective-permute-start.4
  167.0 1.9 collective-permute-done.3.gate_far
  168.9 1.1 collective-permute-done.4.up_far
  170.0 0.9 copy-done.6
  170.9 3.3 %prepare_b.1 = (bf16[512,768]{1,0:T(8,128)(2,1)}, bf16[512,768]{1,0:T(8,128)(2,1)}, bf16[512,768]{1,0:T(8,128)(2,1)}) custom-call(bf16[512,768]{1,0:T(8,128)(2,1)} %get-tuple-element.52.gate, bf16[512,768]{1,0:T(8,128)(2,1)} %copy-done.5, bf16[512,768]{1,0:T(8,128)(2,1)} %get-tuple-element.53.up, bf16[512,768]{1,0:T(8,128)(2,1)} %copy-done.6), custom_call_target="tpu_custom_call" | custom-call | flops 4718592 | bytes 5505024 | tf_op jit(solution)/shard_map/prepare_b/pallas_call | solution.py:252
  174.2 0.0 collective-permute-done.gate_far
  174.2 0.0 collective-permute-done.1.up_far
  174.2 0.9 copy-done.3
  175.1 0.9 copy-done.4
  176.1 3.7 %prepare_a.1 = (bf16[640,768]{1,0:T(8,128)(2,1)}, bf16[640,768]{1,0:T(8,128)(2,1)}, bf16[640,768]{1,0:T(8,128)(2,1)}) custom-call(bf16[640,768]{1,0:T(8,128)(2,1)} %get-tuple-element.41.gate, bf16[640,768]{1,0:T(8,128)(2,1)} %copy-done.3, bf16[640,768]{1,0:T(8,128)(2,1)} %get-tuple-element.42.up, bf16[640,768]{1,0:T(8,128)(2,1)} %copy-done.4), custom_call_target="tpu_custom_call" | custom-call | flops 5898240 | bytes 6881280 | tf_op jit(solution)/shard_map/prepare_a/pallas_call | solution.py:252
  179.8 0.0 collective-permute-done.2.back_far
  179.8 10.3 %pair_a.1 = (bf16[64,304,128]{2,1,0:T(8,128)(2,1)}, bf16[640,768]{1,0:T(8,128)(2,1)}, bf16[640,768]{1,0:T(8,128)(2,1)}, f32[64,128]{1,0:T(8,128)}) custom-call(bf16[640,768]{1,0:T(8,128)(2,1)} %get-tuple-element.43.act, bf16[640,768]{1,0:T(8,128)(2,1)} %get-tuple-element.44.slope, bf16[640,768]{1,0:T(8,128)(2,1)} %get-tuple-element.45.silu, ...), custom_call_target="tpu_custom_call" | custom-call | flops 4026531840 | bytes 15794176 | tf_op jit(solution)/shard_map/pair_a/pallas_call | solution.py:327
  190.1 0.0 all-to-all-done.refs_0_
  190.1 5.3 %back_b.1 = (bf16[512,2048]{1,0:T(8,128)(2,1)}, bf16[512,768]{1,0:T(8,128)(2,1)}) custom-call(bf16[64,128,128]{2,1,0:T(8,128)(2,1)} %all-to-all-done.refs_0_, bf16[2048,768]{1,0:T(8,128)(2,1)} %bitcast.29), custom_call_target="tpu_custom_call" | custom-call | flops 1610612736 | bytes 8126464 | tf_op jit(solution)/shard_map/back_b/pallas_call | solution.py:220
  195.4 0.4 collective-permute-start.5
  195.7 2.1 collective-permute-done.5.back_far
  197.9 0.9 copy-done.8
  198.8 8.7 %pair_b.1 = (bf16[64,304,128]{2,1,0:T(8,128)(2,1)}, bf16[512,768]{1,0:T(8,128)(2,1)}, bf16[512,768]{1,0:T(8,128)(2,1)}) custom-call(bf16[512,768]{1,0:T(8,128)(2,1)} %get-tuple-element.57.act, bf16[512,768]{1,0:T(8,128)(2,1)} %get-tuple-element.58.slope, bf16[512,768]{1,0:T(8,128)(2,1)} %get-tuple-element.59.silu, ...), custom_call_target="tpu_custom_call", output_to_operand_aliasing={{0}: (8, {})} | custom-call | flops 3221225472 | bytes 13893632 | tf_op jit(solution)/shard_map/pair_b/pallas_call | solution.py:327
  207.5 10.9 %all-to-all-start.2 = ((bf16[64,304,128]{2,1,0:T(8,128)(2,1)}), bf16[64,304,128]{2,1,0:T(8,128)(2,1)}, u32[]{:S(2)}, u32[]{:S(2)}) async-start(bf16[64,304,128]{2,1,0:T(8,128)(2,1)} %get-tuple-element.64), calls=%async_computation.2 | async-start | bytes 9961472 | tf_op jit(solution)/shard_map/all_to_all | solution.py:417
  218.4 0.2 constant_dynamic-update-slice_fusion.1
  218.6 1.3 copy-done.2
  219.9 0.2 constant_dynamic-update-slice_fusion
  220.2 0.8 copy-done.9
  220.9 0.2 copy-done.10
  221.2 0.7 copy-done.13
  221.9 5.7 %fusion.9 = bf16[1,768,2048]{2,1,0:T(8,128)(2,1)} fusion(bf16[512,2048]{1,0:T(8,128)(2,1)S(1)} %copy-done.13, bf16[640,2048]{1,0:T(8,128)(2,1)S(1)} %copy-done.9, bf16[512,768]{1,0:T(8,128)(2,1)S(1)} %copy-done.7, bf16[640,768]{1,0:T(8,128)(2,1)S(1)} %copy-done.10), kind=kOutput, calls=%fused_computation.9 | convolution fusion | flops 3638427648 | bytes 9633792 | tf_op jit(solution)/shard_map/dot_general | solution.py:425
  227.5 0.0 copy-done.15
  227.5 5.8 %fusion.7 = bf16[1,2048,768]{2,1,0:T(8,128)(2,1)} fusion(bf16[1152,2048]{1,0:T(8,128)(2,1)S(1)} %constant_dynamic-update-slice_fusion, bf16[512,768]{1,0:T(8,128)(2,1)S(1)} %copy-done.12, bf16[640,768]{1,0:T(8,128)(2,1)S(1)} %copy-done.15), kind=kOutput, calls=%fused_computation.7 | convolution fusion | flops 3628990464 | bytes 9633792 | tf_op jit(solution)/shard_map/dot_general | solution.py:425
  233.4 0.0 copy-done.14
  233.4 5.8 %fusion.8 = bf16[1,2048,768]{2,1,0:T(8,128)(2,1)} fusion(bf16[1152,2048]{1,0:T(8,128)(2,1)S(1)} %constant_dynamic-update-slice_fusion, bf16[512,768]{1,0:T(8,128)(2,1)S(1)} %copy-done.11, bf16[640,768]{1,0:T(8,128)(2,1)S(1)} %copy-done.14), kind=kOutput, calls=%fused_computation.8 | convolution fusion | flops 3628990464 | bytes 9633792 | tf_op jit(solution)/shard_map/dot_general | solution.py:425
  239.2 48.9 %all-to-all-done.2.in_ref.slots_ref = bf16[64,304,128]{2,1,0:T(8,128)(2,1)} async-done(((bf16[64,304,128]{2,1,0:T(8,128)(2,1)}), bf16[64,304,128]{2,1,0:T(8,128)(2,1)}, u32[]{:S(2)}, u32[]{:S(2)}) %all-to-all-start.2) | async-done | bytes 4980768 | tf_op jit(solution)/shard_map/all_to_all | solution.py:417
  288.2 6.6 %combine.1 = (bf16[128,2048]{1,0:T(8,128)(2,1)}, bf16[8,128]{1,0:T(8,128)(2,1)}) custom-call(s32[8,128]{1,0:T(8,128)} %bitcast.36, bf16[8,128]{1,0:T(8,128)(2,1)} %bitcast.39, bf16[64,304,128]{2,1,0:T(8,128)(2,1)} %all-to-all-done.2.in_ref.slots_ref, bf16[64,304,128]{2,1,0:T(8,128)(2,1)} %all-to-all-done.2.in_ref.slots_ref), custom_call_target="tpu_custom_call" | custom-call | flops 603979776 | bytes 4980736 | tf_op jit(solution)/shard_map/combine/pallas_call | solution.py:392
  (21 shorter events, 0.0 us)
Async XLA Ops:
  7.1 114.9 %all-to-all-start.1 = ((bf16[64,448,128]{2,1,0:T(8,128)(2,1)}), bf16[64,448,128]{2,1,0:T(8,128)(2,1)}, u32[]{:S(2)}, u32[]{:S(2)}) async-start(bf16[64,448,128]{2,1,0:T(8,128)(2,1)} %pack_first.1), calls=%async_computation.1 | async-start | bytes 14680064 | tf_op jit(solution)/shard_map/all_to_all | solution.py:417
  122.0 68.1 %all-to-all-start = ((bf16[64,128,128]{2,1,0:T(8,128)(2,1)}), bf16[64,128,128]{2,1,0:T(8,128)(2,1)}, u32[]{:S(2)}, u32[]{:S(2)}) async-start(bf16[64,128,128]{2,1,0:T(8,128)(2,1)} %pack_second.1), calls=%async_computation | async-start | bytes 4194304 | tf_op jit(solution)/shard_map/all_to_all | solution.py:417
  131.5 4.8 %copy-start = (bf16[1,2048,768]{2,1,0:T(8,128)(2,1)S(1)}, bf16[1,2048,768]{2,1,0:T(8,128)(2,1)}, u32[]{:S(2)}) copy-start(bf16[1,2048,768]{2,1,0:T(8,128)(2,1)} %param.11) | copy-start | bytes 9437188
  149.5 30.3 %collective-permute-start.2 = (bf16[640,768]{1,0:T(8,128)(2,1)}, bf16[640,768]{1,0:T(8,128)(2,1)}, u32[]{:S(2)}, u32[]{:S(2)}) collective-permute-start(bf16[640,768]{1,0:T(8,128)(2,1)} %get-tuple-element.47.back), channel_id=1, source_target_pairs={{0,64},{64,0},{1,65},{65,1},{2,66},{66,2},{3,67},{67,3},{4,68},{68... | collective-permute-start | bytes 2949128 | tf_op jit(solution)/shard_map/ppermute | solution.py:421
  158.2 16.0 %collective-permute-start = (bf16[640,768]{1,0:T(8,128)(2,1)}, bf16[640,768]{1,0:T(8,128)(2,1)S(1)}, u32[]{:S(2)}, u32[]{:S(2)}) collective-permute-start(bf16[640,768]{1,0:T(8,128)(2,1)} %get-tuple-element.41.gate), channel_id=1, source_target_pairs={{0,64},{64,0},{1,65},{65,1},{2,66},{66,2},{3,67},{67,3},{4,68},{68... | collective-permute-start | bytes 2949128 | tf_op jit(solution)/shard_map/ppermute | solution.py:421
  158.7 15.5 %collective-permute-start.1 = (bf16[640,768]{1,0:T(8,128)(2,1)}, bf16[640,768]{1,0:T(8,128)(2,1)S(1)}, u32[]{:S(2)}, u32[]{:S(2)}) collective-permute-start(bf16[640,768]{1,0:T(8,128)(2,1)} %get-tuple-element.42.up), channel_id=1, source_target_pairs={{0,64},{64,0},{1,65},{65,1},{2,66},{66,2},{3,67},{67,3},{4,68},{68... | collective-permute-start | bytes 2949128 | tf_op jit(solution)/shard_map/ppermute | solution.py:421
  166.2 2.6 collective-permute-start.3
  166.7 3.2 %collective-permute-start.4 = (bf16[512,768]{1,0:T(8,128)(2,1)}, bf16[512,768]{1,0:T(8,128)(2,1)S(1)}, u32[]{:S(2)}, u32[]{:S(2)}) collective-permute-start(bf16[512,768]{1,0:T(8,128)(2,1)} %get-tuple-element.53.up), channel_id=1, source_target_pairs={{0,64},{64,0},{1,65},{65,1},{2,66},{66,2},{3,67},{67,3},{4,68},{68... | collective-permute-start | bytes 2359304 | tf_op jit(solution)/shard_map/ppermute | solution.py:421
  168.9 1.1 copy-start.5
  170.0 0.9 copy-start.6
  174.2 1.0 copy-start.3
  175.1 0.9 copy-start.4
  195.4 2.5 collective-permute-start.5
  197.9 0.9 copy-start.8
  207.5 10.9 %copy-start.1 = (bf16[640,2048]{1,0:T(8,128)(2,1)S(1)}, bf16[640,2048]{1,0:T(8,128)(2,1)}, u32[]{:S(2)}) copy-start(bf16[640,2048]{1,0:T(8,128)(2,1)} %get-tuple-element.67) | copy-start | bytes 7864324
  207.5 80.7 %all-to-all-start.2 = ((bf16[64,304,128]{2,1,0:T(8,128)(2,1)}), bf16[64,304,128]{2,1,0:T(8,128)(2,1)}, u32[]{:S(2)}, u32[]{:S(2)}) async-start(bf16[64,304,128]{2,1,0:T(8,128)(2,1)} %get-tuple-element.64), calls=%async_computation.2 | async-start | bytes 9961472 | tf_op jit(solution)/shard_map/all_to_all | solution.py:417
  218.3 1.6 copy-start.2
  218.4 1.8 copy-start.7
  218.4 2.6 copy-start.9
  218.4 2.8 copy-start.10
  218.4 3.5 %copy-start.13 = (bf16[512,2048]{1,0:T(8,128)(2,1)S(1)}, bf16[512,2048]{1,0:T(8,128)(2,1)}, u32[]{:S(2)}) copy-start(bf16[512,2048]{1,0:T(8,128)(2,1)} %get-tuple-element.74) | copy-start | bytes 6291460
  221.9 5.7 %copy-start.12 = (bf16[512,768]{1,0:T(8,128)(2,1)S(1)}, bf16[512,768]{1,0:T(8,128)(2,1)}, u32[]{:S(2)}) copy-start(bf16[512,768]{1,0:T(8,128)(2,1)} %get-tuple-element.70) | copy-start | bytes 2359300
  221.9 5.7 %copy-start.15 = (bf16[640,768]{1,0:T(8,128)(2,1)S(1)}, bf16[640,768]{1,0:T(8,128)(2,1)}, u32[]{:S(2)}) copy-start(bf16[640,768]{1,0:T(8,128)(2,1)} %get-tuple-element.69) | copy-start | bytes 2949124
  227.5 5.8 %copy-start.11 = (bf16[512,768]{1,0:T(8,128)(2,1)S(1)}, bf16[512,768]{1,0:T(8,128)(2,1)}, u32[]{:S(2)}) copy-start(bf16[512,768]{1,0:T(8,128)(2,1)} %get-tuple-element.72) | copy-start | bytes 2359300
  227.5 5.9 %copy-start.14 = (bf16[640,768]{1,0:T(8,128)(2,1)S(1)}, bf16[640,768]{1,0:T(8,128)(2,1)}, u32[]{:S(2)}) copy-start(bf16[640,768]{1,0:T(8,128)(2,1)} %get-tuple-element.71) | copy-start | bytes 2949124

commit v4 on v3

v4 whole, which is shorter than its diff:
```python
import functools

import jax
import jax.numpy as jnp
from jax import lax
from jax.experimental import pallas as pl
from jax.experimental.pallas import tpu as pltpu
from jax.sharding import PartitionSpec as P

BF = jnp.bfloat16
F32 = jnp.float32
LANE = 128
HALF = 8
EXTRA = 2
CAP = 2 * HALF + EXTRA
FIRST = HALF + EXTRA
TILE = 16
GROUP = 16
PEERS = 32
VMEM = 60 * 2**20


def iota(shape, dim):
    return lax.broadcasted_iota(jnp.int32, shape, dim)


def dot(a, b):
    return jnp.dot(a, b, preferred_element_type=F32)


def expert_ranks(ids, experts):
    top, tokens = ids.shape
    expert = iota((experts, tokens), 0)
    hit = jnp.zeros((experts, tokens), F32)
    for k in range(top):
        hit = hit + jnp.where(ids[k : k + 1] == expert, 1.0, 0.0)
    earlier = jnp.where(iota((tokens, tokens), 0) < iota((tokens, tokens), 1), 1.0, 0.0)
    rank = dot(hit.astype(BF), earlier.astype(BF))
    return jnp.where(hit > 0.0, rank, -1.0)


def expert_probs(ids, probs, experts):
    top, tokens = ids.shape
    expert = iota((experts, tokens), 0)
    out = jnp.zeros((experts, tokens), F32)
    for k in range(top):
        out = out + jnp.where(ids[k : k + 1] == expert, probs[k : k + 1], 0.0)
    return out


def by_slot(a, slots):
    peers, tokens = a.shape
    return jnp.broadcast_to(a[:, None, :], (peers, slots, tokens)).reshape(peers * slots, tokens)


def extra_order(pack):
    shape = (GROUP * TILE, GROUP * TILE)
    row, col = iota(shape, 0), iota(shape, 1)
    step = GROUP * EXTRA
    if pack:
        source = (row % TILE) // EXTRA * step + row // TILE * EXTRA + row % EXTRA
    else:
        source = (row % step) // EXTRA * TILE + row // step * EXTRA + row % EXTRA
    return jnp.where(col == source, 1.0, 0.0).astype(BF)


def store_half(out_ref, start, values):
    for c in range(0, values.shape[1] // LANE, 2):
        pair = [values[:, k * LANE : (k + 1) * LANE].reshape(-1, HALF, LANE) for k in (c, c + 1)]
        at = start + c * HALF
        out_ref[:, at : at + TILE, :] = jnp.concatenate(pair, axis=1).astype(BF)


def store_extra(out_ref, start, values):
    for g in range(values.shape[1] // LANE):
        at = start + g * TILE
        out_ref[:, at : at + TILE, :] = values[:, g * LANE : (g + 1) * LANE].reshape(-1, TILE, LANE)


def order_extra(out_ref, start, values):
    groups = values.shape[1] // LANE // 8
    order = extra_order(True)
    step = GROUP * EXTRA
    parts = []
    for p in range(values.shape[0] // step):
        some = values[p * step : (p + 1) * step]
        columns = [
            jnp.concatenate([some[:, (g * 8 + c) * LANE : (g * 8 + c + 1) * LANE] for g in range(groups)], axis=1)
            for c in range(8)
        ]
        parts.append(dot(order, jnp.concatenate(columns, axis=0)).astype(BF))
    store_extra(out_ref, start, jnp.concatenate(parts, axis=0))


def unpack_half(in_ref, start, out_ref, first, count):
    rows = in_ref.shape[0] * HALF
    for c in range(0, count, 2):
        at = start + c * HALF
        pair = in_ref[:, at : at + TILE, :].astype(F32)
        for k in range(2):
            column = first + c + k
            out_ref[:rows, column * LANE : (column + 1) * LANE] = (
                pair[:, k * HALF : (k + 1) * HALF, :].reshape(rows, LANE).astype(BF)
            )


def unpack_extra(in_ref, start, out_ref, base):
    groups = out_ref.shape[1] // LANE // 8
    order = extra_order(False)
    step = GROUP * EXTRA
    for p in range(in_ref.shape[0] // GROUP):
        some = in_ref.at[p * GROUP : (p + 1) * GROUP]
        values = jnp.concatenate(
            [some[:, start + g * TILE : start + (g + 1) * TILE, :].reshape(-1, LANE) for g in range(groups)], axis=1
        )
        ordered = dot(order, values).astype(BF)
        for g in range(groups):
            for c in range(8):
                at = (g * 8 + c) * LANE
                out_ref[base + p * step : base + (p + 1) * step, at : at + LANE] = ordered[
                    c * step : (c + 1) * step, g * LANE : (g + 1) * LANE
                ]


def half_rows(rank, value, start):
    rank = by_slot(rank, HALF)
    hit = rank == (start + iota(rank.shape, 0) % HALF).astype(F32)
    return jnp.where(hit, 1.0 if value is None else by_slot(value, HALF), 0.0).astype(BF)


def extra_rows(rank, value):
    rank = by_slot(rank, TILE)
    row = iota(rank.shape, 0)
    hit = rank == (2 * HALF + row % EXTRA).astype(F32)
    extra = jnp.where(hit, 1.0 if value is None else by_slot(value, TILE), 0.0)
    column = (row % TILE) // EXTRA
    return jnp.concatenate([jnp.where(column == c, extra, 0.0).astype(BF) for c in range(8)], axis=1)


def stack_columns(x_ref, side_ref):
    tokens, width = x_ref.shape
    groups = width // LANE // 8
    for c in range(8):
        for g in range(groups):
            at = (g * 8 + c) * LANE
            side_ref[c * tokens : (c + 1) * tokens, g * LANE : (g + 1) * LANE] = x_ref[:, at : at + LANE]


def start_pack(ids_ref, probs_ref, rank_ref, prob_ref):
    experts = rank_ref.shape[0]
    rank_ref[...] = expert_ranks(ids_ref[...], experts)
    prob_ref[...] = expert_probs(ids_ref[...], probs_ref[...].astype(F32), experts)


def pack_first_kernel(ids_ref, probs_ref, x_ref, cot_ref, out_ref, rank_ref, prob_ref, side_ref, cot_side_ref):
    step = pl.program_id(0)
    half = x_ref.shape[1] // LANE * HALF
    part = x_ref.shape[1] // LANE * FIRST

    @pl.when(step == 0)
    def _():
        start_pack(ids_ref, probs_ref, rank_ref, prob_ref)
        stack_columns(x_ref, side_ref)
        stack_columns(cot_ref, cot_side_ref)

    peers = pl.ds(pl.multiple_of(step * PEERS, PEERS), PEERS)
    rank, prob = rank_ref[peers, :], prob_ref[peers, :]
    store_half(out_ref, 0, dot(half_rows(rank, None, 0), x_ref[...]))
    store_extra(out_ref, half, dot(extra_rows(rank, None), side_ref[...]).astype(BF))
    store_half(out_ref, part, dot(half_rows(rank, prob, 0), cot_ref[...]))
    store_extra(out_ref, part + half, dot(extra_rows(rank, prob), cot_side_ref[...]).astype(BF))


def pack_second_kernel(ids_ref, probs_ref, x_ref, cot_ref, out_ref, rank_ref, prob_ref):
    step = pl.program_id(0)
    half = x_ref.shape[1] // LANE * HALF

    @pl.when(step == 0)
    def _():
        start_pack(ids_ref, probs_ref, rank_ref, prob_ref)

    peers = pl.ds(pl.multiple_of(step * PEERS, PEERS), PEERS)
    rank, prob = rank_ref[peers, :], prob_ref[peers, :]
    store_half(out_ref, 0, dot(half_rows(rank, None, HALF), x_ref[...]))
    store_half(out_ref, half, dot(half_rows(rank, prob, HALF), cot_ref[...]))


def pack(name, kernel, slots, sides, ids, probs, values, experts):
    tokens, width = values[0].shape
    rows = width // LANE * slots
    return pl.pallas_call(
        kernel,
        grid=(experts // PEERS,),
        out_shape=jax.ShapeDtypeStruct((experts, rows, LANE), BF),
        in_specs=[pl.BlockSpec(a.shape, lambda i: (0, 0)) for a in (ids, probs, *values)],
        out_specs=pl.BlockSpec((PEERS, rows, LANE), lambda i: (i, 0, 0)),
        scratch_shapes=[pltpu.VMEM((experts, tokens), F32)] * 2 + [pltpu.VMEM((8 * tokens, width // 8), BF)] * sides,
        compiler_params=pltpu.CompilerParams(vmem_limit_bytes=VMEM),
        cost_estimate=pl.CostEstimate(
            flops=4 * experts * slots * tokens * width, bytes_accessed=2 * experts * rows * LANE, transcendentals=0
        ),
        name=name,
    )(ids, probs, *values)


def project_kernel(extra, x_in, cot_in, gate_w, up_w, down_w, x_ref, cot_ref, gate_ref, up_ref, back_ref):
    peers = x_in.shape[0]
    tiles = x_ref.shape[1] // LANE
    for in_ref, rows_ref in ((x_in, x_ref), (cot_in, cot_ref)):
        unpack_half(in_ref, 0, rows_ref, 0, tiles)
        if extra:
            unpack_extra(in_ref, tiles * HALF, rows_ref, peers * HALF)
    gate_ref[...] = dot(x_ref[...], gate_w[...]).astype(BF)
    up_ref[...] = dot(x_ref[...], up_w[...]).astype(BF)
    back_ref[...] = dot(cot_ref[...], down_w[...]).astype(BF)


def project(name, got, weights):
    experts, both, _ = got.shape
    width, hidden = weights[0].shape
    part = both // 2
    slots = part * LANE // width
    total, rows = experts * slots, PEERS * slots
    return pl.pallas_call(
        functools.partial(project_kernel, slots == FIRST),
        grid=(experts // PEERS,),
        out_shape=[jax.ShapeDtypeStruct((total, width), BF)] * 2 + [jax.ShapeDtypeStruct((total, hidden), BF)] * 3,
        in_specs=[pl.BlockSpec((PEERS, part, LANE), lambda i, at=at: (i, at, 0)) for at in range(2)]
        + [pl.BlockSpec(w.shape, lambda i: (0, 0)) for w in weights],
        out_specs=[pl.BlockSpec((rows, width), lambda i: (i, 0))] * 2
        + [pl.BlockSpec((rows, hidden), lambda i: (i, 0))] * 3,
        compiler_params=pltpu.CompilerParams(vmem_limit_bytes=VMEM),
        cost_estimate=pl.CostEstimate(
            flops=6 * total * width * hidden,
            bytes_accessed=2 * (4 * total * width + 3 * (width + total) * hidden),
            transcendentals=0,
        ),
        name=name,
    )(got, got, *weights)


def slots_of(prob_grad, peers, extra):
    total = prob_grad.shape[0]
    main = peers * HALF
    row, lane = iota((total, LANE), 0), iota((total, LANE), 1)
    peer, of = iota((peers, total), 0), iota((peers, total), 1)
    slot, owner = row % HALF, of // HALF
    if extra:
        slot = jnp.where(row < main, slot, HALF + row % EXTRA)
        owner = jnp.where(of < main, owner, (of - main) // EXTRA)
    by_lane = jnp.where(lane == slot, prob_grad, 0.0).astype(BF)
    return dot(jnp.where(peer == owner, 1.0, 0.0).astype(BF), by_lane)


def pair_kernel(extra, gate, gate_far, up, up_far, back, back_far, gate_t, up_t, out_ref, act_ref, gg_ref, ug_ref):
    g = gate[...].astype(F32) + gate_far[...].astype(F32)
    u = up[...].astype(F32) + up_far[...].astype(F32)
    b = back[...].astype(F32) + back_far[...].astype(F32)
    sigmoid = jax.nn.sigmoid(g)
    silu = g * sigmoid
    act = silu * u
    act_ref[...] = act.astype(BF)
    gg_ref[...] = (b * u * sigmoid * (1.0 + g * (1.0 - sigmoid))).astype(BF)
    ug_ref[...] = (b * silu).astype(BF)
    prob_grad = jnp.sum(act * b, axis=1, keepdims=True)
    y = dot(gg_ref[...], gate_t[...]) + dot(ug_ref[...], up_t[...])
    half = y.shape[1] // LANE * HALF
    main = PEERS * HALF
    store_half(out_ref, 0, y[:main])
    if extra:
        order_extra(out_ref, half, y[main:].astype(BF))
    last = out_ref.shape[1] - TILE
    grads = by_slot(slots_of(prob_grad, PEERS, extra), TILE)
    out_ref[:, last:, :] = grads.astype(BF).reshape(PEERS, TILE, LANE)


def pair(name, gate, gate_far, up, up_far, back, back_far, gate_t, up_t, experts):
    total, hidden = gate.shape
    width = gate_t.shape[1]
    slots = total // experts
    rows = width // LANE * slots + TILE
    block = pl.BlockSpec((PEERS * slots, hidden), lambda i: (i, 0))
    whole = pl.BlockSpec(gate_t.shape, lambda i: (0, 0))
    return pl.pallas_call(
        functools.partial(pair_kernel, slots == FIRST),
        grid=(experts // PEERS,),
        out_shape=[jax.ShapeDtypeStruct((experts, rows, LANE), BF)]
        + [jax.ShapeDtypeStruct((total, hidden), BF)] * 3,
        in_specs=[block] * 6 + [whole] * 2,
        out_specs=[pl.BlockSpec((PEERS, rows, LANE), lambda i: (i, 0, 0))] + [block] * 3,
        compiler_params=pltpu.CompilerParams(vmem_limit_bytes=VMEM),
        cost_estimate=pl.CostEstimate(
            flops=4 * total * width * hidden,
            bytes_accessed=2 * (total * width + 9 * total * hidden + 2 * width * hidden),
            transcendentals=total * hidden,
        ),
        name=name,
    )(gate, gate_far, up, up_far, back, back_far, gate_t, up_t)


def combine_kernel(extra, ids_ref, in_ref, slots_ref, *refs):
    if extra:
        out_ref, probs_out_ref, rank_ref, rows_ref = refs
        total_ref = out_ref
    else:
        probs_ref, before_ref, probs_before_ref, out_ref, probs_out_ref, rank_ref, rows_ref, total_ref = refs
    step = pl.program_id(0)
    experts, tokens = rank_ref.shape
    peers, tiles = in_ref.shape[0], out_ref.shape[1] // LANE
    half = tiles * HALF

    @pl.when(step == 0)
    def _():
        rank_ref[...] = expert_ranks(ids_ref[...], experts)
        total_ref[...] = jnp.zeros_like(total_ref) if extra else before_ref[...]

    unpack_half(in_ref, 0, rows_ref, 0, tiles)
    rank = rank_ref[pl.ds(pl.multiple_of(step * peers, peers), peers), :]
    which = half_rows(rank, None, 0 if extra else HALF)
    if extra:
        unpack_extra(in_ref, half, rows_ref, peers * HALF)
        some = by_slot(rank, 8)
        some = jnp.where(some == (2 * HALF + iota(some.shape, 0) % 8).astype(F32), 1.0, 0.0).astype(BF)
        shape = (peers * EXTRA, peers * 8)
        keep = iota(shape, 1) == iota(shape, 0) // EXTRA * 8 + iota(shape, 0) % EXTRA
        which = jnp.concatenate([which, dot(jnp.where(keep, 1.0, 0.0).astype(BF), some).astype(BF)], axis=0)
    total_ref[...] += lax.dot_general(which, rows_ref[...], (((0,), (0,)), ((), ())), preferred_element_type=F32)

    @pl.when(step == pl.num_programs(0) - 1)
    def _():
        slots = slots_ref[:, 0, :].astype(F32)
        rank = rank_ref[...]
        found = jnp.zeros((experts, tokens), F32)
        for lane in range(FIRST if extra else HALF):
            slot = (lane if lane < HALF else lane + HALF) if extra else lane + HALF
            found = found + jnp.where(rank == float(slot), slots[:, lane : lane + 1], 0.0)
        ids = ids_ref[...]
        expert = iota((experts, tokens), 0)
        grads = [
            jnp.sum(jnp.where(ids[k : k + 1] == expert, found, 0.0), axis=0, keepdims=True)
            for k in range(ids.shape[0])
        ]
        grads = jnp.concatenate(grads, axis=0)
        if extra:
            probs_out_ref[...] = grads
        else:
            out_ref[...] = total_ref[...].astype(BF)
            probs_out_ref[...] = ((grads + probs_before_ref[...]) / probs_ref[...].astype(F32)).astype(BF)


def combine(name, ids, got, width, before=()):
    experts, rows, _ = got.shape
    top, tokens = ids.shape
    extra = not before
    slots = FIRST if extra else HALF
    whole = lambda shape: pl.BlockSpec(shape, lambda i: (0, 0))
    kind = F32 if extra else BF
    return pl.pallas_call(
        functools.partial(combine_kernel, extra),
        grid=(experts // PEERS,),
        out_shape=[jax.ShapeDtypeStruct((tokens, width), kind), jax.ShapeDtypeStruct((top, tokens), kind)],
        in_specs=[
            whole(ids.shape),
            pl.BlockSpec((PEERS, rows, LANE), lambda i: (i, 0, 0)),
            pl.BlockSpec((experts, TILE, LANE), lambda i: (0, rows // TILE - 1, 0)),
        ]
        + [whole(a.shape) for a in before],
        out_specs=[whole((tokens, width)), whole((top, tokens))],
        scratch_shapes=[pltpu.VMEM((experts, tokens), F32), pltpu.VMEM((PEERS * slots, width), BF)]
        + ([] if extra else [pltpu.VMEM((tokens, width), F32)]),
        compiler_params=pltpu.CompilerParams(vmem_limit_bytes=VMEM),
        cost_estimate=pl.CostEstimate(
            flops=2 * experts * slots * tokens * width, bytes_accessed=2 * experts * rows * LANE, transcendentals=0
        ),
        name=name,
    )(ids, got, got, *before)


def exchange(x):
    return lax.all_to_all(x, ("ctx", "tp"), split_axis=0, concat_axis=0, tiled=True)


def other_core(x):
    return lax.ppermute(x, "dp", [(0, 1), (1, 0)])


def contract_rows(left, right):
    return lax.dot_general(left, right, (((0,), (0,)), ((), ())), preferred_element_type=F32).astype(BF)


def per_device(tokens, cotangent, probs, expert_ids, gate_weight, up_weight, down_weight):
    experts = lax.axis_size("ctx") * lax.axis_size("tp")
    gate_mat, up_mat, down_mat = gate_weight[0], up_weight[0], down_weight[0]
    ids, weights = expert_ids.T, probs.T
    values = (tokens, cotangent)
    sent_a = pack("pack_a", pack_first_kernel, 2 * FIRST, 2, ids, weights, values, experts)
    got_a = exchange(sent_a)
    sent_b, gate_t, up_t, down_t = lax.optimization_barrier(
        (
            pack("pack_b", pack_second_kernel, 2 * HALF, 0, ids, weights, values, experts),
            gate_mat.T,
            up_mat.T,
            down_mat.T,
        )
    )
    got_b = exchange(sent_b)
    mats = (gate_mat, up_mat, down_t)

    def part(name, got):
        rows, cot_rows, gate, up, back = project("project_" + name, got, mats)
        far = other_core(gate), other_core(up), other_core(back)
        sent, *grads = pair("pair_" + name, gate, far[0], up, far[1], back, far[2], gate_t, up_t, experts)
        return sent, (rows, cot_rows, *grads)

    pairs_a, kept_a = part("a", got_a)
    got_b, pairs_a = lax.optimization_barrier((got_b, pairs_a))
    back_a = exchange(pairs_a)
    pairs_b, kept_b = part("b", got_b)
    back_b = exchange(pairs_b)
    rows, cot_rows, act, gate_grad, up_grad = (jnp.concatenate(ab) for ab in zip(kept_a, kept_b))
    grad_down = contract_rows(act, cot_rows)
    grad_gate = contract_rows(rows, gate_grad)
    grad_up = contract_rows(rows, up_grad)
    width = tokens.shape[1]
    before = combine("combine_a", ids, back_a, width)
    grad_tokens, grad_probs = combine("combine_b", ids, back_b, width, (weights, *before))
    return (grad_tokens, grad_probs.T, grad_gate[None], grad_up[None], grad_down[None])


def solution(mesh):
    return jax.shard_map(
        per_device,
        mesh=mesh,
        in_specs=(
            P(("ctx", "tp"), "dp"),
            P(("ctx", "tp"), "dp"),
            P(("ctx", "tp"), None),
            P(("ctx", "tp"), None),
            P(("ctx", "tp"), "dp", None),
            P(("ctx", "tp"), "dp", None),
            P(("ctx", "tp"), None, "dp"),
        ),
        out_specs=(
            P(("ctx", "tp"), "dp"),
            P(("ctx", "tp"), None),
            P(("ctx", "tp"), "dp", None),
            P(("ctx", "tp"), "dp", None),
            P(("ctx", "tp"), None, "dp"),
        ),
        check_vma=False,
    )
```

time: 296 us -> 231 us (0.78)
  waiting for transfers between devices: 154 us -> 91.3 us
  Pallas kernels: 69.4 us -> 61.8 us
  matrix products: 17.3 us -> 22.9 us
    all_to_all x3 -> x4, waiting for transfers between devices: 149 us -> 86.3 us  [exchange(): lax.all_to_all(x, ('ctx', 'tp'), split_axis=0, concat_axis=0, tiled=True)]
    pallas_call x9 -> x6, Pallas kernels: 59.8 us -> 52 us  [the longest x2 23.4 us: project(): pl.pallas_call(functools.partial(project_kernel, slots == FIRST), grid=(e...]
    dot_general x3, matrix products: 17.3 us -> 22.9 us  [contract_rows(): lax.dot_general(left, right, (((0,), (0,)), ((), ())), preferred_element_...]
    all_to_all x3 -> x4, starting transfers between devices: 32.1 us -> 34.2 us  [exchange(): lax.all_to_all(x, ('ctx', 'tp'), split_axis=0, concat_axis=0, tiled=True)]
  transfers between devices with their start and end apart: 9 -> 10, of which waited for: 5 -> 7; matrix products, arithmetic and copies ran while one was open for 10% -> 15% of each run, Pallas kernels for 14% -> 23%
where the time goes in v4:
time: 231 us; the launch traced here: 230 us
  waiting for transfers between devices  91.3 us (40%)
  Pallas kernels  61.8 us (27%)
  starting transfers between devices  35.5 us (15%)
  matrix products  22.9 us (10%)
  local copies, waits for them, and re-layouts  17.8 us (8%)
    all_to_all x4, waiting for transfers between devices, exchange(): lax.all_to_all(x, ('ctx', 'tp'), split_axis=0, concat_axis=0, tiled=True)  86.3 us
    all_to_all x4, starting transfers between devices, exchange(): lax.all_to_all(x, ('ctx', 'tp'), split_axis=0, concat_axis=0, tiled=True)  34.2 us
    pallas_call x2, Pallas kernels, project(): pl.pallas_call(functools.partial(project_kernel, slots == FIRST), grid=(e...  23.4 us
    dot_general x3, matrix products, contract_rows(): lax.dot_general(left, right, (((0,), (0,)), ((), ())), preferred_element_...  22.9 us
    pallas_call x2, Pallas kernels, pair(): pl.pallas_call(functools.partial(pair_kernel, slots == FIRST), grid=(expe...  19.8 us
    unnamed x36, local copies, waits for them, and re-layouts  17.5 us
    pallas_call x2, Pallas kernels, pack(): pl.pallas_call(kernel, grid=(experts // PEERS,), out_shape=jax.ShapeDtype...  9.84 us
    pallas_call x2, Pallas kernels, combine(): pl.pallas_call(functools.partial(combine_kernel, extra), grid=(experts //...  8.76 us
  transfers between devices with their start and end apart: 10, of which 7 were waited for; matrix products, arithmetic and copies ran while one was open for 15% of the time, Pallas kernels for 23%

profile of v4, /device:TPU:0, one launch (start us, length us, event | category | flops | bytes accessed | tf_op | source)
XLA Modules:
  0.0 230.1 jit_solution(11026777988504560371)
XLA Ops:
  0.6 5.7 %pack_a.1 = bf16[64,320,128]{2,1,0:T(8,128)(2,1)} custom-call(s32[8,128]{1,0:T(8,128)} %bitcast.34, bf16[8,128]{1,0:T(8,128)(2,1)} %bitcast.38, bf16[128,2048]{1,0:T(8,128)(2,1)} %x_ref.3, bf16[128,2048]{1,0:T(8,128)(2,1)} %cot_ref.3), custom_call_target="tpu_custom_call" | custom-call | flops 1342177280 | bytes 5242880 | tf_op jit(solution)/shard_map/pack_a/pallas_call | solution.py:191
  6.3 12.0 %all-to-all-start.1 = ((bf16[64,320,128]{2,1,0:T(8,128)(2,1)}), bf16[64,320,128]{2,1,0:T(8,128)(2,1)}, u32[]{:S(2)}, u32[]{:S(2)}) async-start(bf16[64,320,128]{2,1,0:T(8,128)(2,1)} %pack_a.1), calls=%async_computation.1 | async-start | bytes 10485760 | tf_op jit(solution)/shard_map/all_to_all | solution.py:380
  18.3 0.0 copy-done.1
  18.3 2.8 %copy.14 = bf16[1,768,2048]{1,2,0:T(8,128)(2,1)} copy(bf16[1,768,2048]{2,1,0:T(8,128)(2,1)S(1)} %copy-done.1) | data formatting | bytes 6291456 | tf_op args[6]
  21.1 4.8 %copy.12 = bf16[1,2048,768]{1,2,0:T(8,128)(2,1)} copy(bf16[1,2048,768]{2,1,0:T(8,128)(2,1)} %param.11) | data formatting | bytes 6291456 | tf_op args[4]
  25.9 0.0 copy-done.2
  25.9 2.9 %copy.13 = bf16[1,2048,768]{1,2,0:T(8,128)(2,1)} copy(bf16[1,2048,768]{2,1,0:T(8,128)(2,1)S(1)} %copy-done.2) | data formatting | bytes 6291456 | tf_op args[5]
  28.7 4.2 %pack_b.1 = bf16[64,256,128]{2,1,0:T(8,128)(2,1)} custom-call(s32[8,128]{1,0:T(8,128)} %bitcast.35, bf16[8,128]{1,0:T(8,128)(2,1)} %bitcast.39, bf16[128,2048]{1,0:T(8,128)(2,1)} %x_ref.3, bf16[128,2048]{1,0:T(8,128)(2,1)} %cot_ref.3), custom_call_target="tpu_custom_call" | custom-call | flops 1073741824 | bytes 4194304 | tf_op jit(solution)/shard_map/pack_b/pallas_call | solution.py:191
  32.9 52.3 %all-to-all-done.1.x_in.cot_in = bf16[64,320,128]{2,1,0:T(8,128)(2,1)} async-done(((bf16[64,320,128]{2,1,0:T(8,128)(2,1)}), bf16[64,320,128]{2,1,0:T(8,128)(2,1)}, u32[]{:S(2)}, u32[]{:S(2)}) %all-to-all-start.1) | async-done | bytes 5242912 | tf_op jit(solution)/shard_map/all_to_all | solution.py:380
  85.2 8.3 %all-to-all-start = ((bf16[64,256,128]{2,1,0:T(8,128)(2,1)}), bf16[64,256,128]{2,1,0:T(8,128)(2,1)}, u32[]{:S(2)}, u32[]{:S(2)}) async-start(bf16[64,256,128]{2,1,0:T(8,128)(2,1)} %pack_b.1), calls=%async_computation | async-start | bytes 8388608 | tf_op jit(solution)/shard_map/all_to_all | solution.py:380
  93.5 12.5 %project_a.1 = (bf16[640,2048]{1,0:T(8,128)(2,1)}, bf16[640,2048]{1,0:T(8,128)(2,1)}, bf16[640,768]{1,0:T(8,128)(2,1)}, bf16[640,768]{1,0:T(8,128)(2,1)}, bf16[640,768]{1,0:T(8,128)(2,1)}) custom-call(bf16[64,320,128]{2,1,0:T(8,128)(2,1)} %all-to-all-done.1.x_in.cot_in, bf16[64,320,128]{2,1,0:T(8,128)(2,1)} %all-to-all-done.1.x_in.cot_in, ...), custom_call_target="tpu_custom_call" | custom-call | flops 6039797760 | bytes 22872064 | tf_op jit(solution)/shard_map/project_a/pallas_call | solution.py:224
  106.0 0.0 collective-permute-start
  106.0 0.5 collective-permute-start.1
  106.5 0.1 collective-permute-start.2
  106.6 2.2 collective-permute-done.gate_far
  108.8 1.4 collective-permute-done.1.up_far
  110.2 1.4 collective-permute-done.2.back_far
  111.6 0.0 copy-done.5
  111.6 0.0 copy-done.6
  111.6 1.0 copy-done.7
  112.6 10.8 %pair_a.1 = (bf16[64,176,128]{2,1,0:T(8,128)(2,1)}, bf16[640,768]{1,0:T(8,128)(2,1)}, bf16[640,768]{1,0:T(8,128)(2,1)}, bf16[640,768]{1,0:T(8,128)(2,1)}) custom-call(bf16[640,768]{1,0:T(8,128)(2,1)} %get-tuple-element.35.gate, bf16[640,768]{1,0:T(8,128)(2,1)} %copy-done.5, bf16[640,768]{1,0:T(8,128)(2,1)} %get-tuple-element.36.up, ...), custom_call_target="tpu_custom_call" | custom-call | flops 4026531840 | bytes 17760256 | tf_op jit(solution)/shard_map/pair_a/pallas_call | solution.py:284
  123.4 22.4 %all-to-all-done.x_in.cot_in = bf16[64,256,128]{2,1,0:T(8,128)(2,1)} async-done(((bf16[64,256,128]{2,1,0:T(8,128)(2,1)}), bf16[64,256,128]{2,1,0:T(8,128)(2,1)}, u32[]{:S(2)}, u32[]{:S(2)}) %all-to-all-start) | async-done | bytes 4194336 | tf_op jit(solution)/shard_map/all_to_all | solution.py:380
  145.8 7.3 %all-to-all-start.3 = ((bf16[64,176,128]{2,1,0:T(8,128)(2,1)}), bf16[64,176,128]{2,1,0:T(8,128)(2,1)S(1)}, u32[]{:S(2)}, u32[]{:S(2)}) async-start(bf16[64,176,128]{2,1,0:T(8,128)(2,1)} %get-tuple-element.46), calls=%async_computation.3 | async-start | bytes 5767168 | tf_op jit(solution)/shard_map/all_to_all | solution.py:380
  153.1 10.9 %project_b.1 = (bf16[512,2048]{1,0:T(8,128)(2,1)}, bf16[512,2048]{1,0:T(8,128)(2,1)}, bf16[512,768]{1,0:T(8,128)(2,1)}, bf16[512,768]{1,0:T(8,128)(2,1)}, bf16[512,768]{1,0:T(8,128)(2,1)}) custom-call(bf16[64,256,128]{2,1,0:T(8,128)(2,1)} %all-to-all-done.x_in.cot_in, bf16[64,256,128]{2,1,0:T(8,128)(2,1)} %all-to-all-done.x_in.cot_in, ...), custom_call_target="tpu_custom_call" | custom-call | flops 4831838208 | bytes 20185088 | tf_op jit(solution)/shard_map/project_b/pallas_call | solution.py:224
  164.0 0.1 collective-permute-start.3
  164.1 0.5 collective-permute-start.4
  164.6 0.1 collective-permute-start.5
  164.7 2.1 constant_dynamic-update-slice_fusion.1
  166.8 0.0 copy-done.3
  166.8 0.2 constant_dynamic-update-slice_fusion
  167.0 0.0 copy-start.4
  167.0 2.2 copy-done.4
  169.2 0.0 collective-permute-done.3.gate_far
  169.2 0.9 copy-done.8
  170.1 0.0 collective-permute-done.4.up_far
  170.1 0.9 copy-done.9
  171.0 0.0 collective-permute-done.5.back_far
  171.0 9.0 %pair_b.1 = (bf16[64,144,128]{2,1,0:T(8,128)(2,1)}, bf16[512,768]{1,0:T(8,128)(2,1)}, bf16[512,768]{1,0:T(8,128)(2,1)}, bf16[512,768]{1,0:T(8,128)(2,1)}) custom-call(bf16[512,768]{1,0:T(8,128)(2,1)} %get-tuple-element.42.gate, bf16[512,768]{1,0:T(8,128)(2,1)} %copy-done.8, bf16[512,768]{1,0:T(8,128)(2,1)} %get-tuple-element.43.up, ...), custom_call_target="tpu_custom_call" | custom-call | flops 3221225472 | bytes 15466496 | tf_op jit(solution)/shard_map/pair_b/pallas_call | solution.py:284
  180.1 9.7 %all-to-all-done.3.in_ref.slots_ref = bf16[64,176,128]{2,1,0:T(8,128)(2,1)S(1)} async-done(((bf16[64,176,128]{2,1,0:T(8,128)(2,1)}), bf16[64,176,128]{2,1,0:T(8,128)(2,1)S(1)}, u32[]{:S(2)}, u32[]{:S(2)}) %all-to-all-start.3) | async-done | bytes 2883616 | tf_op jit(solution)/shard_map/all_to_all | solution.py:380
  189.7 6.6 %all-to-all-start.2 = ((bf16[64,144,128]{2,1,0:T(8,128)(2,1)}), bf16[64,144,128]{2,1,0:T(8,128)(2,1)}, u32[]{:S(2)}, u32[]{:S(2)}) async-start(bf16[64,144,128]{2,1,0:T(8,128)(2,1)} %get-tuple-element.45), calls=%async_computation.2 | async-start | bytes 4718592 | tf_op jit(solution)/shard_map/all_to_all | solution.py:380
  196.3 0.0 copy-start.12
  196.4 9.0 %fusion.8 = bf16[1,2048,768]{2,1,0:T(8,128)(2,1)} fusion(bf16[1152,2048]{1,0:T(8,128)(2,1)} %copy-done.4, bf16[512,768]{1,0:T(8,128)(2,1)} %get-tuple-element.56, bf16[640,768]{1,0:T(8,128)(2,1)} %get-tuple-element.55), kind=kOutput, calls=%fused_computation.8 | convolution fusion | flops 3628990464 | bytes 9633792 | tf_op jit(solution)/shard_map/dot_general | solution.py:388
  205.4 0.0 copy-done.15
  205.4 8.3 %fusion.7 = bf16[1,2048,768]{2,1,0:T(8,128)(2,1)} fusion(bf16[1152,2048]{1,0:T(8,128)(2,1)} %copy-done.4, bf16[512,768]{1,0:T(8,128)(2,1)S(1)} %copy-done.12, bf16[640,768]{1,0:T(8,128)(2,1)S(1)} %copy-done.15), kind=kOutput, calls=%fused_computation.7 | convolution fusion | flops 3628990464 | bytes 9633792 | tf_op jit(solution)/shard_map/dot_general | solution.py:388
  213.7 5.7 %fusion.9 = bf16[1,768,2048]{2,1,0:T(8,128)(2,1)} fusion(bf16[512,2048]{1,0:T(8,128)(2,1)S(1)} %copy-done.10, bf16[640,2048]{1,0:T(8,128)(2,1)S(1)} %copy-done.13, bf16[512,768]{1,0:T(8,128)(2,1)S(1)} %copy-done.11, bf16[640,768]{1,0:T(8,128)(2,1)S(1)} %copy-done.14), kind=kOutput, calls=%fused_computation.9 | convolution fusion | flops 3638427648 | bytes 9633792 | tf_op jit(solution)/shard_map/dot_general | solution.py:388
  219.4 4.6 %combine_a.1 = (f32[128,2048]{1,0:T(8,128)}, f32[8,128]{1,0:T(8,128)}) custom-call(s32[8,128]{1,0:T(8,128)} %bitcast.36, bf16[64,176,128]{2,1,0:T(8,128)(2,1)} %copy-done, bf16[64,176,128]{2,1,0:T(8,128)(2,1)} %copy-done), custom_call_target="tpu_custom_call" | custom-call | flops 335544320 | bytes 2883584 | tf_op jit(solution)/shard_map/combine_a/pallas_call | solution.py:358
  224.0 2.0 all-to-all-done.2.in_ref.slots_ref
  225.9 4.2 %combine_b.1 = (bf16[128,2048]{1,0:T(8,128)(2,1)}, bf16[8,128]{1,0:T(8,128)(2,1)}) custom-call(s32[8,128]{1,0:T(8,128)} %bitcast.37, bf16[64,144,128]{2,1,0:T(8,128)(2,1)} %all-to-all-done.2.in_ref.slots_ref, bf16[64,144,128]{2,1,0:T(8,128)(2,1)} %all-to-all-done.2.in_ref.slots_ref, bf16[8,128]{1,0:T(8,128)(2,1)} %bitcast.40, ...), custom_call_target="tpu_custom_call" | custom-call | flops 268435456 | bytes 2359296 | tf_op jit(solution)/shard_map/combine_b/pallas_call | solution.py:358
  (20 shorter events, 0.0 us)
Async XLA Ops:
  6.3 12.0 %copy-start.1 = (bf16[1,768,2048]{2,1,0:T(8,128)(2,1)S(1)}, bf16[1,768,2048]{2,1,0:T(8,128)(2,1)}, u32[]{:S(2)}) copy-start(bf16[1,768,2048]{2,1,0:T(8,128)(2,1)} %param.13) | copy-start | bytes 9437188
  6.3 78.9 %all-to-all-start.1 = ((bf16[64,320,128]{2,1,0:T(8,128)(2,1)}), bf16[64,320,128]{2,1,0:T(8,128)(2,1)}, u32[]{:S(2)}, u32[]{:S(2)}) async-start(bf16[64,320,128]{2,1,0:T(8,128)(2,1)} %pack_a.1), calls=%async_computation.1 | async-start | bytes 10485760 | tf_op jit(solution)/shard_map/all_to_all | solution.py:380
  21.1 4.8 %copy-start.2 = (bf16[1,2048,768]{2,1,0:T(8,128)(2,1)S(1)}, bf16[1,2048,768]{2,1,0:T(8,128)(2,1)}, u32[]{:S(2)}) copy-start(bf16[1,2048,768]{2,1,0:T(8,128)(2,1)} %param.12) | copy-start | bytes 9437188
  85.2 60.6 %all-to-all-start = ((bf16[64,256,128]{2,1,0:T(8,128)(2,1)}), bf16[64,256,128]{2,1,0:T(8,128)(2,1)}, u32[]{:S(2)}, u32[]{:S(2)}) async-start(bf16[64,256,128]{2,1,0:T(8,128)(2,1)} %pack_b.1), calls=%async_computation | async-start | bytes 8388608 | tf_op jit(solution)/shard_map/all_to_all | solution.py:380
  106.0 2.8 %collective-permute-start = (bf16[640,768]{1,0:T(8,128)(2,1)}, bf16[640,768]{1,0:T(8,128)(2,1)S(1)}, u32[]{:S(2)}, u32[]{:S(2)}) collective-permute-start(bf16[640,768]{1,0:T(8,128)(2,1)} %get-tuple-element.35.gate), channel_id=1, source_target_pairs={{0,64},{64,0},{1,65},{65,1},{2,66},{66,2},{3,67},{67,3},{4,68},{68... | collective-permute-start | bytes 2949128 | tf_op jit(solution)/shard_map/ppermute | solution.py:384
  106.0 4.2 %collective-permute-start.1 = (bf16[640,768]{1,0:T(8,128)(2,1)}, bf16[640,768]{1,0:T(8,128)(2,1)S(1)}, u32[]{:S(2)}, u32[]{:S(2)}) collective-permute-start(bf16[640,768]{1,0:T(8,128)(2,1)} %get-tuple-element.36.up), channel_id=1, source_target_pairs={{0,64},{64,0},{1,65},{65,1},{2,66},{66,2},{3,67},{67,3},{4,68},{68... | collective-permute-start | bytes 2949128 | tf_op jit(solution)/shard_map/ppermute | solution.py:384
  106.5 5.1 %collective-permute-start.2 = (bf16[640,768]{1,0:T(8,128)(2,1)}, bf16[640,768]{1,0:T(8,128)(2,1)S(1)}, u32[]{:S(2)}, u32[]{:S(2)}) collective-permute-start(bf16[640,768]{1,0:T(8,128)(2,1)} %get-tuple-element.37.back), channel_id=1, source_target_pairs={{0,64},{64,0},{1,65},{65,1},{2,66},{66,2},{3,67},{67,3},{4,68},{68... | collective-permute-start | bytes 2949128 | tf_op jit(solution)/shard_map/ppermute | solution.py:384
  108.8 2.8 %copy-start.5 = (bf16[640,768]{1,0:T(8,128)(2,1)}, bf16[640,768]{1,0:T(8,128)(2,1)S(1)}, u32[]{:S(2)}) copy-start(bf16[640,768]{1,0:T(8,128)(2,1)S(1)} %collective-permute-done.gate_far) | copy-start | bytes 2949124
  110.2 1.4 copy-start.6
  111.6 1.0 copy-start.7
  145.8 43.9 %all-to-all-start.3 = ((bf16[64,176,128]{2,1,0:T(8,128)(2,1)}), bf16[64,176,128]{2,1,0:T(8,128)(2,1)S(1)}, u32[]{:S(2)}, u32[]{:S(2)}) async-start(bf16[64,176,128]{2,1,0:T(8,128)(2,1)} %get-tuple-element.46), calls=%async_computation.3 | async-start | bytes 5767168 | tf_op jit(solution)/shard_map/all_to_all | solution.py:380
  164.0 2.7 %copy-start.3 = (bf16[512,2048]{1,0:T(8,128)(2,1)S(1)}, bf16[512,2048]{1,0:T(8,128)(2,1)}, u32[]{:S(2)}) copy-start(bf16[512,2048]{1,0:T(8,128)(2,1)} %get-tuple-element.52) | copy-start | bytes 6291460
  164.0 5.2 %collective-permute-start.3 = (bf16[512,768]{1,0:T(8,128)(2,1)}, bf16[512,768]{1,0:T(8,128)(2,1)S(1)}, u32[]{:S(2)}, u32[]{:S(2)}) collective-permute-start(bf16[512,768]{1,0:T(8,128)(2,1)} %get-tuple-element.42.gate), channel_id=1, source_target_pairs={{0,64},{64,0},{1,65},{65,1},{2,66},{66,2},{3,67},{67,3},{4,68},{68... | collective-permute-start | bytes 2359304 | tf_op jit(solution)/shard_map/ppermute | solution.py:384
  164.1 6.0 %collective-permute-start.4 = (bf16[512,768]{1,0:T(8,128)(2,1)}, bf16[512,768]{1,0:T(8,128)(2,1)S(1)}, u32[]{:S(2)}, u32[]{:S(2)}) collective-permute-start(bf16[512,768]{1,0:T(8,128)(2,1)} %get-tuple-element.43.up), channel_id=1, source_target_pairs={{0,64},{64,0},{1,65},{65,1},{2,66},{66,2},{3,67},{67,3},{4,68},{68... | collective-permute-start | bytes 2359304 | tf_op jit(solution)/shard_map/ppermute | solution.py:384
  164.6 6.4 %collective-permute-start.5 = (bf16[512,768]{1,0:T(8,128)(2,1)}, bf16[512,768]{1,0:T(8,128)(2,1)}, u32[]{:S(2)}, u32[]{:S(2)}) collective-permute-start(bf16[512,768]{1,0:T(8,128)(2,1)} %get-tuple-element.44.back), channel_id=1, source_target_pairs={{0,64},{64,0},{1,65},{65,1},{2,66},{66,2},{3,67},{67,3},{4,68},{68... | collective-permute-start | bytes 2359304 | tf_op jit(solution)/shard_map/ppermute | solution.py:384
  167.0 2.2 copy-start.4
  169.2 0.9 copy-start.8
  170.1 0.9 copy-start.9
  189.7 15.6 %copy-start = (bf16[64,176,128]{2,1,0:T(8,128)(2,1)}, bf16[64,176,128]{2,1,0:T(8,128)(2,1)S(1)}, u32[]{:S(2)}) copy-start(bf16[64,176,128]{2,1,0:T(8,128)(2,1)S(1)} %all-to-all-done.3.in_ref.slots_ref) | copy-start | bytes 8650756
  189.7 36.2 %all-to-all-start.2 = ((bf16[64,144,128]{2,1,0:T(8,128)(2,1)}), bf16[64,144,128]{2,1,0:T(8,128)(2,1)}, u32[]{:S(2)}, u32[]{:S(2)}) async-start(bf16[64,144,128]{2,1,0:T(8,128)(2,1)} %get-tuple-element.45), calls=%async_computation.2 | async-start | bytes 4718592 | tf_op jit(solution)/shard_map/all_to_all | solution.py:380
  196.3 9.0 %copy-start.12 = (bf16[512,768]{1,0:T(8,128)(2,1)S(1)}, bf16[512,768]{1,0:T(8,128)(2,1)}, u32[]{:S(2)}) copy-start(bf16[512,768]{1,0:T(8,128)(2,1)} %get-tuple-element.54) | copy-start | bytes 2359300
  196.4 9.0 %copy-start.15 = (bf16[640,768]{1,0:T(8,128)(2,1)S(1)}, bf16[640,768]{1,0:T(8,128)(2,1)}, u32[]{:S(2)}) copy-start(bf16[640,768]{1,0:T(8,128)(2,1)} %get-tuple-element.53) | copy-start | bytes 2949124
  205.4 8.3 %copy-start.10 = (bf16[512,2048]{1,0:T(8,128)(2,1)S(1)}, bf16[512,2048]{1,0:T(8,128)(2,1)}, u32[]{:S(2)}) copy-start(bf16[512,2048]{1,0:T(8,128)(2,1)} %get-tuple-element.60) | copy-start | bytes 6291460
  205.4 8.3 %copy-start.11 = (bf16[512,768]{1,0:T(8,128)(2,1)S(1)}, bf16[512,768]{1,0:T(8,128)(2,1)}, u32[]{:S(2)}) copy-start(bf16[512,768]{1,0:T(8,128)(2,1)} %get-tuple-element.58) | copy-start | bytes 2359300
  205.4 8.3 %copy-start.13 = (bf16[640,2048]{1,0:T(8,128)(2,1)S(1)}, bf16[640,2048]{1,0:T(8,128)(2,1)}, u32[]{:S(2)}) copy-start(bf16[640,2048]{1,0:T(8,128)(2,1)} %get-tuple-element.59) | copy-start | bytes 7864324
  205.4 8.3 %copy-start.14 = (bf16[640,768]{1,0:T(8,128)(2,1)S(1)}, bf16[640,768]{1,0:T(8,128)(2,1)}, u32[]{:S(2)}) copy-start(bf16[640,768]{1,0:T(8,128)(2,1)} %get-tuple-element.57) | copy-start | bytes 2949124

commit v5 on v4

--- a/solution.py
+++ b/solution.py
@@ -17,6 +17,9 @@
 TILE = 16
 GROUP = 16
 PEERS = 32
+SECOND_PEERS = 16
+PACK_PEERS = 32
+SUM_PEERS = 64
 VMEM = 60 * 2**20
 
 
@@ -26,6 +29,10 @@
 
 def dot(a, b):
     return jnp.dot(a, b, preferred_element_type=F32)
+
+
+def contract(left, right):
+    return lax.dot_general(left, right, (((0,), (0,)), ((), ())), preferred_element_type=F32)
 
 
 def expert_ranks(ids, experts):
@@ -129,6 +136,16 @@
 
 
 def extra_rows(rank, value):
+    peers = rank.shape[0]
+    rank = by_slot(rank, 8)
+    hit = rank == (2 * HALF + iota(rank.shape, 0) % 8).astype(F32)
+    eight = jnp.where(hit, 1.0 if value is None else by_slot(value, 8), 0.0).astype(BF)
+    shape = (peers * EXTRA, peers * 8)
+    keep = iota(shape, 1) == iota(shape, 0) // EXTRA * 8 + iota(shape, 0) % EXTRA
+    return dot(jnp.where(keep, 1.0, 0.0).astype(BF), eight).astype(BF)
+
+
+def wide_extra_rows(rank, value):
     rank = by_slot(rank, TILE)
     row = iota(rank.shape, 0)
     hit = rank == (2 * HALF + row % EXTRA).astype(F32)
@@ -156,6 +173,7 @@
     step = pl.program_id(0)
     half = x_ref.shape[1] // LANE * HALF
     part = x_ref.shape[1] // LANE * FIRST
+    count = out_ref.shape[0]
 
     @pl.when(step == 0)
     def _():
@@ -163,12 +181,11 @@
         stack_columns(x_ref, side_ref)
         stack_columns(cot_ref, cot_side_ref)
 
-    peers = pl.ds(pl.multiple_of(step * PEERS, PEERS), PEERS)
+    peers = pl.ds(pl.multiple_of(step * count, count), count)
     rank, prob = rank_ref[peers, :], prob_ref[peers, :]
-    store_half(out_ref, 0, dot(half_rows(rank, None, 0), x_ref[...]))
-    store_extra(out_ref, half, dot(extra_rows(rank, None), side_ref[...]).astype(BF))
-    store_half(out_ref, part, dot(half_rows(rank, prob, 0), cot_ref[...]))
-    store_extra(out_ref, part + half, dot(extra_rows(rank, prob), cot_side_ref[...]).astype(BF))
+    for start, value, ref, side in ((0, None, x_ref, side_ref), (part, prob, cot_ref, cot_side_ref)):
+        store_half(out_ref, start, dot(half_rows(rank, value, 0), ref[...]))
+        store_extra(out_ref, start + half, dot(wide_extra_rows(rank, value), side[...]).astype(BF))
 
 
 def pack_second_kernel(ids_ref, probs_ref, x_ref, cot_ref, out_ref, rank_ref, prob_ref):
@@ -179,7 +196,8 @@
     def _():
         start_pack(ids_ref, probs_ref, rank_ref, prob_ref)
 
-    peers = pl.ds(pl.multiple_of(step * PEERS, PEERS), PEERS)
+    count = out_ref.shape[0]
+    peers = pl.ds(pl.multiple_of(step * count, count), count)
     rank, prob = rank_ref[peers, :], prob_ref[peers, :]
     store_half(out_ref, 0, dot(half_rows(rank, None, HALF), x_ref[...]))
     store_half(out_ref, half, dot(half_rows(rank, prob, HALF), cot_ref[...]))
@@ -190,10 +208,10 @@
     rows = width // LANE * slots
     return pl.pallas_call(
         kernel,
-        grid=(experts // PEERS,),
+        grid=(experts // PACK_PEERS,),
         out_shape=jax.ShapeDtypeStruct((experts, rows, LANE), BF),
         in_specs=[pl.BlockSpec(a.shape, lambda i: (0, 0)) for a in (ids, probs, *values)],
-        out_specs=pl.BlockSpec((PEERS, rows, LANE), lambda i: (i, 0, 0)),
+        out_specs=pl.BlockSpec((PACK_PEERS, rows, LANE), lambda i: (i, 0, 0)),
         scratch_shapes=[pltpu.VMEM((experts, tokens), F32)] * 2 + [pltpu.VMEM((8 * tokens, width // 8), BF)] * sides,
         compiler_params=pltpu.CompilerParams(vmem_limit_bytes=VMEM),
         cost_estimate=pl.CostEstimate(
@@ -203,7 +221,8 @@
     )(ids, probs, *values)
 
 
-def project_kernel(extra, x_in, cot_in, gate_w, up_w, down_w, x_ref, cot_ref, gate_ref, up_ref, back_ref):
+def project_kernel(extra, x_in, cot_in, gate_w, up_w, down_w, *refs):
+    x_ref, cot_ref, gate_ref, up_ref, back_ref = refs[-5:]
     peers = x_in.shape[0]
     tiles = x_ref.shape[1] // LANE
     for in_ref, rows_ref in ((x_in, x_ref), (cot_in, cot_ref)):
@@ -215,20 +234,25 @@
     back_ref[...] = dot(cot_ref[...], down_w[...]).astype(BF)
 
 
-def project(name, got, weights):
+def project(name, got, weights, kept=()):
     experts, both, _ = got.shape
     width, hidden = weights[0].shape
     part = both // 2
     slots = part * LANE // width
-    total, rows = experts * slots, PEERS * slots
+    peers = SECOND_PEERS if kept else PEERS
+    total, rows = experts * slots, peers * slots
+    first = experts * FIRST // rows if kept else 0
+    whole = experts * CAP
     return pl.pallas_call(
-        functools.partial(project_kernel, slots == FIRST),
-        grid=(experts // PEERS,),
-        out_shape=[jax.ShapeDtypeStruct((total, width), BF)] * 2 + [jax.ShapeDtypeStruct((total, hidden), BF)] * 3,
-        in_specs=[pl.BlockSpec((PEERS, part, LANE), lambda i, at=at: (i, at, 0)) for at in range(2)]
-        + [pl.BlockSpec(w.shape, lambda i: (0, 0)) for w in weights],
-        out_specs=[pl.BlockSpec((rows, width), lambda i: (i, 0))] * 2
+        functools.partial(project_kernel, not kept),
+        grid=(experts // peers,),
+        out_shape=[jax.ShapeDtypeStruct((whole, width), BF)] * 2 + [jax.ShapeDtypeStruct((total, hidden), BF)] * 3,
+        in_specs=[pl.BlockSpec((peers, part, LANE), lambda i, at=at: (i, at, 0)) for at in range(2)]
+        + [pl.BlockSpec(w.shape, lambda i: (0, 0)) for w in weights]
+        + [pl.BlockSpec(memory_space=pl.ANY) for _ in kept],
+        out_specs=[pl.BlockSpec((rows, width), lambda i: (first + i, 0))] * 2
         + [pl.BlockSpec((rows, hidden), lambda i: (i, 0))] * 3,
+        input_output_aliases={5 + k: k for k in range(len(kept))},
         compiler_params=pltpu.CompilerParams(vmem_limit_bytes=VMEM),
         cost_estimate=pl.CostEstimate(
             flops=6 * total * width * hidden,
@@ -236,7 +260,7 @@
             transcendentals=0,
         ),
         name=name,
-    )(got, got, *weights)
+    )(got, got, *weights, *kept)
 
 
 def slots_of(prob_grad, peers, extra):
@@ -246,13 +270,20 @@
     peer, of = iota((peers, total), 0), iota((peers, total), 1)
     slot, owner = row % HALF, of // HALF
     if extra:
-        slot = jnp.where(row < main, slot, HALF + row % EXTRA)
+        slot = jnp.where(row < main, slot, 2 * HALF + row % EXTRA)
         owner = jnp.where(of < main, owner, (of - main) // EXTRA)
+    else:
+        slot = slot + HALF
     by_lane = jnp.where(lane == slot, prob_grad, 0.0).astype(BF)
     return dot(jnp.where(peer == owner, 1.0, 0.0).astype(BF), by_lane)
 
 
-def pair_kernel(extra, gate, gate_far, up, up_far, back, back_far, gate_t, up_t, out_ref, act_ref, gg_ref, ug_ref):
+def pair_kernel(extra, *refs):
+    if extra:
+        *refs, out_ref, act_ref, gg_ref, ug_ref, slots_out_ref = refs
+    else:
+        *refs, slots_ref, _, _, _, out_ref, act_ref, gg_ref, ug_ref = refs
+    gate, gate_far, up, up_far, back, back_far, gate_t, up_t = refs
     g = gate[...].astype(F32) + gate_far[...].astype(F32)
     u = up[...].astype(F32) + up_far[...].astype(F32)
     b = back[...].astype(F32) + back_far[...].astype(F32)
@@ -265,29 +296,42 @@
     prob_grad = jnp.sum(act * b, axis=1, keepdims=True)
     y = dot(gg_ref[...], gate_t[...]) + dot(ug_ref[...], up_t[...])
     half = y.shape[1] // LANE * HALF
-    main = PEERS * HALF
+    peers = out_ref.shape[0]
+    main = peers * HALF
     store_half(out_ref, 0, y[:main])
+    slots = slots_of(prob_grad, peers, extra)
     if extra:
         order_extra(out_ref, half, y[main:].astype(BF))
-    last = out_ref.shape[1] - TILE
-    grads = by_slot(slots_of(prob_grad, PEERS, extra), TILE)
-    out_ref[:, last:, :] = grads.astype(BF).reshape(PEERS, TILE, LANE)
-
-
-def pair(name, gate, gate_far, up, up_far, back, back_far, gate_t, up_t, experts):
+        slots_out_ref[...] = slots
+    else:
+        grads = by_slot(slots + slots_ref[...], TILE)
+        out_ref[:, half:, :] = grads.astype(BF).reshape(peers, TILE, LANE)
+
+
+def pair(name, gate, gate_far, up, up_far, back, back_far, gate_t, up_t, experts, slot_grads=None, kept=()):
     total, hidden = gate.shape
     width = gate_t.shape[1]
     slots = total // experts
-    rows = width // LANE * slots + TILE
-    block = pl.BlockSpec((PEERS * slots, hidden), lambda i: (i, 0))
+    extra = not kept
+    peers = PEERS if extra else SECOND_PEERS
+    rows = width // LANE * slots + (0 if extra else TILE)
+    first = 0 if extra else experts * FIRST // (peers * slots)
+    block = pl.BlockSpec((peers * slots, hidden), lambda i: (i, 0))
+    placed = pl.BlockSpec((peers * slots, hidden), lambda i: (first + i, 0))
     whole = pl.BlockSpec(gate_t.shape, lambda i: (0, 0))
+    small = pl.BlockSpec((peers, LANE), lambda i: (i, 0))
+    more = () if extra else (slot_grads, *kept)
     return pl.pallas_call(
-        functools.partial(pair_kernel, slots == FIRST),
-        grid=(experts // PEERS,),
+        functools.partial(pair_kernel, extra),
+        grid=(experts // peers,),
         out_shape=[jax.ShapeDtypeStruct((experts, rows, LANE), BF)]
-        + [jax.ShapeDtypeStruct((total, hidden), BF)] * 3,
-        in_specs=[block] * 6 + [whole] * 2,
-        out_specs=[pl.BlockSpec((PEERS, rows, LANE), lambda i: (i, 0, 0))] + [block] * 3,
+        + [jax.ShapeDtypeStruct((experts * CAP, hidden), BF)] * 3
+        + [jax.ShapeDtypeStruct((experts, LANE), F32)] * extra,
+        in_specs=[block] * 6
+        + [whole] * 2
+        + ([] if extra else [small] + [pl.BlockSpec(memory_space=pl.ANY)] * len(kept)),
+        out_specs=[pl.BlockSpec((peers, rows, LANE), lambda i: (i, 0, 0))] + [placed] * 3 + [small] * extra,
+        input_output_aliases={9 + k: 1 + k for k in range(len(kept))},
         compiler_params=pltpu.CompilerParams(vmem_limit_bytes=VMEM),
         cost_estimate=pl.CostEstimate(
             flops=4 * total * width * hidden,
@@ -295,85 +339,101 @@
             transcendentals=total * hidden,
         ),
         name=name,
-    )(gate, gate_far, up, up_far, back, back_far, gate_t, up_t)
-
-
-def combine_kernel(extra, ids_ref, in_ref, slots_ref, *refs):
-    if extra:
-        out_ref, probs_out_ref, rank_ref, rows_ref = refs
-        total_ref = out_ref
-    else:
-        probs_ref, before_ref, probs_before_ref, out_ref, probs_out_ref, rank_ref, rows_ref, total_ref = refs
+    )(gate, gate_far, up, up_far, back, back_far, gate_t, up_t, *more)
+
+
+def combine_first_kernel(ids_ref, in_ref, total_ref, rank_ref, rows_ref):
+    step = pl.program_id(0)
+    experts = rank_ref.shape[0]
+    peers, tiles = in_ref.shape[0], total_ref.shape[1] // LANE
+
+    @pl.when(step == 0)
+    def _():
+        rank_ref[...] = expert_ranks(ids_ref[...], experts)
+        total_ref[...] = jnp.zeros_like(total_ref)
+
+    unpack_half(in_ref, 0, rows_ref, 0, tiles)
+    unpack_extra(in_ref, tiles * HALF, rows_ref, peers * HALF)
+    rank = rank_ref[pl.ds(pl.multiple_of(step * peers, peers), peers), :]
+    which = jnp.concatenate([half_rows(rank, None, 0), extra_rows(rank, None)], axis=0)
+    total_ref[...] += contract(which, rows_ref[...])
+
+
+def combine_second_kernel(
+    ids_ref, probs_ref, in_ref, slots_ref, before_ref, rank_ref, out_ref, probs_out_ref, rows_ref, total_ref
+):
     step = pl.program_id(0)
     experts, tokens = rank_ref.shape
     peers, tiles = in_ref.shape[0], out_ref.shape[1] // LANE
-    half = tiles * HALF
 
     @pl.when(step == 0)
     def _():
-        rank_ref[...] = expert_ranks(ids_ref[...], experts)
-        total_ref[...] = jnp.zeros_like(total_ref) if extra else before_ref[...]
-
-    unpack_half(in_ref, 0, rows_ref, 0, tiles)
-    rank = rank_ref[pl.ds(pl.multiple_of(step * peers, peers), peers), :]
-    which = half_rows(rank, None, 0 if extra else HALF)
-    if extra:
-        unpack_extra(in_ref, half, rows_ref, peers * HALF)
-        some = by_slot(rank, 8)
-        some = jnp.where(some == (2 * HALF + iota(some.shape, 0) % 8).astype(F32), 1.0, 0.0).astype(BF)
-        shape = (peers * EXTRA, peers * 8)
-        keep = iota(shape, 1) == iota(shape, 0) // EXTRA * 8 + iota(shape, 0) % EXTRA
-        which = jnp.concatenate([which, dot(jnp.where(keep, 1.0, 0.0).astype(BF), some).astype(BF)], axis=0)
-    total_ref[...] += lax.dot_general(which, rows_ref[...], (((0,), (0,)), ((), ())), preferred_element_type=F32)
-
-    @pl.when(step == pl.num_programs(0) - 1)
-    def _():
+        total_ref[...] = before_ref[...]
         slots = slots_ref[:, 0, :].astype(F32)
         rank = rank_ref[...]
         found = jnp.zeros((experts, tokens), F32)
-        for lane in range(FIRST if extra else HALF):
-            slot = (lane if lane < HALF else lane + HALF) if extra else lane + HALF
-            found = found + jnp.where(rank == float(slot), slots[:, lane : lane + 1], 0.0)
+        for s in range(CAP):
+            found = found + jnp.where(rank == float(s), slots[:, s : s + 1], 0.0)
         ids = ids_ref[...]
         expert = iota((experts, tokens), 0)
         grads = [
             jnp.sum(jnp.where(ids[k : k + 1] == expert, found, 0.0), axis=0, keepdims=True)
             for k in range(ids.shape[0])
         ]
-        grads = jnp.concatenate(grads, axis=0)
-        if extra:
-            probs_out_ref[...] = grads
-        else:
-            out_ref[...] = total_ref[...].astype(BF)
-            probs_out_ref[...] = ((grads + probs_before_ref[...]) / probs_ref[...].astype(F32)).astype(BF)
-
-
-def combine(name, ids, got, width, before=()):
+        probs_out_ref[...] = (jnp.concatenate(grads, axis=0) / probs_ref[...].astype(F32)).astype(BF)
+
+    unpack_half(in_ref, 0, rows_ref, 0, tiles)
+    rank = rank_ref[pl.ds(pl.multiple_of(step * peers, peers), peers), :]
+    total_ref[...] += contract(half_rows(rank, None, HALF), rows_ref[...])
+
+    @pl.when(step == pl.num_programs(0) - 1)
+    def _():
+        out_ref[...] = total_ref[...].astype(BF)
+
+
+def combine_first(ids, got, width):
     experts, rows, _ = got.shape
-    top, tokens = ids.shape
-    extra = not before
-    slots = FIRST if extra else HALF
+    tokens = ids.shape[1]
     whole = lambda shape: pl.BlockSpec(shape, lambda i: (0, 0))
-    kind = F32 if extra else BF
     return pl.pallas_call(
-        functools.partial(combine_kernel, extra),
+        combine_first_kernel,
         grid=(experts // PEERS,),
-        out_shape=[jax.ShapeDtypeStruct((tokens, width), kind), jax.ShapeDtypeStruct((top, tokens), kind)],
-        in_specs=[
-            whole(ids.shape),
-            pl.BlockSpec((PEERS, rows, LANE), lambda i: (i, 0, 0)),
-            pl.BlockSpec((experts, TILE, LANE), lambda i: (0, rows // TILE - 1, 0)),
-        ]
-        + [whole(a.shape) for a in before],
-        out_specs=[whole((tokens, width)), whole((top, tokens))],
-        scratch_shapes=[pltpu.VMEM((experts, tokens), F32), pltpu.VMEM((PEERS * slots, width), BF)]
-        + ([] if extra else [pltpu.VMEM((tokens, width), F32)]),
+        out_shape=[jax.ShapeDtypeStruct((tokens, width), F32), jax.ShapeDtypeStruct((experts, tokens), F32)],
+        in_specs=[whole(ids.shape), pl.BlockSpec((PEERS, rows, LANE), lambda i: (i, 0, 0))],
+        out_specs=[whole((tokens, width)), whole((experts, tokens))],
+        scratch_shapes=[pltpu.VMEM((PEERS * FIRST, width), BF)],
         compiler_params=pltpu.CompilerParams(vmem_limit_bytes=VMEM),
         cost_estimate=pl.CostEstimate(
-            flops=2 * experts * slots * tokens * width, bytes_accessed=2 * experts * rows * LANE, transcendentals=0
-        ),
-        name=name,
-    )(ids, got, got, *before)
+            flops=2 * experts * FIRST * tokens * width, bytes_accessed=2 * experts * rows * LANE, transcendentals=0
+        ),
+        name="combine_a",
+    )(ids, got)
+
+
+def combine_second(ids, probs, got, before, rank):
+    experts, rows, _ = got.shape
+    tokens, width = before.shape
+    whole = lambda a: pl.BlockSpec(a.shape, lambda i: (0, 0))
+    return pl.pallas_call(
+        combine_second_kernel,
+        grid=(experts // SUM_PEERS,),
+        out_shape=[jax.ShapeDtypeStruct(before.shape, BF), jax.ShapeDtypeStruct(ids.shape, BF)],
+        in_specs=[
+            whole(ids),
+            whole(probs),
+            pl.BlockSpec((SUM_PEERS, rows - TILE, LANE), lambda i: (i, 0, 0)),
+            pl.BlockSpec((experts, TILE, LANE), lambda i: (0, rows // TILE - 1, 0)),
+            whole(before),
+            whole(rank),
+        ],
+        out_specs=[whole(before), whole(ids)],
+        scratch_shapes=[pltpu.VMEM((SUM_PEERS * HALF, width), BF), pltpu.VMEM((tokens, width), F32)],
+        compiler_params=pltpu.CompilerParams(vmem_limit_bytes=VMEM),
+        cost_estimate=pl.CostEstimate(
+            flops=2 * experts * HALF * tokens * width, bytes_accessed=2 * experts * rows * LANE, transcendentals=0
+        ),
+        name="combine_b",
+    )(ids, probs, got, got, before, rank)
 
 
 def exchange(x):
@@ -382,10 +442,6 @@
 
 def other_core(x):
     return lax.ppermute(x, "dp", [(0, 1), (1, 0)])
-
-
-def contract_rows(left, right):
-    return lax.dot_general(left, right, (((0,), (0,)), ((), ())), preferred_element_type=F32).astype(BF)
 
 
 def per_device(tokens, cotangent, probs, expert_ids, gate_weight, up_weight, down_weight):
@@ -406,24 +462,24 @@
     got_b = exchange(sent_b)
     mats = (gate_mat, up_mat, down_t)
 
-    def part(name, got):
-        rows, cot_rows, gate, up, back = project("project_" + name, got, mats)
+    def part(name, got, slot_grads=None, kept=()):
+        rows, cot_rows, gate, up, back = project("project_" + name, got, mats, kept[:2])
         far = other_core(gate), other_core(up), other_core(back)
-        sent, *grads = pair("pair_" + name, gate, far[0], up, far[1], back, far[2], gate_t, up_t, experts)
-        return sent, (rows, cot_rows, *grads)
-
-    pairs_a, kept_a = part("a", got_a)
+        sent, act, gate_grad, up_grad, *slot_grads = pair(
+            "pair_" + name, gate, far[0], up, far[1], back, far[2], gate_t, up_t, experts, slot_grads, kept[2:]
+        )
+        return sent, slot_grads, (rows, cot_rows, act, gate_grad, up_grad)
+
+    pairs_a, (slot_grads,), kept = part("a", got_a)
     got_b, pairs_a = lax.optimization_barrier((got_b, pairs_a))
     back_a = exchange(pairs_a)
-    pairs_b, kept_b = part("b", got_b)
+    pairs_b, _, (rows, cot_rows, act, gate_grad, up_grad) = part("b", got_b, slot_grads, kept)
     back_b = exchange(pairs_b)
-    rows, cot_rows, act, gate_grad, up_grad = (jnp.concatenate(ab) for ab in zip(kept_a, kept_b))
-    grad_down = contract_rows(act, cot_rows)
-    grad_gate = contract_rows(rows, gate_grad)
-    grad_up = contract_rows(rows, up_grad)
-    width = tokens.shape[1]
-    before = combine("combine_a", ids, back_a, width)
-    grad_tokens, grad_probs = combine("combine_b", ids, back_b, width, (weights, *before))
+    grad_down = contract(act, cot_rows).astype(BF)
+    grad_gate = contract(rows, gate_grad).astype(BF)
+    grad_up = contract(rows, up_grad).astype(BF)
+    before, rank = combine_first(ids, back_a, tokens.shape[1])
+    grad_tokens, grad_probs = combine_second(ids, weights, back_b, before, rank)
     return (grad_tokens, grad_probs.T, grad_gate[None], grad_up[None], grad_down[None])
 
 

time: 231 us -> 230 us (level)
    ppermute x6, waiting for transfers between devices: 5 us -> 9.26 us  [other_core(): return lax.ppermute(x, 'dp', [(0, 1), (1, 0)])]
    all_to_all x4, waiting for transfers between devices: 86.3 us -> 82.9 us  [exchange(): lax.all_to_all(x, ('ctx', 'tp'), split_axis=0, concat_axis=0, tiled=True)]
    unnamed x36 -> x25, local copies, waits for them, and re-layouts: 17.5 us -> 16.1 us
  transfers between devices with their start and end apart: 10 -> 10, of which waited for: 7 -> 10; matrix products, arithmetic and copies ran while one was open for 15% -> 15% of each run, Pallas kernels for 23% -> 23%
where the time goes in v5:
time: 230 us; the launch traced here: 229 us
  waiting for transfers between devices  92.2 us (40%)
  Pallas kernels  62.5 us (27%)
  starting transfers between devices  34.6 us (15%)
  matrix products  23 us (10%)
  local copies, waits for them, and re-layouts  16.1 us (7%)
    all_to_all x4, waiting for transfers between devices, exchange(): lax.all_to_all(x, ('ctx', 'tp'), split_axis=0, concat_axis=0, tiled=True)  82.9 us
    all_to_all x4, starting transfers between devices, exchange(): lax.all_to_all(x, ('ctx', 'tp'), split_axis=0, concat_axis=0, tiled=True)  33.4 us
    pallas_call x2, Pallas kernels, project(): pl.pallas_call(functools.partial(project_kernel, not kept), grid=(experts...  24.4 us
    dot_general x3, matrix products, contract(): lax.dot_general(left, right, (((0,), (0,)), ((), ())), preferred_element_...  23 us
    pallas_call x2, Pallas kernels, pair(): pl.pallas_call(functools.partial(pair_kernel, extra), grid=(experts // pe...  20.4 us
    unnamed x25, local copies, waits for them, and re-layouts  16.1 us
    pallas_call x2, Pallas kernels, pack(): pl.pallas_call(kernel, grid=(experts // PACK_PEERS,), out_shape=jax.Shape...  9.76 us
    ppermute x6, waiting for transfers between devices, other_core(): return lax.ppermute(x, 'dp', [(0, 1), (1, 0)])  9.26 us
  transfers between devices with their start and end apart: 10, of which 10 were waited for; matrix products, arithmetic and copies ran while one was open for 15% of the time, Pallas kernels for 23%

profile of v5, /device:TPU:0, one launch (start us, length us, event | category | flops | bytes accessed | tf_op | source)
XLA Modules:
  0.0 229.0 jit_solution(14028461334156557261)
XLA Ops:
  0.6 5.6 %pack_a.1 = bf16[64,320,128]{2,1,0:T(8,128)(2,1)} custom-call(s32[8,128]{1,0:T(8,128)} %bitcast.40, bf16[8,128]{1,0:T(8,128)(2,1)} %bitcast.44, bf16[128,2048]{1,0:T(8,128)(2,1)} %x_ref.3, bf16[128,2048]{1,0:T(8,128)(2,1)} %cot_ref.3), custom_call_target="tpu_custom_call" | custom-call | flops 1342177280 | bytes 5242880 | tf_op jit(solution)/shard_map/pack_a/pallas_call | solution.py:209
  6.2 11.7 %all-to-all-start.1 = ((bf16[64,320,128]{2,1,0:T(8,128)(2,1)}), bf16[64,320,128]{2,1,0:T(8,128)(2,1)}, u32[]{:S(2)}, u32[]{:S(2)}) async-start(bf16[64,320,128]{2,1,0:T(8,128)(2,1)} %pack_a.1), calls=%async_computation.1 | async-start | bytes 10485760 | tf_op jit(solution)/shard_map/all_to_all | solution.py:440
  17.9 0.0 copy-start.1
  17.9 4.8 %copy.19 = bf16[1,768,2048]{1,2,0:T(8,128)(2,1)} copy(bf16[1,768,2048]{2,1,0:T(8,128)(2,1)} %param.13) | data formatting | bytes 6291456 | tf_op args[6]
  22.7 0.0 copy-done.1
  22.7 2.9 %copy.17 = bf16[1,2048,768]{1,2,0:T(8,128)(2,1)} copy(bf16[1,2048,768]{2,1,0:T(8,128)(2,1)S(1)} %copy-done.1) | data formatting | bytes 6291456 | tf_op args[4]
  25.6 4.6 %copy.18 = bf16[1,2048,768]{1,2,0:T(8,128)(2,1)} copy(bf16[1,2048,768]{2,1,0:T(8,128)(2,1)} %param.12) | data formatting | bytes 6291456 | tf_op args[5]
  30.2 4.2 %pack_b.1 = bf16[64,256,128]{2,1,0:T(8,128)(2,1)} custom-call(s32[8,128]{1,0:T(8,128)} %bitcast.41, bf16[8,128]{1,0:T(8,128)(2,1)} %bitcast.45, bf16[128,2048]{1,0:T(8,128)(2,1)} %x_ref.3, bf16[128,2048]{1,0:T(8,128)(2,1)} %cot_ref.3), custom_call_target="tpu_custom_call" | custom-call | flops 1073741824 | bytes 4194304 | tf_op jit(solution)/shard_map/pack_b/pallas_call | solution.py:209
  34.4 50.4 %all-to-all-done.1.x_in.cot_in = bf16[64,320,128]{2,1,0:T(8,128)(2,1)} async-done(((bf16[64,320,128]{2,1,0:T(8,128)(2,1)}), bf16[64,320,128]{2,1,0:T(8,128)(2,1)}, u32[]{:S(2)}, u32[]{:S(2)}) %all-to-all-start.1) | async-done | bytes 5242912 | tf_op jit(solution)/shard_map/all_to_all | solution.py:440
  84.8 8.3 %all-to-all-start = ((bf16[64,256,128]{2,1,0:T(8,128)(2,1)}), bf16[64,256,128]{2,1,0:T(8,128)(2,1)}, u32[]{:S(2)}, u32[]{:S(2)}) async-start(bf16[64,256,128]{2,1,0:T(8,128)(2,1)} %pack_b.1), calls=%async_computation | async-start | bytes 8388608 | tf_op jit(solution)/shard_map/all_to_all | solution.py:440
  93.1 13.4 %project_a.1 = (bf16[1152,2048]{1,0:T(8,128)(2,1)}, bf16[1152,2048]{1,0:T(8,128)(2,1)}, bf16[640,768]{1,0:T(8,128)(2,1)}, bf16[640,768]{1,0:T(8,128)(2,1)}, bf16[640,768]{1,0:T(8,128)(2,1)}) custom-call(bf16[64,320,128]{2,1,0:T(8,128)(2,1)} %all-to-all-done.1.x_in.cot_in, bf16[64,320,128]{2,1,0:T(8,128)(2,1)} %all-to-all-done.1.x_in.cot_in, ...), custom_call_target="tpu_custom_call" | custom-call | flops 6039797760 | bytes 22872064 | tf_op jit(solution)/shard_map/project_a/pallas_call | solution.py:246
  106.5 0.0 collective-permute-start
  106.5 0.5 collective-permute-start.1
  107.0 0.1 collective-permute-start.2
  107.1 2.2 collective-permute-done.refs_1_
  109.2 1.4 collective-permute-done.1.refs_3_
  110.6 1.4 collective-permute-done.2.refs_5_
  112.0 0.0 copy-done.6
  112.0 0.0 copy-done.7
  112.1 0.9 copy-done.8
  113.0 11.0 %pair_a.1 = (bf16[64,160,128]{2,1,0:T(8,128)(2,1)}, bf16[1152,768]{1,0:T(8,128)(2,1)}, bf16[1152,768]{1,0:T(8,128)(2,1)}, bf16[1152,768]{1,0:T(8,128)(2,1)}, f32[64,128]{1,0:T(8,128)}) custom-call(bf16[640,768]{1,0:T(8,128)(2,1)} %get-tuple-element.36.refs_0_, bf16[640,768]{1,0:T(8,128)(2,1)} %copy-done.6, bf16[640,768]{1,0:T(8,128)(2,1)} %get-tuple-element.37.refs_2_, ...), custom_call_target="tpu_custom_call" | custom-call | flops 4026531840 | bytes 17760256 | tf_op jit(solution)/shard_map/pair_a/pallas_call | solution.py:324
  124.0 21.4 %all-to-all-done.x_in.cot_in = bf16[64,256,128]{2,1,0:T(8,128)(2,1)} async-done(((bf16[64,256,128]{2,1,0:T(8,128)(2,1)}), bf16[64,256,128]{2,1,0:T(8,128)(2,1)}, u32[]{:S(2)}, u32[]{:S(2)}) %all-to-all-start) | async-done | bytes 4194336 | tf_op jit(solution)/shard_map/all_to_all | solution.py:440
  145.4 7.3 %all-to-all-start.3 = ((bf16[64,160,128]{2,1,0:T(8,128)(2,1)}), bf16[64,160,128]{2,1,0:T(8,128)(2,1)S(1)}, u32[]{:S(2)}, u32[]{:S(2)}) async-start(bf16[64,160,128]{2,1,0:T(8,128)(2,1)} %get-tuple-element.53), calls=%async_computation.3 | async-start | bytes 5242880 | tf_op jit(solution)/shard_map/all_to_all | solution.py:440
  152.8 11.1 %project_b.1 = (bf16[1152,2048]{1,0:T(8,128)(2,1)}, bf16[1152,2048]{1,0:T(8,128)(2,1)}, bf16[512,768]{1,0:T(8,128)(2,1)}, bf16[512,768]{1,0:T(8,128)(2,1)}, bf16[512,768]{1,0:T(8,128)(2,1)}) custom-call(bf16[64,256,128]{2,1,0:T(8,128)(2,1)} %all-to-all-done.x_in.cot_in, ...), custom_call_target="tpu_custom_call", output_to_operand_aliasing={{0}: (5, {}), {1}: (6, {})} | custom-call | flops 4831838208 | bytes 20185088 | tf_op jit(solution)/shard_map/project_b/pallas_call | solution.py:246
  163.8 0.0 collective-permute-start.3
  163.8 0.5 collective-permute-start.4
  164.3 0.1 collective-permute-start.5
  164.4 2.1 collective-permute-done.3.refs_1_
  166.6 1.0 collective-permute-done.4.refs_3_
  167.6 1.1 collective-permute-done.5.refs_5_
  168.7 0.0 copy-done.5
  168.7 9.4 %pair_b.1 = (bf16[64,144,128]{2,1,0:T(8,128)(2,1)}, bf16[1152,768]{1,0:T(8,128)(2,1)}, bf16[1152,768]{1,0:T(8,128)(2,1)}, bf16[1152,768]{1,0:T(8,128)(2,1)}) custom-call(bf16[512,768]{1,0:T(8,128)(2,1)} %get-tuple-element.45.refs_0_, bf16[512,768]{1,0:T(8,128)(2,1)} %copy-done.5, ...), custom_call_target="tpu_custom_call", output_to_operand_aliasing={{1}: (9, {}), {2}: (10, {}), {3}: (11, {})} | custom-call | flops 3221225472 | bytes 15466496 | tf_op jit(solution)/shard_map/pair_b/pallas_call | solution.py:324
  178.1 8.4 %all-to-all-done.3.in_ref = bf16[64,160,128]{2,1,0:T(8,128)(2,1)S(1)} async-done(((bf16[64,160,128]{2,1,0:T(8,128)(2,1)}), bf16[64,160,128]{2,1,0:T(8,128)(2,1)S(1)}, u32[]{:S(2)}, u32[]{:S(2)}) %all-to-all-start.3) | async-done | bytes 2621472 | tf_op jit(solution)/shard_map/all_to_all | solution.py:440
  186.5 1.5 copy-done.2
  187.9 6.1 %all-to-all-start.2 = ((bf16[64,144,128]{2,1,0:T(8,128)(2,1)}), bf16[64,144,128]{2,1,0:T(8,128)(2,1)S(1)}, u32[]{:S(2)}, u32[]{:S(2)}) async-start(bf16[64,144,128]{2,1,0:T(8,128)(2,1)} %get-tuple-element.52), calls=%async_computation.2 | async-start | bytes 4718592 | tf_op jit(solution)/shard_map/all_to_all | solution.py:440
  194.0 0.0 copy-start.4
  194.0 0.0 slice-start
  194.0 9.1 %fusion = bf16[1,2048,768]{2,1,0:T(8,128)(2,1)} fusion(bf16[1152,2048]{1,0:T(8,128)(2,1)} %get-tuple-element.58, bf16[1152,768]{1,0:T(8,128)(2,1)} %get-tuple-element.59), kind=kOutput, calls=%fused_computation.3 | convolution fusion | flops 3625451520 | bytes 9633792 | tf_op jit(solution)/shard_map/dot_general | solution.py:35
  203.1 0.0 copy-done.4
  203.1 8.3 %fusion.1 = bf16[1,2048,768]{2,1,0:T(8,128)(2,1)} fusion(bf16[1152,2048]{1,0:T(8,128)(2,1)} %get-tuple-element.58, bf16[1152,768]{1,0:T(8,128)(2,1)S(1)} %copy-done.4), kind=kOutput, calls=%fused_computation.4 | convolution fusion | flops 3625451520 | bytes 9633792 | tf_op jit(solution)/shard_map/dot_general | solution.py:35
  211.3 0.0 slice-done
  211.4 0.0 slice-done.1
  211.4 0.0 copy-done.3
  211.4 5.6 %fusion.2 = bf16[1,768,2048]{2,1,0:T(8,128)(2,1)} fusion(bf16[1152,768]{1,0:T(8,128)(2,1)S(1)} %copy-done.3, bf16[1152,2048]{1,0:T(8,128)(2,1)S(1)} %bitcast.39), kind=kOutput, calls=%fused_computation.5 | convolution fusion | flops 3625451520 | bytes 9633792 | tf_op jit(solution)/shard_map/dot_general | solution.py:35
  217.0 4.0 %combine_a.1 = (f32[128,2048]{1,0:T(8,128)}, f32[64,128]{1,0:T(8,128)}) custom-call(s32[8,128]{1,0:T(8,128)} %bitcast.42, bf16[64,160,128]{2,1,0:T(8,128)(2,1)} %copy-done.2), custom_call_target="tpu_custom_call" | custom-call | flops 335544320 | bytes 2621440 | tf_op jit(solution)/shard_map/combine_a/pallas_call | solution.py:398
  221.0 2.7 %all-to-all-done.2.in_ref.slots_ref = bf16[64,144,128]{2,1,0:T(8,128)(2,1)S(1)} async-done(((bf16[64,144,128]{2,1,0:T(8,128)(2,1)}), bf16[64,144,128]{2,1,0:T(8,128)(2,1)S(1)}, u32[]{:S(2)}, u32[]{:S(2)}) %all-to-all-start.2) | async-done | bytes 2359328 | tf_op jit(solution)/shard_map/all_to_all | solution.py:440
  223.7 1.4 copy-done
  225.1 3.9 %combine_b.1 = (bf16[128,2048]{1,0:T(8,128)(2,1)}, bf16[8,128]{1,0:T(8,128)(2,1)}) custom-call(s32[8,128]{1,0:T(8,128)} %bitcast.43, bf16[8,128]{1,0:T(8,128)(2,1)} %bitcast.46, bf16[64,144,128]{2,1,0:T(8,128)(2,1)} %copy-done, bf16[64,144,128]{2,1,0:T(8,128)(2,1)} %copy-done, f32[128,2048]{1,0:T(8,128)} %get-tuple-element.54.before_ref, ...), custom_call_target="tpu_custom_call" | custom-call | flops 268435456 | bytes 2359296 | tf_op jit(solution)/shard_map/combine_b/pallas_call | solution.py:417
  (9 shorter events, 0.0 us)
Async XLA Ops:
  6.2 78.6 %all-to-all-start.1 = ((bf16[64,320,128]{2,1,0:T(8,128)(2,1)}), bf16[64,320,128]{2,1,0:T(8,128)(2,1)}, u32[]{:S(2)}, u32[]{:S(2)}) async-start(bf16[64,320,128]{2,1,0:T(8,128)(2,1)} %pack_a.1), calls=%async_computation.1 | async-start | bytes 10485760 | tf_op jit(solution)/shard_map/all_to_all | solution.py:440
  17.9 4.8 %copy-start.1 = (bf16[1,2048,768]{2,1,0:T(8,128)(2,1)S(1)}, bf16[1,2048,768]{2,1,0:T(8,128)(2,1)}, u32[]{:S(2)}) copy-start(bf16[1,2048,768]{2,1,0:T(8,128)(2,1)} %param.11) | copy-start | bytes 9437188
  84.8 60.6 %all-to-all-start = ((bf16[64,256,128]{2,1,0:T(8,128)(2,1)}), bf16[64,256,128]{2,1,0:T(8,128)(2,1)}, u32[]{:S(2)}, u32[]{:S(2)}) async-start(bf16[64,256,128]{2,1,0:T(8,128)(2,1)} %pack_b.1), calls=%async_computation | async-start | bytes 8388608 | tf_op jit(solution)/shard_map/all_to_all | solution.py:440
  106.5 2.8 %collective-permute-start = (bf16[640,768]{1,0:T(8,128)(2,1)}, bf16[640,768]{1,0:T(8,128)(2,1)S(1)}, u32[]{:S(2)}, u32[]{:S(2)}) collective-permute-start(bf16[640,768]{1,0:T(8,128)(2,1)} %get-tuple-element.36.refs_0_), channel_id=1, source_target_pairs={{0,64},{64,0},{1,65},{65,1},{2,66},{66,2},{3,67},{67,3},{4,68},{68... | collective-permute-start | bytes 2949128 | tf_op jit(solution)/shard_map/ppermute | solution.py:444
  106.5 4.2 %collective-permute-start.1 = (bf16[640,768]{1,0:T(8,128)(2,1)}, bf16[640,768]{1,0:T(8,128)(2,1)S(1)}, u32[]{:S(2)}, u32[]{:S(2)}) collective-permute-start(bf16[640,768]{1,0:T(8,128)(2,1)} %get-tuple-element.37.refs_2_), channel_id=1, source_target_pairs={{0,64},{64,0},{1,65},{65,1},{2,66},{66,2},{3,67},{67,3},{4,68},{68... | collective-permute-start | bytes 2949128 | tf_op jit(solution)/shard_map/ppermute | solution.py:444
  107.0 5.1 %collective-permute-start.2 = (bf16[640,768]{1,0:T(8,128)(2,1)}, bf16[640,768]{1,0:T(8,128)(2,1)S(1)}, u32[]{:S(2)}, u32[]{:S(2)}) collective-permute-start(bf16[640,768]{1,0:T(8,128)(2,1)} %get-tuple-element.38.refs_4_), channel_id=1, source_target_pairs={{0,64},{64,0},{1,65},{65,1},{2,66},{66,2},{3,67},{67,3},{4,68},{68... | collective-permute-start | bytes 2949128 | tf_op jit(solution)/shard_map/ppermute | solution.py:444
  109.2 2.8 %copy-start.6 = (bf16[640,768]{1,0:T(8,128)(2,1)}, bf16[640,768]{1,0:T(8,128)(2,1)S(1)}, u32[]{:S(2)}) copy-start(bf16[640,768]{1,0:T(8,128)(2,1)S(1)} %collective-permute-done.refs_1_) | copy-start | bytes 2949124
  110.6 1.4 copy-start.7
  112.0 0.9 copy-start.8
  145.4 41.0 %all-to-all-start.3 = ((bf16[64,160,128]{2,1,0:T(8,128)(2,1)}), bf16[64,160,128]{2,1,0:T(8,128)(2,1)S(1)}, u32[]{:S(2)}, u32[]{:S(2)}) async-start(bf16[64,160,128]{2,1,0:T(8,128)(2,1)} %get-tuple-element.53), calls=%async_computation.3 | async-start | bytes 5242880 | tf_op jit(solution)/shard_map/all_to_all | solution.py:440
  163.8 2.7 %collective-permute-start.3 = (bf16[512,768]{1,0:T(8,128)(2,1)}, bf16[512,768]{1,0:T(8,128)(2,1)S(1)}, u32[]{:S(2)}, u32[]{:S(2)}) collective-permute-start(bf16[512,768]{1,0:T(8,128)(2,1)} %get-tuple-element.45.refs_0_), channel_id=1, source_target_pairs={{0,64},{64,0},{1,65},{65,1},{2,66},{66,2},{3,67},{67,3},{4,68},{68... | collective-permute-start | bytes 2359304 | tf_op jit(solution)/shard_map/ppermute | solution.py:444
  163.8 3.7 %collective-permute-start.4 = (bf16[512,768]{1,0:T(8,128)(2,1)}, bf16[512,768]{1,0:T(8,128)(2,1)}, u32[]{:S(2)}, u32[]{:S(2)}) collective-permute-start(bf16[512,768]{1,0:T(8,128)(2,1)} %get-tuple-element.46.refs_2_), channel_id=1, source_target_pairs={{0,64},{64,0},{1,65},{65,1},{2,66},{66,2},{3,67},{67,3},{4,68},{68... | collective-permute-start | bytes 2359304 | tf_op jit(solution)/shard_map/ppermute | solution.py:444
  164.3 4.4 %collective-permute-start.5 = (bf16[512,768]{1,0:T(8,128)(2,1)}, bf16[512,768]{1,0:T(8,128)(2,1)}, u32[]{:S(2)}, u32[]{:S(2)}) collective-permute-start(bf16[512,768]{1,0:T(8,128)(2,1)} %get-tuple-element.47.refs_4_), channel_id=1, source_target_pairs={{0,64},{64,0},{1,65},{65,1},{2,66},{66,2},{3,67},{67,3},{4,68},{68... | collective-permute-start | bytes 2359304 | tf_op jit(solution)/shard_map/ppermute | solution.py:444
  166.6 2.1 copy-start.5
  186.5 1.5 copy-start.2
  187.9 35.8 %all-to-all-start.2 = ((bf16[64,144,128]{2,1,0:T(8,128)(2,1)}), bf16[64,144,128]{2,1,0:T(8,128)(2,1)S(1)}, u32[]{:S(2)}, u32[]{:S(2)}) async-start(bf16[64,144,128]{2,1,0:T(8,128)(2,1)} %get-tuple-element.52), calls=%async_computation.2 | async-start | bytes 4718592 | tf_op jit(solution)/shard_map/all_to_all | solution.py:440
  194.0 9.1 %copy-start.4 = (bf16[1152,768]{1,0:T(8,128)(2,1)S(1)}, bf16[1152,768]{1,0:T(8,128)(2,1)}, u32[]{:S(2)}) copy-start(bf16[1152,768]{1,0:T(8,128)(2,1)} %get-tuple-element.60) | copy-start | bytes 5308420
  194.0 17.3 %slice-start = ((s8[4718592]{0:T(1024)(128)(4,1)}), s8[4194304]{0:T(1024)(128)(4,1)S(1)}, s32[]{:S(2)}) async-start(s8[4718592]{0:T(1024)(128)(4,1)} %bitcast.38), calls=%async_computation.4 | async-start | bytes 8388608
  203.1 8.3 %slice-start.1 = ((s8[4718592]{0:T(1024)(128)(4,1)}), s8[524288]{0:T(1024)(128)(4,1)S(1)}, s32[]{:S(2)}) async-start(s8[4718592]{0:T(1024)(128)(4,1)} %bitcast.38), calls=%async_computation.5 | async-start | bytes 1048576
  203.1 8.3 %copy-start.3 = (bf16[1152,768]{1,0:T(8,128)(2,1)S(1)}, bf16[1152,768]{1,0:T(8,128)(2,1)}, u32[]{:S(2)}) copy-start(bf16[1152,768]{1,0:T(8,128)(2,1)} %get-tuple-element.61) | copy-start | bytes 5308420
  223.7 1.4 copy-start

commit v6 on v5

--- a/solution.py
+++ b/solution.py
@@ -21,6 +21,7 @@
 PACK_PEERS = 32
 SUM_PEERS = 64
 VMEM = 60 * 2**20
+SUM_VMEM = 24 * 2**20
 
 
 def iota(shape, dim):
@@ -261,6 +262,46 @@
         ),
         name=name,
     )(got, got, *weights, *kept)
+
+
+def turn_kernel(core, count, *refs):
+    ins, outs = refs[:count], refs[-5 * count : -4 * count]
+    held, turned = refs[-4 * count : -3 * count], refs[-3 * count : -2 * count]
+    in_sems, out_sems = refs[-2 * count : -count], refs[-count:]
+
+    @pl.when(lax.axis_index("dp") == core)
+    def _():
+        loads = [pltpu.make_async_copy(a, b, sem) for a, b, sem in zip(ins, held, in_sems)]
+        stores = [pltpu.make_async_copy(a, b, sem) for a, b, sem in zip(turned, outs, out_sems)]
+        for load in loads:
+            load.start()
+        for load, store, a, b in zip(loads, stores, held, turned):
+            load.wait()
+            for at in range(0, a.shape[0], 256):
+                b[:, at : at + 256] = a[at : at + 256, :].T
+            store.start()
+        for store in stores:
+            store.wait()
+
+
+def turn(name, core, mats, before=()):
+    shapes = [m.shape for m in mats]
+    anywhere = pl.BlockSpec(memory_space=pl.ANY)
+    return pl.pallas_call(
+        functools.partial(turn_kernel, core, len(mats)),
+        out_shape=[jax.ShapeDtypeStruct(shape[::-1], BF) for shape in shapes],
+        in_specs=[anywhere] * (len(mats) + len(before)),
+        out_specs=[anywhere] * len(mats),
+        input_output_aliases={len(mats) + k: k for k in range(len(before))},
+        scratch_shapes=[pltpu.VMEM(shape, BF) for shape in shapes]
+        + [pltpu.VMEM(shape[::-1], BF) for shape in shapes]
+        + [pltpu.SemaphoreType.DMA] * (2 * len(mats)),
+        compiler_params=pltpu.CompilerParams(vmem_limit_bytes=VMEM),
+        cost_estimate=pl.CostEstimate(
+            flops=0, bytes_accessed=sum(8 * a * b for a, b in shapes), transcendentals=0
+        ),
+        name=name,
+    )(*mats, *before)
 
 
 def slots_of(prob_grad, peers, extra):
@@ -402,7 +443,7 @@
         in_specs=[whole(ids.shape), pl.BlockSpec((PEERS, rows, LANE), lambda i: (i, 0, 0))],
         out_specs=[whole((tokens, width)), whole((experts, tokens))],
         scratch_shapes=[pltpu.VMEM((PEERS * FIRST, width), BF)],
-        compiler_params=pltpu.CompilerParams(vmem_limit_bytes=VMEM),
+        compiler_params=pltpu.CompilerParams(vmem_limit_bytes=SUM_VMEM),
         cost_estimate=pl.CostEstimate(
             flops=2 * experts * FIRST * tokens * width, bytes_accessed=2 * experts * rows * LANE, transcendentals=0
         ),
@@ -428,7 +469,7 @@
         ],
         out_specs=[whole(before), whole(ids)],
         scratch_shapes=[pltpu.VMEM((SUM_PEERS * HALF, width), BF), pltpu.VMEM((tokens, width), F32)],
-        compiler_params=pltpu.CompilerParams(vmem_limit_bytes=VMEM),
+        compiler_params=pltpu.CompilerParams(vmem_limit_bytes=SUM_VMEM),
         cost_estimate=pl.CostEstimate(
             flops=2 * experts * HALF * tokens * width, bytes_accessed=2 * experts * rows * LANE, transcendentals=0
         ),
@@ -449,14 +490,18 @@
     gate_mat, up_mat, down_mat = gate_weight[0], up_weight[0], down_weight[0]
     ids, weights = expert_ids.T, probs.T
     values = (tokens, cotangent)
-    sent_a = pack("pack_a", pack_first_kernel, 2 * FIRST, 2, ids, weights, values, experts)
+    mats = (gate_mat, up_mat, down_mat)
+    sent_a, *turned = lax.optimization_barrier(
+        (
+            pack("pack_a", pack_first_kernel, 2 * FIRST, 2, ids, weights, values, experts),
+            *turn("turn_first", 1, mats),
+        )
+    )
     got_a = exchange(sent_a)
     sent_b, gate_t, up_t, down_t = lax.optimization_barrier(
         (
             pack("pack_b", pack_second_kernel, 2 * HALF, 0, ids, weights, values, experts),
-            gate_mat.T,
-            up_mat.T,
-            down_mat.T,
+            *turn("turn_second", 0, mats, turned),
         )
     )
     got_b = exchange(sent_b)

time: 230 us -> 240 us (1.043)
  local copies, waits for them, and re-layouts: 16.1 us -> 2.43 us
  waiting for transfers between devices: 92.2 us -> 103 us
  starting transfers between devices: 34.6 us -> 44.8 us
  Pallas kernels: 62.5 us -> 65.1 us
    unnamed x25 -> x24, local copies, waits for them, and re-layouts: 16.1 us -> 2.43 us
    all_to_all x4, waiting for transfers between devices: 82.9 us -> 93.9 us  [exchange(): lax.all_to_all(x, ('ctx', 'tp'), split_axis=0, concat_axis=0, tiled=True)]
    all_to_all x4, starting transfers between devices: 33.4 us -> 42.5 us  [exchange(): lax.all_to_all(x, ('ctx', 'tp'), split_axis=0, concat_axis=0, tiled=True)]
    pallas_call x0 -> x2, Pallas kernels: none -> 6.7 us  [turn(): pl.pallas_call(functools.partial(turn_kernel, core, len(mats)), out_shape...]
  transfers between devices with their start and end apart: 10 -> 10, of which waited for: 10 -> 10; matrix products, arithmetic and copies ran while one was open for 15% -> 10% of each run, Pallas kernels for 23% -> 24%
where the time goes in v6:
time: 240 us; the launch traced here: 239 us
  waiting for transfers between devices  103 us (43%)
  Pallas kernels  65.1 us (27%)
  starting transfers between devices  44.8 us (19%)
  matrix products  23 us (10%)
  local copies, waits for them, and re-layouts  2.43 us (1%)
    all_to_all x4, waiting for transfers between devices, exchange(): lax.all_to_all(x, ('ctx', 'tp'), split_axis=0, concat_axis=0, tiled=True)  93.9 us
    all_to_all x4, starting transfers between devices, exchange(): lax.all_to_all(x, ('ctx', 'tp'), split_axis=0, concat_axis=0, tiled=True)  42.5 us
    pallas_call x2, Pallas kernels, project(): pl.pallas_call(functools.partial(project_kernel, not kept), grid=(experts...  24.4 us
    dot_general x3, matrix products, contract(): lax.dot_general(left, right, (((0,), (0,)), ((), ())), preferred_element_...  23 us
    pallas_call x2, Pallas kernels, pair(): pl.pallas_call(functools.partial(pair_kernel, extra), grid=(experts // pe...  20.4 us
    pallas_call x2, Pallas kernels, pack(): pl.pallas_call(kernel, grid=(experts // PACK_PEERS,), out_shape=jax.Shape...  9.8 us
    ppermute x6, waiting for transfers between devices, other_core(): return lax.ppermute(x, 'dp', [(0, 1), (1, 0)])  8.97 us
    pallas_call x2, Pallas kernels, turn(): pl.pallas_call(functools.partial(turn_kernel, core, len(mats)), out_shape...  6.7 us
  transfers between devices with their start and end apart: 10, of which 10 were waited for; matrix products, arithmetic and copies ran while one was open for 10% of the time, Pallas kernels for 24%

profile of v6, /device:TPU:0, one launch (start us, length us, event | category | flops | bytes accessed | tf_op | source)
XLA Modules:
  0.0 239.0 jit_solution(10002092181849573754)
XLA Ops:
  0.6 0.1 turn_first.1
  0.7 5.6 %pack_a.1 = bf16[64,320,128]{2,1,0:T(8,128)(2,1)} custom-call(s32[8,128]{1,0:T(8,128)} %bitcast.18, bf16[8,128]{1,0:T(8,128)(2,1)} %bitcast.22, bf16[128,2048]{1,0:T(8,128)(2,1)} %x_ref.3, bf16[128,2048]{1,0:T(8,128)(2,1)} %cot_ref.3), custom_call_target="tpu_custom_call" | custom-call | flops 1342177280 | bytes 5242880 | tf_op jit(solution)/shard_map/pack_a/pallas_call | solution.py:210
  6.3 11.7 %all-to-all-start.1 = ((bf16[64,320,128]{2,1,0:T(8,128)(2,1)}), bf16[64,320,128]{2,1,0:T(8,128)(2,1)}, u32[]{:S(2)}, u32[]{:S(2)}) async-start(bf16[64,320,128]{2,1,0:T(8,128)(2,1)} %pack_a.1), calls=%async_computation.1 | async-start | bytes 10485760 | tf_op jit(solution)/shard_map/all_to_all | solution.py:481
  18.0 6.6 %turn_second.1 = (bf16[768,2048]{1,0:T(8,128)(2,1)}, bf16[768,2048]{1,0:T(8,128)(2,1)}, bf16[2048,768]{1,0:T(8,128)(2,1)}) custom-call(bf16[2048,768]{1,0:T(8,128)(2,1)} %bitcast.26, bf16[2048,768]{1,0:T(8,128)(2,1)} %bitcast.30, bf16[768,2048]{1,0:T(8,128)(2,1)} %bitcast.34, ...), custom_call_target="tpu_custom_call", output_to_operand_aliasing={{0}: (3, {}), {1}: (4, {}), {2}: (5, {})} | custom-call | bytes 37748736 | tf_op jit(solution)/shard_map/turn_second/pallas_call | solution.py:290
  24.6 4.2 %pack_b.1 = bf16[64,256,128]{2,1,0:T(8,128)(2,1)} custom-call(s32[8,128]{1,0:T(8,128)} %bitcast.19, bf16[8,128]{1,0:T(8,128)(2,1)} %bitcast.23, bf16[128,2048]{1,0:T(8,128)(2,1)} %x_ref.3, bf16[128,2048]{1,0:T(8,128)(2,1)} %cot_ref.3), custom_call_target="tpu_custom_call" | custom-call | flops 1073741824 | bytes 4194304 | tf_op jit(solution)/shard_map/pack_b/pallas_call | solution.py:210
  28.9 50.1 %all-to-all-done.1.x_in.cot_in = bf16[64,320,128]{2,1,0:T(8,128)(2,1)} async-done(((bf16[64,320,128]{2,1,0:T(8,128)(2,1)}), bf16[64,320,128]{2,1,0:T(8,128)(2,1)}, u32[]{:S(2)}, u32[]{:S(2)}) %all-to-all-start.1) | async-done | bytes 5242912 | tf_op jit(solution)/shard_map/all_to_all | solution.py:481
  78.9 12.7 %all-to-all-start = ((bf16[64,256,128]{2,1,0:T(8,128)(2,1)}), bf16[64,256,128]{2,1,0:T(8,128)(2,1)}, u32[]{:S(2)}, u32[]{:S(2)}) async-start(bf16[64,256,128]{2,1,0:T(8,128)(2,1)} %pack_b.1), calls=%async_computation | async-start | bytes 8388608 | tf_op jit(solution)/shard_map/all_to_all | solution.py:481
  91.7 13.4 %project_a.1 = (bf16[1152,2048]{1,0:T(8,128)(2,1)}, bf16[1152,2048]{1,0:T(8,128)(2,1)}, bf16[640,768]{1,0:T(8,128)(2,1)}, bf16[640,768]{1,0:T(8,128)(2,1)}, bf16[640,768]{1,0:T(8,128)(2,1)}) custom-call(bf16[64,320,128]{2,1,0:T(8,128)(2,1)} %all-to-all-done.1.x_in.cot_in, bf16[64,320,128]{2,1,0:T(8,128)(2,1)} %all-to-all-done.1.x_in.cot_in, ...), custom_call_target="tpu_custom_call" | custom-call | flops 6039797760 | bytes 22872064 | tf_op jit(solution)/shard_map/project_a/pallas_call | solution.py:247
  105.0 1.2 collective-permute-start
  106.2 0.1 collective-permute-start.1
  106.3 0.4 collective-permute-start.2
  106.7 1.9 collective-permute-done.refs_1_
  108.6 1.4 collective-permute-done.1.refs_3_
  110.0 1.4 collective-permute-done.2.refs_5_
  111.4 0.0 copy-done.7
  111.4 0.0 copy-done.8
  111.4 0.9 copy-done.9
  112.4 11.0 %pair_a.1 = (bf16[64,160,128]{2,1,0:T(8,128)(2,1)}, bf16[1152,768]{1,0:T(8,128)(2,1)}, bf16[1152,768]{1,0:T(8,128)(2,1)}, bf16[1152,768]{1,0:T(8,128)(2,1)}, f32[64,128]{1,0:T(8,128)}) custom-call(bf16[640,768]{1,0:T(8,128)(2,1)} %get-tuple-element.56.refs_0_, bf16[640,768]{1,0:T(8,128)(2,1)} %copy-done.7, bf16[640,768]{1,0:T(8,128)(2,1)} %get-tuple-element.57.refs_2_, ...), custom_call_target="tpu_custom_call" | custom-call | flops 4026531840 | bytes 17760256 | tf_op jit(solution)/shard_map/pair_a/pallas_call | solution.py:365
  123.4 27.0 %all-to-all-done.x_in.cot_in = bf16[64,256,128]{2,1,0:T(8,128)(2,1)} async-done(((bf16[64,256,128]{2,1,0:T(8,128)(2,1)}), bf16[64,256,128]{2,1,0:T(8,128)(2,1)}, u32[]{:S(2)}, u32[]{:S(2)}) %all-to-all-start) | async-done | bytes 4194336 | tf_op jit(solution)/shard_map/all_to_all | solution.py:481
  150.3 11.1 %all-to-all-start.3 = ((bf16[64,160,128]{2,1,0:T(8,128)(2,1)}), bf16[64,160,128]{2,1,0:T(8,128)(2,1)S(1)}, u32[]{:S(2)}, u32[]{:S(2)}) async-start(bf16[64,160,128]{2,1,0:T(8,128)(2,1)} %get-tuple-element.73), calls=%async_computation.3 | async-start | bytes 5242880 | tf_op jit(solution)/shard_map/all_to_all | solution.py:481
  161.5 11.0 %project_b.1 = (bf16[1152,2048]{1,0:T(8,128)(2,1)}, bf16[1152,2048]{1,0:T(8,128)(2,1)}, bf16[512,768]{1,0:T(8,128)(2,1)}, bf16[512,768]{1,0:T(8,128)(2,1)}, bf16[512,768]{1,0:T(8,128)(2,1)}) custom-call(bf16[64,256,128]{2,1,0:T(8,128)(2,1)} %all-to-all-done.x_in.cot_in, ...), custom_call_target="tpu_custom_call", output_to_operand_aliasing={{0}: (5, {}), {1}: (6, {})} | custom-call | flops 4831838208 | bytes 20185088 | tf_op jit(solution)/shard_map/project_b/pallas_call | solution.py:247
  172.5 0.0 collective-permute-start.3
  172.5 0.5 collective-permute-start.4
  173.0 0.1 collective-permute-start.5
  173.1 2.1 collective-permute-done.3.refs_1_
  175.2 1.1 collective-permute-done.4.refs_3_
  176.3 1.1 collective-permute-done.5.refs_5_
  177.4 0.0 copy-done.6
  177.4 9.4 %pair_b.1 = (bf16[64,144,128]{2,1,0:T(8,128)(2,1)}, bf16[1152,768]{1,0:T(8,128)(2,1)}, bf16[1152,768]{1,0:T(8,128)(2,1)}, bf16[1152,768]{1,0:T(8,128)(2,1)}) custom-call(bf16[512,768]{1,0:T(8,128)(2,1)} %get-tuple-element.65.refs_0_, bf16[512,768]{1,0:T(8,128)(2,1)} %copy-done.6, ...), custom_call_target="tpu_custom_call", output_to_operand_aliasing={{1}: (9, {}), {2}: (10, {}), {3}: (11, {})} | custom-call | flops 3221225472 | bytes 15466496 | tf_op jit(solution)/shard_map/pair_b/pallas_call | solution.py:365
  186.8 10.1 %all-to-all-done.3.in_ref = bf16[64,160,128]{2,1,0:T(8,128)(2,1)S(1)} async-done(((bf16[64,160,128]{2,1,0:T(8,128)(2,1)}), bf16[64,160,128]{2,1,0:T(8,128)(2,1)S(1)}, u32[]{:S(2)}, u32[]{:S(2)}) %all-to-all-start.3) | async-done | bytes 2621472 | tf_op jit(solution)/shard_map/all_to_all | solution.py:481
  196.9 1.4 copy-done
  198.3 6.9 %all-to-all-start.2 = ((bf16[64,144,128]{2,1,0:T(8,128)(2,1)}), bf16[64,144,128]{2,1,0:T(8,128)(2,1)S(1)}, u32[]{:S(2)}, u32[]{:S(2)}) async-start(bf16[64,144,128]{2,1,0:T(8,128)(2,1)} %get-tuple-element.72), calls=%async_computation.2 | async-start | bytes 4718592 | tf_op jit(solution)/shard_map/all_to_all | solution.py:481
  205.2 0.0 copy-start.5
  205.3 0.0 slice-start
  205.3 9.1 %fusion = bf16[1,2048,768]{2,1,0:T(8,128)(2,1)} fusion(bf16[1152,2048]{1,0:T(8,128)(2,1)} %get-tuple-element.78, bf16[1152,768]{1,0:T(8,128)(2,1)} %get-tuple-element.79), kind=kOutput, calls=%fused_computation.3 | convolution fusion | flops 3625451520 | bytes 9633792 | tf_op jit(solution)/shard_map/dot_general | solution.py:36
  214.3 0.0 copy-done.5
  214.3 8.3 %fusion.1 = bf16[1,2048,768]{2,1,0:T(8,128)(2,1)} fusion(bf16[1152,2048]{1,0:T(8,128)(2,1)} %get-tuple-element.78, bf16[1152,768]{1,0:T(8,128)(2,1)S(1)} %copy-done.5), kind=kOutput, calls=%fused_computation.4 | convolution fusion | flops 3625451520 | bytes 9633792 | tf_op jit(solution)/shard_map/dot_general | solution.py:36
  222.6 0.0 slice-done
  222.6 0.0 slice-done.1
  222.6 0.0 copy-done.4
  222.6 0.0 copy-start.1
  222.6 0.0 copy-start.2
  222.6 0.0 copy-start.3
  222.6 5.6 %fusion.2 = bf16[1,768,2048]{2,1,0:T(8,128)(2,1)} fusion(bf16[1152,768]{1,0:T(8,128)(2,1)S(1)} %copy-done.4, bf16[1152,2048]{1,0:T(8,128)(2,1)S(1)} %bitcast.36), kind=kOutput, calls=%fused_computation.5 | convolution fusion | flops 3625451520 | bytes 9633792 | tf_op jit(solution)/shard_map/dot_general | solution.py:36
  228.3 0.0 copy-done.1
  228.3 1.7 combine_a.1
  230.0 6.8 %all-to-all-done.2.in_ref.slots_ref = bf16[64,144,128]{2,1,0:T(8,128)(2,1)S(1)} async-done(((bf16[64,144,128]{2,1,0:T(8,128)(2,1)}), bf16[64,144,128]{2,1,0:T(8,128)(2,1)S(1)}, u32[]{:S(2)}, u32[]{:S(2)}) %all-to-all-start.2) | async-done | bytes 2359328 | tf_op jit(solution)/shard_map/all_to_all | solution.py:481
  236.8 2.2 combine_b.1
  (10 shorter events, 0.0 us)
Async XLA Ops:
  6.3 72.7 %all-to-all-start.1 = ((bf16[64,320,128]{2,1,0:T(8,128)(2,1)}), bf16[64,320,128]{2,1,0:T(8,128)(2,1)}, u32[]{:S(2)}, u32[]{:S(2)}) async-start(bf16[64,320,128]{2,1,0:T(8,128)(2,1)} %pack_a.1), calls=%async_computation.1 | async-start | bytes 10485760 | tf_op jit(solution)/shard_map/all_to_all | solution.py:481
  78.9 71.4 %all-to-all-start = ((bf16[64,256,128]{2,1,0:T(8,128)(2,1)}), bf16[64,256,128]{2,1,0:T(8,128)(2,1)}, u32[]{:S(2)}, u32[]{:S(2)}) async-start(bf16[64,256,128]{2,1,0:T(8,128)(2,1)} %pack_b.1), calls=%async_computation | async-start | bytes 8388608 | tf_op jit(solution)/shard_map/all_to_all | solution.py:481
  105.0 3.6 %collective-permute-start = (bf16[640,768]{1,0:T(8,128)(2,1)}, bf16[640,768]{1,0:T(8,128)(2,1)S(1)}, u32[]{:S(2)}, u32[]{:S(2)}) collective-permute-start(bf16[640,768]{1,0:T(8,128)(2,1)} %get-tuple-element.56.refs_0_), channel_id=1, source_target_pairs={{0,64},{64,0},{1,65},{65,1},{2,66},{66,2},{3,67},{67,3},{4,68},{68... | collective-permute-start | bytes 2949128 | tf_op jit(solution)/shard_map/ppermute | solution.py:485
  106.2 3.8 %collective-permute-start.1 = (bf16[640,768]{1,0:T(8,128)(2,1)}, bf16[640,768]{1,0:T(8,128)(2,1)S(1)}, u32[]{:S(2)}, u32[]{:S(2)}) collective-permute-start(bf16[640,768]{1,0:T(8,128)(2,1)} %get-tuple-element.57.refs_2_), channel_id=1, source_target_pairs={{0,64},{64,0},{1,65},{65,1},{2,66},{66,2},{3,67},{67,3},{4,68},{68... | collective-permute-start | bytes 2949128 | tf_op jit(solution)/shard_map/ppermute | solution.py:485
  106.3 5.1 %collective-permute-start.2 = (bf16[640,768]{1,0:T(8,128)(2,1)}, bf16[640,768]{1,0:T(8,128)(2,1)S(1)}, u32[]{:S(2)}, u32[]{:S(2)}) collective-permute-start(bf16[640,768]{1,0:T(8,128)(2,1)} %get-tuple-element.58.refs_4_), channel_id=1, source_target_pairs={{0,64},{64,0},{1,65},{65,1},{2,66},{66,2},{3,67},{67,3},{4,68},{68... | collective-permute-start | bytes 2949128 | tf_op jit(solution)/shard_map/ppermute | solution.py:485
  108.6 2.8 %copy-start.7 = (bf16[640,768]{1,0:T(8,128)(2,1)}, bf16[640,768]{1,0:T(8,128)(2,1)S(1)}, u32[]{:S(2)}) copy-start(bf16[640,768]{1,0:T(8,128)(2,1)S(1)} %collective-permute-done.refs_1_) | copy-start | bytes 2949124
  110.0 1.4 copy-start.8
  111.4 0.9 copy-start.9
  150.3 46.6 %all-to-all-start.3 = ((bf16[64,160,128]{2,1,0:T(8,128)(2,1)}), bf16[64,160,128]{2,1,0:T(8,128)(2,1)S(1)}, u32[]{:S(2)}, u32[]{:S(2)}) async-start(bf16[64,160,128]{2,1,0:T(8,128)(2,1)} %get-tuple-element.73), calls=%async_computation.3 | async-start | bytes 5242880 | tf_op jit(solution)/shard_map/all_to_all | solution.py:481
  172.5 2.7 %collective-permute-start.3 = (bf16[512,768]{1,0:T(8,128)(2,1)}, bf16[512,768]{1,0:T(8,128)(2,1)S(1)}, u32[]{:S(2)}, u32[]{:S(2)}) collective-permute-start(bf16[512,768]{1,0:T(8,128)(2,1)} %get-tuple-element.65.refs_0_), channel_id=1, source_target_pairs={{0,64},{64,0},{1,65},{65,1},{2,66},{66,2},{3,67},{67,3},{4,68},{68... | collective-permute-start | bytes 2359304 | tf_op jit(solution)/shard_map/ppermute | solution.py:485
  172.5 3.7 %collective-permute-start.4 = (bf16[512,768]{1,0:T(8,128)(2,1)}, bf16[512,768]{1,0:T(8,128)(2,1)}, u32[]{:S(2)}, u32[]{:S(2)}) collective-permute-start(bf16[512,768]{1,0:T(8,128)(2,1)} %get-tuple-element.66.refs_2_), channel_id=1, source_target_pairs={{0,64},{64,0},{1,65},{65,1},{2,66},{66,2},{3,67},{67,3},{4,68},{68... | collective-permute-start | bytes 2359304 | tf_op jit(solution)/shard_map/ppermute | solution.py:485
  173.0 4.4 %collective-permute-start.5 = (bf16[512,768]{1,0:T(8,128)(2,1)}, bf16[512,768]{1,0:T(8,128)(2,1)}, u32[]{:S(2)}, u32[]{:S(2)}) collective-permute-start(bf16[512,768]{1,0:T(8,128)(2,1)} %get-tuple-element.67.refs_4_), channel_id=1, source_target_pairs={{0,64},{64,0},{1,65},{65,1},{2,66},{66,2},{3,67},{67,3},{4,68},{68... | collective-permute-start | bytes 2359304 | tf_op jit(solution)/shard_map/ppermute | solution.py:485
  175.2 2.2 copy-start.6
  196.9 1.4 copy-start
  198.3 38.5 %all-to-all-start.2 = ((bf16[64,144,128]{2,1,0:T(8,128)(2,1)}), bf16[64,144,128]{2,1,0:T(8,128)(2,1)S(1)}, u32[]{:S(2)}, u32[]{:S(2)}) async-start(bf16[64,144,128]{2,1,0:T(8,128)(2,1)} %get-tuple-element.72), calls=%async_computation.2 | async-start | bytes 4718592 | tf_op jit(solution)/shard_map/all_to_all | solution.py:481
  205.2 9.1 %copy-start.5 = (bf16[1152,768]{1,0:T(8,128)(2,1)S(1)}, bf16[1152,768]{1,0:T(8,128)(2,1)}, u32[]{:S(2)}) copy-start(bf16[1152,768]{1,0:T(8,128)(2,1)} %get-tuple-element.80) | copy-start | bytes 5308420
  205.3 17.3 %slice-start = ((s8[4718592]{0:T(1024)(128)(4,1)}), s8[4194304]{0:T(1024)(128)(4,1)S(1)}, s32[]{:S(2)}) async-start(s8[4718592]{0:T(1024)(128)(4,1)} %bitcast.35), calls=%async_computation.4 | async-start | bytes 8388608
  214.3 8.3 %slice-start.1 = ((s8[4718592]{0:T(1024)(128)(4,1)}), s8[524288]{0:T(1024)(128)(4,1)S(1)}, s32[]{:S(2)}) async-start(s8[4718592]{0:T(1024)(128)(4,1)} %bitcast.35), calls=%async_computation.5 | async-start | bytes 1048576
  214.3 8.3 %copy-start.4 = (bf16[1152,768]{1,0:T(8,128)(2,1)S(1)}, bf16[1152,768]{1,0:T(8,128)(2,1)}, u32[]{:S(2)}) copy-start(bf16[1152,768]{1,0:T(8,128)(2,1)} %get-tuple-element.81) | copy-start | bytes 5308420
  222.6 5.7 %copy-start.1 = (bf16[64,160,128]{2,1,0:T(8,128)(2,1)S(1)}, bf16[64,160,128]{2,1,0:T(8,128)(2,1)}, u32[]{:S(2)}) copy-start(bf16[64,160,128]{2,1,0:T(8,128)(2,1)} %copy-done) | copy-start | bytes 7864324
  222.6 5.7 %copy-start.2 = (s32[128,8]{0,1:T(8,128)S(1)}, s32[128,8]{0,1:T(8,128)}, u32[]{:S(2)}) copy-start(s32[128,8]{0,1:T(8,128)} %param.10) | copy-start | bytes 12292
  222.6 14.2 %copy-start.3 = (bf16[128,8]{0,1:T(8,128)(2,1)S(1)}, bf16[128,8]{0,1:T(8,128)(2,1)}, u32[]{:S(2)}) copy-start(bf16[128,8]{0,1:T(8,128)(2,1)} %param.9) | copy-start | bytes 6148

commit v7 on v5

--- a/solution.py
+++ b/solution.py
@@ -20,7 +20,8 @@
 SECOND_PEERS = 16
 PACK_PEERS = 32
 SUM_PEERS = 64
-VMEM = 60 * 2**20
+VMEM = 62 * 2**20
+SUM_VMEM = 24 * 2**20
 
 
 def iota(shape, dim):
@@ -188,21 +189,6 @@
         store_extra(out_ref, start + half, dot(wide_extra_rows(rank, value), side[...]).astype(BF))
 
 
-def pack_second_kernel(ids_ref, probs_ref, x_ref, cot_ref, out_ref, rank_ref, prob_ref):
-    step = pl.program_id(0)
-    half = x_ref.shape[1] // LANE * HALF
-
-    @pl.when(step == 0)
-    def _():
-        start_pack(ids_ref, probs_ref, rank_ref, prob_ref)
-
-    count = out_ref.shape[0]
-    peers = pl.ds(pl.multiple_of(step * count, count), count)
-    rank, prob = rank_ref[peers, :], prob_ref[peers, :]
-    store_half(out_ref, 0, dot(half_rows(rank, None, HALF), x_ref[...]))
-    store_half(out_ref, half, dot(half_rows(rank, prob, HALF), cot_ref[...]))
-
-
 def pack(name, kernel, slots, sides, ids, probs, values, experts):
     tokens, width = values[0].shape
     rows = width // LANE * slots
@@ -219,6 +205,76 @@
         ),
         name=name,
     )(ids, probs, *values)
+
+
+def ahead_kernel(core, count, ids_ref, probs_ref, *refs):
+    mats, (x_ref, cot_ref), refs = refs[:count], refs[count : count + 2], refs[-(4 * count + 9) :]
+    outs, out_ref, refs = refs[:count], refs[count], refs[count + 1 :]
+    held, turned, refs = refs[:count], refs[count : 2 * count], refs[2 * count :]
+    x, cot, packed, rank_ref, prob_ref = refs[:5]
+    mat_sems, x_sem, cot_sem, pack_sems = refs[5 : 5 + count], refs[5 + count], refs[6 + count], refs[7 + count]
+    experts = out_ref.shape[0]
+
+    @pl.when(lax.axis_index("dp") == core)
+    def _():
+        values = [pltpu.make_async_copy(x_ref, x, x_sem), pltpu.make_async_copy(cot_ref, cot, cot_sem)]
+        for copy in values:
+            copy.start()
+        for mat, a, b, out, sem in zip(mats, held, turned, outs, mat_sems):
+            load = pltpu.make_async_copy(mat, a, sem)
+            load.start()
+            load.wait()
+            for at in range(0, a.shape[0], 256):
+                b[:, at : at + 256] = a[at : at + 256, :].T
+            store = pltpu.make_async_copy(b, out, sem)
+            store.start()
+            store.wait()
+        for copy in values:
+            copy.wait()
+        start_pack(ids_ref, probs_ref, rank_ref, prob_ref)
+        half = x.shape[1] // LANE * HALF
+        stores = []
+        for n in range(experts // PACK_PEERS):
+            peers = pl.ds(n * PACK_PEERS, PACK_PEERS)
+            rank, prob = rank_ref[peers, :], prob_ref[peers, :]
+            slot = packed.at[n]
+            store_half(slot, 0, dot(half_rows(rank, None, HALF), x[...]))
+            store_half(slot, half, dot(half_rows(rank, prob, HALF), cot[...]))
+            stores.append(pltpu.make_async_copy(slot, out_ref.at[peers], pack_sems.at[n]))
+            stores[-1].start()
+        for store in stores:
+            store.wait()
+
+
+def ahead(name, core, ids, probs, mats, values, experts, before=()):
+    tokens, width = values[0].shape
+    rows = width // LANE * 2 * HALF
+    steps = experts // PACK_PEERS
+    shapes = [m.shape for m in mats]
+    outs = [shape[::-1] for shape in shapes] + [(experts, rows, LANE)]
+    anywhere = pl.BlockSpec(memory_space=pl.ANY)
+    given = (*mats, *values, *before)
+    return pl.pallas_call(
+        functools.partial(ahead_kernel, core, len(mats)),
+        out_shape=[jax.ShapeDtypeStruct(shape, BF) for shape in outs],
+        in_specs=[pl.BlockSpec(memory_space=pltpu.VMEM)] * 2 + [anywhere] * len(given),
+        out_specs=[anywhere] * len(outs),
+        input_output_aliases={2 + len(given) - len(before) + k: k for k in range(len(before))},
+        scratch_shapes=[pltpu.VMEM(shape, BF) for shape in shapes]
+        + [pltpu.VMEM(shape[::-1], BF) for shape in shapes]
+        + [pltpu.VMEM((tokens, width), BF)] * 2
+        + [pltpu.VMEM((steps, PACK_PEERS, rows, LANE), BF)]
+        + [pltpu.VMEM((experts, tokens), F32)] * 2
+        + [pltpu.SemaphoreType.DMA] * (len(mats) + 2)
+        + [pltpu.SemaphoreType.DMA((steps,))],
+        compiler_params=pltpu.CompilerParams(vmem_limit_bytes=VMEM),
+        cost_estimate=pl.CostEstimate(
+            flops=4 * experts * HALF * tokens * width,
+            bytes_accessed=sum(8 * a * b for a, b in shapes) + 2 * experts * rows * LANE,
+            transcendentals=0,
+        ),
+        name=name,
+    )(ids, probs, *given)
 
 
 def project_kernel(extra, x_in, cot_in, gate_w, up_w, down_w, *refs):
@@ -402,7 +458,7 @@
         in_specs=[whole(ids.shape), pl.BlockSpec((PEERS, rows, LANE), lambda i: (i, 0, 0))],
         out_specs=[whole((tokens, width)), whole((experts, tokens))],
         scratch_shapes=[pltpu.VMEM((PEERS * FIRST, width), BF)],
-        compiler_params=pltpu.CompilerParams(vmem_limit_bytes=VMEM),
+        compiler_params=pltpu.CompilerParams(vmem_limit_bytes=SUM_VMEM),
         cost_estimate=pl.CostEstimate(
             flops=2 * experts * FIRST * tokens * width, bytes_accessed=2 * experts * rows * LANE, transcendentals=0
         ),
@@ -428,7 +484,7 @@
         ],
         out_specs=[whole(before), whole(ids)],
         scratch_shapes=[pltpu.VMEM((SUM_PEERS * HALF, width), BF), pltpu.VMEM((tokens, width), F32)],
-        compiler_params=pltpu.CompilerParams(vmem_limit_bytes=VMEM),
+        compiler_params=pltpu.CompilerParams(vmem_limit_bytes=SUM_VMEM),
         cost_estimate=pl.CostEstimate(
             flops=2 * experts * HALF * tokens * width, bytes_accessed=2 * experts * rows * LANE, transcendentals=0
         ),
@@ -449,16 +505,16 @@
     gate_mat, up_mat, down_mat = gate_weight[0], up_weight[0], down_weight[0]
     ids, weights = expert_ids.T, probs.T
     values = (tokens, cotangent)
-    sent_a = pack("pack_a", pack_first_kernel, 2 * FIRST, 2, ids, weights, values, experts)
-    got_a = exchange(sent_a)
-    sent_b, gate_t, up_t, down_t = lax.optimization_barrier(
+    mats = (gate_mat, up_mat, down_mat)
+    sent_a, *done = lax.optimization_barrier(
         (
-            pack("pack_b", pack_second_kernel, 2 * HALF, 0, ids, weights, values, experts),
-            gate_mat.T,
-            up_mat.T,
-            down_mat.T,
+            pack("pack_a", pack_first_kernel, 2 * FIRST, 2, ids, weights, values, experts),
+            *ahead("ahead_1", 1, ids, weights, mats, values, experts),
         )
     )
+    got_a = exchange(sent_a)
+    gate_t, up_t, down_t, sent_b = ahead("ahead_0", 0, ids, weights, mats, values, experts, done)
+    sent_b, gate_t, up_t, down_t = lax.optimization_barrier((sent_b, gate_t, up_t, down_t))
     got_b = exchange(sent_b)
     mats = (gate_mat, up_mat, down_t)
 

time: 230 us -> 225 us (0.978)
  waiting for transfers between devices: 92.2 us -> 68.6 us
  starting transfers between devices: 34.6 us -> 56.8 us
  local copies, waits for them, and re-layouts: 16.1 us -> 1.61 us
  Pallas kernels: 62.5 us -> 73.8 us
    all_to_all x4, waiting for transfers between devices: 82.9 us -> 59.8 us  [exchange(): lax.all_to_all(x, ('ctx', 'tp'), split_axis=0, concat_axis=0, tiled=True)]
    pallas_call x0 -> x2, Pallas kernels: none -> 18.1 us  [ahead(): pl.pallas_call(functools.partial(ahead_kernel, core, len(mats)), out_shap...]
    unnamed x25 -> x20, local copies, waits for them, and re-layouts: 16.1 us -> 1.61 us
    all_to_all x4, starting transfers between devices: 33.4 us -> 45.9 us  [exchange(): lax.all_to_all(x, ('ctx', 'tp'), split_axis=0, concat_axis=0, tiled=True)]
    ppermute x6, starting transfers between devices: 1.18 us -> 10.9 us  [other_core(): return lax.ppermute(x, 'dp', [(0, 1), (1, 0)])]
    pallas_call x2 -> x1, Pallas kernels: 9.76 us -> 5.64 us  [pack(): pl.pallas_call(kernel, grid=(experts // PACK_PEERS,), out_shape=jax.Shape...]
  transfers between devices with their start and end apart: 10 -> 10, of which waited for: 10 -> 10; matrix products, arithmetic and copies ran while one was open for 15% -> 10% of each run, Pallas kernels for 23% -> 29%
where the time goes in v7:
time: 225 us
  Pallas kernels  73.8 us (33%)
  waiting for transfers between devices  68.6 us (30%)
  starting transfers between devices  56.8 us (25%)
  matrix products  23 us (10%)
    all_to_all x4, waiting for transfers between devices, exchange(): lax.all_to_all(x, ('ctx', 'tp'), split_axis=0, concat_axis=0, tiled=True)  59.8 us
    all_to_all x4, starting transfers between devices, exchange(): lax.all_to_all(x, ('ctx', 'tp'), split_axis=0, concat_axis=0, tiled=True)  45.9 us
    pallas_call x2, Pallas kernels, project(): pl.pallas_call(functools.partial(project_kernel, not kept), grid=(experts...  24.5 us
    dot_general x3, matrix products, contract(): lax.dot_general(left, right, (((0,), (0,)), ((), ())), preferred_element_...  23 us
    pallas_call x2, Pallas kernels, pair(): pl.pallas_call(functools.partial(pair_kernel, extra), grid=(experts // pe...  20.4 us
    pallas_call x2, Pallas kernels, ahead(): pl.pallas_call(functools.partial(ahead_kernel, core, len(mats)), out_shap...  18.1 us
    ppermute x6, starting transfers between devices, other_core(): return lax.ppermute(x, 'dp', [(0, 1), (1, 0)])  10.9 us
    ppermute x6, waiting for transfers between devices, other_core(): return lax.ppermute(x, 'dp', [(0, 1), (1, 0)])  8.82 us
  transfers between devices with their start and end apart: 10, of which 10 were waited for; matrix products, arithmetic and copies ran while one was open for 10% of the time, Pallas kernels for 29%

profile of v7, /device:TPU:0, one launch (start us, length us, event | category | flops | bytes accessed | tf_op | source)
XLA Modules:
  0.0 224.5 jit_solution(13709914476448175745)
XLA Ops:
  0.6 5.6 %pack_a.1 = bf16[64,320,128]{2,1,0:T(8,128)(2,1)} custom-call(s32[8,128]{1,0:T(8,128)} %bitcast.18, bf16[8,128]{1,0:T(8,128)(2,1)} %bitcast.23, bf16[128,2048]{1,0:T(8,128)(2,1)} %refs_3_.3, bf16[128,2048]{1,0:T(8,128)(2,1)} %refs_4_.3), custom_call_target="tpu_custom_call" | custom-call | flops 1342177280 | bytes 5242880 | tf_op jit(solution)/shard_map/pack_a/pallas_call | solution.py:195
  6.3 0.8 ahead_1.1
  7.0 11.7 %all-to-all-start.1 = ((bf16[64,320,128]{2,1,0:T(8,128)(2,1)}), bf16[64,320,128]{2,1,0:T(8,128)(2,1)}, u32[]{:S(2)}, u32[]{:S(2)}) async-start(bf16[64,320,128]{2,1,0:T(8,128)(2,1)} %pack_a.1), calls=%async_computation.1 | async-start | bytes 10485760 | tf_op jit(solution)/shard_map/all_to_all | solution.py:496
  18.8 17.3 %ahead_0.1 = (bf16[768,2048]{1,0:T(8,128)(2,1)}, bf16[768,2048]{1,0:T(8,128)(2,1)}, bf16[2048,768]{1,0:T(8,128)(2,1)}, bf16[64,256,128]{2,1,0:T(8,128)(2,1)}) custom-call(s32[8,128]{1,0:T(8,128)} %bitcast.20, bf16[8,128]{1,0:T(8,128)(2,1)} %bitcast.25, ...), custom_call_target="tpu_custom_call", output_to_operand_aliasing={{0}: (7, {}), {1}: (8, {}), {2}: (9, {}), {3}: (10, {})} | custom-call | flops 536870912 | bytes 41943040 | tf_op jit(solution)/shard_map/ahead_0/pallas_call | solution.py:257
  36.1 36.4 %all-to-all-done.1.x_in.cot_in = bf16[64,320,128]{2,1,0:T(8,128)(2,1)} async-done(((bf16[64,320,128]{2,1,0:T(8,128)(2,1)}), bf16[64,320,128]{2,1,0:T(8,128)(2,1)}, u32[]{:S(2)}, u32[]{:S(2)}) %all-to-all-start.1) | async-done | bytes 5242912 | tf_op jit(solution)/shard_map/all_to_all | solution.py:496
  72.5 14.5 %all-to-all-start = ((bf16[64,256,128]{2,1,0:T(8,128)(2,1)}), bf16[64,256,128]{2,1,0:T(8,128)(2,1)}, u32[]{:S(2)}, u32[]{:S(2)}) async-start(bf16[64,256,128]{2,1,0:T(8,128)(2,1)} %get-tuple-element.59), calls=%async_computation | async-start | bytes 8388608 | tf_op jit(solution)/shard_map/all_to_all | solution.py:496
  87.0 13.6 %project_a.1 = (bf16[1152,2048]{1,0:T(8,128)(2,1)}, bf16[1152,2048]{1,0:T(8,128)(2,1)}, bf16[640,768]{1,0:T(8,128)(2,1)}, bf16[640,768]{1,0:T(8,128)(2,1)}, bf16[640,768]{1,0:T(8,128)(2,1)}) custom-call(bf16[64,320,128]{2,1,0:T(8,128)(2,1)} %all-to-all-done.1.x_in.cot_in, bf16[64,320,128]{2,1,0:T(8,128)(2,1)} %all-to-all-done.1.x_in.cot_in, ...), custom_call_target="tpu_custom_call" | custom-call | flops 6039797760 | bytes 22872064 | tf_op jit(solution)/shard_map/project_a/pallas_call | solution.py:302
  100.5 7.9 %collective-permute-start = (bf16[640,768]{1,0:T(8,128)(2,1)}, bf16[640,768]{1,0:T(8,128)(2,1)S(1)}, u32[]{:S(2)}, u32[]{:S(2)}) collective-permute-start(bf16[640,768]{1,0:T(8,128)(2,1)} %get-tuple-element.62.refs_0_), channel_id=1, source_target_pairs={{0,64},{64,0},{1,65},{65,1},{2,66},{66,2},{3,67},{67,3},{4,68},{68... | collective-permute-start | bytes 2949128 | tf_op jit(solution)/shard_map/ppermute | solution.py:500
  108.4 0.1 collective-permute-start.1
  108.5 0.4 collective-permute-start.2
  108.9 1.9 collective-permute-done.refs_1_
  110.8 0.0 copy-start.6
  110.8 2.8 %collective-permute-done.1.refs_3_ = bf16[640,768]{1,0:T(8,128)(2,1)S(1)} collective-permute-done((bf16[640,768]{1,0:T(8,128)(2,1)}, bf16[640,768]{1,0:T(8,128)(2,1)S(1)}, u32[]{:S(2)}, u32[]{:S(2)}) %collective-permute-start.1) | collective-permute-done | bytes 983072 | tf_op jit(solution)/shard_map/ppermute | solution.py:500
  113.7 0.0 copy-start.7
  113.7 0.1 collective-permute-done.2.refs_5_
  113.8 0.0 copy-done.6
  113.8 0.8 copy-done.7
  114.6 11.0 %pair_a.1 = (bf16[64,160,128]{2,1,0:T(8,128)(2,1)}, bf16[1152,768]{1,0:T(8,128)(2,1)}, bf16[1152,768]{1,0:T(8,128)(2,1)}, bf16[1152,768]{1,0:T(8,128)(2,1)}, f32[64,128]{1,0:T(8,128)}) custom-call(bf16[640,768]{1,0:T(8,128)(2,1)} %get-tuple-element.62.refs_0_, bf16[640,768]{1,0:T(8,128)(2,1)} %copy-done.6, bf16[640,768]{1,0:T(8,128)(2,1)} %get-tuple-element.63.refs_2_, ...), custom_call_target="tpu_custom_call" | custom-call | flops 4026531840 | bytes 17760256 | tf_op jit(solution)/shard_map/pair_a/pallas_call | solution.py:380
  125.6 9.3 %all-to-all-done.x_in.cot_in = bf16[64,256,128]{2,1,0:T(8,128)(2,1)} async-done(((bf16[64,256,128]{2,1,0:T(8,128)(2,1)}), bf16[64,256,128]{2,1,0:T(8,128)(2,1)}, u32[]{:S(2)}, u32[]{:S(2)}) %all-to-all-start) | async-done | bytes 4194336 | tf_op jit(solution)/shard_map/all_to_all | solution.py:496
  134.9 12.1 %all-to-all-start.3 = ((bf16[64,160,128]{2,1,0:T(8,128)(2,1)}), bf16[64,160,128]{2,1,0:T(8,128)(2,1)}, u32[]{:S(2)}, u32[]{:S(2)}) async-start(bf16[64,160,128]{2,1,0:T(8,128)(2,1)} %get-tuple-element.79), calls=%async_computation.3 | async-start | bytes 5242880 | tf_op jit(solution)/shard_map/all_to_all | solution.py:496
  147.0 11.0 %project_b.1 = (bf16[1152,2048]{1,0:T(8,128)(2,1)}, bf16[1152,2048]{1,0:T(8,128)(2,1)}, bf16[512,768]{1,0:T(8,128)(2,1)}, bf16[512,768]{1,0:T(8,128)(2,1)}, bf16[512,768]{1,0:T(8,128)(2,1)}) custom-call(bf16[64,256,128]{2,1,0:T(8,128)(2,1)} %all-to-all-done.x_in.cot_in, ...), custom_call_target="tpu_custom_call", output_to_operand_aliasing={{0}: (5, {}), {1}: (6, {})} | custom-call | flops 4831838208 | bytes 20185088 | tf_op jit(solution)/shard_map/project_b/pallas_call | solution.py:302
  158.0 2.0 collective-permute-start.3
  160.0 0.1 collective-permute-start.4
  160.1 0.4 collective-permute-start.5
  160.5 1.6 collective-permute-done.3.refs_1_
  162.1 2.2 %collective-permute-done.4.refs_3_ = bf16[512,768]{1,0:T(8,128)(2,1)S(1)} collective-permute-done((bf16[512,768]{1,0:T(8,128)(2,1)}, bf16[512,768]{1,0:T(8,128)(2,1)S(1)}, u32[]{:S(2)}, u32[]{:S(2)}) %collective-permute-start.4) | collective-permute-done | bytes 786464 | tf_op jit(solution)/shard_map/ppermute | solution.py:500
  164.4 0.1 collective-permute-done.5.refs_5_
  164.5 0.0 copy-done.4
  164.5 0.8 copy-done.5
  165.3 9.4 %pair_b.1 = (bf16[64,144,128]{2,1,0:T(8,128)(2,1)}, bf16[1152,768]{1,0:T(8,128)(2,1)}, bf16[1152,768]{1,0:T(8,128)(2,1)}, bf16[1152,768]{1,0:T(8,128)(2,1)}) custom-call(bf16[512,768]{1,0:T(8,128)(2,1)} %get-tuple-element.71.refs_0_, bf16[512,768]{1,0:T(8,128)(2,1)} %copy-done.4, ...), custom_call_target="tpu_custom_call", output_to_operand_aliasing={{1}: (9, {}), {2}: (10, {}), {3}: (11, {})} | custom-call | flops 3221225472 | bytes 15466496 | tf_op jit(solution)/shard_map/pair_b/pallas_call | solution.py:380
  174.7 7.6 %all-to-all-done.3.in_ref = bf16[64,160,128]{2,1,0:T(8,128)(2,1)} async-done(((bf16[64,160,128]{2,1,0:T(8,128)(2,1)}), bf16[64,160,128]{2,1,0:T(8,128)(2,1)}, u32[]{:S(2)}, u32[]{:S(2)}) %all-to-all-start.3) | async-done | bytes 2621472 | tf_op jit(solution)/shard_map/all_to_all | solution.py:496
  182.3 7.5 %all-to-all-start.2 = ((bf16[64,144,128]{2,1,0:T(8,128)(2,1)}), bf16[64,144,128]{2,1,0:T(8,128)(2,1)S(1)}, u32[]{:S(2)}, u32[]{:S(2)}) async-start(bf16[64,144,128]{2,1,0:T(8,128)(2,1)} %get-tuple-element.78), calls=%async_computation.2 | async-start | bytes 4718592 | tf_op jit(solution)/shard_map/all_to_all | solution.py:496
  189.8 0.0 copy-start.3
  189.8 0.0 slice-start
  189.8 9.1 %fusion = bf16[1,2048,768]{2,1,0:T(8,128)(2,1)} fusion(bf16[1152,2048]{1,0:T(8,128)(2,1)} %get-tuple-element.84, bf16[1152,768]{1,0:T(8,128)(2,1)} %get-tuple-element.85), kind=kOutput, calls=%fused_computation.3 | convolution fusion | flops 3625451520 | bytes 9633792 | tf_op jit(solution)/shard_map/dot_general | solution.py:36
  198.9 0.0 copy-done.3
  198.9 8.3 %fusion.1 = bf16[1,2048,768]{2,1,0:T(8,128)(2,1)} fusion(bf16[1152,2048]{1,0:T(8,128)(2,1)} %get-tuple-element.84, bf16[1152,768]{1,0:T(8,128)(2,1)S(1)} %copy-done.3), kind=kOutput, calls=%fused_computation.4 | convolution fusion | flops 3625451520 | bytes 9633792 | tf_op jit(solution)/shard_map/dot_general | solution.py:36
  207.2 0.0 slice-done
  207.2 0.0 slice-done.1
  207.2 0.0 copy-done.2
  207.2 0.0 copy-start
  207.2 0.0 copy-start.1
  207.2 5.6 %fusion.2 = bf16[1,768,2048]{2,1,0:T(8,128)(2,1)} fusion(bf16[1152,768]{1,0:T(8,128)(2,1)S(1)} %copy-done.2, bf16[1152,2048]{1,0:T(8,128)(2,1)S(1)} %bitcast.38), kind=kOutput, calls=%fused_computation.5 | convolution fusion | flops 3625451520 | bytes 9633792 | tf_op jit(solution)/shard_map/dot_general | solution.py:36
  212.9 0.0 copy-done
  212.9 3.0 %combine_a.1 = (f32[128,2048]{1,0:T(8,128)S(1)}, f32[64,128]{1,0:T(8,128)S(1)}) custom-call(s32[8,128]{1,0:T(8,128)S(1)} %bitcast.21, bf16[64,160,128]{2,1,0:T(8,128)(2,1)} %all-to-all-done.3.in_ref), custom_call_target="tpu_custom_call" | custom-call | flops 335544320 | bytes 2621440 | tf_op jit(solution)/shard_map/combine_a/pallas_call | solution.py:454
  215.9 6.5 %all-to-all-done.2.in_ref.slots_ref = bf16[64,144,128]{2,1,0:T(8,128)(2,1)S(1)} async-done(((bf16[64,144,128]{2,1,0:T(8,128)(2,1)}), bf16[64,144,128]{2,1,0:T(8,128)(2,1)S(1)}, u32[]{:S(2)}, u32[]{:S(2)}) %all-to-all-start.2) | async-done | bytes 2359328 | tf_op jit(solution)/shard_map/all_to_all | solution.py:496
  222.3 0.0 copy-done.1
  222.4 2.2 combine_b.1
  (5 shorter events, 0.0 us)
Async XLA Ops:
  7.0 65.5 %all-to-all-start.1 = ((bf16[64,320,128]{2,1,0:T(8,128)(2,1)}), bf16[64,320,128]{2,1,0:T(8,128)(2,1)}, u32[]{:S(2)}, u32[]{:S(2)}) async-start(bf16[64,320,128]{2,1,0:T(8,128)(2,1)} %pack_a.1), calls=%async_computation.1 | async-start | bytes 10485760 | tf_op jit(solution)/shard_map/all_to_all | solution.py:496
  72.5 62.3 %all-to-all-start = ((bf16[64,256,128]{2,1,0:T(8,128)(2,1)}), bf16[64,256,128]{2,1,0:T(8,128)(2,1)}, u32[]{:S(2)}, u32[]{:S(2)}) async-start(bf16[64,256,128]{2,1,0:T(8,128)(2,1)} %get-tuple-element.59), calls=%async_computation | async-start | bytes 8388608 | tf_op jit(solution)/shard_map/all_to_all | solution.py:496
  100.5 10.3 %collective-permute-start = (bf16[640,768]{1,0:T(8,128)(2,1)}, bf16[640,768]{1,0:T(8,128)(2,1)S(1)}, u32[]{:S(2)}, u32[]{:S(2)}) collective-permute-start(bf16[640,768]{1,0:T(8,128)(2,1)} %get-tuple-element.62.refs_0_), channel_id=1, source_target_pairs={{0,64},{64,0},{1,65},{65,1},{2,66},{66,2},{3,67},{67,3},{4,68},{68... | collective-permute-start | bytes 2949128 | tf_op jit(solution)/shard_map/ppermute | solution.py:500
  108.4 5.2 %collective-permute-start.1 = (bf16[640,768]{1,0:T(8,128)(2,1)}, bf16[640,768]{1,0:T(8,128)(2,1)S(1)}, u32[]{:S(2)}, u32[]{:S(2)}) collective-permute-start(bf16[640,768]{1,0:T(8,128)(2,1)} %get-tuple-element.63.refs_2_), channel_id=1, source_target_pairs={{0,64},{64,0},{1,65},{65,1},{2,66},{66,2},{3,67},{67,3},{4,68},{68... | collective-permute-start | bytes 2949128 | tf_op jit(solution)/shard_map/ppermute | solution.py:500
  108.5 5.3 %collective-permute-start.2 = (bf16[640,768]{1,0:T(8,128)(2,1)}, bf16[640,768]{1,0:T(8,128)(2,1)}, u32[]{:S(2)}, u32[]{:S(2)}) collective-permute-start(bf16[640,768]{1,0:T(8,128)(2,1)} %get-tuple-element.64.refs_4_), channel_id=1, source_target_pairs={{0,64},{64,0},{1,65},{65,1},{2,66},{66,2},{3,67},{67,3},{4,68},{68... | collective-permute-start | bytes 2949128 | tf_op jit(solution)/shard_map/ppermute | solution.py:500
  110.8 2.9 %copy-start.6 = (bf16[640,768]{1,0:T(8,128)(2,1)}, bf16[640,768]{1,0:T(8,128)(2,1)S(1)}, u32[]{:S(2)}) copy-start(bf16[640,768]{1,0:T(8,128)(2,1)S(1)} %collective-permute-done.refs_1_) | copy-start | bytes 2949124
  113.7 0.9 copy-start.7
  134.9 47.4 %all-to-all-start.3 = ((bf16[64,160,128]{2,1,0:T(8,128)(2,1)}), bf16[64,160,128]{2,1,0:T(8,128)(2,1)}, u32[]{:S(2)}, u32[]{:S(2)}) async-start(bf16[64,160,128]{2,1,0:T(8,128)(2,1)} %get-tuple-element.79), calls=%async_computation.3 | async-start | bytes 5242880 | tf_op jit(solution)/shard_map/all_to_all | solution.py:496
  158.0 4.1 %collective-permute-start.3 = (bf16[512,768]{1,0:T(8,128)(2,1)}, bf16[512,768]{1,0:T(8,128)(2,1)S(1)}, u32[]{:S(2)}, u32[]{:S(2)}) collective-permute-start(bf16[512,768]{1,0:T(8,128)(2,1)} %get-tuple-element.71.refs_0_), channel_id=1, source_target_pairs={{0,64},{64,0},{1,65},{65,1},{2,66},{66,2},{3,67},{67,3},{4,68},{68... | collective-permute-start | bytes 2359304 | tf_op jit(solution)/shard_map/ppermute | solution.py:500
  160.0 4.4 %collective-permute-start.4 = (bf16[512,768]{1,0:T(8,128)(2,1)}, bf16[512,768]{1,0:T(8,128)(2,1)S(1)}, u32[]{:S(2)}, u32[]{:S(2)}) collective-permute-start(bf16[512,768]{1,0:T(8,128)(2,1)} %get-tuple-element.72.refs_2_), channel_id=1, source_target_pairs={{0,64},{64,0},{1,65},{65,1},{2,66},{66,2},{3,67},{67,3},{4,68},{68... | collective-permute-start | bytes 2359304 | tf_op jit(solution)/shard_map/ppermute | solution.py:500
  160.1 4.4 %collective-permute-start.5 = (bf16[512,768]{1,0:T(8,128)(2,1)}, bf16[512,768]{1,0:T(8,128)(2,1)}, u32[]{:S(2)}, u32[]{:S(2)}) collective-permute-start(bf16[512,768]{1,0:T(8,128)(2,1)} %get-tuple-element.73.refs_4_), channel_id=1, source_target_pairs={{0,64},{64,0},{1,65},{65,1},{2,66},{66,2},{3,67},{67,3},{4,68},{68... | collective-permute-start | bytes 2359304 | tf_op jit(solution)/shard_map/ppermute | solution.py:500
  162.1 2.4 %copy-start.4 = (bf16[512,768]{1,0:T(8,128)(2,1)}, bf16[512,768]{1,0:T(8,128)(2,1)S(1)}, u32[]{:S(2)}) copy-start(bf16[512,768]{1,0:T(8,128)(2,1)S(1)} %collective-permute-done.3.refs_1_) | copy-start | bytes 2359300
  164.4 0.9 copy-start.5
  182.3 40.1 %all-to-all-start.2 = ((bf16[64,144,128]{2,1,0:T(8,128)(2,1)}), bf16[64,144,128]{2,1,0:T(8,128)(2,1)S(1)}, u32[]{:S(2)}, u32[]{:S(2)}) async-start(bf16[64,144,128]{2,1,0:T(8,128)(2,1)} %get-tuple-element.78), calls=%async_computation.2 | async-start | bytes 4718592 | tf_op jit(solution)/shard_map/all_to_all | solution.py:496
  189.8 9.1 %copy-start.3 = (bf16[1152,768]{1,0:T(8,128)(2,1)S(1)}, bf16[1152,768]{1,0:T(8,128)(2,1)}, u32[]{:S(2)}) copy-start(bf16[1152,768]{1,0:T(8,128)(2,1)} %get-tuple-element.86) | copy-start | bytes 5308420
  189.8 17.3 %slice-start = ((s8[4718592]{0:T(1024)(128)(4,1)}), s8[4194304]{0:T(1024)(128)(4,1)S(1)}, s32[]{:S(2)}) async-start(s8[4718592]{0:T(1024)(128)(4,1)} %bitcast.37), calls=%async_computation.4 | async-start | bytes 8388608
  198.9 8.3 %slice-start.1 = ((s8[4718592]{0:T(1024)(128)(4,1)}), s8[524288]{0:T(1024)(128)(4,1)S(1)}, s32[]{:S(2)}) async-start(s8[4718592]{0:T(1024)(128)(4,1)} %bitcast.37), calls=%async_computation.5 | async-start | bytes 1048576
  198.9 8.3 %copy-start.2 = (bf16[1152,768]{1,0:T(8,128)(2,1)S(1)}, bf16[1152,768]{1,0:T(8,128)(2,1)}, u32[]{:S(2)}) copy-start(bf16[1152,768]{1,0:T(8,128)(2,1)} %get-tuple-element.87) | copy-start | bytes 5308420
  207.2 5.7 %copy-start = (s32[128,8]{0,1:T(8,128)S(1)}, s32[128,8]{0,1:T(8,128)}, u32[]{:S(2)}) copy-start(s32[128,8]{0,1:T(8,128)} %param.10) | copy-start | bytes 12292
  207.2 15.2 %copy-start.1 = (bf16[128,8]{0,1:T(8,128)(2,1)S(1)}, bf16[128,8]{0,1:T(8,128)(2,1)}, u32[]{:S(2)}) copy-start(bf16[128,8]{0,1:T(8,128)(2,1)} %param.9) | copy-start | bytes 6148

commit v8 on v5

--- a/solution.py
+++ b/solution.py
@@ -20,7 +20,8 @@
 SECOND_PEERS = 16
 PACK_PEERS = 32
 SUM_PEERS = 64
-VMEM = 60 * 2**20
+VMEM = 62 * 2**20
+SUM_VMEM = 24 * 2**20
 
 
 def iota(shape, dim):
@@ -163,62 +164,82 @@
             side_ref[c * tokens : (c + 1) * tokens, g * LANE : (g + 1) * LANE] = x_ref[:, at : at + LANE]
 
 
-def start_pack(ids_ref, probs_ref, rank_ref, prob_ref):
-    experts = rank_ref.shape[0]
-    rank_ref[...] = expert_ranks(ids_ref[...], experts)
-    prob_ref[...] = expert_probs(ids_ref[...], probs_ref[...].astype(F32), experts)
-
-
-def pack_first_kernel(ids_ref, probs_ref, x_ref, cot_ref, out_ref, rank_ref, prob_ref, side_ref, cot_side_ref):
+def pack_kernel(
+    ids_ref, probs_ref, x_ref, cot_ref, out_a_ref, out_b_ref, rank_ref, prob_ref, side_ref, cot_side_ref
+):
     step = pl.program_id(0)
     half = x_ref.shape[1] // LANE * HALF
     part = x_ref.shape[1] // LANE * FIRST
-    count = out_ref.shape[0]
+    count = out_a_ref.shape[0]
 
     @pl.when(step == 0)
     def _():
-        start_pack(ids_ref, probs_ref, rank_ref, prob_ref)
+        rank_ref[...] = expert_ranks(ids_ref[...], rank_ref.shape[0])
+        prob_ref[...] = expert_probs(ids_ref[...], probs_ref[...].astype(F32), rank_ref.shape[0])
         stack_columns(x_ref, side_ref)
         stack_columns(cot_ref, cot_side_ref)
 
     peers = pl.ds(pl.multiple_of(step * count, count), count)
     rank, prob = rank_ref[peers, :], prob_ref[peers, :]
-    for start, value, ref, side in ((0, None, x_ref, side_ref), (part, prob, cot_ref, cot_side_ref)):
-        store_half(out_ref, start, dot(half_rows(rank, value, 0), ref[...]))
-        store_extra(out_ref, start + half, dot(wide_extra_rows(rank, value), side[...]).astype(BF))
-
-
-def pack_second_kernel(ids_ref, probs_ref, x_ref, cot_ref, out_ref, rank_ref, prob_ref):
-    step = pl.program_id(0)
-    half = x_ref.shape[1] // LANE * HALF
-
-    @pl.when(step == 0)
-    def _():
-        start_pack(ids_ref, probs_ref, rank_ref, prob_ref)
-
-    count = out_ref.shape[0]
-    peers = pl.ds(pl.multiple_of(step * count, count), count)
-    rank, prob = rank_ref[peers, :], prob_ref[peers, :]
-    store_half(out_ref, 0, dot(half_rows(rank, None, HALF), x_ref[...]))
-    store_half(out_ref, half, dot(half_rows(rank, prob, HALF), cot_ref[...]))
-
-
-def pack(name, kernel, slots, sides, ids, probs, values, experts):
-    tokens, width = values[0].shape
-    rows = width // LANE * slots
+    for n, value, ref, side in ((0, None, x_ref, side_ref), (1, prob, cot_ref, cot_side_ref)):
+        store_half(out_a_ref, n * part, dot(half_rows(rank, value, 0), ref[...]))
+        store_extra(out_a_ref, n * part + half, dot(wide_extra_rows(rank, value), side[...]).astype(BF))
+        store_half(out_b_ref, n * half, dot(half_rows(rank, value, HALF), ref[...]))
+
+
+def pack(ids, probs, x, cot, experts):
+    tokens, width = x.shape
+    rows = [width // LANE * 2 * slots for slots in (FIRST, HALF)]
     return pl.pallas_call(
-        kernel,
+        pack_kernel,
         grid=(experts // PACK_PEERS,),
-        out_shape=jax.ShapeDtypeStruct((experts, rows, LANE), BF),
-        in_specs=[pl.BlockSpec(a.shape, lambda i: (0, 0)) for a in (ids, probs, *values)],
-        out_specs=pl.BlockSpec((PACK_PEERS, rows, LANE), lambda i: (i, 0, 0)),
-        scratch_shapes=[pltpu.VMEM((experts, tokens), F32)] * 2 + [pltpu.VMEM((8 * tokens, width // 8), BF)] * sides,
+        out_shape=[jax.ShapeDtypeStruct((experts, n, LANE), BF) for n in rows],
+        in_specs=[pl.BlockSpec(a.shape, lambda i: (0, 0)) for a in (ids, probs, x, cot)],
+        out_specs=[pl.BlockSpec((PACK_PEERS, n, LANE), lambda i: (i, 0, 0)) for n in rows],
+        scratch_shapes=[pltpu.VMEM((experts, tokens), F32)] * 2 + [pltpu.VMEM((8 * tokens, width // 8), BF)] * 2,
         compiler_params=pltpu.CompilerParams(vmem_limit_bytes=VMEM),
         cost_estimate=pl.CostEstimate(
-            flops=4 * experts * slots * tokens * width, bytes_accessed=2 * experts * rows * LANE, transcendentals=0
-        ),
+            flops=4 * experts * CAP * tokens * width,
+            bytes_accessed=2 * experts * sum(rows) * LANE,
+            transcendentals=0,
+        ),
+        name="pack",
+    )(ids, probs, x, cot)
+
+
+def turn_kernel(core, count, *refs):
+    ins, outs = refs[:count], refs[-4 * count : -3 * count]
+    held, turned, sems = refs[-3 * count : -2 * count], refs[-2 * count : -count], refs[-count:]
+
+    @pl.when(lax.axis_index("dp") == core)
+    def _():
+        for mat, a, b, out, sem in zip(ins, held, turned, outs, sems):
+            load = pltpu.make_async_copy(mat, a, sem)
+            load.start()
+            load.wait()
+            for at in range(0, a.shape[0], 256):
+                b[:, at : at + 256] = a[at : at + 256, :].T
+            store = pltpu.make_async_copy(b, out, sem)
+            store.start()
+            store.wait()
+
+
+def turn(name, core, mats, before=()):
+    shapes = [m.shape for m in mats]
+    anywhere = pl.BlockSpec(memory_space=pl.ANY)
+    return pl.pallas_call(
+        functools.partial(turn_kernel, core, len(mats)),
+        out_shape=[jax.ShapeDtypeStruct(shape[::-1], BF) for shape in shapes],
+        in_specs=[anywhere] * (len(mats) + len(before)),
+        out_specs=[anywhere] * len(mats),
+        input_output_aliases={len(mats) + k: k for k in range(len(before))},
+        scratch_shapes=[pltpu.VMEM(shape, BF) for shape in shapes]
+        + [pltpu.VMEM(shape[::-1], BF) for shape in shapes]
+        + [pltpu.SemaphoreType.DMA] * len(mats),
+        compiler_params=pltpu.CompilerParams(vmem_limit_bytes=VMEM),
+        cost_estimate=pl.CostEstimate(flops=0, bytes_accessed=sum(4 * a * b for a, b in shapes), transcendentals=0),
         name=name,
-    )(ids, probs, *values)
+    )(*mats, *before)
 
 
 def project_kernel(extra, x_in, cot_in, gate_w, up_w, down_w, *refs):
@@ -402,7 +423,7 @@
         in_specs=[whole(ids.shape), pl.BlockSpec((PEERS, rows, LANE), lambda i: (i, 0, 0))],
         out_specs=[whole((tokens, width)), whole((experts, tokens))],
         scratch_shapes=[pltpu.VMEM((PEERS * FIRST, width), BF)],
-        compiler_params=pltpu.CompilerParams(vmem_limit_bytes=VMEM),
+        compiler_params=pltpu.CompilerParams(vmem_limit_bytes=SUM_VMEM),
         cost_estimate=pl.CostEstimate(
             flops=2 * experts * FIRST * tokens * width, bytes_accessed=2 * experts * rows * LANE, transcendentals=0
         ),
@@ -428,7 +449,7 @@
         ],
         out_specs=[whole(before), whole(ids)],
         scratch_shapes=[pltpu.VMEM((SUM_PEERS * HALF, width), BF), pltpu.VMEM((tokens, width), F32)],
-        compiler_params=pltpu.CompilerParams(vmem_limit_bytes=VMEM),
+        compiler_params=pltpu.CompilerParams(vmem_limit_bytes=SUM_VMEM),
         cost_estimate=pl.CostEstimate(
             flops=2 * experts * HALF * tokens * width, bytes_accessed=2 * experts * rows * LANE, transcendentals=0
         ),
@@ -448,18 +469,13 @@
     experts = lax.axis_size("ctx") * lax.axis_size("tp")
     gate_mat, up_mat, down_mat = gate_weight[0], up_weight[0], down_weight[0]
     ids, weights = expert_ids.T, probs.T
-    values = (tokens, cotangent)
-    sent_a = pack("pack_a", pack_first_kernel, 2 * FIRST, 2, ids, weights, values, experts)
-    got_a = exchange(sent_a)
-    sent_b, gate_t, up_t, down_t = lax.optimization_barrier(
-        (
-            pack("pack_b", pack_second_kernel, 2 * HALF, 0, ids, weights, values, experts),
-            gate_mat.T,
-            up_mat.T,
-            down_mat.T,
-        )
+    mats = (gate_mat, up_mat, down_mat)
+    sent_a, sent_b, *turned = lax.optimization_barrier(
+        (*pack(ids, weights, tokens, cotangent, experts), *turn("turn_1", 1, mats))
     )
+    got_a, sent_b, turned, mats = lax.optimization_barrier((exchange(sent_a), sent_b, turned, mats))
     got_b = exchange(sent_b)
+    gate_t, up_t, down_t = turn("turn_0", 0, mats, turned)
     mats = (gate_mat, up_mat, down_t)
 
     def part(name, got, slot_grads=None, kept=()):

time: 230 us -> 221 us (0.961)
  waiting for transfers between devices: 92.2 us -> 24.8 us
  blocking collectives: 0 us -> 65.1 us
  local copies, waits for them, and re-layouts: 16.1 us -> 1.62 us
  Pallas kernels: 62.5 us -> 71 us
  starting transfers between devices: 34.6 us -> 31.8 us
    all_to_all x4 -> x3, waiting for transfers between devices: 82.9 us -> 15.7 us  [exchange(): lax.all_to_all(x, ('ctx', 'tp'), split_axis=0, concat_axis=0, tiled=True)]
    all_to_all x0 -> x1, blocking collectives: none -> 65.1 us  [exchange(): lax.all_to_all(x, ('ctx', 'tp'), split_axis=0, concat_axis=0, tiled=True)]
    unnamed x25 -> x20, local copies, waits for them, and re-layouts: 16.1 us -> 1.62 us
    pallas_call x2 -> x3, Pallas kernels: 9.76 us -> 20.9 us  [the longest x2 13.5 us: turn(): pl.pallas_call(functools.partial(turn_kernel, core, len(mats)), out_shape...]
    all_to_all x4 -> x3, starting transfers between devices: 33.4 us -> 27.6 us  [exchange(): lax.all_to_all(x, ('ctx', 'tp'), split_axis=0, concat_axis=0, tiled=True)]
    ppermute x6, starting transfers between devices: 1.18 us -> 4.23 us  [other_core(): return lax.ppermute(x, 'dp', [(0, 1), (1, 0)])]
  transfers between devices with their start and end apart: 10 -> 9, of which waited for: 10 -> 9; matrix products, arithmetic and copies ran while one was open for 15% -> 11% of each run, Pallas kernels for 23% -> 28%
where the time goes in v8:
time: 221 us; the launch traced here: 218 us
  Pallas kernels  71 us (32%)
  blocking collectives  65.1 us (29%)
  starting transfers between devices  31.8 us (14%)
  waiting for transfers between devices  24.8 us (11%)
  matrix products  23 us (10%)
    all_to_all x1, blocking collectives, exchange(): lax.all_to_all(x, ('ctx', 'tp'), split_axis=0, concat_axis=0, tiled=True)  65.1 us
    all_to_all x3, starting transfers between devices, exchange(): lax.all_to_all(x, ('ctx', 'tp'), split_axis=0, concat_axis=0, tiled=True)  27.6 us
    pallas_call x2, Pallas kernels, project(): pl.pallas_call(functools.partial(project_kernel, not kept), grid=(experts...  24.6 us
    dot_general x3, matrix products, contract(): lax.dot_general(left, right, (((0,), (0,)), ((), ())), preferred_element_...  23 us
    pallas_call x2, Pallas kernels, pair(): pl.pallas_call(functools.partial(pair_kernel, extra), grid=(experts // pe...  20.4 us
    all_to_all x3, waiting for transfers between devices, exchange(): lax.all_to_all(x, ('ctx', 'tp'), split_axis=0, concat_axis=0, tiled=True)  15.7 us
    pallas_call x2, Pallas kernels, turn(): pl.pallas_call(functools.partial(turn_kernel, core, len(mats)), out_shape...  13.5 us
    ppermute x6, waiting for transfers between devices, other_core(): return lax.ppermute(x, 'dp', [(0, 1), (1, 0)])  9.1 us
  transfers between devices with their start and end apart: 9, of which 9 were waited for; matrix products, arithmetic and copies ran while one was open for 11% of the time, Pallas kernels for 28%

profile of v8, /device:TPU:0, one launch (start us, length us, event | category | flops | bytes accessed | tf_op | source)
XLA Modules:
  0.0 218.1 jit_solution(3389397677807400205)
XLA Ops:
  0.7 7.4 %pack.1 = (bf16[64,320,128]{2,1,0:T(8,128)(2,1)}, bf16[64,256,128]{2,1,0:T(8,128)(2,1)}) custom-call(s32[8,128]{1,0:T(8,128)} %bitcast.18, bf16[8,128]{1,0:T(8,128)(2,1)} %bitcast.21, bf16[128,2048]{1,0:T(8,128)(2,1)} %x_ref.1, bf16[128,2048]{1,0:T(8,128)(2,1)} %cot_ref.1), custom_call_target="tpu_custom_call" | custom-call | flops 1207959552 | bytes 9437184 | tf_op jit(solution)/shard_map/pack/pallas_call | solution.py:193
  8.1 65.1 %all_to_all.20.x_in.cot_in = bf16[64,320,128]{2,1,0:T(8,128)(2,1)} all-to-all(bf16[64,320,128]{2,1,0:T(8,128)(2,1)} %get-tuple-element.56), channel_id=1, replica_groups=mesh['dp'=2,'ctx'=16,'tp'=4] {'ctx','tp'}, dimensions={0} | all-to-all | bytes 10485760 | tf_op jit(solution)/shard_map/all_to_all | solution.py:461
  73.2 9.7 %all-to-all-start.1 = ((bf16[64,256,128]{2,1,0:T(8,128)(2,1)}), bf16[64,256,128]{2,1,0:T(8,128)(2,1)}, u32[]{:S(2)}, u32[]{:S(2)}) async-start(bf16[64,256,128]{2,1,0:T(8,128)(2,1)} %get-tuple-element.61), calls=%async_computation.1 | async-start | bytes 8388608 | tf_op jit(solution)/shard_map/all_to_all | solution.py:461
  82.9 13.4 %turn_0.1 = (bf16[768,2048]{1,0:T(8,128)(2,1)}, bf16[768,2048]{1,0:T(8,128)(2,1)}, bf16[2048,768]{1,0:T(8,128)(2,1)}) custom-call(bf16[2048,768]{1,0:T(8,128)(2,1)} %bitcast.24, bf16[2048,768]{1,0:T(8,128)(2,1)} %bitcast.28, bf16[768,2048]{1,0:T(8,128)(2,1)} %bitcast.32, ...), custom_call_target="tpu_custom_call", output_to_operand_aliasing={{0}: (3, {}), {1}: (4, {}), {2}: (5, {})} | custom-call | bytes 18874368 | tf_op jit(solution)/shard_map/turn_0/pallas_call | solution.py:230
  96.3 13.6 %project_a.1 = (bf16[1152,2048]{1,0:T(8,128)(2,1)}, bf16[1152,2048]{1,0:T(8,128)(2,1)}, bf16[640,768]{1,0:T(8,128)(2,1)}, bf16[640,768]{1,0:T(8,128)(2,1)}, bf16[640,768]{1,0:T(8,128)(2,1)}) custom-call(bf16[64,320,128]{2,1,0:T(8,128)(2,1)} %all_to_all.20.x_in.cot_in, bf16[64,320,128]{2,1,0:T(8,128)(2,1)} %all_to_all.20.x_in.cot_in, ...), custom_call_target="tpu_custom_call" | custom-call | flops 6039797760 | bytes 22872064 | tf_op jit(solution)/shard_map/project_a/pallas_call | solution.py:267
  109.9 0.0 collective-permute-start
  109.9 0.5 collective-permute-start.1
  110.4 0.1 collective-permute-start.2
  110.5 2.2 collective-permute-done.refs_1_
  112.7 0.0 copy-start.6
  112.7 2.8 %collective-permute-done.1.refs_3_ = bf16[640,768]{1,0:T(8,128)(2,1)S(1)} collective-permute-done((bf16[640,768]{1,0:T(8,128)(2,1)}, bf16[640,768]{1,0:T(8,128)(2,1)S(1)}, u32[]{:S(2)}, u32[]{:S(2)}) %collective-permute-start.1) | collective-permute-done | bytes 983072 | tf_op jit(solution)/shard_map/ppermute | solution.py:465
  115.5 0.0 copy-start.7
  115.5 0.1 collective-permute-done.2.refs_5_
  115.7 0.0 copy-done.6
  115.7 0.8 copy-done.7
  116.5 11.0 %pair_a.1 = (bf16[64,160,128]{2,1,0:T(8,128)(2,1)}, bf16[1152,768]{1,0:T(8,128)(2,1)}, bf16[1152,768]{1,0:T(8,128)(2,1)}, bf16[1152,768]{1,0:T(8,128)(2,1)}, f32[64,128]{1,0:T(8,128)}) custom-call(bf16[640,768]{1,0:T(8,128)(2,1)} %get-tuple-element.70.refs_0_, bf16[640,768]{1,0:T(8,128)(2,1)} %copy-done.6, bf16[640,768]{1,0:T(8,128)(2,1)} %get-tuple-element.71.refs_2_, ...), custom_call_target="tpu_custom_call" | custom-call | flops 4026531840 | bytes 17760256 | tf_op jit(solution)/shard_map/pair_a/pallas_call | solution.py:345
  127.5 4.0 %all-to-all-done.1.x_in.cot_in = bf16[64,256,128]{2,1,0:T(8,128)(2,1)} async-done(((bf16[64,256,128]{2,1,0:T(8,128)(2,1)}), bf16[64,256,128]{2,1,0:T(8,128)(2,1)}, u32[]{:S(2)}, u32[]{:S(2)}) %all-to-all-start.1) | async-done | bytes 4194336 | tf_op jit(solution)/shard_map/all_to_all | solution.py:461
  131.5 10.9 %all-to-all-start.3 = ((bf16[64,160,128]{2,1,0:T(8,128)(2,1)}), bf16[64,160,128]{2,1,0:T(8,128)(2,1)}, u32[]{:S(2)}, u32[]{:S(2)}) async-start(bf16[64,160,128]{2,1,0:T(8,128)(2,1)} %get-tuple-element.87), calls=%async_computation.3 | async-start | bytes 5242880 | tf_op jit(solution)/shard_map/all_to_all | solution.py:461
  142.4 11.0 %project_b.1 = (bf16[1152,2048]{1,0:T(8,128)(2,1)}, bf16[1152,2048]{1,0:T(8,128)(2,1)}, bf16[512,768]{1,0:T(8,128)(2,1)}, bf16[512,768]{1,0:T(8,128)(2,1)}, bf16[512,768]{1,0:T(8,128)(2,1)}) custom-call(bf16[64,256,128]{2,1,0:T(8,128)(2,1)} %all-to-all-done.1.x_in.cot_in, ...), custom_call_target="tpu_custom_call", output_to_operand_aliasing={{0}: (5, {}), {1}: (6, {})} | custom-call | flops 4831838208 | bytes 20185088 | tf_op jit(solution)/shard_map/project_b/pallas_call | solution.py:267
  153.4 3.1 %collective-permute-start.3 = (bf16[512,768]{1,0:T(8,128)(2,1)}, bf16[512,768]{1,0:T(8,128)(2,1)S(1)}, u32[]{:S(2)}, u32[]{:S(2)}) collective-permute-start(bf16[512,768]{1,0:T(8,128)(2,1)} %get-tuple-element.79.refs_0_), channel_id=1, source_target_pairs={{0,64},{64,0},{1,65},{65,1},{2,66},{66,2},{3,67},{67,3},{4,68},{68... | collective-permute-start | bytes 2359304 | tf_op jit(solution)/shard_map/ppermute | solution.py:465
  156.5 0.1 collective-permute-start.4
  156.6 0.4 collective-permute-start.5
  157.1 1.6 collective-permute-done.3.refs_1_
  158.7 0.0 copy-start.4
  158.7 2.2 %collective-permute-done.4.refs_3_ = bf16[512,768]{1,0:T(8,128)(2,1)S(1)} collective-permute-done((bf16[512,768]{1,0:T(8,128)(2,1)}, bf16[512,768]{1,0:T(8,128)(2,1)S(1)}, u32[]{:S(2)}, u32[]{:S(2)}) %collective-permute-start.4) | collective-permute-done | bytes 786464 | tf_op jit(solution)/shard_map/ppermute | solution.py:465
  160.9 0.0 copy-start.5
  160.9 0.1 collective-permute-done.5.refs_5_
  161.0 0.0 copy-done.4
  161.1 0.8 copy-done.5
  161.8 9.4 %pair_b.1 = (bf16[64,144,128]{2,1,0:T(8,128)(2,1)}, bf16[1152,768]{1,0:T(8,128)(2,1)}, bf16[1152,768]{1,0:T(8,128)(2,1)}, bf16[1152,768]{1,0:T(8,128)(2,1)}) custom-call(bf16[512,768]{1,0:T(8,128)(2,1)} %get-tuple-element.79.refs_0_, bf16[512,768]{1,0:T(8,128)(2,1)} %copy-done.4, ...), custom_call_target="tpu_custom_call", output_to_operand_aliasing={{1}: (9, {}), {2}: (10, {}), {3}: (11, {})} | custom-call | flops 3221225472 | bytes 15466496 | tf_op jit(solution)/shard_map/pair_b/pallas_call | solution.py:345
  171.2 5.3 %all-to-all-done.3.in_ref = bf16[64,160,128]{2,1,0:T(8,128)(2,1)} async-done(((bf16[64,160,128]{2,1,0:T(8,128)(2,1)}), bf16[64,160,128]{2,1,0:T(8,128)(2,1)}, u32[]{:S(2)}, u32[]{:S(2)}) %all-to-all-start.3) | async-done | bytes 2621472 | tf_op jit(solution)/shard_map/all_to_all | solution.py:461
  176.5 7.0 %all-to-all-start.2 = ((bf16[64,144,128]{2,1,0:T(8,128)(2,1)}), bf16[64,144,128]{2,1,0:T(8,128)(2,1)S(1)}, u32[]{:S(2)}, u32[]{:S(2)}) async-start(bf16[64,144,128]{2,1,0:T(8,128)(2,1)} %get-tuple-element.86), calls=%async_computation.2 | async-start | bytes 4718592 | tf_op jit(solution)/shard_map/all_to_all | solution.py:461
  183.5 0.0 copy-start.3
  183.5 0.0 slice-start
  183.5 9.1 %fusion = bf16[1,2048,768]{2,1,0:T(8,128)(2,1)} fusion(bf16[1152,2048]{1,0:T(8,128)(2,1)} %get-tuple-element.92, bf16[1152,768]{1,0:T(8,128)(2,1)} %get-tuple-element.93), kind=kOutput, calls=%fused_computation.3 | convolution fusion | flops 3625451520 | bytes 9633792 | tf_op jit(solution)/shard_map/dot_general | solution.py:36
  192.5 0.0 copy-done.3
  192.5 8.3 %fusion.1 = bf16[1,2048,768]{2,1,0:T(8,128)(2,1)} fusion(bf16[1152,2048]{1,0:T(8,128)(2,1)} %get-tuple-element.92, bf16[1152,768]{1,0:T(8,128)(2,1)S(1)} %copy-done.3), kind=kOutput, calls=%fused_computation.4 | convolution fusion | flops 3625451520 | bytes 9633792 | tf_op jit(solution)/shard_map/dot_general | solution.py:36
  200.8 0.0 slice-done
  200.8 0.0 slice-done.1
  200.8 0.0 copy-done.2
  200.8 0.0 copy-start
  200.8 0.0 copy-start.1
  200.8 5.6 %fusion.2 = bf16[1,768,2048]{2,1,0:T(8,128)(2,1)} fusion(bf16[1152,768]{1,0:T(8,128)(2,1)S(1)} %copy-done.2, bf16[1152,2048]{1,0:T(8,128)(2,1)S(1)} %bitcast.34), kind=kOutput, calls=%fused_computation.5 | convolution fusion | flops 3625451520 | bytes 9633792 | tf_op jit(solution)/shard_map/dot_general | solution.py:36
  206.5 0.0 copy-done
  206.5 3.0 %combine_a.1 = (f32[128,2048]{1,0:T(8,128)S(1)}, f32[64,128]{1,0:T(8,128)S(1)}) custom-call(s32[8,128]{1,0:T(8,128)S(1)} %bitcast.19, bf16[64,160,128]{2,1,0:T(8,128)(2,1)} %all-to-all-done.3.in_ref), custom_call_target="tpu_custom_call" | custom-call | flops 335544320 | bytes 2621440 | tf_op jit(solution)/shard_map/combine_a/pallas_call | solution.py:419
  209.5 6.4 %all-to-all-done.2.in_ref.slots_ref = bf16[64,144,128]{2,1,0:T(8,128)(2,1)S(1)} async-done(((bf16[64,144,128]{2,1,0:T(8,128)(2,1)}), bf16[64,144,128]{2,1,0:T(8,128)(2,1)S(1)}, u32[]{:S(2)}, u32[]{:S(2)}) %all-to-all-start.2) | async-done | bytes 2359328 | tf_op jit(solution)/shard_map/all_to_all | solution.py:461
  215.9 0.0 copy-done.1
  215.9 2.2 combine_b.1
  (4 shorter events, 0.0 us)
Async XLA Ops:
  73.2 58.3 %all-to-all-start.1 = ((bf16[64,256,128]{2,1,0:T(8,128)(2,1)}), bf16[64,256,128]{2,1,0:T(8,128)(2,1)}, u32[]{:S(2)}, u32[]{:S(2)}) async-start(bf16[64,256,128]{2,1,0:T(8,128)(2,1)} %get-tuple-element.61), calls=%async_computation.1 | async-start | bytes 8388608 | tf_op jit(solution)/shard_map/all_to_all | solution.py:461
  109.9 2.8 %collective-permute-start = (bf16[640,768]{1,0:T(8,128)(2,1)}, bf16[640,768]{1,0:T(8,128)(2,1)S(1)}, u32[]{:S(2)}, u32[]{:S(2)}) collective-permute-start(bf16[640,768]{1,0:T(8,128)(2,1)} %get-tuple-element.70.refs_0_), channel_id=1, source_target_pairs={{0,64},{64,0},{1,65},{65,1},{2,66},{66,2},{3,67},{67,3},{4,68},{68... | collective-permute-start | bytes 2949128 | tf_op jit(solution)/shard_map/ppermute | solution.py:465
  109.9 5.6 %collective-permute-start.1 = (bf16[640,768]{1,0:T(8,128)(2,1)}, bf16[640,768]{1,0:T(8,128)(2,1)S(1)}, u32[]{:S(2)}, u32[]{:S(2)}) collective-permute-start(bf16[640,768]{1,0:T(8,128)(2,1)} %get-tuple-element.71.refs_2_), channel_id=1, source_target_pairs={{0,64},{64,0},{1,65},{65,1},{2,66},{66,2},{3,67},{67,3},{4,68},{68... | collective-permute-start | bytes 2949128 | tf_op jit(solution)/shard_map/ppermute | solution.py:465
  110.4 5.2 %collective-permute-start.2 = (bf16[640,768]{1,0:T(8,128)(2,1)}, bf16[640,768]{1,0:T(8,128)(2,1)}, u32[]{:S(2)}, u32[]{:S(2)}) collective-permute-start(bf16[640,768]{1,0:T(8,128)(2,1)} %get-tuple-element.72.refs_4_), channel_id=1, source_target_pairs={{0,64},{64,0},{1,65},{65,1},{2,66},{66,2},{3,67},{67,3},{4,68},{68... | collective-permute-start | bytes 2949128 | tf_op jit(solution)/shard_map/ppermute | solution.py:465
  112.7 2.9 %copy-start.6 = (bf16[640,768]{1,0:T(8,128)(2,1)}, bf16[640,768]{1,0:T(8,128)(2,1)S(1)}, u32[]{:S(2)}) copy-start(bf16[640,768]{1,0:T(8,128)(2,1)S(1)} %collective-permute-done.refs_1_) | copy-start | bytes 2949124
  115.5 0.9 copy-start.7
  131.5 45.0 %all-to-all-start.3 = ((bf16[64,160,128]{2,1,0:T(8,128)(2,1)}), bf16[64,160,128]{2,1,0:T(8,128)(2,1)}, u32[]{:S(2)}, u32[]{:S(2)}) async-start(bf16[64,160,128]{2,1,0:T(8,128)(2,1)} %get-tuple-element.87), calls=%async_computation.3 | async-start | bytes 5242880 | tf_op jit(solution)/shard_map/all_to_all | solution.py:461
  153.4 5.3 %collective-permute-start.3 = (bf16[512,768]{1,0:T(8,128)(2,1)}, bf16[512,768]{1,0:T(8,128)(2,1)S(1)}, u32[]{:S(2)}, u32[]{:S(2)}) collective-permute-start(bf16[512,768]{1,0:T(8,128)(2,1)} %get-tuple-element.79.refs_0_), channel_id=1, source_target_pairs={{0,64},{64,0},{1,65},{65,1},{2,66},{66,2},{3,67},{67,3},{4,68},{68... | collective-permute-start | bytes 2359304 | tf_op jit(solution)/shard_map/ppermute | solution.py:465
  156.5 4.4 %collective-permute-start.4 = (bf16[512,768]{1,0:T(8,128)(2,1)}, bf16[512,768]{1,0:T(8,128)(2,1)S(1)}, u32[]{:S(2)}, u32[]{:S(2)}) collective-permute-start(bf16[512,768]{1,0:T(8,128)(2,1)} %get-tuple-element.80.refs_2_), channel_id=1, source_target_pairs={{0,64},{64,0},{1,65},{65,1},{2,66},{66,2},{3,67},{67,3},{4,68},{68... | collective-permute-start | bytes 2359304 | tf_op jit(solution)/shard_map/ppermute | solution.py:465
  156.6 4.4 %collective-permute-start.5 = (bf16[512,768]{1,0:T(8,128)(2,1)}, bf16[512,768]{1,0:T(8,128)(2,1)}, u32[]{:S(2)}, u32[]{:S(2)}) collective-permute-start(bf16[512,768]{1,0:T(8,128)(2,1)} %get-tuple-element.81.refs_4_), channel_id=1, source_target_pairs={{0,64},{64,0},{1,65},{65,1},{2,66},{66,2},{3,67},{67,3},{4,68},{68... | collective-permute-start | bytes 2359304 | tf_op jit(solution)/shard_map/ppermute | solution.py:465
  158.7 2.4 %copy-start.4 = (bf16[512,768]{1,0:T(8,128)(2,1)}, bf16[512,768]{1,0:T(8,128)(2,1)S(1)}, u32[]{:S(2)}) copy-start(bf16[512,768]{1,0:T(8,128)(2,1)S(1)} %collective-permute-done.3.refs_1_) | copy-start | bytes 2359300
  160.9 0.9 copy-start.5
  176.5 39.4 %all-to-all-start.2 = ((bf16[64,144,128]{2,1,0:T(8,128)(2,1)}), bf16[64,144,128]{2,1,0:T(8,128)(2,1)S(1)}, u32[]{:S(2)}, u32[]{:S(2)}) async-start(bf16[64,144,128]{2,1,0:T(8,128)(2,1)} %get-tuple-element.86), calls=%async_computation.2 | async-start | bytes 4718592 | tf_op jit(solution)/shard_map/all_to_all | solution.py:461
  183.5 9.1 %copy-start.3 = (bf16[1152,768]{1,0:T(8,128)(2,1)S(1)}, bf16[1152,768]{1,0:T(8,128)(2,1)}, u32[]{:S(2)}) copy-start(bf16[1152,768]{1,0:T(8,128)(2,1)} %get-tuple-element.94) | copy-start | bytes 5308420
  183.5 17.3 %slice-start = ((s8[4718592]{0:T(1024)(128)(4,1)}), s8[4194304]{0:T(1024)(128)(4,1)S(1)}, s32[]{:S(2)}) async-start(s8[4718592]{0:T(1024)(128)(4,1)} %bitcast.33), calls=%async_computation.4 | async-start | bytes 8388608
  192.5 8.3 %slice-start.1 = ((s8[4718592]{0:T(1024)(128)(4,1)}), s8[524288]{0:T(1024)(128)(4,1)S(1)}, s32[]{:S(2)}) async-start(s8[4718592]{0:T(1024)(128)(4,1)} %bitcast.33), calls=%async_computation.5 | async-start | bytes 1048576
  192.5 8.3 %copy-start.2 = (bf16[1152,768]{1,0:T(8,128)(2,1)S(1)}, bf16[1152,768]{1,0:T(8,128)(2,1)}, u32[]{:S(2)}) copy-start(bf16[1152,768]{1,0:T(8,128)(2,1)} %get-tuple-element.95) | copy-start | bytes 5308420
  200.8 5.7 %copy-start = (s32[128,8]{0,1:T(8,128)S(1)}, s32[128,8]{0,1:T(8,128)}, u32[]{:S(2)}) copy-start(s32[128,8]{0,1:T(8,128)} %param.10) | copy-start | bytes 12292
  200.8 15.1 %copy-start.1 = (bf16[128,8]{0,1:T(8,128)(2,1)S(1)}, bf16[128,8]{0,1:T(8,128)(2,1)}, u32[]{:S(2)}) copy-start(bf16[128,8]{0,1:T(8,128)(2,1)} %param.9) | copy-start | bytes 6148

commit v9 on v7

--- a/solution.py
+++ b/solution.py
@@ -277,6 +277,41 @@
     )(ids, probs, *given)
 
 
+def turn_kernel(core, count, *refs):
+    ins, outs = refs[:count], refs[-4 * count : -3 * count]
+    held, turned, sems = refs[-3 * count : -2 * count], refs[-2 * count : -count], refs[-count:]
+
+    @pl.when(lax.axis_index("dp") == core)
+    def _():
+        for mat, a, b, out, sem in zip(ins, held, turned, outs, sems):
+            load = pltpu.make_async_copy(mat, a, sem)
+            load.start()
+            load.wait()
+            for at in range(0, a.shape[0], 256):
+                b[:, at : at + 256] = a[at : at + 256, :].T
+            store = pltpu.make_async_copy(b, out, sem)
+            store.start()
+            store.wait()
+
+
+def turn(name, core, mats, before=()):
+    shapes = [m.shape for m in mats]
+    anywhere = pl.BlockSpec(memory_space=pl.ANY)
+    return pl.pallas_call(
+        functools.partial(turn_kernel, core, len(mats)),
+        out_shape=[jax.ShapeDtypeStruct(shape[::-1], BF) for shape in shapes],
+        in_specs=[anywhere] * (len(mats) + len(before)),
+        out_specs=[anywhere] * len(mats),
+        input_output_aliases={len(mats) + k: k for k in range(len(before))},
+        scratch_shapes=[pltpu.VMEM(shape, BF) for shape in shapes]
+        + [pltpu.VMEM(shape[::-1], BF) for shape in shapes]
+        + [pltpu.SemaphoreType.DMA] * len(mats),
+        compiler_params=pltpu.CompilerParams(vmem_limit_bytes=VMEM),
+        cost_estimate=pl.CostEstimate(flops=0, bytes_accessed=sum(4 * a * b for a, b in shapes), transcendentals=0),
+        name=name,
+    )(*mats, *before)
+
+
 def project_kernel(extra, x_in, cot_in, gate_w, up_w, down_w, *refs):
     x_ref, cot_ref, gate_ref, up_ref, back_ref = refs[-5:]
     peers = x_in.shape[0]
@@ -504,18 +539,18 @@
     experts = lax.axis_size("ctx") * lax.axis_size("tp")
     gate_mat, up_mat, down_mat = gate_weight[0], up_weight[0], down_weight[0]
     ids, weights = expert_ids.T, probs.T
-    values = (tokens, cotangent)
-    mats = (gate_mat, up_mat, down_mat)
-    sent_a, *done = lax.optimization_barrier(
+    mats, values = (gate_mat, up_mat, down_mat), (tokens, cotangent)
+    sent_a, *turned, sent_b = lax.optimization_barrier(
         (
             pack("pack_a", pack_first_kernel, 2 * FIRST, 2, ids, weights, values, experts),
             *ahead("ahead_1", 1, ids, weights, mats, values, experts),
         )
     )
-    got_a = exchange(sent_a)
-    gate_t, up_t, down_t, sent_b = ahead("ahead_0", 0, ids, weights, mats, values, experts, done)
-    sent_b, gate_t, up_t, down_t = lax.optimization_barrier((sent_b, gate_t, up_t, down_t))
+    got_a, sent_b, turned, mats, values = lax.optimization_barrier((exchange(sent_a), sent_b, turned, mats, values))
+    (sent_b,) = ahead("pack_b_0", 0, ids, weights, (), values, experts, (sent_b,))
+    sent_b, turned, mats = lax.optimization_barrier((sent_b, turned, mats))
     got_b = exchange(sent_b)
+    gate_t, up_t, down_t = turn("turn_0", 0, mats, turned)
     mats = (gate_mat, up_mat, down_t)
 
     def part(name, got, slot_grads=None, kept=()):

time: 225 us -> 216 us (0.960)
  blocking collectives: 0 us -> 62 us
  waiting for transfers between devices: 68.6 us -> 24 us
  starting transfers between devices: 56.8 us -> 27.6 us
    all_to_all x0 -> x1, blocking collectives: none -> 62 us  [exchange(): lax.all_to_all(x, ('ctx', 'tp'), split_axis=0, concat_axis=0, tiled=True)]
    all_to_all x4 -> x3, waiting for transfers between devices: 59.8 us -> 14.9 us  [exchange(): lax.all_to_all(x, ('ctx', 'tp'), split_axis=0, concat_axis=0, tiled=True)]
    all_to_all x4 -> x3, starting transfers between devices: 45.9 us -> 23.1 us  [exchange(): lax.all_to_all(x, ('ctx', 'tp'), split_axis=0, concat_axis=0, tiled=True)]
    pallas_call x0 -> x1, Pallas kernels: none -> 13.4 us  [turn(): pl.pallas_call(functools.partial(turn_kernel, core, len(mats)), out_shape...]
    pallas_call x2, Pallas kernels: 18.1 us -> 5.51 us  [ahead(): pl.pallas_call(functools.partial(ahead_kernel, core, len(mats)), out_shap...]
    ppermute x6, starting transfers between devices: 10.9 us -> 4.55 us  [other_core(): return lax.ppermute(x, 'dp', [(0, 1), (1, 0)])]
  transfers between devices with their start and end apart: 10 -> 9, of which waited for: 10 -> 9; matrix products, arithmetic and copies ran while one was open for 10% -> 11% of each run, Pallas kernels for 29% -> 29%
where the time goes in v9:
time: 216 us; the launch traced here: 214 us
  Pallas kernels  74.7 us (35%)
  blocking collectives  62 us (29%)
  starting transfers between devices  27.6 us (13%)
  waiting for transfers between devices  24 us (11%)
  matrix products  23 us (11%)
    all_to_all x1, blocking collectives, exchange(): lax.all_to_all(x, ('ctx', 'tp'), split_axis=0, concat_axis=0, tiled=True)  62 us
    pallas_call x2, Pallas kernels, project(): pl.pallas_call(functools.partial(project_kernel, not kept), grid=(experts...  24.6 us
    all_to_all x3, starting transfers between devices, exchange(): lax.all_to_all(x, ('ctx', 'tp'), split_axis=0, concat_axis=0, tiled=True)  23.1 us
    dot_general x3, matrix products, contract(): lax.dot_general(left, right, (((0,), (0,)), ((), ())), preferred_element_...  23 us
    pallas_call x2, Pallas kernels, pair(): pl.pallas_call(functools.partial(pair_kernel, extra), grid=(experts // pe...  20.4 us
    all_to_all x3, waiting for transfers between devices, exchange(): lax.all_to_all(x, ('ctx', 'tp'), split_axis=0, concat_axis=0, tiled=True)  14.9 us
    pallas_call x1, Pallas kernels, turn(): pl.pallas_call(functools.partial(turn_kernel, core, len(mats)), out_shape...  13.4 us
    ppermute x6, waiting for transfers between devices, other_core(): return lax.ppermute(x, 'dp', [(0, 1), (1, 0)])  9.1 us
  transfers between devices with their start and end apart: 9, of which 9 were waited for; matrix products, arithmetic and copies ran while one was open for 11% of the time, Pallas kernels for 29%

profile of v9, /device:TPU:0, one launch (start us, length us, event | category | flops | bytes accessed | tf_op | source)
XLA Modules:
  0.0 213.7 jit_solution(2705342403985943574)
XLA Ops:
  0.6 5.7 %pack_a.1 = bf16[64,320,128]{2,1,0:T(8,128)(2,1)} custom-call(s32[8,128]{1,0:T(8,128)} %bitcast.18, bf16[8,128]{1,0:T(8,128)(2,1)} %bitcast.23, bf16[128,2048]{1,0:T(8,128)(2,1)} %refs_0_, bf16[128,2048]{1,0:T(8,128)(2,1)} %refs_1_), custom_call_target="tpu_custom_call" | custom-call | flops 1342177280 | bytes 5242880 | tf_op jit(solution)/shard_map/pack_a/pallas_call | solution.py:195
  6.3 0.8 ahead_1.1
  7.1 62.0 %all_to_all.20.x_in.cot_in = bf16[64,320,128]{2,1,0:T(8,128)(2,1)} all-to-all(bf16[64,320,128]{2,1,0:T(8,128)(2,1)} %pack_a.1), channel_id=1, replica_groups=mesh['dp'=2,'ctx'=16,'tp'=4] {'ctx','tp'}, dimensions={0} | all-to-all | bytes 10485760 | tf_op jit(solution)/shard_map/all_to_all | solution.py:531
  69.1 4.8 %pack_b_0.1 = bf16[64,256,128]{2,1,0:T(8,128)(2,1)} custom-call(s32[8,128]{1,0:T(8,128)} %bitcast.20, bf16[8,128]{1,0:T(8,128)(2,1)} %bitcast.25, bf16[128,2048]{1,0:T(8,128)(2,1)} %refs_0_, bf16[128,2048]{1,0:T(8,128)(2,1)} %refs_1_, bf16[64,256,128]{2,1,0:T(8,128)(2,1)} %get-tuple-element.70.refs_2_), custom_call_target="tpu_custom_call", output_to_operand_aliasing={{}: (4, {})} | custom-call | flops 536870912 | bytes 4194304 | tf_op jit(solution)/shard_map/pack_b_0/pallas_call | solution.py:257
  73.9 6.4 %all-to-all-start.1 = ((bf16[64,256,128]{2,1,0:T(8,128)(2,1)}), bf16[64,256,128]{2,1,0:T(8,128)(2,1)}, u32[]{:S(2)}, u32[]{:S(2)}) async-start(bf16[64,256,128]{2,1,0:T(8,128)(2,1)} %pack_b_0.1), calls=%async_computation.1 | async-start | bytes 8388608 | tf_op jit(solution)/shard_map/all_to_all | solution.py:531
  80.3 13.4 %turn_0.1 = (bf16[768,2048]{1,0:T(8,128)(2,1)}, bf16[768,2048]{1,0:T(8,128)(2,1)}, bf16[2048,768]{1,0:T(8,128)(2,1)}) custom-call(bf16[2048,768]{1,0:T(8,128)(2,1)} %bitcast.28, bf16[2048,768]{1,0:T(8,128)(2,1)} %bitcast.32, bf16[768,2048]{1,0:T(8,128)(2,1)} %bitcast.36, ...), custom_call_target="tpu_custom_call", output_to_operand_aliasing={{0}: (3, {}), {1}: (4, {}), {2}: (5, {})} | custom-call | bytes 18874368 | tf_op jit(solution)/shard_map/turn_0/pallas_call | solution.py:300
  93.7 13.6 %project_a.1 = (bf16[1152,2048]{1,0:T(8,128)(2,1)}, bf16[1152,2048]{1,0:T(8,128)(2,1)}, bf16[640,768]{1,0:T(8,128)(2,1)}, bf16[640,768]{1,0:T(8,128)(2,1)}, bf16[640,768]{1,0:T(8,128)(2,1)}) custom-call(bf16[64,320,128]{2,1,0:T(8,128)(2,1)} %all_to_all.20.x_in.cot_in, bf16[64,320,128]{2,1,0:T(8,128)(2,1)} %all_to_all.20.x_in.cot_in, ...), custom_call_target="tpu_custom_call" | custom-call | flops 6039797760 | bytes 22872064 | tf_op jit(solution)/shard_map/project_a/pallas_call | solution.py:337
  107.3 0.0 collective-permute-start
  107.3 0.5 collective-permute-start.1
  107.8 0.1 collective-permute-start.2
  107.9 2.2 %collective-permute-done.refs_1_ = bf16[640,768]{1,0:T(8,128)(2,1)S(1)} collective-permute-done((bf16[640,768]{1,0:T(8,128)(2,1)}, bf16[640,768]{1,0:T(8,128)(2,1)S(1)}, u32[]{:S(2)}, u32[]{:S(2)}) %collective-permute-start) | collective-permute-done | bytes 983072 | tf_op jit(solution)/shard_map/ppermute | solution.py:535
  110.1 2.8 %collective-permute-done.1.refs_3_ = bf16[640,768]{1,0:T(8,128)(2,1)S(1)} collective-permute-done((bf16[640,768]{1,0:T(8,128)(2,1)}, bf16[640,768]{1,0:T(8,128)(2,1)S(1)}, u32[]{:S(2)}, u32[]{:S(2)}) %collective-permute-start.1) | collective-permute-done | bytes 983072 | tf_op jit(solution)/shard_map/ppermute | solution.py:535
  112.9 0.0 copy-start.7
  112.9 0.1 collective-permute-done.2.refs_5_
  113.0 0.0 copy-done.6
  113.0 0.8 copy-done.7
  113.9 11.0 %pair_a.1 = (bf16[64,160,128]{2,1,0:T(8,128)(2,1)}, bf16[1152,768]{1,0:T(8,128)(2,1)}, bf16[1152,768]{1,0:T(8,128)(2,1)}, bf16[1152,768]{1,0:T(8,128)(2,1)}, f32[64,128]{1,0:T(8,128)}) custom-call(bf16[640,768]{1,0:T(8,128)(2,1)} %get-tuple-element.86.refs_0_, bf16[640,768]{1,0:T(8,128)(2,1)} %copy-done.6, bf16[640,768]{1,0:T(8,128)(2,1)} %get-tuple-element.87.refs_2_, ...), custom_call_target="tpu_custom_call" | custom-call | flops 4026531840 | bytes 17760256 | tf_op jit(solution)/shard_map/pair_a/pallas_call | solution.py:415
  124.8 4.0 %all-to-all-done.1.x_in.cot_in = bf16[64,256,128]{2,1,0:T(8,128)(2,1)} async-done(((bf16[64,256,128]{2,1,0:T(8,128)(2,1)}), bf16[64,256,128]{2,1,0:T(8,128)(2,1)}, u32[]{:S(2)}, u32[]{:S(2)}) %all-to-all-start.1) | async-done | bytes 4194336 | tf_op jit(solution)/shard_map/all_to_all | solution.py:531
  128.9 9.8 %all-to-all-start.3 = ((bf16[64,160,128]{2,1,0:T(8,128)(2,1)}), bf16[64,160,128]{2,1,0:T(8,128)(2,1)}, u32[]{:S(2)}, u32[]{:S(2)}) async-start(bf16[64,160,128]{2,1,0:T(8,128)(2,1)} %get-tuple-element.103), calls=%async_computation.3 | async-start | bytes 5242880 | tf_op jit(solution)/shard_map/all_to_all | solution.py:531
  138.7 11.0 %project_b.1 = (bf16[1152,2048]{1,0:T(8,128)(2,1)}, bf16[1152,2048]{1,0:T(8,128)(2,1)}, bf16[512,768]{1,0:T(8,128)(2,1)}, bf16[512,768]{1,0:T(8,128)(2,1)}, bf16[512,768]{1,0:T(8,128)(2,1)}) custom-call(bf16[64,256,128]{2,1,0:T(8,128)(2,1)} %all-to-all-done.1.x_in.cot_in, ...), custom_call_target="tpu_custom_call", output_to_operand_aliasing={{0}: (5, {}), {1}: (6, {})} | custom-call | flops 4831838208 | bytes 20185088 | tf_op jit(solution)/shard_map/project_b/pallas_call | solution.py:337
  149.7 3.4 %collective-permute-start.3 = (bf16[512,768]{1,0:T(8,128)(2,1)}, bf16[512,768]{1,0:T(8,128)(2,1)S(1)}, u32[]{:S(2)}, u32[]{:S(2)}) collective-permute-start(bf16[512,768]{1,0:T(8,128)(2,1)} %get-tuple-element.95.refs_0_), channel_id=1, source_target_pairs={{0,64},{64,0},{1,65},{65,1},{2,66},{66,2},{3,67},{67,3},{4,68},{68... | collective-permute-start | bytes 2359304 | tf_op jit(solution)/shard_map/ppermute | solution.py:535
  153.1 0.1 collective-permute-start.4
  153.2 0.4 collective-permute-start.5
  153.7 1.6 collective-permute-done.3.refs_1_
  155.3 0.0 copy-start.4
  155.3 2.2 %collective-permute-done.4.refs_3_ = bf16[512,768]{1,0:T(8,128)(2,1)S(1)} collective-permute-done((bf16[512,768]{1,0:T(8,128)(2,1)}, bf16[512,768]{1,0:T(8,128)(2,1)S(1)}, u32[]{:S(2)}, u32[]{:S(2)}) %collective-permute-start.4) | collective-permute-done | bytes 786464 | tf_op jit(solution)/shard_map/ppermute | solution.py:535
  157.5 0.1 collective-permute-done.5.refs_5_
  157.6 0.0 copy-done.4
  157.6 0.8 copy-done.5
  158.4 9.4 %pair_b.1 = (bf16[64,144,128]{2,1,0:T(8,128)(2,1)}, bf16[1152,768]{1,0:T(8,128)(2,1)}, bf16[1152,768]{1,0:T(8,128)(2,1)}, bf16[1152,768]{1,0:T(8,128)(2,1)}) custom-call(bf16[512,768]{1,0:T(8,128)(2,1)} %get-tuple-element.95.refs_0_, bf16[512,768]{1,0:T(8,128)(2,1)} %copy-done.4, ...), custom_call_target="tpu_custom_call", output_to_operand_aliasing={{1}: (9, {}), {2}: (10, {}), {3}: (11, {})} | custom-call | flops 3221225472 | bytes 15466496 | tf_op jit(solution)/shard_map/pair_b/pallas_call | solution.py:415
  167.8 4.6 %all-to-all-done.3.in_ref = bf16[64,160,128]{2,1,0:T(8,128)(2,1)} async-done(((bf16[64,160,128]{2,1,0:T(8,128)(2,1)}), bf16[64,160,128]{2,1,0:T(8,128)(2,1)}, u32[]{:S(2)}, u32[]{:S(2)}) %all-to-all-start.3) | async-done | bytes 2621472 | tf_op jit(solution)/shard_map/all_to_all | solution.py:531
  172.4 6.8 %all-to-all-start.2 = ((bf16[64,144,128]{2,1,0:T(8,128)(2,1)}), bf16[64,144,128]{2,1,0:T(8,128)(2,1)S(1)}, u32[]{:S(2)}, u32[]{:S(2)}) async-start(bf16[64,144,128]{2,1,0:T(8,128)(2,1)} %get-tuple-element.102), calls=%async_computation.2 | async-start | bytes 4718592 | tf_op jit(solution)/shard_map/all_to_all | solution.py:531
  179.3 0.0 copy-start.3
  179.3 0.0 slice-start
  179.3 9.1 %fusion = bf16[1,2048,768]{2,1,0:T(8,128)(2,1)} fusion(bf16[1152,2048]{1,0:T(8,128)(2,1)} %get-tuple-element.108, bf16[1152,768]{1,0:T(8,128)(2,1)} %get-tuple-element.109), kind=kOutput, calls=%fused_computation.3 | convolution fusion | flops 3625451520 | bytes 9633792 | tf_op jit(solution)/shard_map/dot_general | solution.py:36
  188.3 0.0 copy-done.3
  188.3 8.3 %fusion.1 = bf16[1,2048,768]{2,1,0:T(8,128)(2,1)} fusion(bf16[1152,2048]{1,0:T(8,128)(2,1)} %get-tuple-element.108, bf16[1152,768]{1,0:T(8,128)(2,1)S(1)} %copy-done.3), kind=kOutput, calls=%fused_computation.4 | convolution fusion | flops 3625451520 | bytes 9633792 | tf_op jit(solution)/shard_map/dot_general | solution.py:36
  196.6 0.0 slice-done
  196.6 0.0 slice-done.1
  196.6 0.0 copy-done.2
  196.6 0.0 copy-start
  196.6 0.0 copy-start.1
  196.6 5.6 %fusion.2 = bf16[1,768,2048]{2,1,0:T(8,128)(2,1)} fusion(bf16[1152,768]{1,0:T(8,128)(2,1)S(1)} %copy-done.2, bf16[1152,2048]{1,0:T(8,128)(2,1)S(1)} %bitcast.38), kind=kOutput, calls=%fused_computation.5 | convolution fusion | flops 3625451520 | bytes 9633792 | tf_op jit(solution)/shard_map/dot_general | solution.py:36
  202.3 0.0 copy-done
  202.3 3.0 %combine_a.1 = (f32[128,2048]{1,0:T(8,128)S(1)}, f32[64,128]{1,0:T(8,128)S(1)}) custom-call(s32[8,128]{1,0:T(8,128)S(1)} %bitcast.21, bf16[64,160,128]{2,1,0:T(8,128)(2,1)} %all-to-all-done.3.in_ref), custom_call_target="tpu_custom_call" | custom-call | flops 335544320 | bytes 2621440 | tf_op jit(solution)/shard_map/combine_a/pallas_call | solution.py:489
  205.3 6.2 %all-to-all-done.2.in_ref.slots_ref = bf16[64,144,128]{2,1,0:T(8,128)(2,1)S(1)} async-done(((bf16[64,144,128]{2,1,0:T(8,128)(2,1)}), bf16[64,144,128]{2,1,0:T(8,128)(2,1)S(1)}, u32[]{:S(2)}, u32[]{:S(2)}) %all-to-all-start.2) | async-done | bytes 2359328 | tf_op jit(solution)/shard_map/all_to_all | solution.py:531
  211.6 0.0 copy-done.1
  211.6 2.2 %combine_b.1 = (bf16[128,2048]{1,0:T(8,128)(2,1)}, bf16[8,128]{1,0:T(8,128)(2,1)}) custom-call(s32[8,128]{1,0:T(8,128)S(1)} %bitcast.22, bf16[8,128]{1,0:T(8,128)(2,1)S(1)} %bitcast.26, bf16[64,144,128]{2,1,0:T(8,128)(2,1)S(1)} %all-to-all-done.2.in_ref.slots_ref, bf16[64,144,128]{2,1,0:T(8,128)(2,1)S(1)} %all-to-all-done.2.in_ref.slots_ref, ...), custom_call_target="tpu_custom_call" | custom-call | flops 268435456 | bytes 2359296 | tf_op jit(solution)/shard_map/combine_b/pallas_call | solution.py:508
  (5 shorter events, 0.0 us)
Async XLA Ops:
  73.9 55.0 %all-to-all-start.1 = ((bf16[64,256,128]{2,1,0:T(8,128)(2,1)}), bf16[64,256,128]{2,1,0:T(8,128)(2,1)}, u32[]{:S(2)}, u32[]{:S(2)}) async-start(bf16[64,256,128]{2,1,0:T(8,128)(2,1)} %pack_b_0.1), calls=%async_computation.1 | async-start | bytes 8388608 | tf_op jit(solution)/shard_map/all_to_all | solution.py:531
  107.3 2.8 %collective-permute-start = (bf16[640,768]{1,0:T(8,128)(2,1)}, bf16[640,768]{1,0:T(8,128)(2,1)S(1)}, u32[]{:S(2)}, u32[]{:S(2)}) collective-permute-start(bf16[640,768]{1,0:T(8,128)(2,1)} %get-tuple-element.86.refs_0_), channel_id=1, source_target_pairs={{0,64},{64,0},{1,65},{65,1},{2,66},{66,2},{3,67},{67,3},{4,68},{68... | collective-permute-start | bytes 2949128 | tf_op jit(solution)/shard_map/ppermute | solution.py:535
  107.3 5.6 %collective-permute-start.1 = (bf16[640,768]{1,0:T(8,128)(2,1)}, bf16[640,768]{1,0:T(8,128)(2,1)S(1)}, u32[]{:S(2)}, u32[]{:S(2)}) collective-permute-start(bf16[640,768]{1,0:T(8,128)(2,1)} %get-tuple-element.87.refs_2_), channel_id=1, source_target_pairs={{0,64},{64,0},{1,65},{65,1},{2,66},{66,2},{3,67},{67,3},{4,68},{68... | collective-permute-start | bytes 2949128 | tf_op jit(solution)/shard_map/ppermute | solution.py:535
  107.8 5.2 %collective-permute-start.2 = (bf16[640,768]{1,0:T(8,128)(2,1)}, bf16[640,768]{1,0:T(8,128)(2,1)}, u32[]{:S(2)}, u32[]{:S(2)}) collective-permute-start(bf16[640,768]{1,0:T(8,128)(2,1)} %get-tuple-element.88.refs_4_), channel_id=1, source_target_pairs={{0,64},{64,0},{1,65},{65,1},{2,66},{66,2},{3,67},{67,3},{4,68},{68... | collective-permute-start | bytes 2949128 | tf_op jit(solution)/shard_map/ppermute | solution.py:535
  110.1 2.9 %copy-start.6 = (bf16[640,768]{1,0:T(8,128)(2,1)}, bf16[640,768]{1,0:T(8,128)(2,1)S(1)}, u32[]{:S(2)}) copy-start(bf16[640,768]{1,0:T(8,128)(2,1)S(1)} %collective-permute-done.refs_1_) | copy-start | bytes 2949124
  112.9 1.0 copy-start.7
  128.9 43.5 %all-to-all-start.3 = ((bf16[64,160,128]{2,1,0:T(8,128)(2,1)}), bf16[64,160,128]{2,1,0:T(8,128)(2,1)}, u32[]{:S(2)}, u32[]{:S(2)}) async-start(bf16[64,160,128]{2,1,0:T(8,128)(2,1)} %get-tuple-element.103), calls=%async_computation.3 | async-start | bytes 5242880 | tf_op jit(solution)/shard_map/all_to_all | solution.py:531
  149.7 5.6 %collective-permute-start.3 = (bf16[512,768]{1,0:T(8,128)(2,1)}, bf16[512,768]{1,0:T(8,128)(2,1)S(1)}, u32[]{:S(2)}, u32[]{:S(2)}) collective-permute-start(bf16[512,768]{1,0:T(8,128)(2,1)} %get-tuple-element.95.refs_0_), channel_id=1, source_target_pairs={{0,64},{64,0},{1,65},{65,1},{2,66},{66,2},{3,67},{67,3},{4,68},{68... | collective-permute-start | bytes 2359304 | tf_op jit(solution)/shard_map/ppermute | solution.py:535
  153.1 4.4 %collective-permute-start.4 = (bf16[512,768]{1,0:T(8,128)(2,1)}, bf16[512,768]{1,0:T(8,128)(2,1)S(1)}, u32[]{:S(2)}, u32[]{:S(2)}) collective-permute-start(bf16[512,768]{1,0:T(8,128)(2,1)} %get-tuple-element.96.refs_2_), channel_id=1, source_target_pairs={{0,64},{64,0},{1,65},{65,1},{2,66},{66,2},{3,67},{67,3},{4,68},{68... | collective-permute-start | bytes 2359304 | tf_op jit(solution)/shard_map/ppermute | solution.py:535
  153.2 4.4 %collective-permute-start.5 = (bf16[512,768]{1,0:T(8,128)(2,1)}, bf16[512,768]{1,0:T(8,128)(2,1)}, u32[]{:S(2)}, u32[]{:S(2)}) collective-permute-start(bf16[512,768]{1,0:T(8,128)(2,1)} %get-tuple-element.97.refs_4_), channel_id=1, source_target_pairs={{0,64},{64,0},{1,65},{65,1},{2,66},{66,2},{3,67},{67,3},{4,68},{68... | collective-permute-start | bytes 2359304 | tf_op jit(solution)/shard_map/ppermute | solution.py:535
  155.3 2.4 %copy-start.4 = (bf16[512,768]{1,0:T(8,128)(2,1)}, bf16[512,768]{1,0:T(8,128)(2,1)S(1)}, u32[]{:S(2)}) copy-start(bf16[512,768]{1,0:T(8,128)(2,1)S(1)} %collective-permute-done.3.refs_1_) | copy-start | bytes 2359300
  157.5 0.9 copy-start.5
  172.4 39.1 %all-to-all-start.2 = ((bf16[64,144,128]{2,1,0:T(8,128)(2,1)}), bf16[64,144,128]{2,1,0:T(8,128)(2,1)S(1)}, u32[]{:S(2)}, u32[]{:S(2)}) async-start(bf16[64,144,128]{2,1,0:T(8,128)(2,1)} %get-tuple-element.102), calls=%async_computation.2 | async-start | bytes 4718592 | tf_op jit(solution)/shard_map/all_to_all | solution.py:531
  179.3 9.1 %copy-start.3 = (bf16[1152,768]{1,0:T(8,128)(2,1)S(1)}, bf16[1152,768]{1,0:T(8,128)(2,1)}, u32[]{:S(2)}) copy-start(bf16[1152,768]{1,0:T(8,128)(2,1)} %get-tuple-element.110) | copy-start | bytes 5308420
  179.3 17.3 %slice-start = ((s8[4718592]{0:T(1024)(128)(4,1)}), s8[4194304]{0:T(1024)(128)(4,1)S(1)}, s32[]{:S(2)}) async-start(s8[4718592]{0:T(1024)(128)(4,1)} %bitcast.37), calls=%async_computation.4 | async-start | bytes 8388608
  188.3 8.3 %slice-start.1 = ((s8[4718592]{0:T(1024)(128)(4,1)}), s8[524288]{0:T(1024)(128)(4,1)S(1)}, s32[]{:S(2)}) async-start(s8[4718592]{0:T(1024)(128)(4,1)} %bitcast.37), calls=%async_computation.5 | async-start | bytes 1048576
  188.3 8.3 %copy-start.2 = (bf16[1152,768]{1,0:T(8,128)(2,1)S(1)}, bf16[1152,768]{1,0:T(8,128)(2,1)}, u32[]{:S(2)}) copy-start(bf16[1152,768]{1,0:T(8,128)(2,1)} %get-tuple-element.111) | copy-start | bytes 5308420
  196.6 5.7 %copy-start = (s32[128,8]{0,1:T(8,128)S(1)}, s32[128,8]{0,1:T(8,128)}, u32[]{:S(2)}) copy-start(s32[128,8]{0,1:T(8,128)} %param.10) | copy-start | bytes 12292
  196.6 14.9 %copy-start.1 = (bf16[128,8]{0,1:T(8,128)(2,1)S(1)}, bf16[128,8]{0,1:T(8,128)(2,1)}, u32[]{:S(2)}) copy-start(bf16[128,8]{0,1:T(8,128)(2,1)} %param.9) | copy-start | bytes 6148

commit v10 on v8

--- a/solution.py
+++ b/solution.py
@@ -208,20 +208,43 @@
 
 
 def turn_kernel(core, count, *refs):
-    ins, outs = refs[:count], refs[-4 * count : -3 * count]
-    held, turned, sems = refs[-3 * count : -2 * count], refs[-2 * count : -count], refs[-count:]
+    ins, outs = refs[:count], refs[-5 * count : -4 * count]
+    held, turned = refs[-4 * count : -3 * count], refs[-3 * count : -2 * count]
+    in_sems, out_sems = refs[-2 * count : -count], refs[-count:]
+
+    def move(mat, a, b, out, in_sem, out_sem, start, size):
+        rows = pl.ds(start, size)
+        load = pltpu.make_async_copy(mat.at[rows], a.at[rows], in_sem)
+        store = pltpu.make_async_copy(b.at[:, rows], out.at[:, rows], out_sem)
+        return load, store
+
+    def flip(a, b, start, size):
+        for at in range(start, start + size, 128):
+            b[:, at : at + 128] = a[at : at + 128, :].T
 
     @pl.when(lax.axis_index("dp") == core)
     def _():
-        for mat, a, b, out, sem in zip(ins, held, turned, outs, sems):
-            load = pltpu.make_async_copy(mat, a, sem)
-            load.start()
-            load.wait()
-            for at in range(0, a.shape[0], 256):
-                b[:, at : at + 256] = a[at : at + 256, :].T
-            store = pltpu.make_async_copy(b, out, sem)
-            store.start()
-            store.wait()
+        given = list(zip(ins, held, turned, outs, in_sems, out_sems))
+        if core:
+            for refs in given:
+                size = refs[0].shape[0] // 2
+                for start in (0, size):
+                    load, store = move(*refs, start, size)
+                    load.start()
+                    load.wait()
+                    flip(refs[1], refs[2], start, size)
+                    store.start()
+                    store.wait()
+        else:
+            moves = [move(*refs, 0, refs[0].shape[0]) for refs in given]
+            for load, _ in moves:
+                load.start()
+            for refs, (load, store) in zip(given, moves):
+                load.wait()
+                flip(refs[1], refs[2], 0, refs[0].shape[0])
+                store.start()
+            for _, store in moves:
+                store.wait()
 
 
 def turn(name, core, mats, before=()):
@@ -235,7 +258,7 @@
         input_output_aliases={len(mats) + k: k for k in range(len(before))},
         scratch_shapes=[pltpu.VMEM(shape, BF) for shape in shapes]
         + [pltpu.VMEM(shape[::-1], BF) for shape in shapes]
-        + [pltpu.SemaphoreType.DMA] * len(mats),
+        + [pltpu.SemaphoreType.DMA] * (2 * len(mats)),
         compiler_params=pltpu.CompilerParams(vmem_limit_bytes=VMEM),
         cost_estimate=pl.CostEstimate(flops=0, bytes_accessed=sum(4 * a * b for a, b in shapes), transcendentals=0),
         name=name,

time: 221 us -> 218 us (0.986)
  starting transfers between devices: 31.8 us -> 41.4 us
  Pallas kernels: 71 us -> 64.3 us
  blocking collectives: 65.1 us -> 60.7 us
    ppermute x6, starting transfers between devices: 4.23 us -> 17.7 us  [other_core(): return lax.ppermute(x, 'dp', [(0, 1), (1, 0)])]
    pallas_call x2, Pallas kernels: 13.5 us -> 6.76 us  [turn(): pl.pallas_call(functools.partial(turn_kernel, core, len(mats)), out_shape...]
    all_to_all x1, blocking collectives: 65.1 us -> 60.7 us  [exchange(): lax.all_to_all(x, ('ctx', 'tp'), split_axis=0, concat_axis=0, tiled=True)]
    all_to_all x3, starting transfers between devices: 27.6 us -> 23.8 us  [exchange(): lax.all_to_all(x, ('ctx', 'tp'), split_axis=0, concat_axis=0, tiled=True)]
  transfers between devices with their start and end apart: 9 -> 9, of which waited for: 9 -> 8; matrix products, arithmetic and copies ran while one was open for 11% -> 11% of each run, Pallas kernels for 28% -> 25%
where the time goes in v10:
time: 218 us; the launch traced here: 217 us
  Pallas kernels  64.3 us (29%)
  blocking collectives  60.7 us (28%)
  starting transfers between devices  41.4 us (19%)
  waiting for transfers between devices  25.4 us (12%)
  matrix products  23 us (11%)
    all_to_all x1, blocking collectives, exchange(): lax.all_to_all(x, ('ctx', 'tp'), split_axis=0, concat_axis=0, tiled=True)  60.7 us
    pallas_call x2, Pallas kernels, project(): pl.pallas_call(functools.partial(project_kernel, not kept), grid=(experts...  24.6 us
    all_to_all x3, starting transfers between devices, exchange(): lax.all_to_all(x, ('ctx', 'tp'), split_axis=0, concat_axis=0, tiled=True)  23.8 us
    dot_general x3, matrix products, contract(): lax.dot_general(left, right, (((0,), (0,)), ((), ())), preferred_element_...  23 us
    pallas_call x2, Pallas kernels, pair(): pl.pallas_call(functools.partial(pair_kernel, extra), grid=(experts // pe...  20.4 us
    ppermute x6, starting transfers between devices, other_core(): return lax.ppermute(x, 'dp', [(0, 1), (1, 0)])  17.7 us
    all_to_all x3, waiting for transfers between devices, exchange(): lax.all_to_all(x, ('ctx', 'tp'), split_axis=0, concat_axis=0, tiled=True)  16.5 us
    ppermute x6, waiting for transfers between devices, other_core(): return lax.ppermute(x, 'dp', [(0, 1), (1, 0)])  8.82 us
  transfers between devices with their start and end apart: 9, of which 8 were waited for; matrix products, arithmetic and copies ran while one was open for 11% of the time, Pallas kernels for 25%

profile of v10, /device:TPU:0, one launch (start us, length us, event | category | flops | bytes accessed | tf_op | source)
XLA Modules:
  0.0 217.2 jit_solution(4781323105936645143)
XLA Ops:
  0.6 0.1 turn_1.1
  0.7 7.4 %pack.1 = (bf16[64,320,128]{2,1,0:T(8,128)(2,1)}, bf16[64,256,128]{2,1,0:T(8,128)(2,1)}) custom-call(s32[8,128]{1,0:T(8,128)} %bitcast.18, bf16[8,128]{1,0:T(8,128)(2,1)} %bitcast.21, bf16[128,2048]{1,0:T(8,128)(2,1)} %x_ref.1, bf16[128,2048]{1,0:T(8,128)(2,1)} %cot_ref.1), custom_call_target="tpu_custom_call" | custom-call | flops 1207959552 | bytes 9437184 | tf_op jit(solution)/shard_map/pack/pallas_call | solution.py:193
  8.1 60.7 %all_to_all.20.x_in.cot_in = bf16[64,320,128]{2,1,0:T(8,128)(2,1)} all-to-all(bf16[64,320,128]{2,1,0:T(8,128)(2,1)} %get-tuple-element.56), channel_id=1, replica_groups=mesh['dp'=2,'ctx'=16,'tp'=4] {'ctx','tp'}, dimensions={0} | all-to-all | bytes 10485760 | tf_op jit(solution)/shard_map/all_to_all | solution.py:484
  68.8 5.7 %all-to-all-start.1 = ((bf16[64,256,128]{2,1,0:T(8,128)(2,1)}), bf16[64,256,128]{2,1,0:T(8,128)(2,1)}, u32[]{:S(2)}, u32[]{:S(2)}) async-start(bf16[64,256,128]{2,1,0:T(8,128)(2,1)} %get-tuple-element.61), calls=%async_computation.1 | async-start | bytes 8388608 | tf_op jit(solution)/shard_map/all_to_all | solution.py:484
  74.5 6.7 %turn_0.1 = (bf16[768,2048]{1,0:T(8,128)(2,1)}, bf16[768,2048]{1,0:T(8,128)(2,1)}, bf16[2048,768]{1,0:T(8,128)(2,1)}) custom-call(bf16[2048,768]{1,0:T(8,128)(2,1)} %bitcast.24, bf16[2048,768]{1,0:T(8,128)(2,1)} %bitcast.28, bf16[768,2048]{1,0:T(8,128)(2,1)} %bitcast.32, ...), custom_call_target="tpu_custom_call", output_to_operand_aliasing={{0}: (3, {}), {1}: (4, {}), {2}: (5, {})} | custom-call | bytes 18874368 | tf_op jit(solution)/shard_map/turn_0/pallas_call | solution.py:253
  81.2 13.6 %project_a.1 = (bf16[1152,2048]{1,0:T(8,128)(2,1)}, bf16[1152,2048]{1,0:T(8,128)(2,1)}, bf16[640,768]{1,0:T(8,128)(2,1)}, bf16[640,768]{1,0:T(8,128)(2,1)}, bf16[640,768]{1,0:T(8,128)(2,1)}) custom-call(bf16[64,320,128]{2,1,0:T(8,128)(2,1)} %all_to_all.20.x_in.cot_in, bf16[64,320,128]{2,1,0:T(8,128)(2,1)} %all_to_all.20.x_in.cot_in, ...), custom_call_target="tpu_custom_call" | custom-call | flops 6039797760 | bytes 22872064 | tf_op jit(solution)/shard_map/project_a/pallas_call | solution.py:290
  94.8 15.9 %collective-permute-start = (bf16[640,768]{1,0:T(8,128)(2,1)}, bf16[640,768]{1,0:T(8,128)(2,1)S(1)}, u32[]{:S(2)}, u32[]{:S(2)}) collective-permute-start(bf16[640,768]{1,0:T(8,128)(2,1)} %get-tuple-element.70.refs_0_), channel_id=1, source_target_pairs={{0,64},{64,0},{1,65},{65,1},{2,66},{66,2},{3,67},{67,3},{4,68},{68... | collective-permute-start | bytes 2949128 | tf_op jit(solution)/shard_map/ppermute | solution.py:488
  110.7 0.1 collective-permute-start.1
  110.8 0.4 collective-permute-start.2
  111.3 1.9 collective-permute-done.refs_1_
  113.1 0.0 copy-start.6
  113.1 2.8 %collective-permute-done.1.refs_3_ = bf16[640,768]{1,0:T(8,128)(2,1)S(1)} collective-permute-done((bf16[640,768]{1,0:T(8,128)(2,1)}, bf16[640,768]{1,0:T(8,128)(2,1)S(1)}, u32[]{:S(2)}, u32[]{:S(2)}) %collective-permute-start.1) | collective-permute-done | bytes 983072 | tf_op jit(solution)/shard_map/ppermute | solution.py:488
  116.0 0.0 copy-start.7
  116.0 0.1 collective-permute-done.2.refs_5_
  116.1 0.0 copy-done.6
  116.1 0.8 copy-done.7
  116.9 11.0 %pair_a.1 = (bf16[64,160,128]{2,1,0:T(8,128)(2,1)}, bf16[1152,768]{1,0:T(8,128)(2,1)}, bf16[1152,768]{1,0:T(8,128)(2,1)}, bf16[1152,768]{1,0:T(8,128)(2,1)}, f32[64,128]{1,0:T(8,128)}) custom-call(bf16[640,768]{1,0:T(8,128)(2,1)} %get-tuple-element.70.refs_0_, bf16[640,768]{1,0:T(8,128)(2,1)} %copy-done.6, bf16[640,768]{1,0:T(8,128)(2,1)} %get-tuple-element.71.refs_2_, ...), custom_call_target="tpu_custom_call" | custom-call | flops 4026531840 | bytes 17760256 | tf_op jit(solution)/shard_map/pair_a/pallas_call | solution.py:368
  127.9 0.0 all-to-all-done.1.x_in.cot_in
  127.9 10.2 %all-to-all-start.3 = ((bf16[64,160,128]{2,1,0:T(8,128)(2,1)}), bf16[64,160,128]{2,1,0:T(8,128)(2,1)}, u32[]{:S(2)}, u32[]{:S(2)}) async-start(bf16[64,160,128]{2,1,0:T(8,128)(2,1)} %get-tuple-element.87), calls=%async_computation.3 | async-start | bytes 5242880 | tf_op jit(solution)/shard_map/all_to_all | solution.py:484
  138.2 11.0 %project_b.1 = (bf16[1152,2048]{1,0:T(8,128)(2,1)}, bf16[1152,2048]{1,0:T(8,128)(2,1)}, bf16[512,768]{1,0:T(8,128)(2,1)}, bf16[512,768]{1,0:T(8,128)(2,1)}, bf16[512,768]{1,0:T(8,128)(2,1)}) custom-call(bf16[64,256,128]{2,1,0:T(8,128)(2,1)} %all-to-all-done.1.x_in.cot_in, ...), custom_call_target="tpu_custom_call", output_to_operand_aliasing={{0}: (5, {}), {1}: (6, {})} | custom-call | flops 4831838208 | bytes 20185088 | tf_op jit(solution)/shard_map/project_b/pallas_call | solution.py:290
  149.1 0.7 collective-permute-start.3
  149.9 0.1 collective-permute-start.4
  149.9 0.4 collective-permute-start.5
  150.4 1.6 collective-permute-done.3.refs_1_
  152.0 0.0 copy-start.4
  152.0 2.2 %collective-permute-done.4.refs_3_ = bf16[512,768]{1,0:T(8,128)(2,1)S(1)} collective-permute-done((bf16[512,768]{1,0:T(8,128)(2,1)}, bf16[512,768]{1,0:T(8,128)(2,1)S(1)}, u32[]{:S(2)}, u32[]{:S(2)}) %collective-permute-start.4) | collective-permute-done | bytes 786464 | tf_op jit(solution)/shard_map/ppermute | solution.py:488
  154.2 0.1 collective-permute-done.5.refs_5_
  154.4 0.0 copy-done.4
  154.4 0.8 copy-done.5
  155.1 9.4 %pair_b.1 = (bf16[64,144,128]{2,1,0:T(8,128)(2,1)}, bf16[1152,768]{1,0:T(8,128)(2,1)}, bf16[1152,768]{1,0:T(8,128)(2,1)}, bf16[1152,768]{1,0:T(8,128)(2,1)}) custom-call(bf16[512,768]{1,0:T(8,128)(2,1)} %get-tuple-element.79.refs_0_, bf16[512,768]{1,0:T(8,128)(2,1)} %copy-done.4, ...), custom_call_target="tpu_custom_call", output_to_operand_aliasing={{1}: (9, {}), {2}: (10, {}), {3}: (11, {})} | custom-call | flops 3221225472 | bytes 15466496 | tf_op jit(solution)/shard_map/pair_b/pallas_call | solution.py:368
  164.5 10.3 %all-to-all-done.3.in_ref = bf16[64,160,128]{2,1,0:T(8,128)(2,1)} async-done(((bf16[64,160,128]{2,1,0:T(8,128)(2,1)}), bf16[64,160,128]{2,1,0:T(8,128)(2,1)}, u32[]{:S(2)}, u32[]{:S(2)}) %all-to-all-start.3) | async-done | bytes 2621472 | tf_op jit(solution)/shard_map/all_to_all | solution.py:484
  174.8 7.8 %all-to-all-start.2 = ((bf16[64,144,128]{2,1,0:T(8,128)(2,1)}), bf16[64,144,128]{2,1,0:T(8,128)(2,1)S(1)}, u32[]{:S(2)}, u32[]{:S(2)}) async-start(bf16[64,144,128]{2,1,0:T(8,128)(2,1)} %get-tuple-element.86), calls=%async_computation.2 | async-start | bytes 4718592 | tf_op jit(solution)/shard_map/all_to_all | solution.py:484
  182.6 0.0 copy-start.3
  182.6 0.0 slice-start
  182.7 9.1 %fusion = bf16[1,2048,768]{2,1,0:T(8,128)(2,1)} fusion(bf16[1152,2048]{1,0:T(8,128)(2,1)} %get-tuple-element.92, bf16[1152,768]{1,0:T(8,128)(2,1)} %get-tuple-element.93), kind=kOutput, calls=%fused_computation.3 | convolution fusion | flops 3625451520 | bytes 9633792 | tf_op jit(solution)/shard_map/dot_general | solution.py:36
  191.7 0.0 copy-done.3
  191.7 8.3 %fusion.1 = bf16[1,2048,768]{2,1,0:T(8,128)(2,1)} fusion(bf16[1152,2048]{1,0:T(8,128)(2,1)} %get-tuple-element.92, bf16[1152,768]{1,0:T(8,128)(2,1)S(1)} %copy-done.3), kind=kOutput, calls=%fused_computation.4 | convolution fusion | flops 3625451520 | bytes 9633792 | tf_op jit(solution)/shard_map/dot_general | solution.py:36
  200.0 0.0 slice-done
  200.0 0.0 slice-done.1
  200.0 0.0 copy-done.2
  200.0 0.0 copy-start
  200.0 0.0 copy-start.1
  200.0 5.6 %fusion.2 = bf16[1,768,2048]{2,1,0:T(8,128)(2,1)} fusion(bf16[1152,768]{1,0:T(8,128)(2,1)S(1)} %copy-done.2, bf16[1152,2048]{1,0:T(8,128)(2,1)S(1)} %bitcast.34), kind=kOutput, calls=%fused_computation.5 | convolution fusion | flops 3625451520 | bytes 9633792 | tf_op jit(solution)/shard_map/dot_general | solution.py:36
  205.7 0.0 copy-done
  205.7 3.0 %combine_a.1 = (f32[128,2048]{1,0:T(8,128)S(1)}, f32[64,128]{1,0:T(8,128)S(1)}) custom-call(s32[8,128]{1,0:T(8,128)S(1)} %bitcast.19, bf16[64,160,128]{2,1,0:T(8,128)(2,1)} %all-to-all-done.3.in_ref), custom_call_target="tpu_custom_call" | custom-call | flops 335544320 | bytes 2621440 | tf_op jit(solution)/shard_map/combine_a/pallas_call | solution.py:442
  208.7 6.3 %all-to-all-done.2.in_ref.slots_ref = bf16[64,144,128]{2,1,0:T(8,128)(2,1)S(1)} async-done(((bf16[64,144,128]{2,1,0:T(8,128)(2,1)}), bf16[64,144,128]{2,1,0:T(8,128)(2,1)S(1)}, u32[]{:S(2)}, u32[]{:S(2)}) %all-to-all-start.2) | async-done | bytes 2359328 | tf_op jit(solution)/shard_map/all_to_all | solution.py:484
  215.0 0.0 copy-done.1
  215.0 2.2 combine_b.1
  (4 shorter events, 0.0 us)
Async XLA Ops:
  68.8 59.1 %all-to-all-start.1 = ((bf16[64,256,128]{2,1,0:T(8,128)(2,1)}), bf16[64,256,128]{2,1,0:T(8,128)(2,1)}, u32[]{:S(2)}, u32[]{:S(2)}) async-start(bf16[64,256,128]{2,1,0:T(8,128)(2,1)} %get-tuple-element.61), calls=%async_computation.1 | async-start | bytes 8388608 | tf_op jit(solution)/shard_map/all_to_all | solution.py:484
  94.8 18.3 %collective-permute-start = (bf16[640,768]{1,0:T(8,128)(2,1)}, bf16[640,768]{1,0:T(8,128)(2,1)S(1)}, u32[]{:S(2)}, u32[]{:S(2)}) collective-permute-start(bf16[640,768]{1,0:T(8,128)(2,1)} %get-tuple-element.70.refs_0_), channel_id=1, source_target_pairs={{0,64},{64,0},{1,65},{65,1},{2,66},{66,2},{3,67},{67,3},{4,68},{68... | collective-permute-start | bytes 2949128 | tf_op jit(solution)/shard_map/ppermute | solution.py:488
  110.7 5.2 %collective-permute-start.1 = (bf16[640,768]{1,0:T(8,128)(2,1)}, bf16[640,768]{1,0:T(8,128)(2,1)S(1)}, u32[]{:S(2)}, u32[]{:S(2)}) collective-permute-start(bf16[640,768]{1,0:T(8,128)(2,1)} %get-tuple-element.71.refs_2_), channel_id=1, source_target_pairs={{0,64},{64,0},{1,65},{65,1},{2,66},{66,2},{3,67},{67,3},{4,68},{68... | collective-permute-start | bytes 2949128 | tf_op jit(solution)/shard_map/ppermute | solution.py:488
  110.8 5.3 %collective-permute-start.2 = (bf16[640,768]{1,0:T(8,128)(2,1)}, bf16[640,768]{1,0:T(8,128)(2,1)}, u32[]{:S(2)}, u32[]{:S(2)}) collective-permute-start(bf16[640,768]{1,0:T(8,128)(2,1)} %get-tuple-element.72.refs_4_), channel_id=1, source_target_pairs={{0,64},{64,0},{1,65},{65,1},{2,66},{66,2},{3,67},{67,3},{4,68},{68... | collective-permute-start | bytes 2949128 | tf_op jit(solution)/shard_map/ppermute | solution.py:488
  113.1 2.9 %copy-start.6 = (bf16[640,768]{1,0:T(8,128)(2,1)}, bf16[640,768]{1,0:T(8,128)(2,1)S(1)}, u32[]{:S(2)}) copy-start(bf16[640,768]{1,0:T(8,128)(2,1)S(1)} %collective-permute-done.refs_1_) | copy-start | bytes 2949124
  116.0 0.9 copy-start.7
  127.9 46.9 %all-to-all-start.3 = ((bf16[64,160,128]{2,1,0:T(8,128)(2,1)}), bf16[64,160,128]{2,1,0:T(8,128)(2,1)}, u32[]{:S(2)}, u32[]{:S(2)}) async-start(bf16[64,160,128]{2,1,0:T(8,128)(2,1)} %get-tuple-element.87), calls=%async_computation.3 | async-start | bytes 5242880 | tf_op jit(solution)/shard_map/all_to_all | solution.py:484
  149.1 2.8 %collective-permute-start.3 = (bf16[512,768]{1,0:T(8,128)(2,1)}, bf16[512,768]{1,0:T(8,128)(2,1)S(1)}, u32[]{:S(2)}, u32[]{:S(2)}) collective-permute-start(bf16[512,768]{1,0:T(8,128)(2,1)} %get-tuple-element.79.refs_0_), channel_id=1, source_target_pairs={{0,64},{64,0},{1,65},{65,1},{2,66},{66,2},{3,67},{67,3},{4,68},{68... | collective-permute-start | bytes 2359304 | tf_op jit(solution)/shard_map/ppermute | solution.py:488
  149.9 4.4 %collective-permute-start.4 = (bf16[512,768]{1,0:T(8,128)(2,1)}, bf16[512,768]{1,0:T(8,128)(2,1)S(1)}, u32[]{:S(2)}, u32[]{:S(2)}) collective-permute-start(bf16[512,768]{1,0:T(8,128)(2,1)} %get-tuple-element.80.refs_2_), channel_id=1, source_target_pairs={{0,64},{64,0},{1,65},{65,1},{2,66},{66,2},{3,67},{67,3},{4,68},{68... | collective-permute-start | bytes 2359304 | tf_op jit(solution)/shard_map/ppermute | solution.py:488
  149.9 4.4 %collective-permute-start.5 = (bf16[512,768]{1,0:T(8,128)(2,1)}, bf16[512,768]{1,0:T(8,128)(2,1)}, u32[]{:S(2)}, u32[]{:S(2)}) collective-permute-start(bf16[512,768]{1,0:T(8,128)(2,1)} %get-tuple-element.81.refs_4_), channel_id=1, source_target_pairs={{0,64},{64,0},{1,65},{65,1},{2,66},{66,2},{3,67},{67,3},{4,68},{68... | collective-permute-start | bytes 2359304 | tf_op jit(solution)/shard_map/ppermute | solution.py:488
  152.0 2.4 %copy-start.4 = (bf16[512,768]{1,0:T(8,128)(2,1)}, bf16[512,768]{1,0:T(8,128)(2,1)S(1)}, u32[]{:S(2)}) copy-start(bf16[512,768]{1,0:T(8,128)(2,1)S(1)} %collective-permute-done.3.refs_1_) | copy-start | bytes 2359300
  154.2 0.9 copy-start.5
  174.8 40.2 %all-to-all-start.2 = ((bf16[64,144,128]{2,1,0:T(8,128)(2,1)}), bf16[64,144,128]{2,1,0:T(8,128)(2,1)S(1)}, u32[]{:S(2)}, u32[]{:S(2)}) async-start(bf16[64,144,128]{2,1,0:T(8,128)(2,1)} %get-tuple-element.86), calls=%async_computation.2 | async-start | bytes 4718592 | tf_op jit(solution)/shard_map/all_to_all | solution.py:484
  182.6 9.1 %copy-start.3 = (bf16[1152,768]{1,0:T(8,128)(2,1)S(1)}, bf16[1152,768]{1,0:T(8,128)(2,1)}, u32[]{:S(2)}) copy-start(bf16[1152,768]{1,0:T(8,128)(2,1)} %get-tuple-element.94) | copy-start | bytes 5308420
  182.6 17.3 %slice-start = ((s8[4718592]{0:T(1024)(128)(4,1)}), s8[4194304]{0:T(1024)(128)(4,1)S(1)}, s32[]{:S(2)}) async-start(s8[4718592]{0:T(1024)(128)(4,1)} %bitcast.33), calls=%async_computation.4 | async-start | bytes 8388608
  191.7 8.3 %slice-start.1 = ((s8[4718592]{0:T(1024)(128)(4,1)}), s8[524288]{0:T(1024)(128)(4,1)S(1)}, s32[]{:S(2)}) async-start(s8[4718592]{0:T(1024)(128)(4,1)} %bitcast.33), calls=%async_computation.5 | async-start | bytes 1048576
  191.7 8.3 %copy-start.2 = (bf16[1152,768]{1,0:T(8,128)(2,1)S(1)}, bf16[1152,768]{1,0:T(8,128)(2,1)}, u32[]{:S(2)}) copy-start(bf16[1152,768]{1,0:T(8,128)(2,1)} %get-tuple-element.95) | copy-start | bytes 5308420
  200.0 5.7 %copy-start = (s32[128,8]{0,1:T(8,128)S(1)}, s32[128,8]{0,1:T(8,128)}, u32[]{:S(2)}) copy-start(s32[128,8]{0,1:T(8,128)} %param.10) | copy-start | bytes 12292
  200.0 15.0 %copy-start.1 = (bf16[128,8]{0,1:T(8,128)(2,1)S(1)}, bf16[128,8]{0,1:T(8,128)(2,1)}, u32[]{:S(2)}) copy-start(bf16[128,8]{0,1:T(8,128)(2,1)} %param.9) | copy-start | bytes 6148

commit v11 on v10

--- a/solution.py
+++ b/solution.py
@@ -227,8 +227,9 @@
         given = list(zip(ins, held, turned, outs, in_sems, out_sems))
         if core:
             for refs in given:
-                size = refs[0].shape[0] // 2
-                for start in (0, size):
+                rows = refs[0].shape[0]
+                size = min(rows, 1024)
+                for start in range(0, rows, size):
                     load, store = move(*refs, start, size)
                     load.start()
                     load.wait()
@@ -265,20 +266,17 @@
     )(*mats, *before)
 
 
-def project_kernel(extra, x_in, cot_in, gate_w, up_w, down_w, *refs):
-    x_ref, cot_ref, gate_ref, up_ref, back_ref = refs[-5:]
-    peers = x_in.shape[0]
-    tiles = x_ref.shape[1] // LANE
-    for in_ref, rows_ref in ((x_in, x_ref), (cot_in, cot_ref)):
-        unpack_half(in_ref, 0, rows_ref, 0, tiles)
-        if extra:
-            unpack_extra(in_ref, tiles * HALF, rows_ref, peers * HALF)
-    gate_ref[...] = dot(x_ref[...], gate_w[...]).astype(BF)
-    up_ref[...] = dot(x_ref[...], up_w[...]).astype(BF)
-    back_ref[...] = dot(cot_ref[...], down_w[...]).astype(BF)
-
-
-def project(name, got, weights, kept=()):
+def project_kernel(count, extra, in_ref, *refs):
+    weights, rows_ref, outs = refs[:count], refs[-1 - count], refs[-count:]
+    tiles = rows_ref.shape[1] // LANE
+    unpack_half(in_ref, 0, rows_ref, 0, tiles)
+    if extra:
+        unpack_extra(in_ref, tiles * HALF, rows_ref, in_ref.shape[0] * HALF)
+    for weight, out in zip(weights, outs):
+        out[...] = dot(rows_ref[...], weight[...]).astype(BF)
+
+
+def project(name, got, at, weights, kept=()):
     experts, both, _ = got.shape
     width, hidden = weights[0].shape
     part = both // 2
@@ -286,25 +284,26 @@
     peers = SECOND_PEERS if kept else PEERS
     total, rows = experts * slots, peers * slots
     first = experts * FIRST // rows if kept else 0
-    whole = experts * CAP
+    count = len(weights)
     return pl.pallas_call(
-        functools.partial(project_kernel, not kept),
+        functools.partial(project_kernel, count, not kept),
         grid=(experts // peers,),
-        out_shape=[jax.ShapeDtypeStruct((whole, width), BF)] * 2 + [jax.ShapeDtypeStruct((total, hidden), BF)] * 3,
-        in_specs=[pl.BlockSpec((peers, part, LANE), lambda i, at=at: (i, at, 0)) for at in range(2)]
+        out_shape=[jax.ShapeDtypeStruct((experts * CAP, width), BF)]
+        + [jax.ShapeDtypeStruct((total, hidden), BF)] * count,
+        in_specs=[pl.BlockSpec((peers, part, LANE), lambda i: (i, at, 0))]
         + [pl.BlockSpec(w.shape, lambda i: (0, 0)) for w in weights]
         + [pl.BlockSpec(memory_space=pl.ANY) for _ in kept],
-        out_specs=[pl.BlockSpec((rows, width), lambda i: (first + i, 0))] * 2
-        + [pl.BlockSpec((rows, hidden), lambda i: (i, 0))] * 3,
-        input_output_aliases={5 + k: k for k in range(len(kept))},
+        out_specs=[pl.BlockSpec((rows, width), lambda i: (first + i, 0))]
+        + [pl.BlockSpec((rows, hidden), lambda i: (i, 0))] * count,
+        input_output_aliases={1 + count: 0} if kept else {},
         compiler_params=pltpu.CompilerParams(vmem_limit_bytes=VMEM),
         cost_estimate=pl.CostEstimate(
-            flops=6 * total * width * hidden,
-            bytes_accessed=2 * (4 * total * width + 3 * (width + total) * hidden),
+            flops=2 * count * total * width * hidden,
+            bytes_accessed=2 * (2 * total * width + count * (width + total) * hidden),
             transcendentals=0,
         ),
         name=name,
-    )(got, got, *weights, *kept)
+    )(got, *weights, *kept)
 
 
 def slots_of(prob_grad, peers, extra):
@@ -502,8 +501,11 @@
     mats = (gate_mat, up_mat, down_t)
 
     def part(name, got, slot_grads=None, kept=()):
-        rows, cot_rows, gate, up, back = project("project_" + name, got, mats, kept[:2])
-        far = other_core(gate), other_core(up), other_core(back)
+        rows, gate, up = project("gate_up_" + name, got, 0, mats[:2], kept[:1])
+        far = other_core(gate), other_core(up)
+        got, gate, up = lax.optimization_barrier((got, gate, up))
+        cot_rows, back = project("back_" + name, got, 1, mats[2:], kept[1:2])
+        far = *far, other_core(back)
         sent, act, gate_grad, up_grad, *slot_grads = pair(
             "pair_" + name, gate, far[0], up, far[1], back, far[2], gate_t, up_t, experts, slot_grads, kept[2:]
         )

time: 218 us -> 222 us (1.018)
  waiting for transfers between devices: 25.4 us -> 18.5 us
  Pallas kernels: 64.3 us -> 69.5 us
  starting transfers between devices: 41.4 us -> 46.5 us
    ppermute x6, starting transfers between devices: 17.7 us -> 23.5 us  [other_core(): return lax.ppermute(x, 'dp', [(0, 1), (1, 0)])]
    pallas_call x2 -> x4, Pallas kernels: 24.6 us -> 29.8 us  [project(): pl.pallas_call(functools.partial(project_kernel, count, not kept), grid=(...]
    all_to_all x3, waiting for transfers between devices: 16.5 us -> 11.7 us  [exchange(): lax.all_to_all(x, ('ctx', 'tp'), split_axis=0, concat_axis=0, tiled=True)]
  transfers between devices with their start and end apart: 9 -> 9, of which waited for: 8 -> 6; matrix products, arithmetic and copies ran while one was open for 11% -> 10% of each run, Pallas kernels for 25% -> 27%
where the time goes in v11:
time: 222 us; the launch traced here: 221 us
  Pallas kernels  69.5 us (31%)
  blocking collectives  61.8 us (28%)
  starting transfers between devices  46.5 us (21%)
  matrix products  23 us (10%)
  waiting for transfers between devices  18.5 us (8%)
    all_to_all x1, blocking collectives, exchange(): lax.all_to_all(x, ('ctx', 'tp'), split_axis=0, concat_axis=0, tiled=True)  61.8 us
    pallas_call x4, Pallas kernels, project(): pl.pallas_call(functools.partial(project_kernel, count, not kept), grid=(...  29.8 us
    ppermute x6, starting transfers between devices, other_core(): return lax.ppermute(x, 'dp', [(0, 1), (1, 0)])  23.5 us
    all_to_all x3, starting transfers between devices, exchange(): lax.all_to_all(x, ('ctx', 'tp'), split_axis=0, concat_axis=0, tiled=True)  23 us
    dot_general x3, matrix products, contract(): lax.dot_general(left, right, (((0,), (0,)), ((), ())), preferred_element_...  23 us
    pallas_call x2, Pallas kernels, pair(): pl.pallas_call(functools.partial(pair_kernel, extra), grid=(experts // pe...  20.4 us
    all_to_all x3, waiting for transfers between devices, exchange(): lax.all_to_all(x, ('ctx', 'tp'), split_axis=0, concat_axis=0, tiled=True)  11.7 us
    pallas_call x1, Pallas kernels, pack(): pl.pallas_call(pack_kernel, grid=(experts // PACK_PEERS,), out_shape=[jax...  7.35 us
  transfers between devices with their start and end apart: 9, of which 6 were waited for; matrix products, arithmetic and copies ran while one was open for 10% of the time, Pallas kernels for 27%

profile of v11, /device:TPU:0, one launch (start us, length us, event | category | flops | bytes accessed | tf_op | source)
XLA Modules:
  0.0 221.0 jit_solution(6878946763379906192)
XLA Ops:
  0.6 0.1 turn_1.1
  0.7 7.4 %pack.1 = (bf16[64,320,128]{2,1,0:T(8,128)(2,1)}, bf16[64,256,128]{2,1,0:T(8,128)(2,1)}) custom-call(s32[8,128]{1,0:T(8,128)} %bitcast.18, bf16[8,128]{1,0:T(8,128)(2,1)} %bitcast.21, bf16[128,2048]{1,0:T(8,128)(2,1)} %x_ref.1, bf16[128,2048]{1,0:T(8,128)(2,1)} %cot_ref.1), custom_call_target="tpu_custom_call" | custom-call | flops 1207959552 | bytes 9437184 | tf_op jit(solution)/shard_map/pack/pallas_call | solution.py:193
  8.1 61.8 %all_to_all.20.in_ref = bf16[64,320,128]{2,1,0:T(8,128)(2,1)} all-to-all(bf16[64,320,128]{2,1,0:T(8,128)(2,1)} %get-tuple-element.62), channel_id=1, replica_groups=mesh['dp'=2,'ctx'=16,'tp'=4] {'ctx','tp'}, dimensions={0} | all-to-all | bytes 10485760 | tf_op jit(solution)/shard_map/all_to_all | solution.py:483
  69.9 5.9 %all-to-all-start.1 = ((bf16[64,256,128]{2,1,0:T(8,128)(2,1)}), bf16[64,256,128]{2,1,0:T(8,128)(2,1)}, u32[]{:S(2)}, u32[]{:S(2)}) async-start(bf16[64,256,128]{2,1,0:T(8,128)(2,1)} %get-tuple-element.67), calls=%async_computation.1 | async-start | bytes 8388608 | tf_op jit(solution)/shard_map/all_to_all | solution.py:483
  75.8 9.4 %gate_up_a.1 = (bf16[1152,2048]{1,0:T(8,128)(2,1)}, bf16[640,768]{1,0:T(8,128)(2,1)}, bf16[640,768]{1,0:T(8,128)(2,1)}) custom-call(bf16[64,320,128]{2,1,0:T(8,128)(2,1)} %all_to_all.20.in_ref, bf16[2048,768]{1,0:T(8,128)(2,1)} %bitcast.24, bf16[2048,768]{1,0:T(8,128)(2,1)} %bitcast.28), custom_call_target="tpu_custom_call" | custom-call | flops 4026531840 | bytes 13500416 | tf_op jit(solution)/shard_map/gate_up_a/pallas_call | solution.py:288
  85.2 22.9 %collective-permute-start = (bf16[640,768]{1,0:T(8,128)(2,1)}, bf16[640,768]{1,0:T(8,128)(2,1)S(1)}, u32[]{:S(2)}, u32[]{:S(2)}) collective-permute-start(bf16[640,768]{1,0:T(8,128)(2,1)} %get-tuple-element.71.refs_0_), channel_id=1, source_target_pairs={{0,64},{64,0},{1,65},{65,1},{2,66},{66,2},{3,67},{67,3},{4,68},{68... | collective-permute-start | bytes 2949128 | tf_op jit(solution)/shard_map/ppermute | solution.py:487
  108.0 0.0 collective-permute-start.1
  108.0 6.7 %turn_0.1 = (bf16[768,2048]{1,0:T(8,128)(2,1)}, bf16[768,2048]{1,0:T(8,128)(2,1)}, bf16[2048,768]{1,0:T(8,128)(2,1)}) custom-call(bf16[2048,768]{1,0:T(8,128)(2,1)} %bitcast.25, bf16[2048,768]{1,0:T(8,128)(2,1)} %bitcast.29, bf16[768,2048]{1,0:T(8,128)(2,1)} %bitcast.32, ...), custom_call_target="tpu_custom_call", output_to_operand_aliasing={{0}: (3, {}), {1}: (4, {}), {2}: (5, {})} | custom-call | bytes 18874368 | tf_op jit(solution)/shard_map/turn_0/pallas_call | solution.py:254
  114.7 6.1 %back_a.1 = (bf16[1152,2048]{1,0:T(8,128)(2,1)}, bf16[640,768]{1,0:T(8,128)(2,1)}) custom-call(bf16[64,320,128]{2,1,0:T(8,128)(2,1)} %all_to_all.20.in_ref, bf16[2048,768]{1,0:T(8,128)(2,1)} %get-tuple-element.80.refs_0_), custom_call_target="tpu_custom_call" | custom-call | flops 2013265920 | bytes 9371648 | tf_op jit(solution)/shard_map/back_a/pallas_call | solution.py:288
  120.9 0.0 collective-permute-start.2
  120.9 0.0 collective-permute-done.refs_1_
  120.9 0.0 copy-start.9
  120.9 0.0 collective-permute-done.1.refs_3_
  120.9 0.0 copy-start.10
  120.9 2.9 %collective-permute-done.2.refs_5_ = bf16[640,768]{1,0:T(8,128)(2,1)} collective-permute-done((bf16[640,768]{1,0:T(8,128)(2,1)}, bf16[640,768]{1,0:T(8,128)(2,1)}, u32[]{:S(2)}, u32[]{:S(2)}) %collective-permute-start.2) | collective-permute-done | bytes 983072 | tf_op jit(solution)/shard_map/ppermute | solution.py:487
  123.8 0.0 copy-done.9
  123.8 0.0 copy-done.10
  123.8 11.0 %pair_a.1 = (bf16[64,160,128]{2,1,0:T(8,128)(2,1)}, bf16[1152,768]{1,0:T(8,128)(2,1)}, bf16[1152,768]{1,0:T(8,128)(2,1)}, bf16[1152,768]{1,0:T(8,128)(2,1)}, f32[64,128]{1,0:T(8,128)}) custom-call(bf16[640,768]{1,0:T(8,128)(2,1)} %get-tuple-element.71.refs_0_, bf16[640,768]{1,0:T(8,128)(2,1)} %copy-done.9, bf16[640,768]{1,0:T(8,128)(2,1)} %get-tuple-element.72.refs_2_, ...), custom_call_target="tpu_custom_call" | custom-call | flops 4026531840 | bytes 17760256 | tf_op jit(solution)/shard_map/pair_a/pallas_call | solution.py:367
  134.8 0.0 all-to-all-done.1.in_ref
  134.8 10.2 %all-to-all-start.3 = ((bf16[64,160,128]{2,1,0:T(8,128)(2,1)}), bf16[64,160,128]{2,1,0:T(8,128)(2,1)}, u32[]{:S(2)}, u32[]{:S(2)}) async-start(bf16[64,160,128]{2,1,0:T(8,128)(2,1)} %get-tuple-element.99), calls=%async_computation.3 | async-start | bytes 5242880 | tf_op jit(solution)/shard_map/all_to_all | solution.py:483
  145.0 8.1 %gate_up_b.1 = (bf16[1152,2048]{1,0:T(8,128)(2,1)}, bf16[512,768]{1,0:T(8,128)(2,1)}, bf16[512,768]{1,0:T(8,128)(2,1)}) custom-call(bf16[64,256,128]{2,1,0:T(8,128)(2,1)} %all-to-all-done.1.in_ref, bf16[2048,768]{1,0:T(8,128)(2,1)} %bitcast.26, bf16[2048,768]{1,0:T(8,128)(2,1)} %bitcast.30, ...), custom_call_target="tpu_custom_call", output_to_operand_aliasing={{0}: (3, {})} | custom-call | flops 3221225472 | bytes 12058624 | tf_op jit(solution)/shard_map/gate_up_b/pallas_call | solution.py:288
  153.2 6.1 %back_b.1 = (bf16[1152,2048]{1,0:T(8,128)(2,1)}, bf16[512,768]{1,0:T(8,128)(2,1)}) custom-call(bf16[64,256,128]{2,1,0:T(8,128)(2,1)} %all-to-all-done.1.in_ref, bf16[2048,768]{1,0:T(8,128)(2,1)} %get-tuple-element.80.refs_0_, bf16[1152,2048]{1,0:T(8,128)(2,1)} %get-tuple-element.92.refs_1_), custom_call_target="tpu_custom_call", output_to_operand_aliasing={{0}: (2, {})} | custom-call | flops 1610612736 | bytes 8126464 | tf_op jit(solution)/shard_map/back_b/pallas_call | solution.py:288
  159.3 0.0 collective-permute-start.5
  159.3 0.0 copy-done.4
  159.3 0.5 collective-permute-start.3
  159.8 0.1 collective-permute-start.4
  159.9 2.1 collective-permute-done.5.refs_5_
  162.1 0.7 collective-permute-done.3.refs_1_
  162.7 1.1 collective-permute-done.4.refs_3_
  163.9 0.0 copy-done.6
  163.9 0.0 copy-done.7
  163.9 0.9 copy-done.8
  164.8 9.4 %pair_b.1 = (bf16[64,144,128]{2,1,0:T(8,128)(2,1)}, bf16[1152,768]{1,0:T(8,128)(2,1)}, bf16[1152,768]{1,0:T(8,128)(2,1)}, bf16[1152,768]{1,0:T(8,128)(2,1)}) custom-call(bf16[512,768]{1,0:T(8,128)(2,1)} %get-tuple-element.89.refs_0_, bf16[512,768]{1,0:T(8,128)(2,1)} %copy-done.7, ...), custom_call_target="tpu_custom_call", output_to_operand_aliasing={{1}: (9, {}), {2}: (10, {}), {3}: (11, {})} | custom-call | flops 3221225472 | bytes 15466496 | tf_op jit(solution)/shard_map/pair_b/pallas_call | solution.py:367
  174.2 6.2 %all-to-all-done.3.in_ref = bf16[64,160,128]{2,1,0:T(8,128)(2,1)} async-done(((bf16[64,160,128]{2,1,0:T(8,128)(2,1)}), bf16[64,160,128]{2,1,0:T(8,128)(2,1)}, u32[]{:S(2)}, u32[]{:S(2)}) %all-to-all-start.3) | async-done | bytes 2621472 | tf_op jit(solution)/shard_map/all_to_all | solution.py:483
  180.4 6.9 %all-to-all-start.2 = ((bf16[64,144,128]{2,1,0:T(8,128)(2,1)}), bf16[64,144,128]{2,1,0:T(8,128)(2,1)S(1)}, u32[]{:S(2)}, u32[]{:S(2)}) async-start(bf16[64,144,128]{2,1,0:T(8,128)(2,1)} %get-tuple-element.98), calls=%async_computation.2 | async-start | bytes 4718592 | tf_op jit(solution)/shard_map/all_to_all | solution.py:483
  187.3 0.0 copy-start.3
  187.3 0.0 slice-start
  187.3 9.1 %fusion = bf16[1,2048,768]{2,1,0:T(8,128)(2,1)} fusion(bf16[1152,2048]{1,0:T(8,128)(2,1)} %get-tuple-element.104, bf16[1152,768]{1,0:T(8,128)(2,1)} %get-tuple-element.105), kind=kOutput, calls=%fused_computation.3 | convolution fusion | flops 3625451520 | bytes 9633792 | tf_op jit(solution)/shard_map/dot_general | solution.py:36
  196.4 8.3 %fusion.1 = bf16[1,2048,768]{2,1,0:T(8,128)(2,1)} fusion(bf16[1152,2048]{1,0:T(8,128)(2,1)} %get-tuple-element.104, bf16[1152,768]{1,0:T(8,128)(2,1)S(1)} %copy-done.3), kind=kOutput, calls=%fused_computation.4 | convolution fusion | flops 3625451520 | bytes 9633792 | tf_op jit(solution)/shard_map/dot_general | solution.py:36
  204.6 0.0 slice-done.1
  204.6 0.0 copy-start
  204.6 0.0 copy-start.1
  204.7 5.6 %fusion.2 = bf16[1,768,2048]{2,1,0:T(8,128)(2,1)} fusion(bf16[1152,768]{1,0:T(8,128)(2,1)S(1)} %copy-done.2, bf16[1152,2048]{1,0:T(8,128)(2,1)S(1)} %bitcast.34), kind=kOutput, calls=%fused_computation.5 | convolution fusion | flops 3625451520 | bytes 9633792 | tf_op jit(solution)/shard_map/dot_general | solution.py:36
  210.3 0.0 copy-done
  210.3 3.0 %combine_a.1 = (f32[128,2048]{1,0:T(8,128)S(1)}, f32[64,128]{1,0:T(8,128)S(1)}) custom-call(s32[8,128]{1,0:T(8,128)S(1)} %bitcast.19, bf16[64,160,128]{2,1,0:T(8,128)(2,1)} %all-to-all-done.3.in_ref), custom_call_target="tpu_custom_call" | custom-call | flops 335544320 | bytes 2621440 | tf_op jit(solution)/shard_map/combine_a/pallas_call | solution.py:441
  213.3 5.5 %all-to-all-done.2.in_ref.slots_ref = bf16[64,144,128]{2,1,0:T(8,128)(2,1)S(1)} async-done(((bf16[64,144,128]{2,1,0:T(8,128)(2,1)}), bf16[64,144,128]{2,1,0:T(8,128)(2,1)S(1)}, u32[]{:S(2)}, u32[]{:S(2)}) %all-to-all-start.2) | async-done | bytes 2359328 | tf_op jit(solution)/shard_map/all_to_all | solution.py:483
  218.8 0.0 copy-done.1
  218.8 2.2 combine_b.1
  (12 shorter events, 0.0 us)
Async XLA Ops:
  69.9 64.9 %all-to-all-start.1 = ((bf16[64,256,128]{2,1,0:T(8,128)(2,1)}), bf16[64,256,128]{2,1,0:T(8,128)(2,1)}, u32[]{:S(2)}, u32[]{:S(2)}) async-start(bf16[64,256,128]{2,1,0:T(8,128)(2,1)} %get-tuple-element.67), calls=%async_computation.1 | async-start | bytes 8388608 | tf_op jit(solution)/shard_map/all_to_all | solution.py:483
  85.2 35.7 %collective-permute-start = (bf16[640,768]{1,0:T(8,128)(2,1)}, bf16[640,768]{1,0:T(8,128)(2,1)S(1)}, u32[]{:S(2)}, u32[]{:S(2)}) collective-permute-start(bf16[640,768]{1,0:T(8,128)(2,1)} %get-tuple-element.71.refs_0_), channel_id=1, source_target_pairs={{0,64},{64,0},{1,65},{65,1},{2,66},{66,2},{3,67},{67,3},{4,68},{68... | collective-permute-start | bytes 2949128 | tf_op jit(solution)/shard_map/ppermute | solution.py:487
  108.0 12.9 %collective-permute-start.1 = (bf16[640,768]{1,0:T(8,128)(2,1)}, bf16[640,768]{1,0:T(8,128)(2,1)S(1)}, u32[]{:S(2)}, u32[]{:S(2)}) collective-permute-start(bf16[640,768]{1,0:T(8,128)(2,1)} %get-tuple-element.72.refs_2_), channel_id=1, source_target_pairs={{0,64},{64,0},{1,65},{65,1},{2,66},{66,2},{3,67},{67,3},{4,68},{68... | collective-permute-start | bytes 2949128 | tf_op jit(solution)/shard_map/ppermute | solution.py:487
  120.9 2.9 %collective-permute-start.2 = (bf16[640,768]{1,0:T(8,128)(2,1)}, bf16[640,768]{1,0:T(8,128)(2,1)}, u32[]{:S(2)}, u32[]{:S(2)}) collective-permute-start(bf16[640,768]{1,0:T(8,128)(2,1)} %get-tuple-element.81.refs_4_), channel_id=1, source_target_pairs={{0,64},{64,0},{1,65},{65,1},{2,66},{66,2},{3,67},{67,3},{4,68},{68... | collective-permute-start | bytes 2949128 | tf_op jit(solution)/shard_map/ppermute | solution.py:487
  120.9 2.9 %copy-start.9 = (bf16[640,768]{1,0:T(8,128)(2,1)}, bf16[640,768]{1,0:T(8,128)(2,1)S(1)}, u32[]{:S(2)}) copy-start(bf16[640,768]{1,0:T(8,128)(2,1)S(1)} %collective-permute-done.refs_1_) | copy-start | bytes 2949124
  120.9 2.9 %copy-start.10 = (bf16[640,768]{1,0:T(8,128)(2,1)}, bf16[640,768]{1,0:T(8,128)(2,1)S(1)}, u32[]{:S(2)}) copy-start(bf16[640,768]{1,0:T(8,128)(2,1)S(1)} %collective-permute-done.1.refs_3_) | copy-start | bytes 2949124
  134.8 45.6 %all-to-all-start.3 = ((bf16[64,160,128]{2,1,0:T(8,128)(2,1)}), bf16[64,160,128]{2,1,0:T(8,128)(2,1)}, u32[]{:S(2)}, u32[]{:S(2)}) async-start(bf16[64,160,128]{2,1,0:T(8,128)(2,1)} %get-tuple-element.99), calls=%async_computation.3 | async-start | bytes 5242880 | tf_op jit(solution)/shard_map/all_to_all | solution.py:483
  153.2 6.1 %copy-start.4 = (bf16[512,768]{1,0:T(8,128)(2,1)S(1)}, bf16[512,768]{1,0:T(8,128)(2,1)}, u32[]{:S(2)}) copy-start(bf16[512,768]{1,0:T(8,128)(2,1)} %get-tuple-element.89.refs_0_) | copy-start | bytes 2359300
  153.2 6.7 %copy-start.5 = (bf16[512,768]{1,0:T(8,128)(2,1)S(1)}, bf16[512,768]{1,0:T(8,128)(2,1)}, u32[]{:S(2)}) copy-start(bf16[512,768]{1,0:T(8,128)(2,1)} %get-tuple-element.90.refs_2_) | copy-start | bytes 2359300
  159.3 2.7 %collective-permute-start.5 = (bf16[512,768]{1,0:T(8,128)(2,1)}, bf16[512,768]{1,0:T(8,128)(2,1)S(1)}, u32[]{:S(2)}, u32[]{:S(2)}) collective-permute-start(bf16[512,768]{1,0:T(8,128)(2,1)} %get-tuple-element.93.refs_4_), channel_id=1, source_target_pairs={{0,64},{64,0},{1,65},{65,1},{2,66},{66,2},{3,67},{67,3},{4,68},{68... | collective-permute-start | bytes 2359304 | tf_op jit(solution)/shard_map/ppermute | solution.py:487
  159.3 3.4 %collective-permute-start.3 = (bf16[512,768]{1,0:T(8,128)(2,1)S(1)}, bf16[512,768]{1,0:T(8,128)(2,1)S(1)}, u32[]{:S(2)}, u32[]{:S(2)}) collective-permute-start(bf16[512,768]{1,0:T(8,128)(2,1)S(1)} %copy-done.4), channel_id=1, source_target_pairs={{0,64},{64,0},{1,65},{65,1},{2,66},{66,2},{3,67},{67,3},{4,68},{68... | collective-permute-start | bytes 2359304 | tf_op jit(solution)/shard_map/ppermute | solution.py:487
  159.8 4.0 %collective-permute-start.4 = (bf16[512,768]{1,0:T(8,128)(2,1)S(1)}, bf16[512,768]{1,0:T(8,128)(2,1)S(1)}, u32[]{:S(2)}, u32[]{:S(2)}) collective-permute-start(bf16[512,768]{1,0:T(8,128)(2,1)S(1)} %copy-done.5), channel_id=1, source_target_pairs={{0,64},{64,0},{1,65},{65,1},{2,66},{66,2},{3,67},{67,3},{4,68},{68... | collective-permute-start | bytes 2359304 | tf_op jit(solution)/shard_map/ppermute | solution.py:487
  162.1 1.8 copy-start.6
  162.7 1.1 copy-start.7
  163.9 0.9 copy-start.8
  180.4 38.4 %all-to-all-start.2 = ((bf16[64,144,128]{2,1,0:T(8,128)(2,1)}), bf16[64,144,128]{2,1,0:T(8,128)(2,1)S(1)}, u32[]{:S(2)}, u32[]{:S(2)}) async-start(bf16[64,144,128]{2,1,0:T(8,128)(2,1)} %get-tuple-element.98), calls=%async_computation.2 | async-start | bytes 4718592 | tf_op jit(solution)/shard_map/all_to_all | solution.py:483
  187.3 9.1 %copy-start.3 = (bf16[1152,768]{1,0:T(8,128)(2,1)S(1)}, bf16[1152,768]{1,0:T(8,128)(2,1)}, u32[]{:S(2)}) copy-start(bf16[1152,768]{1,0:T(8,128)(2,1)} %get-tuple-element.106) | copy-start | bytes 5308420
  187.3 17.3 %slice-start = ((s8[4718592]{0:T(1024)(128)(4,1)}), s8[4194304]{0:T(1024)(128)(4,1)S(1)}, s32[]{:S(2)}) async-start(s8[4718592]{0:T(1024)(128)(4,1)} %bitcast.33), calls=%async_computation.4 | async-start | bytes 8388608
  196.3 8.3 %slice-start.1 = ((s8[4718592]{0:T(1024)(128)(4,1)}), s8[524288]{0:T(1024)(128)(4,1)S(1)}, s32[]{:S(2)}) async-start(s8[4718592]{0:T(1024)(128)(4,1)} %bitcast.33), calls=%async_computation.5 | async-start | bytes 1048576
  196.4 8.3 %copy-start.2 = (bf16[1152,768]{1,0:T(8,128)(2,1)S(1)}, bf16[1152,768]{1,0:T(8,128)(2,1)}, u32[]{:S(2)}) copy-start(bf16[1152,768]{1,0:T(8,128)(2,1)} %get-tuple-element.107) | copy-start | bytes 5308420
  204.6 5.7 %copy-start = (s32[128,8]{0,1:T(8,128)S(1)}, s32[128,8]{0,1:T(8,128)}, u32[]{:S(2)}) copy-start(s32[128,8]{0,1:T(8,128)} %param.10) | copy-start | bytes 12292
  204.6 14.2 %copy-start.1 = (bf16[128,8]{0,1:T(8,128)(2,1)S(1)}, bf16[128,8]{0,1:T(8,128)(2,1)}, u32[]{:S(2)}) copy-start(bf16[128,8]{0,1:T(8,128)(2,1)} %param.9) | copy-start | bytes 6148

commit v12 on v9

--- a/solution.py
+++ b/solution.py
@@ -278,19 +278,22 @@
 
 
 def turn_kernel(core, count, *refs):
-    ins, outs = refs[:count], refs[-4 * count : -3 * count]
-    held, turned, sems = refs[-3 * count : -2 * count], refs[-2 * count : -count], refs[-count:]
+    ins, outs = refs[:count], refs[-5 * count : -4 * count]
+    held, turned = refs[-4 * count : -3 * count], refs[-3 * count : -2 * count]
+    in_sems, out_sems = refs[-2 * count : -count], refs[-count:]
 
     @pl.when(lax.axis_index("dp") == core)
     def _():
-        for mat, a, b, out, sem in zip(ins, held, turned, outs, sems):
-            load = pltpu.make_async_copy(mat, a, sem)
+        loads = [pltpu.make_async_copy(a, b, sem) for a, b, sem in zip(ins, held, in_sems)]
+        stores = [pltpu.make_async_copy(a, b, sem) for a, b, sem in zip(turned, outs, out_sems)]
+        for load in loads:
             load.start()
+        for load, store, a, b in zip(loads, stores, held, turned):
             load.wait()
             for at in range(0, a.shape[0], 256):
                 b[:, at : at + 256] = a[at : at + 256, :].T
-            store = pltpu.make_async_copy(b, out, sem)
             store.start()
+        for store in stores:
             store.wait()
 
 
@@ -305,7 +308,7 @@
         input_output_aliases={len(mats) + k: k for k in range(len(before))},
         scratch_shapes=[pltpu.VMEM(shape, BF) for shape in shapes]
         + [pltpu.VMEM(shape[::-1], BF) for shape in shapes]
-        + [pltpu.SemaphoreType.DMA] * len(mats),
+        + [pltpu.SemaphoreType.DMA] * (2 * len(mats)),
         compiler_params=pltpu.CompilerParams(vmem_limit_bytes=VMEM),
         cost_estimate=pl.CostEstimate(flops=0, bytes_accessed=sum(4 * a * b for a, b in shapes), transcendentals=0),
         name=name,

time: 216 us -> 216 us (level)
  Pallas kernels: 74.7 us -> 67.9 us
  waiting for transfers between devices: 24 us -> 27.6 us
  starting transfers between devices: 27.6 us -> 30.9 us
    pallas_call x1, Pallas kernels: 13.4 us -> 6.63 us  [turn(): pl.pallas_call(functools.partial(turn_kernel, core, len(mats)), out_shape...]
    all_to_all x3, waiting for transfers between devices: 14.9 us -> 18.7 us  [exchange(): lax.all_to_all(x, ('ctx', 'tp'), split_axis=0, concat_axis=0, tiled=True)]
    ppermute x6, starting transfers between devices: 4.55 us -> 7.8 us  [other_core(): return lax.ppermute(x, 'dp', [(0, 1), (1, 0)])]
  transfers between devices with their start and end apart: 9 -> 9, of which waited for: 9 -> 9; matrix products, arithmetic and copies ran while one was open for 11% -> 11% of each run, Pallas kernels for 29% -> 26%
where the time goes in v12:
time: 216 us; the launch traced here: 214 us
  Pallas kernels  67.9 us (31%)
  blocking collectives  62 us (29%)
  starting transfers between devices  30.9 us (14%)
  waiting for transfers between devices  27.6 us (13%)
  matrix products  23 us (11%)
    all_to_all x1, blocking collectives, exchange(): lax.all_to_all(x, ('ctx', 'tp'), split_axis=0, concat_axis=0, tiled=True)  62 us
    pallas_call x2, Pallas kernels, project(): pl.pallas_call(functools.partial(project_kernel, not kept), grid=(experts...  24.6 us
    all_to_all x3, starting transfers between devices, exchange(): lax.all_to_all(x, ('ctx', 'tp'), split_axis=0, concat_axis=0, tiled=True)  23.1 us
    dot_general x3, matrix products, contract(): lax.dot_general(left, right, (((0,), (0,)), ((), ())), preferred_element_...  23 us
    pallas_call x2, Pallas kernels, pair(): pl.pallas_call(functools.partial(pair_kernel, extra), grid=(experts // pe...  20.4 us
    all_to_all x3, waiting for transfers between devices, exchange(): lax.all_to_all(x, ('ctx', 'tp'), split_axis=0, concat_axis=0, tiled=True)  18.7 us
    ppermute x6, waiting for transfers between devices, other_core(): return lax.ppermute(x, 'dp', [(0, 1), (1, 0)])  8.82 us
    ppermute x6, starting transfers between devices, other_core(): return lax.ppermute(x, 'dp', [(0, 1), (1, 0)])  7.8 us
  transfers between devices with their start and end apart: 9, of which 9 were waited for; matrix products, arithmetic and copies ran while one was open for 11% of the time, Pallas kernels for 26%

profile of v12, /device:TPU:0, one launch (start us, length us, event | category | flops | bytes accessed | tf_op | source)
XLA Modules:
  0.0 213.7 jit_solution(7519161424964476771)
XLA Ops:
  0.6 5.7 %pack_a.1 = bf16[64,320,128]{2,1,0:T(8,128)(2,1)} custom-call(s32[8,128]{1,0:T(8,128)} %bitcast.18, bf16[8,128]{1,0:T(8,128)(2,1)} %bitcast.23, bf16[128,2048]{1,0:T(8,128)(2,1)} %refs_0_, bf16[128,2048]{1,0:T(8,128)(2,1)} %refs_1_), custom_call_target="tpu_custom_call" | custom-call | flops 1342177280 | bytes 5242880 | tf_op jit(solution)/shard_map/pack_a/pallas_call | solution.py:195
  6.3 0.8 ahead_1.1
  7.1 62.0 %all_to_all.20.x_in.cot_in = bf16[64,320,128]{2,1,0:T(8,128)(2,1)} all-to-all(bf16[64,320,128]{2,1,0:T(8,128)(2,1)} %pack_a.1), channel_id=1, replica_groups=mesh['dp'=2,'ctx'=16,'tp'=4] {'ctx','tp'}, dimensions={0} | all-to-all | bytes 10485760 | tf_op jit(solution)/shard_map/all_to_all | solution.py:534
  69.1 4.8 %pack_b_0.1 = bf16[64,256,128]{2,1,0:T(8,128)(2,1)} custom-call(s32[8,128]{1,0:T(8,128)} %bitcast.20, bf16[8,128]{1,0:T(8,128)(2,1)} %bitcast.25, bf16[128,2048]{1,0:T(8,128)(2,1)} %refs_0_, bf16[128,2048]{1,0:T(8,128)(2,1)} %refs_1_, bf16[64,256,128]{2,1,0:T(8,128)(2,1)} %get-tuple-element.70.refs_2_), custom_call_target="tpu_custom_call", output_to_operand_aliasing={{}: (4, {})} | custom-call | flops 536870912 | bytes 4194304 | tf_op jit(solution)/shard_map/pack_b_0/pallas_call | solution.py:257
  73.9 6.4 %all-to-all-start.1 = ((bf16[64,256,128]{2,1,0:T(8,128)(2,1)}), bf16[64,256,128]{2,1,0:T(8,128)(2,1)}, u32[]{:S(2)}, u32[]{:S(2)}) async-start(bf16[64,256,128]{2,1,0:T(8,128)(2,1)} %pack_b_0.1), calls=%async_computation.1 | async-start | bytes 8388608 | tf_op jit(solution)/shard_map/all_to_all | solution.py:534
  80.3 6.6 %turn_0.1 = (bf16[768,2048]{1,0:T(8,128)(2,1)}, bf16[768,2048]{1,0:T(8,128)(2,1)}, bf16[2048,768]{1,0:T(8,128)(2,1)}) custom-call(bf16[2048,768]{1,0:T(8,128)(2,1)} %bitcast.28, bf16[2048,768]{1,0:T(8,128)(2,1)} %bitcast.32, bf16[768,2048]{1,0:T(8,128)(2,1)} %bitcast.36, ...), custom_call_target="tpu_custom_call", output_to_operand_aliasing={{0}: (3, {}), {1}: (4, {}), {2}: (5, {})} | custom-call | bytes 18874368 | tf_op jit(solution)/shard_map/turn_0/pallas_call | solution.py:303
  86.9 13.6 %project_a.1 = (bf16[1152,2048]{1,0:T(8,128)(2,1)}, bf16[1152,2048]{1,0:T(8,128)(2,1)}, bf16[640,768]{1,0:T(8,128)(2,1)}, bf16[640,768]{1,0:T(8,128)(2,1)}, bf16[640,768]{1,0:T(8,128)(2,1)}) custom-call(bf16[64,320,128]{2,1,0:T(8,128)(2,1)} %all_to_all.20.x_in.cot_in, bf16[64,320,128]{2,1,0:T(8,128)(2,1)} %all_to_all.20.x_in.cot_in, ...), custom_call_target="tpu_custom_call" | custom-call | flops 6039797760 | bytes 22872064 | tf_op jit(solution)/shard_map/project_a/pallas_call | solution.py:340
  100.5 3.3 %collective-permute-start = (bf16[640,768]{1,0:T(8,128)(2,1)}, bf16[640,768]{1,0:T(8,128)(2,1)S(1)}, u32[]{:S(2)}, u32[]{:S(2)}) collective-permute-start(bf16[640,768]{1,0:T(8,128)(2,1)} %get-tuple-element.86.refs_0_), channel_id=1, source_target_pairs={{0,64},{64,0},{1,65},{65,1},{2,66},{66,2},{3,67},{67,3},{4,68},{68... | collective-permute-start | bytes 2949128 | tf_op jit(solution)/shard_map/ppermute | solution.py:538
  103.8 0.1 collective-permute-start.1
  103.9 0.4 collective-permute-start.2
  104.3 1.9 collective-permute-done.refs_1_
  106.2 0.0 copy-start.6
  106.2 2.8 %collective-permute-done.1.refs_3_ = bf16[640,768]{1,0:T(8,128)(2,1)S(1)} collective-permute-done((bf16[640,768]{1,0:T(8,128)(2,1)}, bf16[640,768]{1,0:T(8,128)(2,1)S(1)}, u32[]{:S(2)}, u32[]{:S(2)}) %collective-permute-start.1) | collective-permute-done | bytes 983072 | tf_op jit(solution)/shard_map/ppermute | solution.py:538
  109.1 0.0 copy-start.7
  109.1 0.1 collective-permute-done.2.refs_5_
  109.2 0.0 copy-done.6
  109.2 0.8 copy-done.7
  110.0 11.0 %pair_a.1 = (bf16[64,160,128]{2,1,0:T(8,128)(2,1)}, bf16[1152,768]{1,0:T(8,128)(2,1)}, bf16[1152,768]{1,0:T(8,128)(2,1)}, bf16[1152,768]{1,0:T(8,128)(2,1)}, f32[64,128]{1,0:T(8,128)}) custom-call(bf16[640,768]{1,0:T(8,128)(2,1)} %get-tuple-element.86.refs_0_, bf16[640,768]{1,0:T(8,128)(2,1)} %copy-done.6, bf16[640,768]{1,0:T(8,128)(2,1)} %get-tuple-element.87.refs_2_, ...), custom_call_target="tpu_custom_call" | custom-call | flops 4026531840 | bytes 17760256 | tf_op jit(solution)/shard_map/pair_a/pallas_call | solution.py:418
  121.0 7.9 %all-to-all-done.1.x_in.cot_in = bf16[64,256,128]{2,1,0:T(8,128)(2,1)} async-done(((bf16[64,256,128]{2,1,0:T(8,128)(2,1)}), bf16[64,256,128]{2,1,0:T(8,128)(2,1)}, u32[]{:S(2)}, u32[]{:S(2)}) %all-to-all-start.1) | async-done | bytes 4194336 | tf_op jit(solution)/shard_map/all_to_all | solution.py:534
  128.9 9.8 %all-to-all-start.3 = ((bf16[64,160,128]{2,1,0:T(8,128)(2,1)}), bf16[64,160,128]{2,1,0:T(8,128)(2,1)}, u32[]{:S(2)}, u32[]{:S(2)}) async-start(bf16[64,160,128]{2,1,0:T(8,128)(2,1)} %get-tuple-element.103), calls=%async_computation.3 | async-start | bytes 5242880 | tf_op jit(solution)/shard_map/all_to_all | solution.py:534
  138.7 11.0 %project_b.1 = (bf16[1152,2048]{1,0:T(8,128)(2,1)}, bf16[1152,2048]{1,0:T(8,128)(2,1)}, bf16[512,768]{1,0:T(8,128)(2,1)}, bf16[512,768]{1,0:T(8,128)(2,1)}, bf16[512,768]{1,0:T(8,128)(2,1)}) custom-call(bf16[64,256,128]{2,1,0:T(8,128)(2,1)} %all-to-all-done.1.x_in.cot_in, ...), custom_call_target="tpu_custom_call", output_to_operand_aliasing={{0}: (5, {}), {1}: (6, {})} | custom-call | flops 4831838208 | bytes 20185088 | tf_op jit(solution)/shard_map/project_b/pallas_call | solution.py:340
  149.7 3.4 %collective-permute-start.3 = (bf16[512,768]{1,0:T(8,128)(2,1)}, bf16[512,768]{1,0:T(8,128)(2,1)S(1)}, u32[]{:S(2)}, u32[]{:S(2)}) collective-permute-start(bf16[512,768]{1,0:T(8,128)(2,1)} %get-tuple-element.95.refs_0_), channel_id=1, source_target_pairs={{0,64},{64,0},{1,65},{65,1},{2,66},{66,2},{3,67},{67,3},{4,68},{68... | collective-permute-start | bytes 2359304 | tf_op jit(solution)/shard_map/ppermute | solution.py:538
  153.1 0.1 collective-permute-start.4
  153.2 0.4 collective-permute-start.5
  153.7 1.6 collective-permute-done.3.refs_1_
  155.3 2.2 %collective-permute-done.4.refs_3_ = bf16[512,768]{1,0:T(8,128)(2,1)S(1)} collective-permute-done((bf16[512,768]{1,0:T(8,128)(2,1)}, bf16[512,768]{1,0:T(8,128)(2,1)S(1)}, u32[]{:S(2)}, u32[]{:S(2)}) %collective-permute-start.4) | collective-permute-done | bytes 786464 | tf_op jit(solution)/shard_map/ppermute | solution.py:538
  157.5 0.1 collective-permute-done.5.refs_5_
  157.6 0.0 copy-done.4
  157.6 0.8 copy-done.5
  158.4 9.4 %pair_b.1 = (bf16[64,144,128]{2,1,0:T(8,128)(2,1)}, bf16[1152,768]{1,0:T(8,128)(2,1)}, bf16[1152,768]{1,0:T(8,128)(2,1)}, bf16[1152,768]{1,0:T(8,128)(2,1)}) custom-call(bf16[512,768]{1,0:T(8,128)(2,1)} %get-tuple-element.95.refs_0_, bf16[512,768]{1,0:T(8,128)(2,1)} %copy-done.4, ...), custom_call_target="tpu_custom_call", output_to_operand_aliasing={{1}: (9, {}), {2}: (10, {}), {3}: (11, {})} | custom-call | flops 3221225472 | bytes 15466496 | tf_op jit(solution)/shard_map/pair_b/pallas_call | solution.py:418
  167.8 4.6 %all-to-all-done.3.in_ref = bf16[64,160,128]{2,1,0:T(8,128)(2,1)} async-done(((bf16[64,160,128]{2,1,0:T(8,128)(2,1)}), bf16[64,160,128]{2,1,0:T(8,128)(2,1)}, u32[]{:S(2)}, u32[]{:S(2)}) %all-to-all-start.3) | async-done | bytes 2621472 | tf_op jit(solution)/shard_map/all_to_all | solution.py:534
  172.4 6.8 %all-to-all-start.2 = ((bf16[64,144,128]{2,1,0:T(8,128)(2,1)}), bf16[64,144,128]{2,1,0:T(8,128)(2,1)S(1)}, u32[]{:S(2)}, u32[]{:S(2)}) async-start(bf16[64,144,128]{2,1,0:T(8,128)(2,1)} %get-tuple-element.102), calls=%async_computation.2 | async-start | bytes 4718592 | tf_op jit(solution)/shard_map/all_to_all | solution.py:534
  179.3 0.0 copy-start.3
  179.3 0.0 slice-start
  179.3 9.1 %fusion = bf16[1,2048,768]{2,1,0:T(8,128)(2,1)} fusion(bf16[1152,2048]{1,0:T(8,128)(2,1)} %get-tuple-element.108, bf16[1152,768]{1,0:T(8,128)(2,1)} %get-tuple-element.109), kind=kOutput, calls=%fused_computation.3 | convolution fusion | flops 3625451520 | bytes 9633792 | tf_op jit(solution)/shard_map/dot_general | solution.py:36
  188.3 0.0 copy-done.3
  188.3 8.3 %fusion.1 = bf16[1,2048,768]{2,1,0:T(8,128)(2,1)} fusion(bf16[1152,2048]{1,0:T(8,128)(2,1)} %get-tuple-element.108, bf16[1152,768]{1,0:T(8,128)(2,1)S(1)} %copy-done.3), kind=kOutput, calls=%fused_computation.4 | convolution fusion | flops 3625451520 | bytes 9633792 | tf_op jit(solution)/shard_map/dot_general | solution.py:36
  196.6 0.0 slice-done
  196.6 0.0 slice-done.1
  196.6 0.0 copy-done.2
  196.6 0.0 copy-start
  196.6 0.0 copy-start.1
  196.6 5.6 %fusion.2 = bf16[1,768,2048]{2,1,0:T(8,128)(2,1)} fusion(bf16[1152,768]{1,0:T(8,128)(2,1)S(1)} %copy-done.2, bf16[1152,2048]{1,0:T(8,128)(2,1)S(1)} %bitcast.38), kind=kOutput, calls=%fused_computation.5 | convolution fusion | flops 3625451520 | bytes 9633792 | tf_op jit(solution)/shard_map/dot_general | solution.py:36
  202.3 0.0 copy-done
  202.3 3.0 %combine_a.1 = (f32[128,2048]{1,0:T(8,128)S(1)}, f32[64,128]{1,0:T(8,128)S(1)}) custom-call(s32[8,128]{1,0:T(8,128)S(1)} %bitcast.21, bf16[64,160,128]{2,1,0:T(8,128)(2,1)} %all-to-all-done.3.in_ref), custom_call_target="tpu_custom_call" | custom-call | flops 335544320 | bytes 2621440 | tf_op jit(solution)/shard_map/combine_a/pallas_call | solution.py:492
  205.3 6.2 %all-to-all-done.2.in_ref.slots_ref = bf16[64,144,128]{2,1,0:T(8,128)(2,1)S(1)} async-done(((bf16[64,144,128]{2,1,0:T(8,128)(2,1)}), bf16[64,144,128]{2,1,0:T(8,128)(2,1)S(1)}, u32[]{:S(2)}, u32[]{:S(2)}) %all-to-all-start.2) | async-done | bytes 2359328 | tf_op jit(solution)/shard_map/all_to_all | solution.py:534
  211.6 0.0 copy-done.1
  211.6 2.2 %combine_b.1 = (bf16[128,2048]{1,0:T(8,128)(2,1)}, bf16[8,128]{1,0:T(8,128)(2,1)}) custom-call(s32[8,128]{1,0:T(8,128)S(1)} %bitcast.22, bf16[8,128]{1,0:T(8,128)(2,1)S(1)} %bitcast.26, bf16[64,144,128]{2,1,0:T(8,128)(2,1)S(1)} %all-to-all-done.2.in_ref.slots_ref, bf16[64,144,128]{2,1,0:T(8,128)(2,1)S(1)} %all-to-all-done.2.in_ref.slots_ref, ...), custom_call_target="tpu_custom_call" | custom-call | flops 268435456 | bytes 2359296 | tf_op jit(solution)/shard_map/combine_b/pallas_call | solution.py:511
  (5 shorter events, 0.0 us)
Async XLA Ops:
  73.9 55.0 %all-to-all-start.1 = ((bf16[64,256,128]{2,1,0:T(8,128)(2,1)}), bf16[64,256,128]{2,1,0:T(8,128)(2,1)}, u32[]{:S(2)}, u32[]{:S(2)}) async-start(bf16[64,256,128]{2,1,0:T(8,128)(2,1)} %pack_b_0.1), calls=%async_computation.1 | async-start | bytes 8388608 | tf_op jit(solution)/shard_map/all_to_all | solution.py:534
  100.5 5.7 %collective-permute-start = (bf16[640,768]{1,0:T(8,128)(2,1)}, bf16[640,768]{1,0:T(8,128)(2,1)S(1)}, u32[]{:S(2)}, u32[]{:S(2)}) collective-permute-start(bf16[640,768]{1,0:T(8,128)(2,1)} %get-tuple-element.86.refs_0_), channel_id=1, source_target_pairs={{0,64},{64,0},{1,65},{65,1},{2,66},{66,2},{3,67},{67,3},{4,68},{68... | collective-permute-start | bytes 2949128 | tf_op jit(solution)/shard_map/ppermute | solution.py:538
  103.8 5.2 %collective-permute-start.1 = (bf16[640,768]{1,0:T(8,128)(2,1)}, bf16[640,768]{1,0:T(8,128)(2,1)S(1)}, u32[]{:S(2)}, u32[]{:S(2)}) collective-permute-start(bf16[640,768]{1,0:T(8,128)(2,1)} %get-tuple-element.87.refs_2_), channel_id=1, source_target_pairs={{0,64},{64,0},{1,65},{65,1},{2,66},{66,2},{3,67},{67,3},{4,68},{68... | collective-permute-start | bytes 2949128 | tf_op jit(solution)/shard_map/ppermute | solution.py:538
  103.9 5.3 %collective-permute-start.2 = (bf16[640,768]{1,0:T(8,128)(2,1)}, bf16[640,768]{1,0:T(8,128)(2,1)}, u32[]{:S(2)}, u32[]{:S(2)}) collective-permute-start(bf16[640,768]{1,0:T(8,128)(2,1)} %get-tuple-element.88.refs_4_), channel_id=1, source_target_pairs={{0,64},{64,0},{1,65},{65,1},{2,66},{66,2},{3,67},{67,3},{4,68},{68... | collective-permute-start | bytes 2949128 | tf_op jit(solution)/shard_map/ppermute | solution.py:538
  106.2 2.9 %copy-start.6 = (bf16[640,768]{1,0:T(8,128)(2,1)}, bf16[640,768]{1,0:T(8,128)(2,1)S(1)}, u32[]{:S(2)}) copy-start(bf16[640,768]{1,0:T(8,128)(2,1)S(1)} %collective-permute-done.refs_1_) | copy-start | bytes 2949124
  109.1 1.0 copy-start.7
  128.9 43.5 %all-to-all-start.3 = ((bf16[64,160,128]{2,1,0:T(8,128)(2,1)}), bf16[64,160,128]{2,1,0:T(8,128)(2,1)}, u32[]{:S(2)}, u32[]{:S(2)}) async-start(bf16[64,160,128]{2,1,0:T(8,128)(2,1)} %get-tuple-element.103), calls=%async_computation.3 | async-start | bytes 5242880 | tf_op jit(solution)/shard_map/all_to_all | solution.py:534
  149.7 5.6 %collective-permute-start.3 = (bf16[512,768]{1,0:T(8,128)(2,1)}, bf16[512,768]{1,0:T(8,128)(2,1)S(1)}, u32[]{:S(2)}, u32[]{:S(2)}) collective-permute-start(bf16[512,768]{1,0:T(8,128)(2,1)} %get-tuple-element.95.refs_0_), channel_id=1, source_target_pairs={{0,64},{64,0},{1,65},{65,1},{2,66},{66,2},{3,67},{67,3},{4,68},{68... | collective-permute-start | bytes 2359304 | tf_op jit(solution)/shard_map/ppermute | solution.py:538
  153.1 4.4 %collective-permute-start.4 = (bf16[512,768]{1,0:T(8,128)(2,1)}, bf16[512,768]{1,0:T(8,128)(2,1)S(1)}, u32[]{:S(2)}, u32[]{:S(2)}) collective-permute-start(bf16[512,768]{1,0:T(8,128)(2,1)} %get-tuple-element.96.refs_2_), channel_id=1, source_target_pairs={{0,64},{64,0},{1,65},{65,1},{2,66},{66,2},{3,67},{67,3},{4,68},{68... | collective-permute-start | bytes 2359304 | tf_op jit(solution)/shard_map/ppermute | solution.py:538
  153.2 4.4 %collective-permute-start.5 = (bf16[512,768]{1,0:T(8,128)(2,1)}, bf16[512,768]{1,0:T(8,128)(2,1)}, u32[]{:S(2)}, u32[]{:S(2)}) collective-permute-start(bf16[512,768]{1,0:T(8,128)(2,1)} %get-tuple-element.97.refs_4_), channel_id=1, source_target_pairs={{0,64},{64,0},{1,65},{65,1},{2,66},{66,2},{3,67},{67,3},{4,68},{68... | collective-permute-start | bytes 2359304 | tf_op jit(solution)/shard_map/ppermute | solution.py:538
  155.3 2.4 %copy-start.4 = (bf16[512,768]{1,0:T(8,128)(2,1)}, bf16[512,768]{1,0:T(8,128)(2,1)S(1)}, u32[]{:S(2)}) copy-start(bf16[512,768]{1,0:T(8,128)(2,1)S(1)} %collective-permute-done.3.refs_1_) | copy-start | bytes 2359300
  157.5 0.9 copy-start.5
  172.4 39.1 %all-to-all-start.2 = ((bf16[64,144,128]{2,1,0:T(8,128)(2,1)}), bf16[64,144,128]{2,1,0:T(8,128)(2,1)S(1)}, u32[]{:S(2)}, u32[]{:S(2)}) async-start(bf16[64,144,128]{2,1,0:T(8,128)(2,1)} %get-tuple-element.102), calls=%async_computation.2 | async-start | bytes 4718592 | tf_op jit(solution)/shard_map/all_to_all | solution.py:534
  179.3 9.1 %copy-start.3 = (bf16[1152,768]{1,0:T(8,128)(2,1)S(1)}, bf16[1152,768]{1,0:T(8,128)(2,1)}, u32[]{:S(2)}) copy-start(bf16[1152,768]{1,0:T(8,128)(2,1)} %get-tuple-element.110) | copy-start | bytes 5308420
  179.3 17.3 %slice-start = ((s8[4718592]{0:T(1024)(128)(4,1)}), s8[4194304]{0:T(1024)(128)(4,1)S(1)}, s32[]{:S(2)}) async-start(s8[4718592]{0:T(1024)(128)(4,1)} %bitcast.37), calls=%async_computation.4 | async-start | bytes 8388608
  188.3 8.3 %slice-start.1 = ((s8[4718592]{0:T(1024)(128)(4,1)}), s8[524288]{0:T(1024)(128)(4,1)S(1)}, s32[]{:S(2)}) async-start(s8[4718592]{0:T(1024)(128)(4,1)} %bitcast.37), calls=%async_computation.5 | async-start | bytes 1048576
  188.3 8.3 %copy-start.2 = (bf16[1152,768]{1,0:T(8,128)(2,1)S(1)}, bf16[1152,768]{1,0:T(8,128)(2,1)}, u32[]{:S(2)}) copy-start(bf16[1152,768]{1,0:T(8,128)(2,1)} %get-tuple-element.111) | copy-start | bytes 5308420
  196.6 5.7 %copy-start = (s32[128,8]{0,1:T(8,128)S(1)}, s32[128,8]{0,1:T(8,128)}, u32[]{:S(2)}) copy-start(s32[128,8]{0,1:T(8,128)} %param.10) | copy-start | bytes 12292
  196.6 14.9 %copy-start.1 = (bf16[128,8]{0,1:T(8,128)(2,1)S(1)}, bf16[128,8]{0,1:T(8,128)(2,1)}, u32[]{:S(2)}) copy-start(bf16[128,8]{0,1:T(8,128)(2,1)} %param.9) | copy-start | bytes 6148
